TPU v7x, 32 devices: a whole 2x2x4 slice. The times are simulated.
32 devices in a mesh: ctx: 4 (over z), fsdp: 8 (over y, x, core).
Axes of the slice: x: 2, y: 2, z: 4, core: 2. Of those that a mesh axis runs over, the one named last changes fastest.
Arguments:
- hidden: bfloat16 [8, 1536, 2048], P('fsdp', 'ctx'), may hold values from -6 to 6
- token_order: int32 [8, 1536], P('fsdp'), may hold values from 0 to 1535, each once within a row
- lengths: int32 [8, 3], P('fsdp'), may hold values from 1 to 1024, 1536 in all within a row
- routes: int32 [8, 1536, 8], P('fsdp', 'ctx'), may hold values from 0 to 31, all different within a row; in each aligned block of 384 rows (0 to 383, 384 to 767, ..., all dimensions but the last counted through in order) at most 120 rows name the same one
- grad_output: bfloat16 [8, 1536, 2048], P('fsdp', 'ctx'), may hold values from -6 to 6
- w_query: bfloat16 [2048, 2048], P(('ctx', 'fsdp')), may hold values from -0.125 to 0.125
- w_key: bfloat16 [2048, 2048], P(('ctx', 'fsdp')), may hold values from -0.125 to 0.125
- w_value: bfloat16 [2048, 2048], P(('ctx', 'fsdp')), may hold values from -0.125 to 0.125
- w_out: bfloat16 [2048, 2048], P(('ctx', 'fsdp')), may hold values from -1 to 1
- w_router: bfloat16 [2048, 32], P(('ctx', 'fsdp')), may hold values from -0.1875 to 0.1875
- attn_gain: bfloat16 [2048], P(('ctx', 'fsdp')), may hold values from 0.099609375 to 1.8984375
- ffn_gain: bfloat16 [2048], P(('ctx', 'fsdp')), may hold values from 0.099609375 to 1.8984375
- query_gain: bfloat16 [2048], P(('ctx', 'fsdp')), may hold values from 0.099609375 to 1.8984375
- key_gain: bfloat16 [2048], P(('ctx', 'fsdp')), may hold values from 0.099609375 to 1.8984375
- w_gate: bfloat16 [32, 2048, 1024], P('fsdp', 'ctx'), may hold values from -0.125 to 0.125
- w_up: bfloat16 [32, 2048, 1024], P('fsdp', 'ctx'), may hold values from -0.125 to 0.125
- w_down: bfloat16 [32, 1024, 2048], P('fsdp', 'ctx'), may hold values from -0.1875 to 0.1875
Outputs:
- output: bfloat16 [8, 1536, 2048], P('fsdp', 'ctx')
- grad_hidden: float32 [8, 1536, 2048], P('fsdp', 'ctx')
- grad_w_query: float32 [2048, 2048], P(('ctx', 'fsdp'))
- grad_w_key: float32 [2048, 2048], P(('ctx', 'fsdp'))
- grad_w_value: float32 [2048, 2048], P(('ctx', 'fsdp'))
- grad_w_out: float32 [2048, 2048], P(('ctx', 'fsdp'))
- grad_w_router: float32 [2048, 32], P(('ctx', 'fsdp'))
- grad_attn_gain: float32 [2048], P(('ctx', 'fsdp'))
- grad_ffn_gain: float32 [2048], P(('ctx', 'fsdp'))
- grad_query_gain: float32 [2048], P(('ctx', 'fsdp'))
- grad_key_gain: float32 [2048], P(('ctx', 'fsdp'))
- grad_w_gate: float32 [32, 2048, 1024], P('fsdp', 'ctx')
- grad_w_up: float32 [32, 2048, 1024], P('fsdp', 'ctx')
- grad_w_down: float32 [32, 1024, 2048], P('fsdp', 'ctx')
Inputs may be any that keep to these rules, and one draw needn't show every extreme that they name: `token_order`: each row of a group is a permutation of the 1536 packed positions. The 3 lengths of a group add up to 1536; the longest is exactly 1024. `routes`: A token names 8 different experts. Among the rows of one device no expert is named by more than 120 rows, a bound that some block reaches.
All inputs are finite; a program needn't handle non-finite values.
Results may differ from a plain program's by a relative error of at most 0.018.
Values may be sent and summed in bfloat16 or wider, within the bound.
A program may use at most 448 MiB of HBM per device.

v0:
```python
from functools import partial
import math

import jax
import jax.numpy as jnp
from jax import lax
from jax.sharding import PartitionSpec as P

HEAD_DIM = 128


epsilon = 1e-06
rope_base = 10000.0
masked_value = -1e30


def rms_scaled(values, gain):
    return values * lax.rsqrt(jnp.mean(values * values, axis=-1, keepdims=True) + epsilon) * gain


def rotate(values, places):
    row_count = values.shape[0]
    head_count = values.shape[1] // HEAD_DIM
    half_width = HEAD_DIM // 2
    frequency = rope_base ** (-2.0 * jnp.arange(half_width).astype(jnp.float32) / HEAD_DIM)
    angles = places.astype(jnp.float32)[:, None] * frequency[None, :]
    cosine = jnp.cos(angles)[:, None, :]
    sine_part = jnp.sin(angles)[:, None, :]
    split_heads = values.reshape(row_count, head_count, HEAD_DIM)
    first_half = split_heads[:, :, :half_width]
    second_half = split_heads[:, :, half_width:]
    turned = jnp.concatenate(
        [
            first_half * cosine - second_half * sine_part,
            second_half * cosine + first_half * sine_part,
        ],
        axis=-1,
    )
    return turned.reshape(row_count, head_count * HEAD_DIM)


def qk_post(values, gain, places):
    return rotate(rms_scaled(values, gain), places)


def route_weights(logits, chosen):
    router_probs = jax.nn.softmax(logits, axis=-1)
    return jnp.sum(jnp.where(chosen, router_probs[:, None, :], 0.0), axis=-1)


def seq_layout(order_row, seq_lengths):
    seq_ends = jnp.cumsum(seq_lengths)
    seq_ids = jnp.sum((order_row[:, None] >= seq_ends[None, :]).astype(jnp.int32), axis=1)
    starts = seq_ends - seq_lengths
    chosen = seq_ids[:, None] == jnp.arange(seq_lengths.shape[0], dtype=jnp.int32)[None, :]
    seq_start = jnp.sum(jnp.where(chosen, starts[None, :], 0), axis=1)
    return (seq_ids, order_row - seq_start)


def shards(
    hidden,
    token_order,
    lengths,
    routes,
    grad_output,
    w_query,
    w_key,
    w_value,
    w_out,
    w_router,
    attn_gain,
    ffn_gain,
    query_gain,
    key_gain,
    w_gate,
    w_up,
    w_down,
):
    hidden_in = hidden[0].astype(jnp.float32)
    row_count = hidden_in.shape[0]
    model_width = hidden_in.shape[1]
    head_count = model_width // HEAD_DIM
    score_scale = 1.0 / math.sqrt(HEAD_DIM)
    seq_all, place_all = seq_layout(token_order[0], lengths[0])
    first_row = lax.axis_index("ctx") * row_count
    seq_mine = lax.dynamic_slice_in_dim(seq_all, first_row, row_count)
    place_mine = lax.dynamic_slice_in_dim(place_all, first_row, row_count)
    same_seq = seq_mine[:, None] == seq_all[None, :]
    gathered = (
        lax.all_gather(w_query, ("ctx", "fsdp"), axis=0, tiled=True),
        lax.all_gather(w_key, ("ctx", "fsdp"), axis=0, tiled=True),
        lax.all_gather(w_value, ("ctx", "fsdp"), axis=0, tiled=True),
        lax.all_gather(w_out, ("ctx", "fsdp"), axis=0, tiled=True),
        lax.all_gather(w_router, ("ctx", "fsdp"), axis=0, tiled=True),
        lax.all_gather(attn_gain, ("ctx", "fsdp"), axis=0, tiled=True),
        lax.all_gather(ffn_gain, ("ctx", "fsdp"), axis=0, tiled=True),
        lax.all_gather(query_gain, ("ctx", "fsdp"), axis=0, tiled=True),
        lax.all_gather(key_gain, ("ctx", "fsdp"), axis=0, tiled=True),
    )
    (
        full_query,
        full_key,
        full_value,
        full_out,
        full_router,
        gain_attn,
        gain_ffn,
        gain_query,
        gain_key,
    ) = gathered
    gain_attn = gain_attn.astype(jnp.float32)
    gain_ffn = gain_ffn.astype(jnp.float32)
    gain_query = gain_query.astype(jnp.float32)
    gain_key = gain_key.astype(jnp.float32)
    h_one, norm_one_back = jax.vjp(rms_scaled, hidden_in, gain_attn)
    h_one_low = h_one.astype(jnp.bfloat16)
    query_raw = jnp.dot(h_one_low, full_query, preferred_element_type=jnp.float32)
    key_raw = jnp.dot(h_one_low, full_key, preferred_element_type=jnp.float32)
    values_low = jnp.dot(h_one_low, full_value, preferred_element_type=jnp.float32).astype(
        jnp.bfloat16
    )
    query_rot, query_back = jax.vjp(partial(qk_post, places=place_mine), query_raw, gain_query)
    key_rot, key_back = jax.vjp(partial(qk_post, places=place_mine), key_raw, gain_key)
    query_low = query_rot.astype(jnp.bfloat16)
    key_low = key_rot.astype(jnp.bfloat16)
    key_all, value_all = (
        lax.all_gather(key_low, "ctx", axis=0, tiled=True),
        lax.all_gather(values_low, "ctx", axis=0, tiled=True),
    )
    query_heads = query_low.reshape(row_count, head_count, HEAD_DIM)
    key_heads = key_all.reshape(-1, head_count, HEAD_DIM)
    value_heads = value_all.reshape(-1, head_count, HEAD_DIM)

    def scores_of():
        raw_scores = (
            jnp.einsum("thd,khd->htk", query_heads, key_heads, preferred_element_type=jnp.float32)
            * score_scale
        )
        return jnp.where(same_seq[None, :, :], raw_scores, masked_value)

    scores = scores_of()
    row_top = jnp.max(scores, axis=-1, keepdims=True)
    log_total = row_top + jnp.log(jnp.sum(jnp.exp(scores - row_top), axis=-1, keepdims=True))
    probs_low = jnp.exp(scores - log_total).astype(jnp.bfloat16)
    attended = jnp.einsum(
        "htk,khd->thd", probs_low, value_heads, preferred_element_type=jnp.float32
    )
    attended_low = attended.reshape(row_count, model_width).astype(jnp.bfloat16)
    middle = hidden_in + jnp.dot(attended_low, full_out, preferred_element_type=jnp.float32)
    h_two, norm_two_back = jax.vjp(rms_scaled, middle, gain_ffn)
    h_two_low = h_two.astype(jnp.bfloat16)
    logits = jnp.dot(h_two_low, full_router, preferred_element_type=jnp.float32)
    expert_count = full_router.shape[1]
    route_rows = routes[0]
    top_k = route_rows.shape[1]
    chosen = route_rows[:, :, None] == jnp.arange(expert_count, dtype=jnp.int32)[None, None, :]
    picked, route_back = jax.vjp(partial(route_weights, chosen=chosen), logits)
    pair_count = row_count * top_k
    capacity = 5 * row_count * top_k // (4 * expert_count)
    slot_count = expert_count * capacity
    group_size = lax.axis_size("fsdp")
    local_experts = w_gate.shape[0]
    pair_expert = route_rows.reshape(pair_count)
    one_hot = (pair_expert[:, None] == jnp.arange(expert_count, dtype=jnp.int32)[None, :]).astype(
        jnp.int32
    )
    slot_rank = jnp.sum(one_hot * (jnp.cumsum(one_hot, axis=0) - 1), axis=1)
    slot_ids = pair_expert * capacity + slot_rank
    source = (
        jnp.full((slot_count,), pair_count, jnp.int32)
        .at[slot_ids]
        .set(jnp.arange(pair_count, dtype=jnp.int32))
    )
    filled = source < pair_count
    source_pair = jnp.minimum(source, pair_count - 1)
    send_rows = jnp.where(
        filled[:, None], h_two_low[source_pair // top_k], jnp.zeros((), jnp.bfloat16)
    )
    send_rows = send_rows.reshape(group_size, local_experts, capacity, model_width)
    gate_full, up_full, down_full = (
        lax.all_gather(w_gate, "ctx", axis=1, tiled=True),
        lax.all_gather(w_up, "ctx", axis=1, tiled=True),
        lax.all_gather(w_down, "ctx", axis=1, tiled=True),
    )
    arrived_rows = lax.all_to_all(send_rows, "fsdp", split_axis=0, concat_axis=0, tiled=True)
    gate_part = jnp.einsum(
        "secd,edf->secf", arrived_rows, gate_full, preferred_element_type=jnp.float32
    )
    up_part = jnp.einsum(
        "secd,edf->secf", arrived_rows, up_full, preferred_element_type=jnp.float32
    )
    act_part = (jax.nn.silu(gate_part) * up_part).astype(jnp.bfloat16)
    result = jnp.einsum(
        "secf,efd->secd", act_part, down_full, preferred_element_type=jnp.float32
    ).astype(jnp.bfloat16)
    returned = lax.all_to_all(result, "fsdp", split_axis=0, concat_axis=0, tiled=True).reshape(
        slot_count, model_width
    )
    pair_out = returned[slot_ids].reshape(row_count, top_k, model_width)
    output = (middle + jnp.sum(picked[:, :, None] * pair_out, axis=1)).astype(jnp.bfloat16)
    grad_top = grad_output[0].astype(jnp.float32)
    grad_picked = jnp.sum(grad_top[:, None, :] * pair_out, axis=-1)
    grad_pair = (
        (picked[:, :, None] * grad_top[:, None, :])
        .astype(jnp.bfloat16)
        .reshape(pair_count, model_width)
    )
    grad_send = jnp.where(filled[:, None], grad_pair[source_pair], jnp.zeros((), jnp.bfloat16))
    grad_send = grad_send.reshape(group_size, local_experts, capacity, model_width)
    grad_arrived = lax.all_to_all(grad_send, "fsdp", split_axis=0, concat_axis=0, tiled=True)
    sigma = jax.nn.sigmoid(gate_part)
    act_low = (gate_part * sigma * up_part).astype(jnp.bfloat16)
    grad_act = jnp.einsum(
        "secd,efd->secf", grad_arrived, down_full, preferred_element_type=jnp.float32
    )
    grad_gate = (grad_act * up_part * sigma * (1.0 + gate_part * (1.0 - sigma))).astype(
        jnp.bfloat16
    )
    grad_up = (grad_act * gate_part * sigma).astype(jnp.bfloat16)
    grad_back = jnp.einsum(
        "secf,edf->secd", grad_gate, gate_full, preferred_element_type=jnp.float32
    )
    grad_back = (
        grad_back
        + jnp.einsum("secf,edf->secd", grad_up, up_full, preferred_element_type=jnp.float32)
    ).astype(jnp.bfloat16)
    grad_return = lax.all_to_all(
        grad_back, "fsdp", split_axis=0, concat_axis=0, tiled=True
    ).reshape(slot_count, model_width)
    grad_h_two = jnp.sum(
        grad_return[slot_ids].reshape(row_count, top_k, model_width).astype(jnp.float32), axis=1
    )
    (grad_logits,) = route_back(grad_picked)
    grad_logits_low = grad_logits.astype(jnp.bfloat16)
    grad_h_two = grad_h_two + jnp.einsum(
        "te,de->td", grad_logits_low, full_router, preferred_element_type=jnp.float32
    )
    grad_router = jnp.einsum(
        "td,te->de", h_two_low, grad_logits_low, preferred_element_type=jnp.float32
    )
    grad_middle, grad_ffn_gain = norm_two_back(grad_h_two)
    grad_middle = grad_middle + grad_top
    grad_branch = grad_middle.astype(jnp.bfloat16)
    grad_out_w = jnp.einsum(
        "td,te->de", attended_low, grad_branch, preferred_element_type=jnp.float32
    )
    grad_att = jnp.einsum(
        "te,de->td", grad_branch, full_out, preferred_element_type=jnp.float32
    ).astype(jnp.bfloat16)
    grad_att = grad_att.reshape(row_count, head_count, HEAD_DIM)
    scores = scores_of()
    probs_full = jnp.exp(scores - log_total)
    probs_again = probs_full.astype(jnp.bfloat16)
    grad_probs = jnp.einsum(
        "thd,khd->htk", grad_att, value_heads, preferred_element_type=jnp.float32
    )
    spread = jnp.sum(probs_full * grad_probs, axis=-1, keepdims=True)
    grad_scores = (probs_full * (grad_probs - spread)).astype(jnp.bfloat16)
    grad_query = (
        jnp.einsum(
            "htk,khd->thd", grad_scores, key_heads, preferred_element_type=jnp.float32
        ).reshape(row_count, model_width)
        * score_scale
    )
    grad_key_part = (
        jnp.einsum(
            "htk,thd->khd", grad_scores, query_heads, preferred_element_type=jnp.float32
        ).reshape(-1, model_width)
        * score_scale
    )
    grad_value_part = jnp.einsum(
        "htk,thd->khd", probs_again, grad_att, preferred_element_type=jnp.float32
    ).reshape(-1, model_width)
    grad_key, grad_value = (
        lax.psum_scatter(
            grad_key_part.astype(jnp.bfloat16), "ctx", scatter_dimension=0, tiled=True
        ).astype(jnp.float32),
        lax.psum_scatter(
            grad_value_part.astype(jnp.bfloat16), "ctx", scatter_dimension=0, tiled=True
        ).astype(jnp.float32),
    )
    grad_q_raw, grad_q_gain = query_back(grad_query)
    grad_k_raw, grad_k_gain = key_back(grad_key)
    grad_q_low = grad_q_raw.astype(jnp.bfloat16)
    grad_k_low = grad_k_raw.astype(jnp.bfloat16)
    grad_v_low = grad_value.astype(jnp.bfloat16)
    grad_query_w = jnp.einsum(
        "td,te->de", h_one_low, grad_q_low, preferred_element_type=jnp.float32
    )
    grad_key_w = jnp.einsum("td,te->de", h_one_low, grad_k_low, preferred_element_type=jnp.float32)
    grad_value_w = jnp.einsum(
        "td,te->de", h_one_low, grad_v_low, preferred_element_type=jnp.float32
    )
    grad_h_one = jnp.einsum("te,de->td", grad_q_low, full_query, preferred_element_type=jnp.float32)
    grad_h_one = grad_h_one + jnp.einsum(
        "te,de->td", grad_k_low, full_key, preferred_element_type=jnp.float32
    )
    grad_h_one = grad_h_one + jnp.einsum(
        "te,de->td", grad_v_low, full_value, preferred_element_type=jnp.float32
    )
    grad_input_norm, grad_attn_gain = norm_one_back(grad_h_one)
    grad_input = grad_middle + grad_input_norm
    totals = (
        lax.psum_scatter(grad_query_w, ("ctx", "fsdp"), scatter_dimension=0, tiled=True),
        lax.psum_scatter(grad_key_w, ("ctx", "fsdp"), scatter_dimension=0, tiled=True),
        lax.psum_scatter(grad_value_w, ("ctx", "fsdp"), scatter_dimension=0, tiled=True),
        lax.psum_scatter(grad_out_w, ("ctx", "fsdp"), scatter_dimension=0, tiled=True),
        lax.psum_scatter(grad_router, ("ctx", "fsdp"), scatter_dimension=0, tiled=True),
        lax.psum_scatter(grad_attn_gain, ("ctx", "fsdp"), scatter_dimension=0, tiled=True),
        lax.psum_scatter(grad_ffn_gain, ("ctx", "fsdp"), scatter_dimension=0, tiled=True),
        lax.psum_scatter(grad_q_gain, ("ctx", "fsdp"), scatter_dimension=0, tiled=True),
        lax.psum_scatter(grad_k_gain, ("ctx", "fsdp"), scatter_dimension=0, tiled=True),
    )
    grad_down_w = jnp.einsum(
        "secf,secd->efd", act_low, grad_arrived, preferred_element_type=jnp.float32
    )
    grad_gate_w = jnp.einsum(
        "secd,secf->edf", arrived_rows, grad_gate, preferred_element_type=jnp.float32
    )
    grad_up_w = jnp.einsum(
        "secd,secf->edf", arrived_rows, grad_up, preferred_element_type=jnp.float32
    )
    gate_grad, up_grad, down_grad = (
        lax.psum_scatter(
            grad_gate_w.astype(jnp.bfloat16), "ctx", scatter_dimension=1, tiled=True
        ).astype(jnp.float32),
        lax.psum_scatter(
            grad_up_w.astype(jnp.bfloat16), "ctx", scatter_dimension=1, tiled=True
        ).astype(jnp.float32),
        lax.psum_scatter(
            grad_down_w.astype(jnp.bfloat16), "ctx", scatter_dimension=1, tiled=True
        ).astype(jnp.float32),
    )
    return (
        output[None],
        grad_input[None],
        totals[0],
        totals[1],
        totals[2],
        totals[3],
        totals[4],
        totals[5],
        totals[6],
        totals[7],
        totals[8],
        gate_grad,
        up_grad,
        down_grad,
    )


def solution(mesh):
    placed = (
        P("fsdp", "ctx", None),
        P("fsdp", None),
        P("fsdp", None),
        P("fsdp", "ctx", None),
        P("fsdp", "ctx", None),
        P(("ctx", "fsdp"), None),
        P(("ctx", "fsdp"), None),
        P(("ctx", "fsdp"), None),
        P(("ctx", "fsdp"), None),
        P(("ctx", "fsdp"), None),
        P(("ctx", "fsdp")),
        P(("ctx", "fsdp")),
        P(("ctx", "fsdp")),
        P(("ctx", "fsdp")),
        P("fsdp", "ctx", None),
        P("fsdp", "ctx", None),
        P("fsdp", "ctx", None),
    )
    return jax.shard_map(
        shards,
        mesh=mesh,
        in_specs=placed,
        out_specs=(
            P("fsdp", "ctx", None),
            P("fsdp", "ctx", None),
            P(("ctx", "fsdp"), None),
            P(("ctx", "fsdp"), None),
            P(("ctx", "fsdp"), None),
            P(("ctx", "fsdp"), None),
            P(("ctx", "fsdp"), None),
            P(("ctx", "fsdp")),
            P(("ctx", "fsdp")),
            P(("ctx", "fsdp")),
            P(("ctx", "fsdp")),
            P("fsdp", "ctx", None),
            P("fsdp", "ctx", None),
            P("fsdp", "ctx", None),
        ),
        check_vma=False,
    )
```

profile of v0, /device:TPU:0, one launch (start us, length us, event | category | flops | bytes accessed | tf_op | source)
XLA Modules:
  0.0 3951.1 jit_solution(29655878358708534)
XLA Ops:
  12.9 42.6 %all-reduce.13 = (bf16[2048]{0:T(1024)(128)(2,1)S(1)}, bf16[2048]{0:T(1024)(128)(2,1)S(1)}, bf16[2048]{0:T(1024)(128)(2,1)S(1)}, bf16[2048]{0:T(1024)(128)(2,1)S(1)}) all-reduce(bf16[2048]{0:T(1024)(128)(2,1)S(1)} %dynamic-update-slice, bf16[2048]{0:T(1024)(128)(2,1)S(1)} %dynamic-update-slice.2, ...), channel_id=1, replica_groups=mesh['ctx'=4,'fsdp'=8] {'ctx','fsdp'}, use_global_device_ids=true, to_apply=%add.4 | all-reduce | flops 8192 | bytes 32768
  101.9 68.4 %all-gather.15.cloned.1.call-done = bf16[2048,2048]{1,0:T(8,128)(2,1)} async-done(((bf16[64,2048]{1,0:T(8,128)(2,1)}), bf16[2048,2048]{1,0:T(8,128)(2,1)}) %all-gather.15.cloned.1.call-update) | async-done | bytes 8388624 | tf_op jit(solution)/shard_map/all_gather | solution.py:90
  204.0 45.3 %all-gather.11.cloned.1.call-done = bf16[2048,2048]{1,0:T(8,128)(2,1)} async-done(((bf16[64,2048]{1,0:T(8,128)(2,1)}), bf16[2048,2048]{1,0:T(8,128)(2,1)}) %all-gather.11.cloned.1.call-update) | async-done | bytes 8388624 | tf_op jit(solution)/shard_map/all_gather | solution.py:92
  259.9 41.5 %all-gather = bf16[32,64,32]{1,2,0:T(8,128)(2,1)S(1)} all-gather(bf16[1,64,32]{1,2,0:T(8,128)(2,1)S(1)} %bitcast.276), channel_id=1, replica_groups=mesh['ctx'=4,'fsdp'=8] {'ctx','fsdp'}, dimensions={0}, use_global_device_ids=true | all-gather | bytes 135168 | tf_op jit(solution)/shard_map/all_gather | solution.py:94
  328.3 38.0 all-gather.19.cloned.1.call-done
  404.0 78.1 %all-gather.13.cloned.1.call-done = bf16[1536,2048]{1,0:T(8,128)(2,1)} async-done(((bf16[384,2048]{1,0:T(8,128)(2,1)}), bf16[1536,2048]{1,0:T(8,128)(2,1)}) %all-gather.13.cloned.1.call-update) | async-done | bytes 6291472 | tf_op jit(solution)/shard_map/all_gather | solution.py:128
  501.7 59.0 %all-gather.21.cloned.1.call-done = bf16[2048,2048]{1,0:T(8,128)(2,1)} async-done(((bf16[64,2048]{1,0:T(8,128)(2,1)}), bf16[2048,2048]{1,0:T(8,128)(2,1)}) %all-gather.21.cloned.1.call-update) | async-done | bytes 8388624 | tf_op jit(solution)/shard_map/all_gather | solution.py:93
  593.3 35.7 gather_fusion.2
  657.3 172.0 %all-to-all-done = bf16[8,4,120,2048]{3,2,1,0:T(8,128)(2,1)} async-done(((bf16[8,4,120,2048]{3,2,1,0:T(8,128)(2,1)}), bf16[8,4,120,2048]{3,2,1,0:T(8,128)(2,1)}, u32[]{:S(2)}, u32[]{:S(2)}) %all-to-all-start) | async-done | bytes 15728672 | tf_op jit(solution)/shard_map/all_to_all | solution.py:185
  873.9 260.2 %all-gather.23.cloned.1.call-done = bf16[4,2048,1024]{2,1,0:T(8,128)(2,1)} async-done(((bf16[4,512,1024]{2,1,0:T(8,128)(2,1)}), bf16[4,2048,1024]{2,1,0:T(8,128)(2,1)}) %all-gather.23.cloned.1.call-update) | async-done | bytes 16777232 | tf_op jit(solution)/shard_map/all_gather | solution.py:181
  1160.4 260.4 %all-gather.27.cloned.1.call-done = bf16[4,1024,2048]{2,1,0:T(8,128)(2,1)} async-done(((bf16[4,256,2048]{2,1,0:T(8,128)(2,1)}), bf16[4,1024,2048]{2,1,0:T(8,128)(2,1)}) %all-gather.27.cloned.1.call-update) | async-done | bytes 16777232 | tf_op jit(solution)/shard_map/all_gather | solution.py:183
  1420.7 35.5 fusion.20
  1569.3 104.6 %all-to-all-done.1 = bf16[8,4,120,2048]{3,2,1,0:T(8,128)(2,1)} async-done(((bf16[8,4,120,2048]{3,2,1,0:T(8,128)(2,1)}), bf16[8,4,120,2048]{3,2,1,0:T(8,128)(2,1)}, u32[]{:S(2)}, u32[]{:S(2)}) %all-to-all-start.1) | async-done | bytes 15728672 | tf_op jit(solution)/shard_map/all_to_all | solution.py:196
  1725.7 126.5 %all-to-all-done.3 = bf16[8,4,120,2048]{3,2,1,0:T(8,128)(2,1)} async-done(((bf16[8,4,120,2048]{3,2,1,0:T(8,128)(2,1)}), bf16[8,4,120,2048]{3,2,1,0:T(8,128)(2,1)}, u32[]{:S(2)}, u32[]{:S(2)}) %all-to-all-start.3) | async-done | bytes 15728672 | tf_op jit(solution)/shard_map/all_to_all | solution.py:227
  2171.1 41.3 %reduce-scatter.33.cloned.1.call-done = bf16[384,2048]{1,0:T(8,128)(2,1)} async-done(((bf16[1536,2048]{1,0:T(8,128)(2,1)}), bf16[384,2048]{1,0:T(8,128)(2,1)}) %reduce-scatter.33.cloned.1.call-update) | async-done | bytes 1572880
  2222.1 127.6 %reduce-scatter.35.cloned.1.call-done = f32[64,32]{1,0:T(8,128)} async-done(((f32[2048,32]{1,0:T(8,128)}), f32[64,32]{1,0:T(8,128)}) %reduce-scatter.35.cloned.1.call-update) | async-done | bytes 8208
  2373.1 40.8 %all-reduce.12 = (f32[2048]{0:T(1024)S(1)}, f32[2048]{0:T(1024)S(1)}, f32[2048]{0:T(1024)S(1)}, f32[2048]{0:T(1024)S(1)}) all-reduce(f32[2048]{0:T(1024)S(1)} %get-tuple-element.22, f32[2048]{0:T(1024)S(1)} %copy-done.60, f32[2048]{0:T(1024)S(1)} %get-tuple-element.18, ...), channel_id=9, replica_groups=mesh['ctx'=4,'fsdp'=8] {'ctx','fsdp'}, use_global_device_ids=true, to_apply=%region_34.35.clone | all-reduce | flops 8192 | bytes 65536
  2421.5 208.1 %reduce-scatter.25.cloned.1.call-done = bf16[4,512,1024]{2,1,0:T(8,128)(2,1)} async-done(((bf16[4,2048,1024]{2,1,0:T(8,128)(2,1)}), bf16[4,512,1024]{2,1,0:T(8,128)(2,1)}) %reduce-scatter.25.cloned.1.call-update) | async-done | bytes 4194320 | tf_op jit(solution)/shard_map/reduce_scatter | solution.py:324
  2636.2 276.6 %reduce-scatter.27.cloned.1.call-done = bf16[4,512,1024]{2,1,0:T(8,128)(2,1)} async-done(((bf16[4,2048,1024]{2,1,0:T(8,128)(2,1)}), bf16[4,512,1024]{2,1,0:T(8,128)(2,1)}) %reduce-scatter.27.cloned.1.call-update) | async-done | bytes 4194320 | tf_op jit(solution)/shard_map/reduce_scatter | solution.py:327
  2919.5 276.7 %reduce-scatter.29.cloned.1.call-done = bf16[4,256,2048]{2,1,0:T(8,128)(2,1)} async-done(((bf16[4,1024,2048]{2,1,0:T(8,128)(2,1)}), bf16[4,256,2048]{2,1,0:T(8,128)(2,1)}) %reduce-scatter.29.cloned.1.call-update) | async-done | bytes 4194320 | tf_op jit(solution)/shard_map/reduce_scatter | solution.py:330
  3202.9 179.5 %reduce-scatter.23.cloned.1.call-done = f32[64,2048]{1,0:T(8,128)} async-done(((f32[2048,2048]{1,0:T(8,128)}), f32[64,2048]{1,0:T(8,128)}) %reduce-scatter.23.cloned.1.call-update) | async-done | bytes 524304 | tf_op jit(solution)/shard_map/reduce_scatter | solution.py:307
  3382.4 187.2 %reduce-scatter.19.cloned.1.call-done = f32[64,2048]{1,0:T(8,128)} async-done(((f32[2048,2048]{1,0:T(8,128)}), f32[64,2048]{1,0:T(8,128)}) %reduce-scatter.19.cloned.1.call-update) | async-done | bytes 524304 | tf_op jit(solution)/shard_map/reduce_scatter | solution.py:305
  3569.7 187.3 %reduce-scatter.17.cloned.1.call-done = f32[64,2048]{1,0:T(8,128)} async-done(((f32[2048,2048]{1,0:T(8,128)}), f32[64,2048]{1,0:T(8,128)}) %reduce-scatter.17.cloned.1.call-update) | async-done | bytes 524304 | tf_op jit(solution)/shard_map/reduce_scatter | solution.py:304
  3756.9 187.4 %reduce-scatter.21.cloned.1.call-done = f32[64,2048]{1,0:T(8,128)} async-done(((f32[2048,2048]{1,0:T(8,128)}), f32[64,2048]{1,0:T(8,128)}) %reduce-scatter.21.cloned.1.call-update) | async-done | bytes 524304 | tf_op jit(solution)/shard_map/reduce_scatter | solution.py:306
  (338 shorter events, 855.5 us)
Async XLA Ops:
  7.2 84.2 %all-gather.17.cloned.1.call-start = ((), (), s32[]{:S(2)}) async-start(), calls=%async_computation.17 | async-start | bytes 8650752 | tf_op jit(solution)/shard_map/all_gather | solution.py:91
  7.9 162.4 %all-gather.15.cloned.1.call-start = ((), (), s32[]{:S(2)}) async-start(), calls=%async_computation.16 | async-start | bytes 8650752 | tf_op jit(solution)/shard_map/all_gather | solution.py:90
  8.7 240.6 %all-gather.11.cloned.1.call-start = ((), (), s32[]{:S(2)}) async-start(), calls=%async_computation.14 | async-start | bytes 8650752 | tf_op jit(solution)/shard_map/all_gather | solution.py:92
  9.4 357.0 %all-gather.19.cloned.1.call-start = ((), (), s32[]{:S(2)}) async-start(), calls=%async_computation.18 | async-start | bytes 7864320 | tf_op jit(solution)/shard_map/all_gather | solution.py:127
  204.0 278.2 %all-gather.13.cloned.1.call-start = ((), (), s32[]{:S(2)}) async-start(), calls=%async_computation.15 | async-start | bytes 7864320 | tf_op jit(solution)/shard_map/all_gather | solution.py:128
  257.3 303.3 %all-gather.21.cloned.1.call-start = ((), (), s32[]{:S(2)}) async-start(), calls=%async_computation.19 | async-start | bytes 8650752 | tf_op jit(solution)/shard_map/all_gather | solution.py:93
  257.9 589.7 %all-gather.25.cloned.1.call-start = ((), (), s32[]{:S(2)}) async-start(), calls=%async_computation.21 | async-start | bytes 20971520 | tf_op jit(solution)/shard_map/all_gather | solution.py:182
  258.7 875.5 %all-gather.23.cloned.1.call-start = ((), (), s32[]{:S(2)}) async-start(), calls=%async_computation.20 | async-start | bytes 20971520 | tf_op jit(solution)/shard_map/all_gather | solution.py:181
  259.9 307.3 %copy-start.44 = (f32[2048]{0:T(1024)}, f32[2048]{0:T(1024)S(1)}, u32[]{:S(2)}) copy-start(f32[2048]{0:T(1024)S(1)} %convert_element_type.194) | copy-start | bytes 24580
  650.9 178.4 %all-to-all-start = ((bf16[8,4,120,2048]{3,2,1,0:T(8,128)(2,1)}), bf16[8,4,120,2048]{3,2,1,0:T(8,128)(2,1)}, u32[]{:S(2)}, u32[]{:S(2)}) async-start(bf16[8,4,120,2048]{3,2,1,0:T(8,128)(2,1)} %get-tuple-element.58), calls=%async_computation | async-start | bytes 31457280 | tf_op jit(solution)/shard_map/all_to_all | solution.py:185
  656.5 764.2 %all-gather.27.cloned.1.call-start = ((), (), s32[]{:S(2)}) async-start(), calls=%async_computation.22 | async-start | bytes 20971520 | tf_op jit(solution)/shard_map/all_gather | solution.py:183
  829.2 591.5 %all-to-all-start.2 = ((bf16[8,4,120,2048]{3,2,1,0:T(8,128)(2,1)}), bf16[8,4,120,2048]{3,2,1,0:T(8,128)(2,1)}, u32[]{:S(2)}, u32[]{:S(2)}) async-start(bf16[8,4,120,2048]{3,2,1,0:T(8,128)(2,1)} %get-tuple-element.57), calls=%async_computation.2 | async-start | bytes 31457280 | tf_op jit(solution)/shard_map/all_to_all | solution.py:210
  1495.3 178.5 %all-to-all-start.1 = ((bf16[8,4,120,2048]{3,2,1,0:T(8,128)(2,1)}), bf16[8,4,120,2048]{3,2,1,0:T(8,128)(2,1)}, u32[]{:S(2)}, u32[]{:S(2)}) async-start(bf16[8,4,120,2048]{3,2,1,0:T(8,128)(2,1)} %copy.155), calls=%async_computation.1 | async-start | bytes 31457280 | tf_op jit(solution)/shard_map/all_to_all | solution.py:196
  1673.9 178.3 %all-to-all-start.3 = ((bf16[8,4,120,2048]{3,2,1,0:T(8,128)(2,1)}), bf16[8,4,120,2048]{3,2,1,0:T(8,128)(2,1)}, u32[]{:S(2)}, u32[]{:S(2)}) async-start(bf16[8,4,120,2048]{3,2,1,0:T(8,128)(2,1)} %copy.158), calls=%async_computation.3 | async-start | bytes 31457280 | tf_op jit(solution)/shard_map/all_to_all | solution.py:227
  1679.5 442.7 %reduce-scatter.31.cloned.1.call-start = ((), (), s32[]{:S(2)}) async-start(), calls=%async_computation.30 | async-start | bytes 7864320
  1991.4 221.0 %reduce-scatter.33.cloned.1.call-start = ((), (), s32[]{:S(2)}) async-start(), calls=%async_computation.31 | async-start | bytes 7864320
  2021.3 328.5 %reduce-scatter.35.cloned.1.call-start = ((), (), s32[]{:S(2)}) async-start(), calls=%async_computation.32 | async-start | bytes 1081344
  2024.4 605.1 %reduce-scatter.25.cloned.1.call-start = ((), (), s32[]{:S(2)}) async-start(), calls=%async_computation.27 | async-start | bytes 20971520 | tf_op jit(solution)/shard_map/reduce_scatter | solution.py:324
  2049.3 863.6 %reduce-scatter.27.cloned.1.call-start = ((), (), s32[]{:S(2)}) async-start(), calls=%async_computation.28 | async-start | bytes 20971520 | tf_op jit(solution)/shard_map/reduce_scatter | solution.py:327
  2073.9 1122.3 %reduce-scatter.29.cloned.1.call-start = ((), (), s32[]{:S(2)}) async-start(), calls=%async_computation.29 | async-start | bytes 20971520 | tf_op jit(solution)/shard_map/reduce_scatter | solution.py:330
  2098.8 1283.6 %reduce-scatter.23.cloned.1.call-start = ((), (), s32[]{:S(2)}) async-start(), calls=%async_computation.26 | async-start | bytes 17301504 | tf_op jit(solution)/shard_map/reduce_scatter | solution.py:307
  2110.9 1458.8 %reduce-scatter.19.cloned.1.call-start = ((), (), s32[]{:S(2)}) async-start(), calls=%async_computation.24 | async-start | bytes 17301504 | tf_op jit(solution)/shard_map/reduce_scatter | solution.py:305
  2152.6 1604.3 %reduce-scatter.17.cloned.1.call-start = ((), (), s32[]{:S(2)}) async-start(), calls=%async_computation.23 | async-start | bytes 17301504 | tf_op jit(solution)/shard_map/reduce_scatter | solution.py:304
  2171.0 1773.3 %reduce-scatter.21.cloned.1.call-start = ((), (), s32[]{:S(2)}) async-start(), calls=%async_computation.25 | async-start | bytes 17301504 | tf_op jit(solution)/shard_map/reduce_scatter | solution.py:306
  (75 other events, 2169.3 us)
Sparse Core Ops, SparseCore 0:
  10.9 80.4 all-gather.16
  94.2 76.0 all-gather.14
  173.2 76.0 all-gather.10
  251.3 115.0 all-gather.18
  368.3 113.7 all-gather.12
  484.9 75.6 all-gather.20
  562.2 285.3 all-gather.24
  849.2 284.9 all-gather.22
  1135.7 284.9 all-gather.26
  1991.5 107.1 reduce-scatter.30
  2101.0 111.2 reduce-scatter.32
  2214.4 135.2 reduce-scatter.34
  2352.2 277.2 reduce-scatter.24
  2631.8 281.0 reduce-scatter.26
  2915.2 281.0 reduce-scatter.28
  3198.9 183.4 reduce-scatter.22
  3385.1 184.4 reduce-scatter.18
  3572.4 184.4 reduce-scatter.16
  3759.8 184.4 reduce-scatter.20
where the time goes:
time: 3960 us; the launch traced here: 3950 us
  waiting for transfers between devices  2930 us (74%)
  matrix products  452 us (11%)
  local copies, waits for them, and re-layouts  225 us (6%)
  other arithmetic  178 us (4%)
  blocking collectives  125 us (3%)
    reduce_scatter x1, waiting for transfers between devices, shards(): lax.psum_scatter(grad_down_w.astype(jnp.bfloat16), 'ctx', scatter_dimensi...  277 us
    reduce_scatter x1, waiting for transfers between devices, shards(): lax.psum_scatter(grad_up_w.astype(jnp.bfloat16), 'ctx', scatter_dimension...  277 us
    all_gather x1, waiting for transfers between devices, shards(): lax.all_gather(w_down, 'ctx', axis=1, tiled=True)  260 us
    all_gather x1, waiting for transfers between devices, shards(): lax.all_gather(w_gate, 'ctx', axis=1, tiled=True)  260 us
    reduce_scatter x1, waiting for transfers between devices, shards(): lax.psum_scatter(grad_gate_w.astype(jnp.bfloat16), 'ctx', scatter_dimensi...  208 us
    reduce_scatter x1, waiting for transfers between devices, shards(): lax.psum_scatter(grad_value_w, ('ctx', 'fsdp'), scatter_dimension=0, tile...  187 us
    reduce_scatter x1, waiting for transfers between devices, shards(): lax.psum_scatter(grad_query_w, ('ctx', 'fsdp'), scatter_dimension=0, tile...  187 us
    reduce_scatter x1, waiting for transfers between devices, shards(): lax.psum_scatter(grad_key_w, ('ctx', 'fsdp'), scatter_dimension=0, tiled=...  187 us
  transfers between devices with their start and end apart: 23, of which 21 were waited for; matrix products, arithmetic and copies ran while one was open for 16% of the time, Pallas kernels for 0%

commit v1 on v0

--- a/solution.py
+++ b/solution.py
@@ -4,6 +4,8 @@
 import jax
 import jax.numpy as jnp
 from jax import lax
+from jax.experimental import pallas as pl
+from jax.experimental.pallas import tpu as pltpu
 from jax.sharding import PartitionSpec as P
 
 HEAD_DIM = 128
@@ -57,7 +59,7 @@
     return (seq_ids, order_row - seq_start)
 
 
-def shards(
+def general_shards(
     hidden,
     token_order,
     lengths,
@@ -349,6 +351,410 @@
     )
 
 
+def masked_probs(query, key, seq_rows, seq_cols, scale):
+    scores = (
+        lax.dot_general(query, key, (((1,), (1,)), ((), ())), preferred_element_type=jnp.float32)
+        * scale
+    )
+    scores = jnp.where(seq_rows == seq_cols, scores, masked_value)
+    top = jnp.max(scores, axis=-1, keepdims=True)
+    weights = jnp.exp(scores - top)
+    return weights / jnp.sum(weights, axis=-1, keepdims=True)
+
+
+def attend_kernel(scale, seq_rows, seq_cols, query, key, value, out):
+    probs = masked_probs(query[...], key[...], seq_rows[...], seq_cols[...], scale)
+    out[...] = jnp.dot(
+        probs.astype(jnp.bfloat16), value[...], preferred_element_type=jnp.float32
+    ).astype(out.dtype)
+
+
+def attend_back_kernel(
+    scale, seq_rows, seq_cols, query, key, value, grad, grad_query, grad_key, grad_value
+):
+    @pl.when(pl.program_id(1) == 0)
+    def _():
+        grad_key[...] = jnp.zeros_like(grad_key)
+        grad_value[...] = jnp.zeros_like(grad_value)
+
+    probs = masked_probs(query[...], key[...], seq_rows[...], seq_cols[...], scale)
+    grad_probs = lax.dot_general(
+        grad[...], value[...], (((1,), (1,)), ((), ())), preferred_element_type=jnp.float32
+    )
+    spread = jnp.sum(probs * grad_probs, axis=-1, keepdims=True)
+    grad_scores = (probs * (grad_probs - spread)).astype(jnp.bfloat16)
+    grad_query[...] = (
+        jnp.dot(grad_scores, key[...], preferred_element_type=jnp.float32) * scale
+    )
+    grad_key[...] += (
+        lax.dot_general(
+            grad_scores,
+            query[...],
+            (((0,), (0,)), ((), ())),
+            preferred_element_type=jnp.float32,
+        )
+        * scale
+    )
+    grad_value[...] += lax.dot_general(
+        probs.astype(jnp.bfloat16),
+        grad[...],
+        (((0,), (0,)), ((), ())),
+        preferred_element_type=jnp.float32,
+    )
+
+
+def attention_specs(rows, block):
+    per_block = pl.BlockSpec((block, HEAD_DIM), lambda h, i: (i, h))
+    per_head = pl.BlockSpec((rows, HEAD_DIM), lambda h, i: (0, h))
+    seqs = [
+        pl.BlockSpec((block, 1), lambda h, i: (i, 0)),
+        pl.BlockSpec((1, rows), lambda h, i: (0, 0)),
+    ]
+    return per_block, per_head, seqs
+
+
+def attend(seq_ids, query, key, value):
+    rows, width = query.shape
+    block = math.gcd(rows, 256)
+    per_block, per_head, seqs = attention_specs(rows, block)
+    pairs = rows * rows * width
+    return pl.pallas_call(
+        partial(attend_kernel, 1.0 / math.sqrt(HEAD_DIM)),
+        grid=(width // HEAD_DIM, rows // block),
+        in_specs=seqs + [per_block, per_head, per_head],
+        out_specs=per_block,
+        out_shape=jax.ShapeDtypeStruct((rows, width), jnp.bfloat16),
+        cost_estimate=pl.CostEstimate(
+            flops=4 * pairs, bytes_accessed=8 * rows * width, transcendentals=pairs // HEAD_DIM
+        ),
+        compiler_params=pltpu.CompilerParams(vmem_limit_bytes=48 << 20),
+        name="attend",
+    )(seq_ids[:, None], seq_ids[None, :], query, key, value)
+
+
+def attend_back(seq_ids, query, key, value, grad):
+    rows, width = query.shape
+    block = math.gcd(rows, 256)
+    per_block, per_head, seqs = attention_specs(rows, block)
+    pairs = rows * rows * width
+    return pl.pallas_call(
+        partial(attend_back_kernel, 1.0 / math.sqrt(HEAD_DIM)),
+        grid=(width // HEAD_DIM, rows // block),
+        in_specs=seqs + [per_block, per_head, per_head, per_block],
+        out_specs=(per_block, per_head, per_head),
+        out_shape=(jax.ShapeDtypeStruct((rows, width), jnp.float32),) * 3,
+        cost_estimate=pl.CostEstimate(
+            flops=10 * pairs, bytes_accessed=20 * rows * width, transcendentals=pairs // HEAD_DIM
+        ),
+        compiler_params=pltpu.CompilerParams(vmem_limit_bytes=48 << 20),
+        name="attend_back",
+    )(seq_ids[:, None], seq_ids[None, :], query, key, value, grad)
+
+
+def turn(values, cosine, sine, inverse=False):
+    rows, width = values.shape
+    split = values.reshape(rows, width // HEAD_DIM, 2, HEAD_DIM // 2)
+    first, second = split[:, :, 0], split[:, :, 1]
+    cosine = cosine[:, None, :]
+    sine = sine[:, None, :]
+    if inverse:
+        sine = -sine
+    return jnp.stack(
+        [first * cosine - second * sine, second * cosine + first * sine], axis=2
+    ).reshape(rows, width)
+
+
+def tie(array, *others):
+    anywhere = pl.BlockSpec(memory_space=pl.ANY)
+    return pl.pallas_call(
+        lambda *refs: None,
+        in_specs=[anywhere] * (1 + len(others)),
+        out_specs=anywhere,
+        out_shape=jax.ShapeDtypeStruct(array.shape, array.dtype),
+        input_output_aliases={0: 0},
+        name="tie",
+    )(array, *others)
+
+
+def mm(left, right):
+    return jnp.dot(left, right, preferred_element_type=jnp.float32)
+
+
+def mm_t(left, right):
+    return lax.dot_general(
+        left, right, (((1,), (1,)), ((), ())), preferred_element_type=jnp.float32
+    )
+
+
+def t_mm(left, right):
+    return lax.dot_general(
+        left, right, (((0,), (0,)), ((), ())), preferred_element_type=jnp.float32
+    )
+
+
+def plane_shards(
+    hidden,
+    token_order,
+    lengths,
+    routes,
+    grad_output,
+    w_query,
+    w_key,
+    w_value,
+    w_out,
+    w_router,
+    attn_gain,
+    ffn_gain,
+    query_gain,
+    key_gain,
+    w_gate,
+    w_up,
+    w_down,
+):
+    f32, bf16 = jnp.float32, jnp.bfloat16
+    both = ("ctx", "fsdp")
+    planes = lax.axis_size("ctx")
+    columns = lax.axis_size("fsdp")
+    plane = lax.axis_index("ctx")
+    row_count, width = hidden.shape[1:]
+    group_rows = row_count * planes
+    share = width // planes
+    strip = w_query.shape[0]
+    first_row = plane * row_count
+
+    hidden_all = lax.all_gather(hidden[0], "ctx", axis=0, tiled=True)
+    experts = w_router.shape[1]
+    qkv = jnp.stack([w_query, w_key, w_value], axis=1).reshape(strip, 3, planes, share)
+    qkv = qkv.transpose(2, 0, 1, 3).reshape(planes, strip, 3 * share)
+    small = jnp.concatenate(
+        [w_router] + [g[:, None] for g in (attn_gain, ffn_gain, query_gain, key_gain)], axis=1
+    )
+    small_rows = -(-small.size // (3 * share))
+    route_size = routes.size // (3 * share)
+    small_flat = jnp.pad(small.reshape(-1), (0, small_rows * 3 * share - small.size))
+    tail = jnp.concatenate(
+        [small_flat.reshape(small_rows, -1), routes.astype(bf16).reshape(route_size, -1)]
+    )
+    tail = jnp.broadcast_to(tail[None], (planes,) + tail.shape)
+    packed = lax.all_to_all(jnp.concatenate([qkv, tail], axis=1), "ctx", 0, 0, tiled=True)
+    routes_all = packed[:, strip + small_rows :].astype(jnp.int32).reshape(group_rows, -1)
+    packed = lax.all_gather(packed[:, : strip + small_rows], "fsdp", axis=1, tiled=True)
+    packed = packed.reshape(planes, columns, strip + small_rows, 3 * share)
+    qkv = packed[:, :, :strip].reshape(width, 3 * share)
+    small = packed[:, :, strip:].reshape(planes * columns, -1)[:, : small.size]
+    small = small.reshape(width, experts + 4)
+    full_router = small[:, :experts]
+    gain_attn, gain_ffn, gain_query, gain_key = [
+        small[:, experts + i].astype(f32) for i in range(4)
+    ]
+    out_rows = lax.all_gather(w_out, "fsdp", axis=0, tiled=True)
+    def exchange(parts):
+        came = [parts[plane]]
+        for step in range(1, 4):
+            pairs = [(i, i ^ step) for i in range(4)]
+            came.append(lax.ppermute(parts[plane ^ step], "ctx", pairs))
+        came = jnp.stack(came)
+        return [came[plane ^ i] for i in range(4)]
+
+    gate = jnp.concatenate(exchange(w_gate))
+    up = jnp.concatenate(exchange(w_up))
+    down = jnp.concatenate(exchange(w_down))
+    grad_all = lax.all_gather(grad_output[0], "ctx", axis=0, tiled=True)
+
+    seq_ids, places = seq_layout(token_order[0], lengths[0])
+    experts_here = w_gate.shape[0]
+    column_expert = experts_here * jnp.arange(columns, dtype=jnp.int32) + plane
+    named = jnp.any(routes_all[:, :, None] == column_expert[None, None, :], axis=1)
+    named = named.reshape(planes, row_count, columns)
+    capacity = 5 * row_count * routes.shape[2] // (4 * experts)
+    rank = jnp.cumsum(named.astype(jnp.int32), axis=1) - 1
+    position = jnp.where(named, rank, -1).transpose(2, 0, 1)
+    slots = jnp.arange(capacity, dtype=jnp.int32)
+    holds = position[:, :, None, :] == slots[None, None, :, None]
+    select = holds.astype(bf16)
+
+    def dispatch(rows):
+        rows = rows.reshape(planes, row_count, width)
+        picked_rows = jnp.einsum("fbsr,brd->fbsd", select, rows, preferred_element_type=f32)
+        return picked_rows.astype(bf16)
+
+    def combine(rows):
+        rows = rows.reshape(columns, planes, capacity, width)
+        sums = jnp.einsum("fbsr,fbsd->brd", select, rows, preferred_element_type=f32)
+        return sums.reshape(group_rows, width).astype(bf16)
+
+    grad_send = dispatch(grad_all)
+    grad_in = lax.all_to_all(grad_send, "fsdp", 0, 0, tiled=True).reshape(-1, width)
+
+    frequency = rope_base ** (
+        -2.0 * jnp.arange(HEAD_DIM // 2).astype(f32) / HEAD_DIM
+    )
+    angles = places.astype(f32)[:, None] * frequency[None, :]
+    cosine, sine = lax.optimization_barrier((jnp.cos(angles), jnp.sin(angles)))
+    hidden_wide = hidden_all.astype(f32)
+    scale_one = lax.rsqrt(jnp.mean(hidden_wide * hidden_wide, axis=-1, keepdims=True) + epsilon)
+    h_one = (hidden_wide * scale_one * gain_attn).astype(bf16)
+    raw = mm(h_one, qkv)
+    query_raw, key_raw = raw[:, :share], raw[:, share : 2 * share]
+    values = raw[:, 2 * share :].astype(bf16)
+    squares = jnp.stack([jnp.sum(query_raw**2, axis=1), jnp.sum(key_raw**2, axis=1)])
+    squares = lax.psum(squares, "ctx")
+    scales = lax.rsqrt(squares / width + epsilon)[:, :, None]
+    query_hat, key_hat = query_raw * scales[0], key_raw * scales[1]
+    my_query_gain = lax.dynamic_slice_in_dim(gain_query, plane * share, share)
+    my_key_gain = lax.dynamic_slice_in_dim(gain_key, plane * share, share)
+    query = turn(query_hat * my_query_gain, cosine, sine).astype(bf16)
+    key = turn(key_hat * my_key_gain, cosine, sine).astype(bf16)
+    attended = attend(seq_ids, query, key, values)
+    attended = tie(attended, gate, grad_send)
+    branch = lax.psum_scatter(
+        mm(attended, out_rows).astype(bf16), "ctx", scatter_dimension=0, tiled=True
+    )
+    middle = hidden[0].astype(f32) + branch.astype(f32)
+    scale_two = lax.rsqrt(jnp.mean(middle * middle, axis=-1, keepdims=True) + epsilon)
+    middle_hat = middle * scale_two
+    h_two = (middle_hat * gain_ffn).astype(bf16)
+
+    h_all = tie(lax.all_gather(h_two, "ctx", axis=0, tiled=True), grad_in)
+    probs_all = jax.nn.softmax(mm(h_all, full_router), axis=-1)
+    probs = jax.nn.softmax(mm(h_two, full_router), axis=-1)
+    probs_plane = lax.dynamic_index_in_dim(
+        probs_all.reshape(group_rows, columns, experts_here), plane, 2, keepdims=False
+    )
+    rows_in = lax.all_to_all(dispatch(h_all), "fsdp", 0, 0, tiled=True).reshape(-1, width)
+    probs_plane = probs_plane.reshape(planes, row_count, columns).transpose(2, 0, 1)
+    slot_probs = jnp.sum(jnp.where(holds, probs_plane[:, :, None, :], 0.0), axis=3)
+    picked = lax.all_to_all(slot_probs, "fsdp", 0, 0, tiled=True).reshape(-1, 1)
+    gate_pre = mm(rows_in, gate)
+    up_pre = mm(rows_in, up)
+    sigma = jax.nn.sigmoid(gate_pre)
+    silu = gate_pre * sigma
+    act = (silu * up_pre).astype(bf16)
+    grad_raw = mm_t(grad_in, down)
+    grad_act = grad_raw * picked
+    grad_gate = (grad_act * up_pre * sigma * (1.0 + gate_pre * (1.0 - sigma))).astype(bf16)
+    grad_up = (grad_act * silu).astype(bf16)
+    grad_picked = jnp.sum(grad_raw * act.astype(f32), axis=1)
+    grad_rows = (mm_t(grad_gate, gate) + mm_t(grad_up, up)).astype(bf16)
+    grad_rows = lax.all_to_all(
+        grad_rows.reshape(columns, planes * capacity, width), "fsdp", 0, 0, tiled=True
+    )
+    grad_picked = lax.all_to_all(
+        grad_picked.reshape(columns, planes, capacity), "fsdp", 0, 0, tiled=True
+    )
+    act_picked = (act.astype(f32) * picked).astype(bf16)
+    grad_gate_w = t_mm(rows_in, grad_gate).astype(bf16)
+    grad_up_w = t_mm(rows_in, grad_up).astype(bf16)
+
+    def spread_out(whole):
+        parts = whole.reshape(planes, whole.shape[0] // planes, whole.shape[1])
+        return jnp.stack(exchange(parts)).astype(f32)
+
+    gate_grad, up_grad = spread_out(grad_gate_w), spread_out(grad_up_w)
+    grad_rows = tie(grad_rows, gate_grad, up_grad)
+    grad_h_two = lax.psum_scatter(
+        combine(grad_rows), "ctx", scatter_dimension=0, tiled=True
+    ).astype(f32)
+    expert_out = (mm(act, down) * picked).astype(bf16)
+    expert_out = lax.all_to_all(
+        expert_out.reshape(columns, planes * capacity, width), "fsdp", 0, 0, tiled=True
+    )
+    mixed_part = combine(expert_out)
+    mixed = lax.psum_scatter(mixed_part, "ctx", scatter_dimension=0, tiled=True)
+    output = (middle + mixed.astype(f32)).astype(bf16)
+    down_grad = spread_out(t_mm(act_picked, grad_in).astype(bf16))
+
+    u_plane = jnp.sum(jnp.where(holds, grad_picked[..., None], 0.0), axis=2)
+    u_mine = lax.all_to_all(
+        u_plane, "ctx", 1, 1, tiled=True
+    )
+    u_mine = u_mine.reshape(experts, row_count).T
+    grad_logits = probs * (u_mine - jnp.sum(probs * u_mine, axis=-1, keepdims=True))
+    grad_logits = grad_logits.astype(bf16)
+    grad_h_two = grad_h_two + mm_t(grad_logits, full_router)
+    grad_router = t_mm(h_two, grad_logits)
+
+    grad_top = grad_output[0].astype(f32)
+    grad_ffn_gain = jnp.sum(grad_h_two * middle_hat, axis=0)
+    grad_hat = grad_h_two * gain_ffn
+    grad_middle = grad_top + scale_two * (
+        grad_hat - middle_hat * jnp.mean(grad_hat * middle_hat, axis=-1, keepdims=True)
+    )
+    grad_branch = lax.all_gather(grad_middle.astype(bf16), "ctx", axis=0, tiled=True)
+    grad_att = tie(mm_t(grad_branch, out_rows).astype(bf16), mixed_part)
+    grad_query, grad_key, grad_value = attend_back(seq_ids, query, key, values, grad_att)
+    grad_out_w = lax.psum_scatter(
+        t_mm(attended, grad_branch).astype(bf16), "fsdp", scatter_dimension=0, tiled=True
+    ).astype(f32)
+    grad_query = turn(grad_query, cosine, sine, inverse=True)
+    grad_key = turn(grad_key, cosine, sine, inverse=True)
+    grad_q_gain = jnp.sum(grad_query * query_hat, axis=0)
+    grad_k_gain = jnp.sum(grad_key * key_hat, axis=0)
+    grad_query = grad_query * my_query_gain
+    grad_key = grad_key * my_key_gain
+    dots = jnp.stack(
+        [jnp.sum(grad_query * query_hat, axis=1), jnp.sum(grad_key * key_hat, axis=1)]
+    )
+    dots = (lax.psum(dots, "ctx") / width)[:, :, None]
+    grad_qkv = jnp.concatenate(
+        [
+            scales[0] * (grad_query - query_hat * dots[0]),
+            scales[1] * (grad_key - key_hat * dots[1]),
+            grad_value,
+        ],
+        axis=1,
+    ).astype(bf16)
+    grad_qkv = tie(grad_qkv, down_grad, mixed)
+    grad_part = mm_t(grad_qkv, qkv)
+    grad_h_one = lax.psum_scatter(
+        grad_part.astype(bf16), "ctx", scatter_dimension=0, tiled=True
+    ).astype(f32)
+    grad_attn_gain = jnp.sum(grad_part * (hidden_wide * scale_one), axis=0)
+    grad_qkv_w = t_mm(h_one, grad_qkv).reshape(planes, columns, strip, 3 * share)
+    grad_qkv_w = lax.all_to_all(
+        grad_qkv_w.transpose(1, 0, 2, 3).astype(bf16), "fsdp", 0, 0, tiled=True
+    )
+    grad_qkv_w = jnp.sum(grad_qkv_w.astype(f32), axis=0).astype(bf16)
+    grad_qkv_w = lax.all_to_all(grad_qkv_w, "ctx", 0, 0, tiled=True)
+    grad_qkv_w = grad_qkv_w.reshape(planes, strip, 3, share).transpose(2, 1, 0, 3)
+    grad_qkv_w = grad_qkv_w.reshape(3, strip, width).astype(f32)
+
+    x_hat = hidden[0].astype(f32)
+    scale_mine = lax.rsqrt(jnp.mean(x_hat * x_hat, axis=-1, keepdims=True) + epsilon)
+    x_hat = x_hat * scale_mine
+    grad_hat = grad_h_one * gain_attn
+    grad_input = grad_middle + scale_mine * (
+        grad_hat - x_hat * jnp.mean(grad_hat * x_hat, axis=-1, keepdims=True)
+    )
+
+    def summed(arrays):
+        parts = jnp.concatenate(
+            [x.reshape(planes * columns, -1) for x in arrays], axis=1
+        )
+        return jnp.sum(lax.all_to_all(parts, both, 0, 0, tiled=True), axis=0)
+
+    totals = summed([grad_router, grad_ffn_gain])
+    own = jnp.arange(planes)[:, None] == plane
+    gains = [jnp.where(own, g[None], 0.0) for g in (grad_q_gain, grad_k_gain)]
+    gains = summed([grad_attn_gain] + gains)
+    return (
+        output[None],
+        grad_input[None],
+        grad_qkv_w[0],
+        grad_qkv_w[1],
+        grad_qkv_w[2],
+        grad_out_w,
+        totals[: strip * experts].reshape(strip, experts),
+        gains[:strip],
+        totals[strip * experts :],
+        gains[strip : 2 * strip],
+        gains[2 * strip :],
+        gate_grad,
+        up_grad,
+        down_grad,
+    )
+
+
 def solution(mesh):
     placed = (
         P("fsdp", "ctx", None),
@@ -369,6 +775,14 @@
         P("fsdp", "ctx", None),
         P("fsdp", "ctx", None),
     )
+
+    def shards(*operands):
+        experts_here = operands[14].shape[0]
+        heads = operands[0].shape[2] // HEAD_DIM
+        planes = mesh.shape["ctx"]
+        whole_experts = experts_here == planes and heads % planes == 0
+        return (plane_shards if whole_experts else general_shards)(*operands)
+
     return jax.shard_map(
         shards,
         mesh=mesh,

time: 3960 us -> 2100 us (0.53)
  waiting for transfers between devices: 2930 us -> 1220 us
  local copies, waits for them, and re-layouts: 225 us -> 112 us
  matrix products: 452 us -> 346 us
  starting transfers between devices: 23.4 us -> 113 us
  Pallas kernels: 0 us -> 73.7 us
  other arithmetic: 178 us -> 113 us
    reduce_scatter x7 -> x5, waiting for transfers between devices: 1500 us -> 179 us  [the longest x1 102 us: plane_shards(): lax.psum_scatter(mm(attended, out_rows).astype(bf16), 'ctx', scatter_dime...]
    all_gather x9 -> x6, waiting for transfers between devices: 853 us -> 173 us  [the longest x1 90.9 us: plane_shards(): grad_all = lax.all_gather(grad_output[0], 'ctx', axis=0, tiled=True)]
    ppermute x0 -> x18, waiting for transfers between devices: none -> 617 us  [exchange(): came.append(lax.ppermute(parts[plane ^ step], 'ctx', pairs))]
    unnamed x22 -> x11, waiting for transfers between devices: 174 us -> 1.52 us
    all_to_all x4 -> x10, waiting for transfers between devices: 403 us -> 253 us  [the longest x1 84.5 us: plane_shards(): lax.all_to_all(expert_out.reshape(columns, planes * capacity, width), 'fs...]
    gather x4 -> x0, local copies, waits for them, and re-layouts: 114 us -> none  [the longest x1 35.7 us: shards(): grad_pair[source_pair]]
    dot_general x29 -> x23, matrix products: 450 us -> 346 us  [the longest x6 112 us: mm_t(): lax.dot_general(left, right, (((1,), (1,)), ((), ())), preferred_element_...]
    unnamed x2 -> x0, blocking collectives: 83.4 us -> none
  transfers between devices with their start and end apart: 23 -> 39, of which waited for: 21 -> 21; matrix products, arithmetic and copies ran while one was open for 16% -> 16% of each run, Pallas kernels for 0% -> 4%
where the time goes in v1:
time: 2100 us
  waiting for transfers between devices  1220 us (58%)
  matrix products  346 us (16%)
  starting transfers between devices  113 us (5%)
  other arithmetic  113 us (5%)
  local copies, waits for them, and re-layouts  112 us (5%)
  blocking collectives  97.7 us (5%)
  Pallas kernels  73.7 us (4%)
    ppermute x18, waiting for transfers between devices, exchange(): came.append(lax.ppermute(parts[plane ^ step], 'ctx', pairs))  617 us
    dot_general x6, matrix products, mm_t(): lax.dot_general(left, right, (((1,), (1,)), ((), ())), preferred_element_...  112 us
    reduce_scatter x1, waiting for transfers between devices, plane_shards(): lax.psum_scatter(mm(attended, out_rows).astype(bf16), 'ctx', scatter_dime...  102 us
    dot_general x7, matrix products, mm(): return jnp.dot(left, right, preferred_element_type=jnp.float32)  94.4 us
    all_gather x1, waiting for transfers between devices, plane_shards(): grad_all = lax.all_gather(grad_output[0], 'ctx', axis=0, tiled=True)  90.9 us
    dot_general x6, matrix products, t_mm(): lax.dot_general(left, right, (((0,), (0,)), ((), ())), preferred_element_...  87.4 us
    all_to_all x1, waiting for transfers between devices, plane_shards(): lax.all_to_all(expert_out.reshape(columns, planes * capacity, width), 'fs...  84.5 us
    reduce_scatter x1, waiting for transfers between devices, plane_shards(): lax.psum_scatter(combine(grad_rows), 'ctx', scatter_dimension=0, tiled=True)  77.4 us
  transfers between devices with their start and end apart: 39, of which 21 were waited for; matrix products, arithmetic and copies ran while one was open for 16% of the time, Pallas kernels for 4%

profile of v1, /device:TPU:0, one launch (start us, length us, event | category | flops | bytes accessed | tf_op | source)
XLA Modules:
  0.0 2096.2 jit_solution(6937510403264898607)
XLA Ops:
  17.3 53.9 %all_to_all.68 = bf16[4,68,1536]{2,1,0:T(8,128)(2,1)S(1)} all-to-all(bf16[4,68,1536]{2,1,0:T(8,128)(2,1)S(1)} %pad_maximum_fusion.14), channel_id=1, replica_groups=mesh['ctx'=4,'fsdp'=8] {'ctx'}, dimensions={0} | all-to-all | bytes 1671168 | tf_op jit(solution)/shard_map/all_to_all | solution.py:539
  84.1 86.9 %collective-permute-done = bf16[512,1024]{1,0:T(8,128)(2,1)} collective-permute-done((bf16[512,1024]{1,0:T(8,128)(2,1)}, bf16[512,1024]{1,0:T(8,128)(2,1)}, u32[]{:S(2)}, u32[]{:S(2)}) %collective-permute-start) | collective-permute-done | bytes 1048608 | tf_op jit(solution)/shard_map/ppermute | solution.py:555
  171.1 64.8 %collective-permute-done.1 = bf16[512,1024]{1,0:T(8,128)(2,1)} collective-permute-done((bf16[512,1024]{1,0:T(8,128)(2,1)S(1)}, bf16[512,1024]{1,0:T(8,128)(2,1)}, u32[]{:S(2)}, u32[]{:S(2)}) %collective-permute-start.1) | collective-permute-done | bytes 1048608 | tf_op jit(solution)/shard_map/ppermute | solution.py:555
  250.8 90.9 %all-gather.19.cloned.1.call-done = bf16[1,1536,2048]{2,1,0:T(8,128)(2,1)} async-done(((bf16[1,384,2048]{2,1,0:T(8,128)(2,1)}), bf16[1,1536,2048]{2,1,0:T(8,128)(2,1)}) %all-gather.19.cloned.1.call-update) | async-done | bytes 6291472 | tf_op jit(solution)/shard_map/all_gather | solution.py:562
  355.9 32.9 %all-gather.9.cloned.1.call-done = bf16[4,528,1536]{2,0,1:T(4,128)(2,1)} async-done(((bf16[4,66,1536]{2,0,1:T(4,128)(2,1)}), bf16[4,528,1536]{2,0,1:T(4,128)(2,1)}) %all-gather.9.cloned.1.call-update) | async-done | bytes 6488080 | tf_op jit(solution)/shard_map/all_gather | solution.py:541
  467.4 28.0 %attend.1.refs_0_ = bf16[1536,512]{1,0:T(8,128)(2,1)S(1)} custom-call(s32[1536,1]{1,0:T(8,128)S(1)} %copy-done.7, s32[1,1536]{1,0:T(1,128)S(1)} %broadcast_in_dim.154.seq_cols, bf16[1536,512]{1,0:T(8,128)(2,1)S(1)} %copy.253.query, bf16[1536,512]{1,0:T(8,128)(2,1)S(1)} %copy.254.key, bf16[1536,512]{1,0:T(8,128)(2,1)} %slice.240.value), custom_call_target="tpu_custom_call" | custom-call | flops 4831838208 | bytes 6291456 | tf_op jit(solution)/shard_map/attend/pallas_call | solution.py:421
  511.0 101.9 %reduce-scatter.6.cloned.1.call-done = bf16[384,2048]{1,0:T(8,128)(2,1)} async-done(((bf16[1536,2048]{1,0:T(8,128)(2,1)}), bf16[384,2048]{1,0:T(8,128)(2,1)}) %reduce-scatter.6.cloned.1.call-update) | async-done | bytes 1572880 | tf_op jit(solution)/shard_map/reduce_scatter | solution.py:610
  617.1 66.6 %all-to-all-done.1 = bf16[8,4,120,2048]{3,2,1,0:T(8,128)(2,1)} async-done(((bf16[8,4,120,2048]{3,2,1,0:T(8,128)(2,1)}), bf16[8,4,120,2048]{3,2,1,0:T(8,128)(2,1)}, u32[]{:S(2)}, u32[]{:S(2)}) %all-to-all-start.1) | async-done | bytes 15728672 | tf_op jit(solution)/shard_map/all_to_all | solution.py:587
  683.7 49.4 %all-gather.13.cloned.1.call-done.refs_0_ = bf16[1536,2048]{1,0:T(8,128)(2,1)} async-done(((bf16[384,2048]{1,0:T(8,128)(2,1)}), bf16[1536,2048]{1,0:T(8,128)(2,1)}) %all-gather.13.cloned.1.call-update) | async-done | bytes 6291472 | tf_op jit(solution)/shard_map/all_gather | solution.py:618
  777.1 41.1 %collective-permute-done.3 = bf16[512,1024]{1,0:T(8,128)(2,1)S(1)} collective-permute-done((bf16[512,1024]{1,0:T(8,128)(2,1)S(1)}, bf16[512,1024]{1,0:T(8,128)(2,1)S(1)}, u32[]{:S(2)}, u32[]{:S(2)}) %collective-permute-start.3) | collective-permute-done | bytes 1048608 | tf_op jit(solution)/shard_map/ppermute | solution.py:555
  818.6 91.2 %collective-permute-done.4 = bf16[512,1024]{1,0:T(8,128)(2,1)S(1)} collective-permute-done((bf16[512,1024]{1,0:T(8,128)(2,1)S(1)}, bf16[512,1024]{1,0:T(8,128)(2,1)S(1)}, u32[]{:S(2)}, u32[]{:S(2)}) %collective-permute-start.4) | collective-permute-done | bytes 1048608 | tf_op jit(solution)/shard_map/ppermute | solution.py:555
  912.4 41.6 %collective-permute-done.7 = bf16[256,2048]{1,0:T(8,128)(2,1)S(1)} collective-permute-done((bf16[256,2048]{1,0:T(8,128)(2,1)S(1)}, bf16[256,2048]{1,0:T(8,128)(2,1)S(1)}, u32[]{:S(2)}, u32[]{:S(2)}) %collective-permute-start.7) | collective-permute-done | bytes 1048608 | tf_op jit(solution)/shard_map/ppermute | solution.py:555
  1006.4 32.3 %fusion = (f32[3840]{0:T(1024)S(1)}, bf16[3840,1024]{0,1:T(8,128)(2,1)}, f32[3840,1024]{0,1:T(8,128)}) fusion(f32[3840,1024]{0,1:T(8,128)} %fusion.42, f32[3840,1024]{0,1:T(8,128)} %fusion.65, bf16[3840,2048]{1,0:T(8,128)(2,1)} %bitcast.38.refs_1_, bf16[256,2048]{1,0:T(8,128)(2,1)} %get-tuple-element.178, bf16[256,2048]{1,0:T(8,128)(2,1)} %get-tuple-element.179, ...), kind=kOutput, calls=%fused_computation.4 | convolution fusion | flops 16158289920 | bytes 74988544 | tf_op jit(solution)/shard_map/dot_general | solution.py:484
  1078.9 24.5 %fusion.64 = f32[3840,2048]{1,0:T(8,128)} fusion(bf16[3840,1024]{0,1:T(8,128)(2,1)S(1)} %get-tuple-element.130, bf16[512,1024]{1,0:T(8,128)(2,1)S(1)} %copy-done.29, bf16[512,1024]{1,0:T(8,128)(2,1)S(1)} %copy-done.31, bf16[512,1024]{1,0:T(8,128)(2,1)} %copy-done.32, bf16[512,1024]{1,0:T(8,128)(2,1)S(1)} %copy-done.27), kind=kOutput, calls=%fused_computation.218 | convolution fusion | flops 16122904576 | bytes 43515904 | tf_op jit(solution)/shard_map/dot_general | solution.py:484
  1103.4 26.8 %add_convert_fusion = bf16[3840,2048]{1,0:T(8,128)(2,1)} fusion(f32[3840,2048]{1,0:T(8,128)} %fusion.64, bf16[3840,1024]{0,1:T(8,128)(2,1)} %get-tuple-element.129, bf16[512,1024]{1,0:T(8,128)(2,1)} %get-tuple-element.162, bf16[512,1024]{1,0:T(8,128)(2,1)} %get-tuple-element.163, bf16[512,1024]{1,0:T(8,128)(2,1)} %get-tuple-element.164, ...), kind=kOutput, calls=%fused_computation | convolution fusion | flops 16138633216 | bytes 59244544 | tf_op jit(solution)/shard_map/dot_general | solution.py:484
  1186.6 41.3 %collective-permute-start.12 = (bf16[512,1024]{1,0:T(8,128)(2,1)S(1)}, bf16[512,1024]{1,0:T(8,128)(2,1)S(1)}, u32[]{:S(2)}, u32[]{:S(2)}) collective-permute-start(bf16[512,1024]{1,0:T(8,128)(2,1)S(1)} %get-tuple-element.152), channel_id=1, source_target_pairs={{0,8},{8,0},{16,24},{24,16},{1,9},{9,1},{17,25},{25,17},{2,10},{10... | collective-permute-start | bytes 3145736 | tf_op jit(solution)/shard_map/ppermute | solution.py:555
  1227.9 66.9 %collective-permute-done.10 = bf16[512,1024]{1,0:T(8,128)(2,1)S(1)} collective-permute-done((bf16[512,1024]{1,0:T(8,128)(2,1)S(1)}, bf16[512,1024]{1,0:T(8,128)(2,1)S(1)}, u32[]{:S(2)}, u32[]{:S(2)}) %collective-permute-start.10) | collective-permute-done | bytes 1048608 | tf_op jit(solution)/shard_map/ppermute | solution.py:555
  1295.8 43.3 %collective-permute-done.13 = bf16[512,1024]{1,0:T(8,128)(2,1)S(1)} collective-permute-done((bf16[512,1024]{1,0:T(8,128)(2,1)S(1)}, bf16[512,1024]{1,0:T(8,128)(2,1)S(1)}, u32[]{:S(2)}, u32[]{:S(2)}) %collective-permute-start.13) | collective-permute-done | bytes 1048608 | tf_op jit(solution)/shard_map/ppermute | solution.py:555
  1394.8 77.4 %reduce-scatter.10.cloned.1.call-done = bf16[384,2048]{1,0:T(8,128)(2,1)} async-done(((bf16[1536,2048]{1,0:T(8,128)(2,1)}), bf16[384,2048]{1,0:T(8,128)(2,1)}) %reduce-scatter.10.cloned.1.call-update) | async-done | bytes 1572880 | tf_op jit(solution)/shard_map/reduce_scatter | solution.py:655
  1480.8 84.5 %all-to-all-done.4 = bf16[8,480,2048]{2,1,0:T(8,128)(2,1)} async-done(((bf16[8,480,2048]{2,1,0:T(8,128)(2,1)}), bf16[8,480,2048]{2,1,0:T(8,128)(2,1)}, u32[]{:S(2)}, u32[]{:S(2)}) %all-to-all-start.4) | async-done | bytes 15728672 | tf_op jit(solution)/shard_map/all_to_all | solution.py:659
  1605.0 44.5 %collective-permute-done.17 = bf16[256,2048]{1,0:T(8,128)(2,1)S(1)} collective-permute-done((bf16[256,2048]{1,0:T(8,128)(2,1)S(1)}, bf16[256,2048]{1,0:T(8,128)(2,1)S(1)}, u32[]{:S(2)}, u32[]{:S(2)}) %collective-permute-start.17) | collective-permute-done | bytes 1048608 | tf_op jit(solution)/shard_map/ppermute | solution.py:555
  1649.6 136.5 %collective-permute-done.16 = bf16[256,2048]{1,0:T(8,128)(2,1)S(1)} collective-permute-done((bf16[256,2048]{1,0:T(8,128)(2,1)S(1)}, bf16[256,2048]{1,0:T(8,128)(2,1)S(1)}, u32[]{:S(2)}, u32[]{:S(2)}) %collective-permute-start.16) | collective-permute-done | bytes 1048608 | tf_op jit(solution)/shard_map/ppermute | solution.py:555
  1802.8 45.7 %attend_back.1 = (f32[1536,512]{1,0:T(8,128)}, f32[1536,512]{1,0:T(8,128)}, f32[1536,512]{1,0:T(8,128)}) custom-call(s32[1536,1]{1,0:T(8,128)S(1)} %copy-done.8, s32[1,1536]{1,0:T(1,128)S(1)} %broadcast_in_dim.154.seq_cols, bf16[1536,512]{1,0:T(8,128)(2,1)S(1)} %copy-done.6, bf16[1536,512]{1,0:T(8,128)(2,1)S(1)} %copy-done.4, ...), custom_call_target="tpu_custom_call" | custom-call | flops 12079595520 | bytes 15728640 | tf_op jit(solution)/shard_map/attend_back/pallas_call | solution.py:440
  1954.0 70.4 %all-to-all-done.8 = bf16[8,4,64,1536]{3,2,1,0:T(8,128)(2,1)} async-done(((bf16[8,4,64,1536]{3,2,1,0:T(8,128)(2,1)}), bf16[8,4,64,1536]{3,2,1,0:T(8,128)(2,1)}, u32[]{:S(2)}, u32[]{:S(2)}) %all-to-all-start.8) | async-done | bytes 6291488 | tf_op jit(solution)/shard_map/all_to_all | solution.py:714
  (424 shorter events, 637.1 us)
Async XLA Ops:
  7.2 239.5 %all-gather.17.cloned.1.call-start = ((), (), s32[]{:S(2)}) async-start(), calls=%async_computation.26 | async-start | bytes 7864320 | tf_op jit(solution)/shard_map/all_gather | solution.py:525
  7.9 333.8 %all-gather.19.cloned.1.call-start = ((), (), s32[]{:S(2)}) async-start(), calls=%async_computation.27 | async-start | bytes 7864320 | tf_op jit(solution)/shard_map/all_gather | solution.py:562
  8.7 380.1 %all-gather.9.cloned.1.call-start = ((), (), s32[]{:S(2)}) async-start(), calls=%async_computation.17 | async-start | bytes 7299072 | tf_op jit(solution)/shard_map/all_gather | solution.py:541
  72.5 424.2 %all-gather.11.cloned.1.call-start = ((), (), s32[]{:S(2)}) async-start(), calls=%async_computation.18 | async-start | bytes 2359296 | tf_op jit(solution)/shard_map/all_gather | solution.py:550
  77.5 158.4 %collective-permute-start.1 = (bf16[512,1024]{1,0:T(8,128)(2,1)S(1)}, bf16[512,1024]{1,0:T(8,128)(2,1)}, u32[]{:S(2)}, u32[]{:S(2)}) collective-permute-start(bf16[512,1024]{1,0:T(8,128)(2,1)S(1)} %get-tuple-element.176), channel_id=1, source_target_pairs={{0,16},{8,24},{16,0},{24,8},{1,17},{9,25},{17,1},{25,9},{2,18},{10... | collective-permute-start | bytes 3145736 | tf_op jit(solution)/shard_map/ppermute | solution.py:555
  80.0 533.0 %reduce-scatter.6.cloned.1.call-start = ((), (), s32[]{:S(2)}) async-start(), calls=%async_computation.19 | async-start | bytes 7864320 | tf_op jit(solution)/shard_map/reduce_scatter | solution.py:610
  504.9 178.8 %all-to-all-start.1 = ((bf16[8,4,120,2048]{3,2,1,0:T(8,128)(2,1)}), bf16[8,4,120,2048]{3,2,1,0:T(8,128)(2,1)}, u32[]{:S(2)}, u32[]{:S(2)}) async-start(bf16[8,4,120,2048]{3,2,1,0:T(8,128)(2,1)} %convert_bitcast_fusion.1.refs_2_), calls=%async_computation.2 | async-start | bytes 31457280 | tf_op jit(solution)/shard_map/all_to_all | solution.py:587
  511.0 222.1 %all-gather.13.cloned.1.call-start = ((), (), s32[]{:S(2)}) async-start(), calls=%async_computation.20 | async-start | bytes 7864320 | tf_op jit(solution)/shard_map/all_gather | solution.py:618
  761.2 199.4 %all-to-all-start.2 = ((bf16[8,4,120,2048]{3,2,1,0:T(8,128)(2,1)}), bf16[8,4,120,2048]{3,2,1,0:T(8,128)(2,1)}, u32[]{:S(2)}, u32[]{:S(2)}) async-start(bf16[8,4,120,2048]{3,2,1,0:T(8,128)(2,1)} %copy.259), calls=%async_computation.3 | async-start | bytes 31457280 | tf_op jit(solution)/shard_map/all_to_all | solution.py:624
  772.1 137.7 %collective-permute-start.4 = (bf16[512,1024]{1,0:T(8,128)(2,1)S(1)}, bf16[512,1024]{1,0:T(8,128)(2,1)S(1)}, u32[]{:S(2)}, u32[]{:S(2)}) collective-permute-start(bf16[512,1024]{1,0:T(8,128)(2,1)S(1)} %get-tuple-element.168), channel_id=1, source_target_pairs={{0,16},{8,24},{16,0},{24,8},{1,17},{9,25},{17,1},{25,9},{2,18},{10... | collective-permute-start | bytes 3145736 | tf_op jit(solution)/shard_map/ppermute | solution.py:555
  774.0 138.4 %collective-permute-start.6 = (bf16[256,2048]{1,0:T(8,128)(2,1)S(1)}, bf16[256,2048]{1,0:T(8,128)(2,1)S(1)}, u32[]{:S(2)}, u32[]{:S(2)}) collective-permute-start(bf16[256,2048]{1,0:T(8,128)(2,1)S(1)} %get-tuple-element.182), channel_id=1, source_target_pairs={{0,8},{8,0},{16,24},{24,16},{1,9},{9,1},{17,25},{25,17},{2,10},{10... | collective-permute-start | bytes 3145736 | tf_op jit(solution)/shard_map/ppermute | solution.py:555
  775.1 137.3 %collective-permute-start.8 = (bf16[256,2048]{1,0:T(8,128)(2,1)S(1)}, bf16[256,2048]{1,0:T(8,128)(2,1)S(1)}, u32[]{:S(2)}, u32[]{:S(2)}) collective-permute-start(bf16[256,2048]{1,0:T(8,128)(2,1)S(1)} %get-tuple-element.183), channel_id=1, source_target_pairs={{0,24},{8,16},{16,8},{24,0},{1,25},{9,17},{17,9},{25,1},{2,26},{10... | collective-permute-start | bytes 3145736 | tf_op jit(solution)/shard_map/ppermute | solution.py:555
  818.2 135.7 %collective-permute-start.7 = (bf16[256,2048]{1,0:T(8,128)(2,1)S(1)}, bf16[256,2048]{1,0:T(8,128)(2,1)S(1)}, u32[]{:S(2)}, u32[]{:S(2)}) collective-permute-start(bf16[256,2048]{1,0:T(8,128)(2,1)S(1)} %get-tuple-element.184), channel_id=1, source_target_pairs={{0,16},{8,24},{16,0},{24,8},{1,17},{9,25},{17,1},{25,9},{2,18},{10... | collective-permute-start | bytes 3145736 | tf_op jit(solution)/shard_map/ppermute | solution.py:555
  1130.3 217.5 %all-to-all-start.5 = ((bf16[8,480,2048]{2,1,0:T(8,128)(2,1)}), bf16[8,480,2048]{2,1,0:T(8,128)(2,1)}, u32[]{:S(2)}, u32[]{:S(2)}) async-start(bf16[8,480,2048]{2,1,0:T(8,128)(2,1)} %bitcast.254), calls=%async_computation.7 | async-start | bytes 31457280 | tf_op jit(solution)/shard_map/all_to_all | solution.py:639
  1135.9 336.2 %reduce-scatter.10.cloned.1.call-start = ((), (), s32[]{:S(2)}) async-start(), calls=%async_computation.22 | async-start | bytes 7864320 | tf_op jit(solution)/shard_map/reduce_scatter | solution.py:655
  1186.3 152.8 %collective-permute-start.13 = (bf16[512,1024]{1,0:T(8,128)(2,1)S(1)}, bf16[512,1024]{1,0:T(8,128)(2,1)S(1)}, u32[]{:S(2)}, u32[]{:S(2)}) collective-permute-start(bf16[512,1024]{1,0:T(8,128)(2,1)S(1)} %get-tuple-element.151), channel_id=1, source_target_pairs={{0,16},{8,24},{16,0},{24,8},{1,17},{9,25},{17,1},{25,9},{2,18},{10... | collective-permute-start | bytes 3145736 | tf_op jit(solution)/shard_map/ppermute | solution.py:555
  1186.6 152.5 %collective-permute-start.12 = (bf16[512,1024]{1,0:T(8,128)(2,1)S(1)}, bf16[512,1024]{1,0:T(8,128)(2,1)S(1)}, u32[]{:S(2)}, u32[]{:S(2)}) collective-permute-start(bf16[512,1024]{1,0:T(8,128)(2,1)S(1)} %get-tuple-element.152), channel_id=1, source_target_pairs={{0,8},{8,0},{16,24},{24,16},{1,9},{9,1},{17,25},{25,17},{2,10},{10... | collective-permute-start | bytes 3145736 | tf_op jit(solution)/shard_map/ppermute | solution.py:555
  1386.8 178.5 %all-to-all-start.4 = ((bf16[8,480,2048]{2,1,0:T(8,128)(2,1)}), bf16[8,480,2048]{2,1,0:T(8,128)(2,1)}, u32[]{:S(2)}, u32[]{:S(2)}) async-start(bf16[8,480,2048]{2,1,0:T(8,128)(2,1)} %bitcast.255), calls=%async_computation.5 | async-start | bytes 31457280 | tf_op jit(solution)/shard_map/all_to_all | solution.py:659
  1392.6 398.4 %all-gather.15.cloned.1.call-start = ((), (), s32[]{:S(2)}) async-start(), calls=%async_computation.23 | async-start | bytes 7864320 | tf_op jit(solution)/shard_map/all_gather | solution.py:683
  1480.7 425.1 %reduce-scatter.8.cloned.1.call-start = ((), (), s32[]{:S(2)}) async-start(), calls=%async_computation.21 | async-start | bytes 7864320 | tf_op jit(solution)/shard_map/reduce_scatter | solution.py:663
  1577.2 466.9 %reduce-scatter.14.cloned.1.call-start = ((), (), s32[]{:S(2)}) async-start(), calls=%async_computation.25 | async-start | bytes 2359296 | tf_op jit(solution)/shard_map/reduce_scatter | solution.py:686
  1603.6 182.5 %collective-permute-start.16 = (bf16[256,2048]{1,0:T(8,128)(2,1)S(1)}, bf16[256,2048]{1,0:T(8,128)(2,1)S(1)}, u32[]{:S(2)}, u32[]{:S(2)}) collective-permute-start(bf16[256,2048]{1,0:T(8,128)(2,1)S(1)} %get-tuple-element.143), channel_id=1, source_target_pairs={{0,16},{8,24},{16,0},{24,8},{1,17},{9,25},{17,1},{25,9},{2,18},{10... | collective-permute-start | bytes 3145736 | tf_op jit(solution)/shard_map/ppermute | solution.py:555
  1603.6 182.5 %collective-permute-start.15 = (bf16[256,2048]{1,0:T(8,128)(2,1)S(1)}, bf16[256,2048]{1,0:T(8,128)(2,1)S(1)}, u32[]{:S(2)}, u32[]{:S(2)}) collective-permute-start(bf16[256,2048]{1,0:T(8,128)(2,1)S(1)} %get-tuple-element.144), channel_id=1, source_target_pairs={{0,8},{8,0},{16,24},{24,16},{1,9},{9,1},{17,25},{25,17},{2,10},{10... | collective-permute-start | bytes 3145736 | tf_op jit(solution)/shard_map/ppermute | solution.py:555
  1897.4 183.8 %reduce-scatter.12.cloned.1.call-start = ((), (), s32[]{:S(2)}) async-start(), calls=%async_computation.24 | async-start | bytes 7864320 | tf_op jit(solution)/shard_map/reduce_scatter | solution.py:709
  (94 other events, 2873.2 us)
Sparse Core Ops, SparseCore 0:
  9.6 216.9 all-gather.16
  228.2 113.4 all-gather.18
  344.2 44.5 all-gather.8
  390.5 27.8 all-gather.10
  505.0 107.9 reduce-scatter.5
  617.2 115.8 all-gather.12
  1360.7 111.4 reduce-scatter.9
  1480.8 115.5 all-gather.14
  1598.7 177.8 reduce-scatter.7
  1897.5 42.0 reduce-scatter.13
  1942.0 119.1 reduce-scatter.11

commit v2 on v1

--- a/solution.py
+++ b/solution.py
@@ -451,17 +451,180 @@
     )(seq_ids[:, None], seq_ids[None, :], query, key, value, grad)
 
 
-def turn(values, cosine, sine, inverse=False):
-    rows, width = values.shape
-    split = values.reshape(rows, width // HEAD_DIM, 2, HEAD_DIM // 2)
-    first, second = split[:, :, 0], split[:, :, 1]
-    cosine = cosine[:, None, :]
-    sine = sine[:, None, :]
-    if inverse:
-        sine = -sine
-    return jnp.stack(
-        [first * cosine - second * sine, second * cosine + first * sine], axis=2
-    ).reshape(rows, width)
+def dispatch_kernel(position, rows, out):
+    columns, _, capacity, width = out.shape
+    count = rows.shape[1]
+    slots = lax.broadcasted_iota(jnp.int32, (columns, capacity, count), 1)
+    select = jnp.where(slots == position[:, 0], 1.0, 0.0)
+    select = select.reshape(columns * capacity, count).astype(jnp.bfloat16)
+    step = math.gcd(width, 512)
+    for at in range(0, width, step):
+        part = jnp.dot(select, rows[0, :, at : at + step], preferred_element_type=jnp.float32)
+        part = part.reshape(columns, capacity, step).astype(out.dtype)
+        out[:, 0, :, at : at + step] = part
+
+
+def dispatch(position, capacity, rows):
+    columns, planes, count = position.shape
+    width = rows.shape[1]
+    return pl.pallas_call(
+        dispatch_kernel,
+        grid=(planes,),
+        in_specs=[
+            pl.BlockSpec((columns, 1, 1, count), lambda b: (0, b, 0, 0)),
+            pl.BlockSpec((1, count, width), lambda b: (b, 0, 0)),
+        ],
+        out_specs=pl.BlockSpec((columns, 1, capacity, width), lambda b: (0, b, 0, 0)),
+        out_shape=jax.ShapeDtypeStruct((columns, planes, capacity, width), jnp.bfloat16),
+        cost_estimate=pl.CostEstimate(
+            flops=2 * position.size * capacity * width,
+            bytes_accessed=2 * columns * planes * capacity * width,
+            transcendentals=0,
+        ),
+        compiler_params=pltpu.CompilerParams(vmem_limit_bytes=40 << 20),
+        name="dispatch",
+    )(position[:, :, None], rows.reshape(planes, count, width))
+
+
+def heads_of(width):
+    return [slice(at, at + HEAD_DIM) for at in range(0, width, HEAD_DIM)]
+
+
+def turn_kernel(raw, scales, gains, cosine, sine, query, key, value):
+    width = query.shape[1]
+    for which, out in ((0, query), (1, key)):
+        scale = scales[:, which : which + 1]
+        for head in heads_of(width):
+            part = raw[:, which * width + head.start : which * width + head.stop]
+            part = part * scale * gains[which : which + 1, head]
+            swapped = pltpu.roll(part, HEAD_DIM // 2, 1)
+            out[:, head] = (part * cosine[...] + swapped * sine[...]).astype(out.dtype)
+    value[...] = raw[:, 2 * width : 3 * width].astype(value.dtype)
+
+
+def turn_back_kernel(
+    raw, scales, gains, cosine, sine, grad_query, grad_key, out_query, out_key, dots, grad_gains
+):
+    @pl.when(pl.program_id(0) == 0)
+    def _():
+        grad_gains[...] = jnp.zeros_like(grad_gains)
+
+    width = grad_query.shape[1]
+    for which, grad, out in ((0, grad_query, out_query), (1, grad_key, out_key)):
+        scale = scales[:, which : which + 1]
+        total = jnp.zeros_like(scale)
+        for head in heads_of(width):
+            part = grad[:, head]
+            part = part * cosine[...] - pltpu.roll(part, HEAD_DIM // 2, 1) * sine[...]
+            hat = raw[:, which * width + head.start : which * width + head.stop] * scale
+            grad_gains[which : which + 1, head] += jnp.sum(part * hat, axis=0, keepdims=True)
+            part = part * gains[which : which + 1, head]
+            total += jnp.sum(part * hat, axis=1, keepdims=True)
+            out[:, head] = part
+        dots[:, which : which + 1] = total
+
+
+def turn_specs(raw, gains):
+    block = math.gcd(raw.shape[0], 256)
+    return block, [
+        pl.BlockSpec((block, raw.shape[1]), lambda i: (i, 0)),
+        pl.BlockSpec((block, 2), lambda i: (i, 0)),
+        pl.BlockSpec(gains.shape, lambda i: (0, 0)),
+        pl.BlockSpec((block, HEAD_DIM), lambda i: (i, 0)),
+        pl.BlockSpec((block, HEAD_DIM), lambda i: (i, 0)),
+    ]
+
+
+def turn(raw, scales, gains, cosine, sine):
+    rows, width = raw.shape[0], gains.shape[1]
+    block, specs = turn_specs(raw, gains)
+    return pl.pallas_call(
+        turn_kernel,
+        grid=(rows // block,),
+        in_specs=specs,
+        out_specs=(pl.BlockSpec((block, width), lambda i: (i, 0)),) * 3,
+        out_shape=(jax.ShapeDtypeStruct((rows, width), jnp.bfloat16),) * 3,
+        cost_estimate=pl.CostEstimate(
+            flops=16 * rows * width, bytes_accessed=18 * rows * width, transcendentals=0
+        ),
+        compiler_params=pltpu.CompilerParams(vmem_limit_bytes=40 << 20),
+        name="turn",
+    )(raw, scales, gains, cosine, sine)
+
+
+def turn_back(raw, scales, gains, cosine, sine, grad_query, grad_key):
+    rows, width = grad_query.shape
+    block, specs = turn_specs(raw, gains)
+    wide = pl.BlockSpec((block, width), lambda i: (i, 0))
+    f32 = jnp.float32
+    return pl.pallas_call(
+        turn_back_kernel,
+        grid=(rows // block,),
+        in_specs=specs + [wide, wide],
+        out_specs=(
+            wide,
+            wide,
+            pl.BlockSpec((block, 2), lambda i: (i, 0)),
+            pl.BlockSpec((2, width), lambda i: (0, 0)),
+        ),
+        out_shape=(
+            jax.ShapeDtypeStruct((rows, width), f32),
+            jax.ShapeDtypeStruct((rows, width), f32),
+            jax.ShapeDtypeStruct((rows, 2), f32),
+            jax.ShapeDtypeStruct((2, width), f32),
+        ),
+        cost_estimate=pl.CostEstimate(
+            flops=24 * rows * width, bytes_accessed=28 * rows * width, transcendentals=0
+        ),
+        compiler_params=pltpu.CompilerParams(vmem_limit_bytes=40 << 20),
+        name="turn_back",
+    )(raw, scales, gains, cosine, sine, grad_query, grad_key)
+
+
+def expert_kernel(
+    rows, grad, picked, gate, up, down, act_out, grad_gate, grad_up, grad_picked
+):
+    gate_pre = jnp.dot(rows[...], gate[...], preferred_element_type=jnp.float32)
+    up_pre = jnp.dot(rows[...], up[...], preferred_element_type=jnp.float32)
+    grad_raw = lax.dot_general(
+        grad[...], down[...], (((1,), (1,)), ((), ())), preferred_element_type=jnp.float32
+    )
+    sigma = jax.nn.sigmoid(gate_pre)
+    silu = gate_pre * sigma
+    act = (silu * up_pre).astype(jnp.bfloat16).astype(jnp.float32)
+    act_out[...] = (act * picked[...]).astype(jnp.bfloat16)
+    grad_picked[...] = jnp.sum(grad_raw * act, axis=1, keepdims=True)
+    grad_act = grad_raw * picked[...]
+    grad_gate[...] = (
+        grad_act * up_pre * (sigma + silu * (1.0 - sigma))
+    ).astype(jnp.bfloat16)
+    grad_up[...] = (grad_act * silu).astype(jnp.bfloat16)
+
+
+def expert(rows, grad, picked, gate, up, down, block):
+    count, width = rows.shape
+    hidden = gate.shape[1]
+    once = pl.Buffered(1)
+    wide = pl.BlockSpec((block, width), lambda i: (i, 0))
+    narrow = pl.BlockSpec((block, hidden), lambda i: (i, 0))
+    one = pl.BlockSpec((block, 1), lambda i: (i, 0))
+    into = pl.BlockSpec((width, hidden), lambda i: (0, 0), pipeline_mode=once)
+    outof = pl.BlockSpec((hidden, width), lambda i: (0, 0), pipeline_mode=once)
+    low = jax.ShapeDtypeStruct((count, hidden), jnp.bfloat16)
+    return pl.pallas_call(
+        expert_kernel,
+        grid=(count // block,),
+        in_specs=[wide, wide, one, into, into, outof],
+        out_specs=(narrow, narrow, narrow, one),
+        out_shape=(low, low, low, jax.ShapeDtypeStruct((count, 1), jnp.float32)),
+        cost_estimate=pl.CostEstimate(
+            flops=6 * count * width * hidden,
+            bytes_accessed=4 * count * width + 6 * (count + width) * hidden,
+            transcendentals=count * hidden,
+        ),
+        compiler_params=pltpu.CompilerParams(vmem_limit_bytes=56 << 20),
+        name="expert",
+    )(rows, grad, picked, gate, up, down)
 
 
 def tie(array, *others):
@@ -526,40 +689,55 @@
     experts = w_router.shape[1]
     qkv = jnp.stack([w_query, w_key, w_value], axis=1).reshape(strip, 3, planes, share)
     qkv = qkv.transpose(2, 0, 1, 3).reshape(planes, strip, 3 * share)
-    small = jnp.concatenate(
-        [w_router] + [g[:, None] for g in (attn_gain, ffn_gain, query_gain, key_gain)], axis=1
-    )
-    small_rows = -(-small.size // (3 * share))
-    route_size = routes.size // (3 * share)
-    small_flat = jnp.pad(small.reshape(-1), (0, small_rows * 3 * share - small.size))
-    tail = jnp.concatenate(
-        [small_flat.reshape(small_rows, -1), routes.astype(bf16).reshape(route_size, -1)]
-    )
-    tail = jnp.broadcast_to(tail[None], (planes,) + tail.shape)
-    packed = lax.all_to_all(jnp.concatenate([qkv, tail], axis=1), "ctx", 0, 0, tiled=True)
-    routes_all = packed[:, strip + small_rows :].astype(jnp.int32).reshape(group_rows, -1)
-    packed = lax.all_gather(packed[:, : strip + small_rows], "fsdp", axis=1, tiled=True)
-    packed = packed.reshape(planes, columns, strip + small_rows, 3 * share)
-    qkv = packed[:, :, :strip].reshape(width, 3 * share)
-    small = packed[:, :, strip:].reshape(planes * columns, -1)[:, : small.size]
-    small = small.reshape(width, experts + 4)
-    full_router = small[:, :experts]
+    small = [w_router] + [g[:, None] for g in (attn_gain, ffn_gain, query_gain, key_gain)]
+    small = jnp.concatenate(small + [routes.astype(bf16).reshape(strip, -1)], axis=1)
+    spare = -small.shape[1] % 128
+    small = jnp.pad(small, ((0, 0), (0, spare)))
+    small = jnp.broadcast_to(small[None], (planes,) + small.shape)
+    own_out = jnp.broadcast_to(w_out[None], (planes,) + w_out.shape)
+    packed = jnp.concatenate([qkv, small, own_out], axis=2)
+    packed = lax.all_to_all(packed, "ctx", 0, 0, tiled=True)
+    packed, out_rows = packed[:, :, :-width], packed[:, :, -width:]
+    routes_at = 3 * share + experts + 4
+    routes_all = packed[:, :, routes_at : packed.shape[2] - spare].astype(jnp.int32)
+    routes_all = routes_all.reshape(group_rows, -1)
+    packed = jnp.broadcast_to(packed[None], (columns,) + packed.shape)
+    packed = lax.all_to_all(packed, "fsdp", 0, 0, tiled=True)
+    packed = packed.transpose(1, 0, 2, 3).reshape(width, -1)
+    full_router = packed[:, 3 * share : 3 * share + experts]
     gain_attn, gain_ffn, gain_query, gain_key = [
-        small[:, experts + i].astype(f32) for i in range(4)
+        packed[:, 3 * share + experts + i].astype(f32) for i in range(4)
     ]
-    out_rows = lax.all_gather(w_out, "fsdp", axis=0, tiled=True)
-    def exchange(parts):
+    def swap(part, step):
+        return lax.ppermute(part, "ctx", [(i, i ^ step) for i in range(planes)])
+
+    def by_plane(came):
+        came = jnp.stack(came)
+        return [came[plane ^ i] for i in range(planes)]
+
+    def exchange(parts, first=None, last=None):
         came = [parts[plane]]
-        for step in range(1, 4):
-            pairs = [(i, i ^ step) for i in range(4)]
-            came.append(lax.ppermute(parts[plane ^ step], "ctx", pairs))
-        came = jnp.stack(came)
-        return [came[plane ^ i] for i in range(4)]
-
-    gate = jnp.concatenate(exchange(w_gate))
-    up = jnp.concatenate(exchange(w_up))
-    down = jnp.concatenate(exchange(w_down))
-    grad_all = lax.all_gather(grad_output[0], "ctx", axis=0, tiled=True)
+        for step in range(1, planes):
+            part = parts[plane ^ step]
+            part = swap(part if first is None else tie(part, first), step)
+            came.append(part if last is None else tie(part, last))
+        return by_plane(came)
+
+    def exchange_after(parts, earlier):
+        came = [
+            swap(part if before is None else tie(part, before), step)
+            for step, before in enumerate(earlier, 1)
+            for part in [parts[plane ^ step]]
+        ]
+        return came, jnp.stack(by_plane([parts[plane]] + came)).astype(f32)
+
+    def plane_sum(part):
+        return part + sum(swap(part, step) for step in range(1, planes))
+
+    grad_all = lax.all_gather(tie(grad_output[0], hidden_all), "ctx", axis=0, tiled=True)
+    full_out = jnp.broadcast_to(tie(out_rows, packed)[None], (columns,) + out_rows.shape)
+    full_out = lax.all_to_all(full_out, "fsdp", 0, 0, tiled=True)
+    full_out = full_out.transpose(1, 0, 2, 3).reshape(width, width)
 
     seq_ids, places = seq_layout(token_order[0], lengths[0])
     experts_here = w_gate.shape[0]
@@ -573,102 +751,90 @@
     holds = position[:, :, None, :] == slots[None, None, :, None]
     select = holds.astype(bf16)
 
-    def dispatch(rows):
-        rows = rows.reshape(planes, row_count, width)
-        picked_rows = jnp.einsum("fbsr,brd->fbsd", select, rows, preferred_element_type=f32)
-        return picked_rows.astype(bf16)
-
     def combine(rows):
         rows = rows.reshape(columns, planes, capacity, width)
         sums = jnp.einsum("fbsr,fbsd->brd", select, rows, preferred_element_type=f32)
         return sums.reshape(group_rows, width).astype(bf16)
 
-    grad_send = dispatch(grad_all)
-    grad_in = lax.all_to_all(grad_send, "fsdp", 0, 0, tiled=True).reshape(-1, width)
 
     frequency = rope_base ** (
         -2.0 * jnp.arange(HEAD_DIM // 2).astype(f32) / HEAD_DIM
     )
     angles = places.astype(f32)[:, None] * frequency[None, :]
-    cosine, sine = lax.optimization_barrier((jnp.cos(angles), jnp.sin(angles)))
+    cosine, sine = jnp.cos(angles), jnp.sin(angles)
+    cosine = jnp.concatenate([cosine, cosine], axis=1)
+    sine = jnp.concatenate([-sine, sine], axis=1)
     hidden_wide = hidden_all.astype(f32)
     scale_one = lax.rsqrt(jnp.mean(hidden_wide * hidden_wide, axis=-1, keepdims=True) + epsilon)
     h_one = (hidden_wide * scale_one * gain_attn).astype(bf16)
-    raw = mm(h_one, qkv)
-    query_raw, key_raw = raw[:, :share], raw[:, share : 2 * share]
-    values = raw[:, 2 * share :].astype(bf16)
-    squares = jnp.stack([jnp.sum(query_raw**2, axis=1), jnp.sum(key_raw**2, axis=1)])
-    squares = lax.psum(squares, "ctx")
-    scales = lax.rsqrt(squares / width + epsilon)[:, :, None]
-    query_hat, key_hat = query_raw * scales[0], key_raw * scales[1]
-    my_query_gain = lax.dynamic_slice_in_dim(gain_query, plane * share, share)
-    my_key_gain = lax.dynamic_slice_in_dim(gain_key, plane * share, share)
-    query = turn(query_hat * my_query_gain, cosine, sine).astype(bf16)
-    key = turn(key_hat * my_key_gain, cosine, sine).astype(bf16)
+    raw = mm(h_one, packed)
+    squares = jnp.stack(
+        [jnp.sum(raw[:, :share] ** 2, axis=1), jnp.sum(raw[:, share : 2 * share] ** 2, axis=1)]
+    )
+    squares = plane_sum(squares)
+    scales = lax.rsqrt(squares / width + epsilon).T
+    gains = lax.dynamic_slice_in_dim(
+        jnp.stack([gain_query, gain_key]), plane * share, share, axis=1
+    )
+    query, key, values = turn(raw, scales, gains, cosine, sine)
     attended = attend(seq_ids, query, key, values)
-    attended = tie(attended, gate, grad_send)
-    branch = lax.psum_scatter(
-        mm(attended, out_rows).astype(bf16), "ctx", scatter_dimension=0, tiled=True
-    )
-    middle = hidden[0].astype(f32) + branch.astype(f32)
+    grad_send = dispatch(position, capacity, tie(grad_all, attended, full_out))
+    grad_in = lax.all_to_all(grad_send, "fsdp", 0, 0, tiled=True).reshape(-1, width)
+    attended = tie(attended, grad_send).reshape(planes, row_count, share)
+    attended = jnp.concatenate(exchange(attended), axis=1)
+    middle = hidden[0].astype(f32) + mm(attended, full_out)
     scale_two = lax.rsqrt(jnp.mean(middle * middle, axis=-1, keepdims=True) + epsilon)
     middle_hat = middle * scale_two
     h_two = (middle_hat * gain_ffn).astype(bf16)
 
-    h_all = tie(lax.all_gather(h_two, "ctx", axis=0, tiled=True), grad_in)
+    h_two_all = lax.all_gather(h_two, "ctx", axis=0, tiled=True)
+    h_all = tie(h_two_all, grad_in)
+    gate = jnp.concatenate(exchange(w_gate, h_two_all))
+    up = jnp.concatenate(exchange(w_up, h_all))
+    down = jnp.concatenate(exchange(w_down, h_all))
     probs_all = jax.nn.softmax(mm(h_all, full_router), axis=-1)
     probs = jax.nn.softmax(mm(h_two, full_router), axis=-1)
     probs_plane = lax.dynamic_index_in_dim(
         probs_all.reshape(group_rows, columns, experts_here), plane, 2, keepdims=False
     )
-    rows_in = lax.all_to_all(dispatch(h_all), "fsdp", 0, 0, tiled=True).reshape(-1, width)
+    rows_in = lax.all_to_all(dispatch(position, capacity, h_all), "fsdp", 0, 0, tiled=True).reshape(-1, width)
     probs_plane = probs_plane.reshape(planes, row_count, columns).transpose(2, 0, 1)
     slot_probs = jnp.sum(jnp.where(holds, probs_plane[:, :, None, :], 0.0), axis=3)
     picked = lax.all_to_all(slot_probs, "fsdp", 0, 0, tiled=True).reshape(-1, 1)
-    gate_pre = mm(rows_in, gate)
-    up_pre = mm(rows_in, up)
-    sigma = jax.nn.sigmoid(gate_pre)
-    silu = gate_pre * sigma
-    act = (silu * up_pre).astype(bf16)
-    grad_raw = mm_t(grad_in, down)
-    grad_act = grad_raw * picked
-    grad_gate = (grad_act * up_pre * sigma * (1.0 + gate_pre * (1.0 - sigma))).astype(bf16)
-    grad_up = (grad_act * silu).astype(bf16)
-    grad_picked = jnp.sum(grad_raw * act.astype(f32), axis=1)
+    act_picked, grad_gate, grad_up, grad_picked = expert(
+        rows_in, grad_in, picked, gate, up, down, planes * capacity
+    )
+    grad_picked = lax.all_to_all(
+        grad_picked.reshape(columns, planes, capacity), "fsdp", 0, 0, tiled=True
+    )
+    grad_down_w = t_mm(act_picked, grad_in).astype(bf16)
+    grad_gate = tie(grad_gate, grad_down_w, grad_picked)
+
+    def blocks(whole):
+        return whole.reshape(planes, whole.shape[0] // planes, whole.shape[1])
+
+    came, down_grad = exchange_after(blocks(grad_down_w), [None] * (planes - 1))
     grad_rows = (mm_t(grad_gate, gate) + mm_t(grad_up, up)).astype(bf16)
+    grad_rows = tie(grad_rows, *came[:-1])
     grad_rows = lax.all_to_all(
         grad_rows.reshape(columns, planes * capacity, width), "fsdp", 0, 0, tiled=True
     )
-    grad_picked = lax.all_to_all(
-        grad_picked.reshape(columns, planes, capacity), "fsdp", 0, 0, tiled=True
-    )
-    act_picked = (act.astype(f32) * picked).astype(bf16)
     grad_gate_w = t_mm(rows_in, grad_gate).astype(bf16)
     grad_up_w = t_mm(rows_in, grad_up).astype(bf16)
-
-    def spread_out(whole):
-        parts = whole.reshape(planes, whole.shape[0] // planes, whole.shape[1])
-        return jnp.stack(exchange(parts)).astype(f32)
-
-    gate_grad, up_grad = spread_out(grad_gate_w), spread_out(grad_up_w)
-    grad_rows = tie(grad_rows, gate_grad, up_grad)
+    came, up_grad = exchange_after(blocks(grad_up_w), came)
+    came, gate_grad = exchange_after(blocks(grad_gate_w), came)
+    expert_out = mm(act_picked, down).astype(bf16)
+    grad_rows = tie(grad_rows, *came, expert_out)
+    expert_out = lax.all_to_all(
+        expert_out.reshape(columns, planes * capacity, width), "fsdp", 0, 0, tiled=True
+    )
     grad_h_two = lax.psum_scatter(
         combine(grad_rows), "ctx", scatter_dimension=0, tiled=True
     ).astype(f32)
-    expert_out = (mm(act, down) * picked).astype(bf16)
-    expert_out = lax.all_to_all(
-        expert_out.reshape(columns, planes * capacity, width), "fsdp", 0, 0, tiled=True
-    )
-    mixed_part = combine(expert_out)
-    mixed = lax.psum_scatter(mixed_part, "ctx", scatter_dimension=0, tiled=True)
-    output = (middle + mixed.astype(f32)).astype(bf16)
-    down_grad = spread_out(t_mm(act_picked, grad_in).astype(bf16))
 
     u_plane = jnp.sum(jnp.where(holds, grad_picked[..., None], 0.0), axis=2)
-    u_mine = lax.all_to_all(
-        u_plane, "ctx", 1, 1, tiled=True
-    )
-    u_mine = u_mine.reshape(experts, row_count).T
+    u_mine = exchange(u_plane.transpose(1, 0, 2))
+    u_mine = jnp.stack(u_mine, axis=1).reshape(experts, row_count).T
     grad_logits = probs * (u_mine - jnp.sum(probs * u_mine, axis=-1, keepdims=True))
     grad_logits = grad_logits.astype(bf16)
     grad_h_two = grad_h_two + mm_t(grad_logits, full_router)
@@ -680,32 +846,35 @@
     grad_middle = grad_top + scale_two * (
         grad_hat - middle_hat * jnp.mean(grad_hat * middle_hat, axis=-1, keepdims=True)
     )
-    grad_branch = lax.all_gather(grad_middle.astype(bf16), "ctx", axis=0, tiled=True)
-    grad_att = tie(mm_t(grad_branch, out_rows).astype(bf16), mixed_part)
+    grad_branch = grad_middle.astype(bf16)
+    grad_att = mm_t(grad_branch, full_out).astype(bf16)
+    grad_att = grad_att.reshape(row_count, planes, share).transpose(1, 0, 2)
+    grad_att = jnp.concatenate(exchange(grad_att))
+    mixed_part = combine(tie(expert_out, grad_att))
+    mixed = lax.psum_scatter(mixed_part, "ctx", scatter_dimension=0, tiled=True)
+    output = (middle + mixed.astype(f32)).astype(bf16)
+    grad_out_w = t_mm(attended, grad_branch).astype(bf16)
+    grad_out_w = grad_out_w.reshape(planes, columns, strip, width).transpose(1, 0, 2, 3)
+    grad_out_w = lax.all_to_all(
+        tie(grad_out_w, mixed_part), "fsdp", 0, 0, tiled=True
+    )
+    grad_att = tie(grad_att, mixed_part)
     grad_query, grad_key, grad_value = attend_back(seq_ids, query, key, values, grad_att)
-    grad_out_w = lax.psum_scatter(
-        t_mm(attended, grad_branch).astype(bf16), "fsdp", scatter_dimension=0, tiled=True
-    ).astype(f32)
-    grad_query = turn(grad_query, cosine, sine, inverse=True)
-    grad_key = turn(grad_key, cosine, sine, inverse=True)
-    grad_q_gain = jnp.sum(grad_query * query_hat, axis=0)
-    grad_k_gain = jnp.sum(grad_key * key_hat, axis=0)
-    grad_query = grad_query * my_query_gain
-    grad_key = grad_key * my_key_gain
-    dots = jnp.stack(
-        [jnp.sum(grad_query * query_hat, axis=1), jnp.sum(grad_key * key_hat, axis=1)]
-    )
-    dots = (lax.psum(dots, "ctx") / width)[:, :, None]
+    grad_query, grad_key, dots, grad_gains = turn_back(
+        raw, scales, gains, cosine, sine, grad_query, grad_key
+    )
+    dots = plane_sum(dots.T).T * (scales * scales) / width
     grad_qkv = jnp.concatenate(
         [
-            scales[0] * (grad_query - query_hat * dots[0]),
-            scales[1] * (grad_key - key_hat * dots[1]),
+            scales[:, :1] * grad_query - raw[:, :share] * (scales[:, :1] * dots[:, :1]),
+            scales[:, 1:] * grad_key - raw[:, share : 2 * share] * (scales[:, 1:] * dots[:, 1:]),
             grad_value,
         ],
         axis=1,
     ).astype(bf16)
-    grad_qkv = tie(grad_qkv, down_grad, mixed)
-    grad_part = mm_t(grad_qkv, qkv)
+    grad_qkv = tie(grad_qkv, mixed, grad_out_w)
+    grad_out_w = jnp.sum(grad_out_w.astype(f32), axis=0).astype(bf16)
+    grad_part = mm_t(grad_qkv, packed[:, : 3 * share])
     grad_h_one = lax.psum_scatter(
         grad_part.astype(bf16), "ctx", scatter_dimension=0, tiled=True
     ).astype(f32)
@@ -715,8 +884,10 @@
         grad_qkv_w.transpose(1, 0, 2, 3).astype(bf16), "fsdp", 0, 0, tiled=True
     )
     grad_qkv_w = jnp.sum(grad_qkv_w.astype(f32), axis=0).astype(bf16)
+    grad_qkv_w = jnp.concatenate([grad_qkv_w, grad_out_w], axis=2)
     grad_qkv_w = lax.all_to_all(grad_qkv_w, "ctx", 0, 0, tiled=True)
-    grad_qkv_w = grad_qkv_w.reshape(planes, strip, 3, share).transpose(2, 1, 0, 3)
+    grad_out_w = jnp.sum(grad_qkv_w[:, :, 3 * share :].astype(f32), axis=0)
+    grad_qkv_w = grad_qkv_w[:, :, : 3 * share].reshape(planes, strip, 3, share).transpose(2, 1, 0, 3)
     grad_qkv_w = grad_qkv_w.reshape(3, strip, width).astype(f32)
 
     x_hat = hidden[0].astype(f32)
@@ -731,12 +902,13 @@
         parts = jnp.concatenate(
             [x.reshape(planes * columns, -1) for x in arrays], axis=1
         )
+        parts = tie(parts, grad_qkv_w)
         return jnp.sum(lax.all_to_all(parts, both, 0, 0, tiled=True), axis=0)
 
-    totals = summed([grad_router, grad_ffn_gain])
     own = jnp.arange(planes)[:, None] == plane
-    gains = [jnp.where(own, g[None], 0.0) for g in (grad_q_gain, grad_k_gain)]
-    gains = summed([grad_attn_gain] + gains)
+    gains = [jnp.where(own, g[None], 0.0) for g in grad_gains]
+    totals = summed([grad_router, grad_attn_gain, grad_ffn_gain] + gains)
+    gains = totals[strip * experts :].reshape(4, strip)
     return (
         output[None],
         grad_input[None],
@@ -745,10 +917,10 @@
         grad_qkv_w[2],
         grad_out_w,
         totals[: strip * experts].reshape(strip, experts),
-        gains[:strip],
-        totals[strip * experts :],
-        gains[strip : 2 * strip],
-        gains[2 * strip :],
+        gains[0],
+        gains[1],
+        gains[2],
+        gains[3],
         gate_grad,
         up_grad,
         down_grad,
@@ -780,7 +952,7 @@
         experts_here = operands[14].shape[0]
         heads = operands[0].shape[2] // HEAD_DIM
         planes = mesh.shape["ctx"]
-        whole_experts = experts_here == planes and heads % planes == 0
+        whole_experts = experts_here == planes and heads % planes == 0 and planes in (2, 4)
         return (plane_shards if whole_experts else general_shards)(*operands)
 
     return jax.shard_map(

time: 2100 us -> 1760 us (0.84)
  waiting for transfers between devices: 1220 us -> 729 us
  starting transfers between devices: 113 us -> 236 us
  matrix products: 346 us -> 242 us
  Pallas kernels: 73.7 us -> 174 us
  local copies, waits for them, and re-layouts: 112 us -> 148 us
    ppermute x18 -> x33, waiting for transfers between devices: 617 us -> 317 us  [swap(): return lax.ppermute(part, 'ctx', [(i, i ^ step) for i in range(planes)])]
    ppermute x18 -> x33, starting transfers between devices: 61.9 us -> 177 us  [swap(): return lax.ppermute(part, 'ctx', [(i, i ^ step) for i in range(planes)])]
    reduce_scatter x2 -> x0, waiting for transfers between devices: 102 us -> none  [the longest x1 102 us: plane_shards(): lax.psum_scatter(mm(attended, out_rows).astype(bf16), 'ctx', scatter_dime...]
    pallas_call x0 -> x5, Pallas kernels: none -> 101 us  [the longest x1 63 us: expert(): pl.pallas_call(expert_kernel, grid=(count // block,), in_specs=[wide, wid...]
    all_to_all x1, waiting for transfers between devices: 84.5 us -> 9.99 us  [plane_shards(): lax.all_to_all(expert_out.reshape(columns, planes * capacity, width), 'fs...]
    all_to_all x2 -> x5, waiting for transfers between devices: 0.01 us -> 59.8 us  [the longest x1 36.3 us: plane_shards(): packed = lax.all_to_all(packed, 'fsdp', 0, 0, tiled=True)]
    all_to_all x1, waiting for transfers between devices: 66.6 us -> 9.35 us  [plane_shards(): lax.all_to_all(grad_send, 'fsdp', 0, 0, tiled=True).reshape(-1, width)]
    all_gather x5 -> x2, waiting for transfers between devices: 173 us -> 117 us  [the longest x1 117 us: plane_shards(): h_two_all = lax.all_gather(h_two, 'ctx', axis=0, tiled=True)]
  transfers between devices with their start and end apart: 39 -> 51, of which waited for: 21 -> 30; matrix products, arithmetic and copies ran while one was open for 16% -> 21% of each run, Pallas kernels for 4% -> 6%
where the time goes in v2:
time: 1760 us; the launch traced here: 1750 us
  waiting for transfers between devices  729 us (41%)
  matrix products  242 us (14%)
  starting transfers between devices  236 us (13%)
  Pallas kernels  174 us (10%)
  local copies, waits for them, and re-layouts  148 us (8%)
  blocking collectives  104 us (6%)
  other arithmetic  96.8 us (6%)
    ppermute x33, waiting for transfers between devices, swap(): return lax.ppermute(part, 'ctx', [(i, i ^ step) for i in range(planes)])  317 us
    ppermute x33, starting transfers between devices, swap(): return lax.ppermute(part, 'ctx', [(i, i ^ step) for i in range(planes)])  177 us
    all_gather x1, waiting for transfers between devices, plane_shards(): h_two_all = lax.all_gather(h_two, 'ctx', axis=0, tiled=True)  117 us
    all_to_all x1, blocking collectives, plane_shards(): packed = lax.all_to_all(packed, 'ctx', 0, 0, tiled=True)  104 us
    reduce_scatter x1, waiting for transfers between devices, plane_shards(): lax.psum_scatter(combine(grad_rows), 'ctx', scatter_dimension=0, tiled=True)  92.8 us
    dot_general x6, matrix products, t_mm(): lax.dot_general(left, right, (((0,), (0,)), ((), ())), preferred_element_...  91.2 us
    dot_general x5, matrix products, mm_t(): lax.dot_general(left, right, (((1,), (1,)), ((), ())), preferred_element_...  74.8 us
    pallas_call x1, Pallas kernels, expert(): pl.pallas_call(expert_kernel, grid=(count // block,), in_specs=[wide, wid...  63 us
  transfers between devices with their start and end apart: 51, of which 30 were waited for; matrix products, arithmetic and copies ran while one was open for 21% of the time, Pallas kernels for 6%

profile of v2, /device:TPU:0, one launch (start us, length us, event | category | flops | bytes accessed | tf_op | source)
XLA Modules:
  0.0 1747.1 jit_solution(9516336667306287703)
XLA Ops:
  16.0 104.3 %all_to_all.69 = bf16[4,64,3712]{2,1,0:T(8,128)(2,1)S(1)} all-to-all(bf16[4,64,3712]{2,1,0:T(8,128)(2,1)S(1)} %pad_maximum_fusion.10), channel_id=1, replica_groups=mesh['ctx'=4,'fsdp'=8] {'ctx'}, dimensions={0} | all-to-all | bytes 3801088 | tf_op jit(solution)/shard_map/all_to_all | solution.py:699
  131.7 36.0 %all-gather.9.cloned.1.call-done = bf16[1,1536,2048]{2,1,0:T(8,128)(2,1)} async-done(((bf16[1,384,2048]{2,1,0:T(8,128)(2,1)}), bf16[1,1536,2048]{2,1,0:T(8,128)(2,1)}) %all-gather.9.cloned.1.call-update) | async-done | bytes 6291472 | tf_op jit(solution)/shard_map/all_gather | solution.py:688
  169.8 36.3 %all-to-all-done.1 = bf16[8,4,64,1664]{3,2,1,0:T(8,128)(2,1)} async-done(((bf16[8,4,64,1664]{3,2,1,0:T(8,128)(2,1)}), bf16[8,4,64,1664]{3,2,1,0:T(8,128)(2,1)}, u32[]{:S(2)}, u32[]{:S(2)}) %all-to-all-start.1) | async-done | bytes 6815776 | tf_op jit(solution)/shard_map/all_to_all | solution.py:705
  273.8 27.7 %attend.1.refs_1_.refs_0_ = bf16[1536,512]{1,0:T(8,128)(2,1)S(1)} custom-call(s32[1536,1]{1,0:T(8,128)S(1)} %broadcast_in_dim.188.seq_rows, s32[1,1536]{1,0:T(1,128)S(1)} %broadcast_in_dim.160.seq_cols, bf16[1536,512]{1,0:T(8,128)(2,1)S(1)} %get-tuple-element.28.query, bf16[1536,512]{1,0:T(8,128)(2,1)S(1)} %get-tuple-element.29.key, bf16[1536,512]{1,0:T(8,128)(2,1)} %copy-done.12), custom_call_target="tpu_custom_call" | custom-call | flops 4831838208 | bytes 6291456 | tf_op jit(solution)/shard_map/attend/pallas_call | solution.py:421
  391.4 117.3 %all-gather.7.cloned.1.call-done.refs_0_.refs_1_ = bf16[1536,2048]{1,0:T(8,128)(2,1)} async-done(((bf16[384,2048]{1,0:T(8,128)(2,1)}), bf16[1536,2048]{1,0:T(8,128)(2,1)}) %all-gather.7.cloned.1.call-update) | async-done | bytes 6291472 | tf_op jit(solution)/shard_map/all_gather | solution.py:790
  558.9 36.9 %collective-permute-done.6 = bf16[512,1024]{1,0:T(8,128)(2,1)} collective-permute-done((bf16[512,1024]{1,0:T(8,128)(2,1)}, bf16[512,1024]{1,0:T(8,128)(2,1)}, u32[]{:S(2)}, u32[]{:S(2)}) %collective-permute-start.6) | collective-permute-done | bytes 1048608 | tf_op jit(solution)/shard_map/ppermute | solution.py:712
  624.8 68.0 %collective-permute-start.12 = (bf16[256,2048]{1,0:T(8,128)(2,1)}, bf16[256,2048]{1,0:T(8,128)(2,1)}, u32[]{:S(2)}, u32[]{:S(2)}) collective-permute-start(bf16[256,2048]{1,0:T(8,128)(2,1)} %tie.39), channel_id=1, source_target_pairs={{0,8},{8,0},{16,24},{24,16},{1,9},{9,1},{17,25},{25,17},{2,10},{10... | collective-permute-start | bytes 3145736 | tf_op jit(solution)/shard_map/ppermute | solution.py:712
  733.1 67.9 %collective-permute-done.13 = bf16[256,2048]{1,0:T(8,128)(2,1)} collective-permute-done((bf16[256,2048]{1,0:T(8,128)(2,1)}, bf16[256,2048]{1,0:T(8,128)(2,1)}, u32[]{:S(2)}, u32[]{:S(2)}) %collective-permute-start.13) | collective-permute-done | bytes 1048608 | tf_op jit(solution)/shard_map/ppermute | solution.py:712
  809.4 63.0 %expert.1 = (bf16[3840,1024]{1,0:T(8,128)(2,1)}, bf16[3840,1024]{1,0:T(8,128)(2,1)}, bf16[3840,1024]{1,0:T(8,128)(2,1)}, f32[3840,1]{1,0:T(8,128)}) custom-call(bf16[3840,2048]{1,0:T(8,128)(2,1)} %bitcast.37.rows, bf16[3840,2048]{1,0:T(8,128)(2,1)} %bitcast.35.refs_1_.grad, f32[3840,1]{1,0:T(8,128)} %reshape.353.picked, ...), custom_call_target="tpu_custom_call" | custom-call | flops 48318382080 | bytes 67633152 | tf_op jit(solution)/shard_map/expert/pallas_call | solution.py:614
  872.4 23.0 %convolution_convert_fusion.5.refs_1_ = bf16[1024,2048]{1,0:T(8,128)(2,1)} fusion(bf16[3840,1024]{1,0:T(8,128)(2,1)} %get-tuple-element.31, bf16[3840,2048]{1,0:T(8,128)(2,1)} %bitcast.35.refs_1_.grad), kind=kOutput, calls=%fused_computation.42 | convolution fusion | flops 16108224512 | bytes 27787264 | tf_op jit(solution)/shard_map/dot_general | solution.py:653
  906.8 22.2 %collective-permute-start.15 = (bf16[256,2048]{1,0:T(8,128)(2,1)}, bf16[256,2048]{1,0:T(8,128)(2,1)}, u32[]{:S(2)}, u32[]{:S(2)}) collective-permute-start(bf16[256,2048]{1,0:T(8,128)(2,1)} %get-tuple-element.153), channel_id=1, source_target_pairs={{0,8},{8,0},{16,24},{24,16},{1,9},{9,1},{17,25},{25,17},{2,10},{10... | collective-permute-start | bytes 3145736 | tf_op jit(solution)/shard_map/ppermute | solution.py:712
  929.6 23.9 %fusion.65 = f32[3840,2048]{1,0:T(8,128)} fusion(bf16[3840,1024]{1,0:T(8,128)(2,1)} %tie.42, bf16[512,1024]{1,0:T(8,128)(2,1)} %copy-done.37, bf16[512,1024]{1,0:T(8,128)(2,1)} %copy-done.38, bf16[512,1024]{1,0:T(8,128)(2,1)} %copy-done.39, bf16[512,1024]{1,0:T(8,128)(2,1)} %copy-done.36), kind=kOutput, calls=%fused_computation.237 | convolution fusion | flops 16122904576 | bytes 43515904 | tf_op jit(solution)/shard_map/dot_general | solution.py:647
  953.5 25.2 %add_convert_fusion.refs_0_ = bf16[3840,2048]{1,0:T(8,128)(2,1)} fusion(f32[3840,2048]{1,0:T(8,128)} %fusion.65, bf16[3840,1024]{1,0:T(8,128)(2,1)} %get-tuple-element.34, bf16[512,1024]{1,0:T(8,128)(2,1)} %copy-done.41, bf16[512,1024]{1,0:T(8,128)(2,1)} %copy-done.42, bf16[512,1024]{1,0:T(8,128)(2,1)} %copy-done.43, bf16[512,1024]{1,0:T(8,128)(2,1)} %copy-done.40), kind=kOutput, calls=%fused_computation | convolution fusion | flops 16138633216 | bytes 59244544 | tf_op jit(solution)/shard_map/dot_general | solution.py:647
  986.9 21.6 %convolution_convert_fusion.3 = bf16[2048,1024]{1,0:T(8,128)(2,1)S(1)} fusion(bf16[3840,2048]{1,0:T(8,128)(2,1)} %bitcast.37.rows, bf16[3840,1024]{1,0:T(8,128)(2,1)} %get-tuple-element.34), kind=kOutput, calls=%fused_computation.40 | convolution fusion | flops 16108224512 | bytes 27787264 | tf_op jit(solution)/shard_map/dot_general | solution.py:653
  1014.5 44.1 %collective-permute-start.19 = (bf16[512,1024]{1,0:T(8,128)(2,1)}, bf16[512,1024]{1,0:T(8,128)(2,1)}, u32[]{:S(2)}, u32[]{:S(2)}) collective-permute-start(bf16[512,1024]{1,0:T(8,128)(2,1)} %tie.46), channel_id=1, source_target_pairs={{0,16},{8,24},{16,0},{24,8},{1,17},{9,25},{17,1},{25,9},{2,18},{10... | collective-permute-start | bytes 3145736 | tf_op jit(solution)/shard_map/ppermute | solution.py:712
  1058.6 21.4 %convolution_convert_fusion.4 = bf16[2048,1024]{1,0:T(8,128)(2,1)S(1)} fusion(bf16[3840,2048]{1,0:T(8,128)(2,1)} %bitcast.37.rows, bf16[3840,1024]{1,0:T(8,128)(2,1)} %tie.42), kind=kOutput, calls=%fused_computation.41 | convolution fusion | flops 16108224512 | bytes 27787264 | tf_op jit(solution)/shard_map/dot_general | solution.py:653
  1084.6 65.8 %collective-permute-done.19.refs_1_ = bf16[512,1024]{1,0:T(8,128)(2,1)} collective-permute-done((bf16[512,1024]{1,0:T(8,128)(2,1)}, bf16[512,1024]{1,0:T(8,128)(2,1)}, u32[]{:S(2)}, u32[]{:S(2)}) %collective-permute-start.19) | collective-permute-done | bytes 1048608 | tf_op jit(solution)/shard_map/ppermute | solution.py:712
  1153.2 22.2 %convolution_convert_fusion.refs_4_ = bf16[3840,2048]{1,0:T(8,128)(2,1)} fusion(bf16[3840,1024]{1,0:T(8,128)(2,1)} %get-tuple-element.31, bf16[256,2048]{1,0:T(8,128)(2,1)} %copy-done.32, bf16[256,2048]{1,0:T(8,128)(2,1)} %copy-done.33, bf16[256,2048]{1,0:T(8,128)(2,1)} %copy-done.34, bf16[256,2048]{1,0:T(8,128)(2,1)} %copy-done.31), kind=kOutput, calls=%fused_computation.7 | convolution fusion | flops 16130768896 | bytes 27787264 | tf_op jit(solution)/shard_map/dot_general | solution.py:643
  1175.4 41.0 %collective-permute-done.20.refs_2_ = bf16[512,1024]{1,0:T(8,128)(2,1)} collective-permute-done((bf16[512,1024]{1,0:T(8,128)(2,1)}, bf16[512,1024]{1,0:T(8,128)(2,1)}, u32[]{:S(2)}, u32[]{:S(2)}) %collective-permute-start.20) | collective-permute-done | bytes 1048608 | tf_op jit(solution)/shard_map/ppermute | solution.py:712
  1247.5 92.8 %reduce-scatter.4.cloned.1.call-done = bf16[384,2048]{1,0:T(8,128)(2,1)} async-done(((bf16[1536,2048]{1,0:T(8,128)(2,1)}), bf16[384,2048]{1,0:T(8,128)(2,1)}) %reduce-scatter.4.cloned.1.call-update) | async-done | bytes 1572880 | tf_op jit(solution)/shard_map/reduce_scatter | solution.py:831
  1369.0 25.3 %collective-permute-done.28 = bf16[384,512]{1,0:T(8,128)(2,1)S(1)} collective-permute-done((bf16[384,512]{1,0:T(8,128)(2,1)S(1)}, bf16[384,512]{1,0:T(8,128)(2,1)S(1)}, u32[]{:S(2)}, u32[]{:S(2)}) %collective-permute-start.28) | collective-permute-done | bytes 393248 | tf_op jit(solution)/shard_map/ppermute | solution.py:712
  1447.8 45.6 %attend_back.1 = (f32[1536,512]{1,0:T(8,128)}, f32[1536,512]{1,0:T(8,128)}, f32[1536,512]{1,0:T(8,128)}) custom-call(s32[1536,1]{1,0:T(8,128)S(1)} %broadcast_in_dim.188.seq_rows, s32[1,1536]{1,0:T(1,128)S(1)} %broadcast_in_dim.160.seq_cols, bf16[1536,512]{1,0:T(8,128)(2,1)S(1)} %copy-done.9, bf16[1536,512]{1,0:T(8,128)(2,1)S(1)} %copy-done.11, ...), custom_call_target="tpu_custom_call" | custom-call | flops 12079595520 | bytes 15728640 | tf_op jit(solution)/shard_map/attend_back/pallas_call | solution.py:440
  1588.3 60.9 %all-to-all-done.10 = bf16[8,4,64,1536]{3,2,1,0:T(8,128)(2,1)} async-done(((bf16[8,4,64,1536]{3,2,1,0:T(8,128)(2,1)}), bf16[8,4,64,1536]{3,2,1,0:T(8,128)(2,1)}, u32[]{:S(2)}, u32[]{:S(2)}) %all-to-all-start.10) | async-done | bytes 6291488 | tf_op jit(solution)/shard_map/all_to_all | solution.py:883
  1679.2 22.8 %all-to-all-done.11 = bf16[4,64,3584]{2,1,0:T(8,128)(2,1)S(1)} async-done(((bf16[4,64,3584]{2,1,0:T(8,128)(2,1)}), bf16[4,64,3584]{2,1,0:T(8,128)(2,1)S(1)}, u32[]{:S(2)}, u32[]{:S(2)}) %all-to-all-start.11) | async-done | bytes 1835040 | tf_op jit(solution)/shard_map/all_to_all | solution.py:888
  (475 shorter events, 615.9 us)
Async XLA Ops:
  7.2 160.4 %all-gather.9.cloned.1.call-start = ((), (), s32[]{:S(2)}) async-start(), calls=%async_computation.21 | async-start | bytes 7864320 | tf_op jit(solution)/shard_map/all_gather | solution.py:688
  124.0 82.1 %all-to-all-start.1 = ((bf16[8,4,64,1664]{3,2,1,0:T(8,128)(2,1)}), bf16[8,4,64,1664]{3,2,1,0:T(8,128)(2,1)}, u32[]{:S(2)}, u32[]{:S(2)}) async-start(bf16[8,4,64,1664]{3,2,1,0:T(8,128)(2,1)} %broadcast_in_dim.167), calls=%async_computation.1 | async-start | bytes 13631488 | tf_op jit(solution)/shard_map/all_to_all | solution.py:705
  128.9 197.3 %all-gather.5.cloned.1.call-start = ((), (), s32[]{:S(2)}) async-start(), calls=%async_computation.16 | async-start | bytes 7864320 | tf_op jit(solution)/shard_map/all_gather | solution.py:737
  218.1 99.6 %all-to-all-start.2 = ((bf16[8,4,64,2048]{3,2,1,0:T(8,128)(2,1)}), bf16[8,4,64,2048]{3,2,1,0:T(8,128)(2,1)}, u32[]{:S(2)}, u32[]{:S(2)}) async-start(bf16[8,4,64,2048]{3,2,1,0:T(8,128)(2,1)} %broadcast_in_dim.172), calls=%async_computation.2 | async-start | bytes 16777216 | tf_op jit(solution)/shard_map/all_to_all | solution.py:739
  339.7 178.4 %all-to-all-start.3 = ((bf16[8,4,120,2048]{3,2,1,0:T(8,128)(2,1)}), bf16[8,4,120,2048]{3,2,1,0:T(8,128)(2,1)}, u32[]{:S(2)}, u32[]{:S(2)}) async-start(bf16[8,4,120,2048]{3,2,1,0:T(8,128)(2,1)} %dispatch.2.refs_1_), calls=%async_computation.3 | async-start | bytes 31457280 | tf_op jit(solution)/shard_map/all_to_all | solution.py:782
  345.4 163.4 %all-gather.7.cloned.1.call-start = ((), (), s32[]{:S(2)}) async-start(), calls=%async_computation.17 | async-start | bytes 7864320 | tf_op jit(solution)/shard_map/all_gather | solution.py:790
  543.0 266.4 %all-to-all-start.4 = ((bf16[8,4,120,2048]{3,2,1,0:T(8,128)(2,1)}), bf16[8,4,120,2048]{3,2,1,0:T(8,128)(2,1)}, u32[]{:S(2)}, u32[]{:S(2)}) async-start(bf16[8,4,120,2048]{3,2,1,0:T(8,128)(2,1)} %dispatch.3), calls=%async_computation.4 | async-start | bytes 31457280 | tf_op jit(solution)/shard_map/all_to_all | solution.py:800
  548.9 72.3 %collective-permute-start.7 = (bf16[512,1024]{1,0:T(8,128)(2,1)}, bf16[512,1024]{1,0:T(8,128)(2,1)}, u32[]{:S(2)}, u32[]{:S(2)}) collective-permute-start(bf16[512,1024]{1,0:T(8,128)(2,1)} %tie.34), channel_id=1, source_target_pairs={{0,16},{8,24},{16,0},{24,8},{1,17},{9,25},{17,1},{25,9},{2,18},{10... | collective-permute-start | bytes 3145736 | tf_op jit(solution)/shard_map/ppermute | solution.py:712
  557.5 135.3 %collective-permute-start.9 = (bf16[512,1024]{1,0:T(8,128)(2,1)}, bf16[512,1024]{1,0:T(8,128)(2,1)}, u32[]{:S(2)}, u32[]{:S(2)}) collective-permute-start(bf16[512,1024]{1,0:T(8,128)(2,1)} %tie.36), channel_id=1, source_target_pairs={{0,8},{8,0},{16,24},{24,16},{1,9},{9,1},{17,25},{25,17},{2,10},{10... | collective-permute-start | bytes 3145736 | tf_op jit(solution)/shard_map/ppermute | solution.py:712
  557.5 153.6 %collective-permute-start.10 = (bf16[512,1024]{1,0:T(8,128)(2,1)}, bf16[512,1024]{1,0:T(8,128)(2,1)}, u32[]{:S(2)}, u32[]{:S(2)}) collective-permute-start(bf16[512,1024]{1,0:T(8,128)(2,1)} %tie.37), channel_id=1, source_target_pairs={{0,16},{8,24},{16,0},{24,8},{1,17},{9,25},{17,1},{25,9},{2,18},{10... | collective-permute-start | bytes 3145736 | tf_op jit(solution)/shard_map/ppermute | solution.py:712
  595.8 115.3 %collective-permute-start.11 = (bf16[512,1024]{1,0:T(8,128)(2,1)}, bf16[512,1024]{1,0:T(8,128)(2,1)}, u32[]{:S(2)}, u32[]{:S(2)}) collective-permute-start(bf16[512,1024]{1,0:T(8,128)(2,1)} %tie.38), channel_id=1, source_target_pairs={{0,24},{8,16},{16,8},{24,0},{1,25},{9,17},{17,9},{25,1},{2,26},{10... | collective-permute-start | bytes 3145736 | tf_op jit(solution)/shard_map/ppermute | solution.py:712
  624.8 108.3 %collective-permute-start.12 = (bf16[256,2048]{1,0:T(8,128)(2,1)}, bf16[256,2048]{1,0:T(8,128)(2,1)}, u32[]{:S(2)}, u32[]{:S(2)}) collective-permute-start(bf16[256,2048]{1,0:T(8,128)(2,1)} %tie.39), channel_id=1, source_target_pairs={{0,8},{8,0},{16,24},{24,16},{1,9},{9,1},{17,25},{25,17},{2,10},{10... | collective-permute-start | bytes 3145736 | tf_op jit(solution)/shard_map/ppermute | solution.py:712
  692.8 108.2 %collective-permute-start.13 = (bf16[256,2048]{1,0:T(8,128)(2,1)}, bf16[256,2048]{1,0:T(8,128)(2,1)}, u32[]{:S(2)}, u32[]{:S(2)}) collective-permute-start(bf16[256,2048]{1,0:T(8,128)(2,1)} %tie.40), channel_id=1, source_target_pairs={{0,16},{8,24},{16,0},{24,8},{1,17},{9,25},{17,1},{25,9},{2,18},{10... | collective-permute-start | bytes 3145736 | tf_op jit(solution)/shard_map/ppermute | solution.py:712
  692.8 108.2 %collective-permute-start.14 = (bf16[256,2048]{1,0:T(8,128)(2,1)}, bf16[256,2048]{1,0:T(8,128)(2,1)}, u32[]{:S(2)}, u32[]{:S(2)}) collective-permute-start(bf16[256,2048]{1,0:T(8,128)(2,1)} %tie.41), channel_id=1, source_target_pairs={{0,24},{8,16},{16,8},{24,0},{1,25},{9,17},{17,9},{25,1},{2,26},{10... | collective-permute-start | bytes 3145736 | tf_op jit(solution)/shard_map/ppermute | solution.py:712
  978.8 237.6 %all-to-all-start.8 = ((bf16[8,480,2048]{2,1,0:T(8,128)(2,1)}), bf16[8,480,2048]{2,1,0:T(8,128)(2,1)}, u32[]{:S(2)}, u32[]{:S(2)}) async-start(bf16[8,480,2048]{2,1,0:T(8,128)(2,1)} %bitcast.286), calls=%async_computation.8 | async-start | bytes 31457280 | tf_op jit(solution)/shard_map/all_to_all | solution.py:819
  984.5 355.8 %reduce-scatter.4.cloned.1.call-start = ((), (), s32[]{:S(2)}) async-start(), calls=%async_computation.18 | async-start | bytes 7864320 | tf_op jit(solution)/shard_map/reduce_scatter | solution.py:831
  1014.5 135.9 %collective-permute-start.19 = (bf16[512,1024]{1,0:T(8,128)(2,1)}, bf16[512,1024]{1,0:T(8,128)(2,1)}, u32[]{:S(2)}, u32[]{:S(2)}) collective-permute-start(bf16[512,1024]{1,0:T(8,128)(2,1)} %tie.46), channel_id=1, source_target_pairs={{0,16},{8,24},{16,0},{24,8},{1,17},{9,25},{17,1},{25,9},{2,18},{10... | collective-permute-start | bytes 3145736 | tf_op jit(solution)/shard_map/ppermute | solution.py:712
  1058.6 91.8 %collective-permute-start.17 = (bf16[512,1024]{1,0:T(8,128)(2,1)}, bf16[512,1024]{1,0:T(8,128)(2,1)}, u32[]{:S(2)}, u32[]{:S(2)}) collective-permute-start(bf16[512,1024]{1,0:T(8,128)(2,1)} %tie.44), channel_id=1, source_target_pairs={{0,8},{8,0},{16,24},{24,16},{1,9},{9,1},{17,25},{25,17},{2,10},{10... | collective-permute-start | bytes 3145736 | tf_op jit(solution)/shard_map/ppermute | solution.py:712
  1082.2 93.2 %collective-permute-start.23 = (bf16[512,1024]{1,0:T(8,128)(2,1)}, bf16[512,1024]{1,0:T(8,128)(2,1)}, u32[]{:S(2)}, u32[]{:S(2)}) collective-permute-start(bf16[512,1024]{1,0:T(8,128)(2,1)} %tie.49), channel_id=1, source_target_pairs={{0,24},{8,16},{16,8},{24,0},{1,25},{9,17},{17,9},{25,1},{2,26},{10... | collective-permute-start | bytes 3145736 | tf_op jit(solution)/shard_map/ppermute | solution.py:712
  1228.3 178.4 %all-to-all-start.6 = ((bf16[8,480,2048]{2,1,0:T(8,128)(2,1)}), bf16[8,480,2048]{2,1,0:T(8,128)(2,1)}, u32[]{:S(2)}, u32[]{:S(2)}) async-start(bf16[8,480,2048]{2,1,0:T(8,128)(2,1)} %bitcast.285), calls=%async_computation.6 | async-start | bytes 31457280 | tf_op jit(solution)/shard_map/all_to_all | solution.py:828
  1234.0 303.5 %reduce-scatter.6.cloned.1.call-start = ((), (), s32[]{:S(2)}) async-start(), calls=%async_computation.19 | async-start | bytes 7864320 | tf_op jit(solution)/shard_map/reduce_scatter | solution.py:854
  1438.5 99.1 %all-to-all-start.9 = ((bf16[8,4,64,2048]{3,2,1,0:T(8,128)(2,1)}), bf16[8,4,64,2048]{3,2,1,0:T(8,128)(2,1)}, u32[]{:S(2)}, u32[]{:S(2)}) async-start(bf16[8,4,64,2048]{3,2,1,0:T(8,128)(2,1)} %tie.53), calls=%async_computation.11 | async-start | bytes 16777216 | tf_op jit(solution)/shard_map/all_to_all | solution.py:858
  1443.5 290.2 %reduce-scatter.8.cloned.1.call-start = ((), (), s32[]{:S(2)}) async-start(), calls=%async_computation.20 | async-start | bytes 7864320 | tf_op jit(solution)/shard_map/reduce_scatter | solution.py:878
  1572.5 76.6 %all-to-all-start.10 = ((bf16[8,4,64,1536]{3,2,1,0:T(8,128)(2,1)}), bf16[8,4,64,1536]{3,2,1,0:T(8,128)(2,1)}, u32[]{:S(2)}, u32[]{:S(2)}) async-start(bf16[8,4,64,1536]{3,2,1,0:T(8,128)(2,1)} %bitcast.304), calls=%async_computation.13 | async-start | bytes 12582912 | tf_op jit(solution)/shard_map/all_to_all | solution.py:883
  (104 other events, 2300.0 us)
Sparse Core Ops, SparseCore 0:
  9.6 157.9 all-gather.8
  169.8 114.9 all-gather.4
  387.2 121.5 all-gather.6
  1228.4 111.8 reduce-scatter.3
  1419.0 109.8 reduce-scatter.5
  1554.3 111.9 reduce-scatter.7

commit v3 on v2

--- a/solution.py
+++ b/solution.py
@@ -581,50 +581,111 @@
     )(raw, scales, gains, cosine, sine, grad_query, grad_key)
 
 
-def expert_kernel(
-    rows, grad, picked, gate, up, down, act_out, grad_gate, grad_up, grad_picked
+def expert_in_kernel(
+    rows, gate, up, router, own, gate_out, up_out, act_out, picked_out
 ):
+    logits = jnp.dot(rows[...], router[...], preferred_element_type=jnp.float32)
+    weights = jnp.exp(logits - jnp.max(logits, axis=1, keepdims=True))
+    picked = jnp.sum(weights * own[...], axis=1, keepdims=True)
+    picked = picked / jnp.sum(weights, axis=1, keepdims=True)
     gate_pre = jnp.dot(rows[...], gate[...], preferred_element_type=jnp.float32)
     up_pre = jnp.dot(rows[...], up[...], preferred_element_type=jnp.float32)
+    act = (gate_pre * jax.nn.sigmoid(gate_pre) * up_pre).astype(jnp.bfloat16)
+    gate_out[...] = gate_pre
+    up_out[...] = up_pre
+    act_out[...] = (act.astype(jnp.float32) * picked).astype(jnp.bfloat16)
+    picked_out[...] = picked
+
+
+def expert_back_kernel(
+    grad, gate_in, up_in, picked, gate, up, down, grad_gate, grad_up, grad_picked, grad_rows
+):
     grad_raw = lax.dot_general(
         grad[...], down[...], (((1,), (1,)), ((), ())), preferred_element_type=jnp.float32
     )
+    gate_pre, up_pre = gate_in[...], up_in[...]
     sigma = jax.nn.sigmoid(gate_pre)
     silu = gate_pre * sigma
     act = (silu * up_pre).astype(jnp.bfloat16).astype(jnp.float32)
-    act_out[...] = (act * picked[...]).astype(jnp.bfloat16)
     grad_picked[...] = jnp.sum(grad_raw * act, axis=1, keepdims=True)
     grad_act = grad_raw * picked[...]
-    grad_gate[...] = (
-        grad_act * up_pre * (sigma + silu * (1.0 - sigma))
-    ).astype(jnp.bfloat16)
-    grad_up[...] = (grad_act * silu).astype(jnp.bfloat16)
-
-
-def expert(rows, grad, picked, gate, up, down, block):
+    low_gate = (grad_act * up_pre * (sigma + silu * (1.0 - sigma))).astype(jnp.bfloat16)
+    low_up = (grad_act * silu).astype(jnp.bfloat16)
+    grad_gate[...] = low_gate
+    grad_up[...] = low_up
+    back = lax.dot_general(
+        low_gate, gate[...], (((1,), (1,)), ((), ())), preferred_element_type=jnp.float32
+    )
+    back = back + lax.dot_general(
+        low_up, up[...], (((1,), (1,)), ((), ())), preferred_element_type=jnp.float32
+    )
+    grad_rows[...] = back.astype(jnp.bfloat16)
+
+
+def whole(shape):
+    return pl.BlockSpec(shape, lambda i: (0, 0), pipeline_mode=pl.Buffered(1))
+
+
+def row_blocks(block, width):
+    return pl.BlockSpec((block, width), lambda i: (i, 0))
+
+
+def expert_in(rows, gate, up, router, own, block):
     count, width = rows.shape
     hidden = gate.shape[1]
-    once = pl.Buffered(1)
-    wide = pl.BlockSpec((block, width), lambda i: (i, 0))
-    narrow = pl.BlockSpec((block, hidden), lambda i: (i, 0))
-    one = pl.BlockSpec((block, 1), lambda i: (i, 0))
-    into = pl.BlockSpec((width, hidden), lambda i: (0, 0), pipeline_mode=once)
-    outof = pl.BlockSpec((hidden, width), lambda i: (0, 0), pipeline_mode=once)
+    narrow = row_blocks(block, hidden)
+    f32 = jnp.float32
+    return pl.pallas_call(
+        expert_in_kernel,
+        grid=(count // block,),
+        in_specs=[
+            row_blocks(block, width),
+            whole(gate.shape),
+            whole(up.shape),
+            whole(router.shape),
+            whole(own.shape),
+        ],
+        out_specs=(narrow, narrow, narrow, row_blocks(block, 1)),
+        out_shape=(
+            jax.ShapeDtypeStruct((count, hidden), f32),
+            jax.ShapeDtypeStruct((count, hidden), f32),
+            jax.ShapeDtypeStruct((count, hidden), jnp.bfloat16),
+            jax.ShapeDtypeStruct((count, 1), f32),
+        ),
+        cost_estimate=pl.CostEstimate(
+            flops=4 * count * width * hidden,
+            bytes_accessed=2 * count * width + (10 * count + 4 * width) * hidden,
+            transcendentals=count * hidden,
+        ),
+        compiler_params=pltpu.CompilerParams(vmem_limit_bytes=56 << 20),
+        name="expert_in",
+    )(rows, gate, up, router, own)
+
+
+def expert_back(grad, gate_pre, up_pre, picked, gate, up, down, block):
+    count, width = grad.shape
+    hidden = down.shape[0]
+    wide, narrow, one = [row_blocks(block, size) for size in (width, hidden, 1)]
     low = jax.ShapeDtypeStruct((count, hidden), jnp.bfloat16)
     return pl.pallas_call(
-        expert_kernel,
+        expert_back_kernel,
         grid=(count // block,),
-        in_specs=[wide, wide, one, into, into, outof],
-        out_specs=(narrow, narrow, narrow, one),
-        out_shape=(low, low, low, jax.ShapeDtypeStruct((count, 1), jnp.float32)),
+        in_specs=[wide, narrow, narrow, one, whole(gate.shape), whole(up.shape), whole(down.shape)],
+        out_specs=(narrow, narrow, one, wide),
+        out_shape=(
+            low,
+            low,
+            jax.ShapeDtypeStruct((count, 1), jnp.float32),
+            jax.ShapeDtypeStruct((count, width), jnp.bfloat16),
+        ),
         cost_estimate=pl.CostEstimate(
             flops=6 * count * width * hidden,
-            bytes_accessed=4 * count * width + 6 * (count + width) * hidden,
+            bytes_accessed=4 * count * width + (12 * count + 6 * width) * hidden,
             transcendentals=count * hidden,
         ),
-        compiler_params=pltpu.CompilerParams(vmem_limit_bytes=56 << 20),
-        name="expert",
-    )(rows, grad, picked, gate, up, down)
+        compiler_params=pltpu.CompilerParams(vmem_limit_bytes=58 << 20),
+        name="expert_back",
+    )(grad, gate_pre, up_pre, picked, gate, up, down)
 
 
 def tie(array, *others):
@@ -685,7 +746,6 @@
     strip = w_query.shape[0]
     first_row = plane * row_count
 
-    hidden_all = lax.all_gather(hidden[0], "ctx", axis=0, tiled=True)
     experts = w_router.shape[1]
     qkv = jnp.stack([w_query, w_key, w_value], axis=1).reshape(strip, 3, planes, share)
     qkv = qkv.transpose(2, 0, 1, 3).reshape(planes, strip, 3 * share)
@@ -697,6 +757,7 @@
     own_out = jnp.broadcast_to(w_out[None], (planes,) + w_out.shape)
     packed = jnp.concatenate([qkv, small, own_out], axis=2)
     packed = lax.all_to_all(packed, "ctx", 0, 0, tiled=True)
+    hidden_all = lax.all_gather(tie(hidden[0], packed), "ctx", axis=0, tiled=True)
     packed, out_rows = packed[:, :, :-width], packed[:, :, -width:]
     routes_at = 3 * share + experts + 4
     routes_all = packed[:, :, routes_at : packed.shape[2] - spare].astype(jnp.int32)
@@ -734,9 +795,11 @@
     def plane_sum(part):
         return part + sum(swap(part, step) for step in range(1, planes))
 
-    grad_all = lax.all_gather(tie(grad_output[0], hidden_all), "ctx", axis=0, tiled=True)
-    full_out = jnp.broadcast_to(tie(out_rows, packed)[None], (columns,) + out_rows.shape)
-    full_out = lax.all_to_all(full_out, "fsdp", 0, 0, tiled=True)
+    out_rows = jnp.broadcast_to(out_rows[None], (columns,) + out_rows.shape)
+    grad_all = lax.all_gather(
+        tie(grad_output[0], hidden_all, packed, out_rows), "ctx", axis=0, tiled=True
+    )
+    full_out = lax.all_to_all(out_rows, "fsdp", 0, 0, tiled=True)
     full_out = full_out.transpose(1, 0, 2, 3).reshape(width, width)
 
     seq_ids, places = seq_layout(token_order[0], lengths[0])
@@ -778,44 +841,40 @@
     )
     query, key, values = turn(raw, scales, gains, cosine, sine)
     attended = attend(seq_ids, query, key, values)
-    grad_send = dispatch(position, capacity, tie(grad_all, attended, full_out))
+    attended = attended.reshape(planes, row_count, share)
+    attended = jnp.concatenate(exchange(attended), axis=1)
+    grad_send = dispatch(position, capacity, tie(grad_all, attended))
     grad_in = lax.all_to_all(grad_send, "fsdp", 0, 0, tiled=True).reshape(-1, width)
-    attended = tie(attended, grad_send).reshape(planes, row_count, share)
-    attended = jnp.concatenate(exchange(attended), axis=1)
     middle = hidden[0].astype(f32) + mm(attended, full_out)
     scale_two = lax.rsqrt(jnp.mean(middle * middle, axis=-1, keepdims=True) + epsilon)
     middle_hat = middle * scale_two
     h_two = (middle_hat * gain_ffn).astype(bf16)
 
-    h_two_all = lax.all_gather(h_two, "ctx", axis=0, tiled=True)
-    h_all = tie(h_two_all, grad_in)
-    gate = jnp.concatenate(exchange(w_gate, h_two_all))
-    up = jnp.concatenate(exchange(w_up, h_all))
-    down = jnp.concatenate(exchange(w_down, h_all))
-    probs_all = jax.nn.softmax(mm(h_all, full_router), axis=-1)
+    h_two_all = lax.all_gather(tie(h_two, grad_send), "ctx", axis=0, tiled=True)
+    came = [swap(tie(w_gate[plane ^ step], h_two_all), step) for step in range(1, planes)]
+    gate = jnp.concatenate(by_plane([w_gate[plane]] + came))
+    h_all = tie(h_two_all, grad_in, *came[:-1])
+    up = jnp.concatenate(exchange(w_up, h_two_all))
     probs = jax.nn.softmax(mm(h_two, full_router), axis=-1)
-    probs_plane = lax.dynamic_index_in_dim(
-        probs_all.reshape(group_rows, columns, experts_here), plane, 2, keepdims=False
-    )
-    rows_in = lax.all_to_all(dispatch(position, capacity, h_all), "fsdp", 0, 0, tiled=True).reshape(-1, width)
-    probs_plane = probs_plane.reshape(planes, row_count, columns).transpose(2, 0, 1)
-    slot_probs = jnp.sum(jnp.where(holds, probs_plane[:, :, None, :], 0.0), axis=3)
-    picked = lax.all_to_all(slot_probs, "fsdp", 0, 0, tiled=True).reshape(-1, 1)
-    act_picked, grad_gate, grad_up, grad_picked = expert(
-        rows_in, grad_in, picked, gate, up, down, planes * capacity
-    )
-    grad_picked = lax.all_to_all(
-        grad_picked.reshape(columns, planes, capacity), "fsdp", 0, 0, tiled=True
-    )
+    rows_in = lax.all_to_all(dispatch(position, capacity, h_all), "fsdp", 0, 0, tiled=True)
+    rows_in = rows_in.reshape(-1, width)
+    own = experts_here * lax.axis_index("fsdp") + plane
+    own = (jnp.arange(experts)[None, :] == own).astype(f32)
+    slot_block = planes * capacity
+    gate_pre, up_pre, act_picked, picked = expert_in(
+        rows_in, gate, up, full_router, own, slot_block
+    )
+    down = jnp.concatenate(exchange(w_down, h_two_all, act_picked))
     grad_down_w = t_mm(act_picked, grad_in).astype(bf16)
-    grad_gate = tie(grad_gate, grad_down_w, grad_picked)
-
-    def blocks(whole):
-        return whole.reshape(planes, whole.shape[0] // planes, whole.shape[1])
+    grad_gate, grad_up, grad_picked, grad_rows = expert_back(
+        grad_in, tie(gate_pre, grad_down_w), up_pre, picked, gate, up, down, slot_block
+    )
+
+    def blocks(matrix):
+        return matrix.reshape(planes, matrix.shape[0] // planes, matrix.shape[1])
 
     came, down_grad = exchange_after(blocks(grad_down_w), [None] * (planes - 1))
-    grad_rows = (mm_t(grad_gate, gate) + mm_t(grad_up, up)).astype(bf16)
-    grad_rows = tie(grad_rows, *came[:-1])
+    grad_rows = tie(grad_rows, *came)
     grad_rows = lax.all_to_all(
         grad_rows.reshape(columns, planes * capacity, width), "fsdp", 0, 0, tiled=True
     )
@@ -824,7 +883,10 @@
     came, up_grad = exchange_after(blocks(grad_up_w), came)
     came, gate_grad = exchange_after(blocks(grad_gate_w), came)
     expert_out = mm(act_picked, down).astype(bf16)
-    grad_rows = tie(grad_rows, *came, expert_out)
+    grad_picked = lax.all_to_all(
+        tie(grad_picked, grad_rows).reshape(columns, planes, capacity), "fsdp", 0, 0, tiled=True
+    )
+    grad_rows = tie(grad_rows, *came, expert_out, grad_picked)
     expert_out = lax.all_to_all(
         expert_out.reshape(columns, planes * capacity, width), "fsdp", 0, 0, tiled=True
     )
@@ -850,11 +912,11 @@
     grad_att = mm_t(grad_branch, full_out).astype(bf16)
     grad_att = grad_att.reshape(row_count, planes, share).transpose(1, 0, 2)
     grad_att = jnp.concatenate(exchange(grad_att))
-    mixed_part = combine(tie(expert_out, grad_att))
+    grad_out_w = t_mm(attended, grad_branch).astype(bf16)
+    grad_out_w = grad_out_w.reshape(planes, columns, strip, width).transpose(1, 0, 2, 3)
+    mixed_part = combine(tie(expert_out, grad_att, grad_out_w))
     mixed = lax.psum_scatter(mixed_part, "ctx", scatter_dimension=0, tiled=True)
     output = (middle + mixed.astype(f32)).astype(bf16)
-    grad_out_w = t_mm(attended, grad_branch).astype(bf16)
-    grad_out_w = grad_out_w.reshape(planes, columns, strip, width).transpose(1, 0, 2, 3)
     grad_out_w = lax.all_to_all(
         tie(grad_out_w, mixed_part), "fsdp", 0, 0, tiled=True
     )
@@ -879,15 +941,20 @@
         grad_part.astype(bf16), "ctx", scatter_dimension=0, tiled=True
     ).astype(f32)
     grad_attn_gain = jnp.sum(grad_part * (hidden_wide * scale_one), axis=0)
-    grad_qkv_w = t_mm(h_one, grad_qkv).reshape(planes, columns, strip, 3 * share)
-    grad_qkv_w = lax.all_to_all(
-        grad_qkv_w.transpose(1, 0, 2, 3).astype(bf16), "fsdp", 0, 0, tiled=True
-    )
-    grad_qkv_w = jnp.sum(grad_qkv_w.astype(f32), axis=0).astype(bf16)
-    grad_qkv_w = jnp.concatenate([grad_qkv_w, grad_out_w], axis=2)
-    grad_qkv_w = lax.all_to_all(grad_qkv_w, "ctx", 0, 0, tiled=True)
-    grad_out_w = jnp.sum(grad_qkv_w[:, :, 3 * share :].astype(f32), axis=0)
-    grad_qkv_w = grad_qkv_w[:, :, : 3 * share].reshape(planes, strip, 3, share).transpose(2, 1, 0, 3)
+    rows_of = jnp.arange(planes)[:, None] == plane
+    gains = [jnp.where(rows_of, g[None], 0.0).reshape(width) for g in grad_gains]
+    gains = [g[:, None] for g in [grad_attn_gain, grad_ffn_gain] + gains]
+    small = jnp.concatenate([grad_router] + gains, axis=1).reshape(planes * columns, -1)
+    small = lax.all_to_all(small, both, 0, 0, tiled=True)
+    grad_qkv = tie(grad_qkv, small)
+    small = jnp.sum(small, axis=0).reshape(strip, -1)
+    grad_out_w = sum(x.astype(f32) for x in exchange(grad_out_w))
+    sums = t_mm(h_one, grad_qkv).astype(bf16)
+    sums = sums.reshape(planes, columns, strip, -1).transpose(1, 0, 2, 3)
+    sums = lax.all_to_all(sums, "fsdp", 0, 0, tiled=True)
+    sums = jnp.sum(sums.astype(f32), axis=0).astype(bf16)
+    sums = lax.all_to_all(sums, "ctx", 0, 0, tiled=True)
+    grad_qkv_w = sums.reshape(planes, strip, 3, share).transpose(2, 1, 0, 3)
     grad_qkv_w = grad_qkv_w.reshape(3, strip, width).astype(f32)
 
     x_hat = hidden[0].astype(f32)
@@ -898,17 +965,6 @@
         grad_hat - x_hat * jnp.mean(grad_hat * x_hat, axis=-1, keepdims=True)
     )
 
-    def summed(arrays):
-        parts = jnp.concatenate(
-            [x.reshape(planes * columns, -1) for x in arrays], axis=1
-        )
-        parts = tie(parts, grad_qkv_w)
-        return jnp.sum(lax.all_to_all(parts, both, 0, 0, tiled=True), axis=0)
-
-    own = jnp.arange(planes)[:, None] == plane
-    gains = [jnp.where(own, g[None], 0.0) for g in grad_gains]
-    totals = summed([grad_router, grad_attn_gain, grad_ffn_gain] + gains)
-    gains = totals[strip * experts :].reshape(4, strip)
     return (
         output[None],
         grad_input[None],
@@ -916,11 +972,11 @@
         grad_qkv_w[1],
         grad_qkv_w[2],
         grad_out_w,
-        totals[: strip * experts].reshape(strip, experts),
-        gains[0],
-        gains[1],
-        gains[2],
-        gains[3],
+        small[:, :experts],
+        small[:, experts],
+        small[:, experts + 1],
+        small[:, experts + 2],
+        small[:, experts + 3],
         gate_grad,
         up_grad,
         down_grad,

time: 1760 us -> 1640 us (0.932)
  starting transfers between devices: 236 us -> 142 us
  blocking collectives: 104 us -> 24.9 us
  waiting for transfers between devices: 729 us -> 800 us
  matrix products: 242 us -> 185 us
  Pallas kernels: 174 us -> 220 us
    ppermute x33 -> x36, starting transfers between devices: 177 us -> 83.4 us  [swap(): return lax.ppermute(part, 'ctx', [(i, i ^ step) for i in range(planes)])]
    all_to_all x1, blocking collectives: 104 us -> 24.9 us  [plane_shards(): small = lax.all_to_all(small, both, 0, 0, tiled=True)]
    all_to_all x1, waiting for transfers between devices: 0.01 us -> 50.2 us  [plane_shards(): lax.all_to_all(dispatch(position, capacity, h_all), 'fsdp', 0, 0, tiled=T...]
    dot_general x5 -> x3, matrix products: 74.8 us -> 25.3 us  [mm_t(): lax.dot_general(left, right, (((1,), (1,)), ((), ())), preferred_element_...]
    pallas_call x1 -> x2, Pallas kernels: 63 us -> 108 us  [the longest x1 63.4 us: expert_back(): pl.pallas_call(expert_back_kernel, grid=(count // block,), in_specs=[wide...]
    all_to_all x1, waiting for transfers between devices: 36.3 us -> 76 us  [plane_shards(): packed = lax.all_to_all(packed, 'fsdp', 0, 0, tiled=True)]
    all_to_all x1, waiting for transfers between devices: 0.01 us -> 32.4 us  [plane_shards(): lax.all_to_all(grad_rows.reshape(columns, planes * capacity, width), 'fsd...]
    all_gather x3, waiting for transfers between devices: 153 us -> 128 us  [the longest x1 107 us: plane_shards(): h_two_all = lax.all_gather(tie(h_two, grad_send), 'ctx', axis=0, tiled=True)]
  transfers between devices with their start and end apart: 51 -> 53, of which waited for: 30 -> 31; matrix products, arithmetic and copies ran while one was open for 21% -> 20% of each run, Pallas kernels for 6% -> 13%
where the time goes in v3:
time: 1640 us; the launch traced here: 1630 us
  waiting for transfers between devices  800 us (49%)
  Pallas kernels  220 us (13%)
  matrix products  185 us (11%)
  local copies, waits for them, and re-layouts  143 us (9%)
  starting transfers between devices  142 us (9%)
  other arithmetic  98.5 us (6%)
  blocking collectives  24.9 us (2%)
    ppermute x36, waiting for transfers between devices, swap(): return lax.ppermute(part, 'ctx', [(i, i ^ step) for i in range(planes)])  301 us
    all_gather x1, waiting for transfers between devices, plane_shards(): h_two_all = lax.all_gather(tie(h_two, grad_send), 'ctx', axis=0, tiled=True)  107 us
    reduce_scatter x1, waiting for transfers between devices, plane_shards(): lax.psum_scatter(combine(grad_rows), 'ctx', scatter_dimension=0, tiled=True)  95.3 us
    dot_general x6, matrix products, t_mm(): lax.dot_general(left, right, (((0,), (0,)), ((), ())), preferred_element_...  86.8 us
    ppermute x36, starting transfers between devices, swap(): return lax.ppermute(part, 'ctx', [(i, i ^ step) for i in range(planes)])  83.4 us
    all_to_all x1, waiting for transfers between devices, plane_shards(): packed = lax.all_to_all(packed, 'fsdp', 0, 0, tiled=True)  76 us
    pallas_call x1, Pallas kernels, expert_back(): pl.pallas_call(expert_back_kernel, grid=(count // block,), in_specs=[wide...  63.4 us
    all_to_all x1, waiting for transfers between devices, plane_shards(): lax.all_to_all(dispatch(position, capacity, h_all), 'fsdp', 0, 0, tiled=T...  50.2 us
  transfers between devices with their start and end apart: 53, of which 31 were waited for; matrix products, arithmetic and copies ran while one was open for 20% of the time, Pallas kernels for 13%

profile of v3, /device:TPU:0, one launch (start us, length us, event | category | flops | bytes accessed | tf_op | source)
XLA Modules:
  0.0 1628.8 jit_solution(3421221492674880704)
XLA Ops:
  28.8 42.8 %all-to-all-done.refs_1_ = bf16[4,64,3712]{2,1,0:T(8,128)(2,1)S(1)} async-done(((bf16[4,64,3712]{2,1,0:T(8,128)(2,1)}), bf16[4,64,3712]{2,1,0:T(8,128)(2,1)S(1)}, u32[]{:S(2)}, u32[]{:S(2)}) %all-to-all-start) | async-done | bytes 1900576 | tf_op jit(solution)/shard_map/all_to_all | solution.py:759
  84.2 76.0 %all-to-all-done.1 = bf16[8,4,64,1664]{3,2,1,0:T(8,128)(2,1)} async-done(((bf16[8,4,64,1664]{3,2,1,0:T(8,128)(2,1)}), bf16[8,4,64,1664]{3,2,1,0:T(8,128)(2,1)}, u32[]{:S(2)}, u32[]{:S(2)}) %all-to-all-start.1) | async-done | bytes 6815776 | tf_op jit(solution)/shard_map/all_to_all | solution.py:766
  166.6 20.9 %all-gather.4.cloned.1.call-done.refs_1_ = bf16[1536,2048]{1,0:T(8,128)(2,1)} async-done(((bf16[384,2048]{1,0:T(8,128)(2,1)}), bf16[1536,2048]{1,0:T(8,128)(2,1)}) %all-gather.4.cloned.1.call-update) | async-done | bytes 6291472 | tf_op jit(solution)/shard_map/all_gather | solution.py:760
  215.7 17.8 %fusion.26.raw = f32[1536,1664]{1,0:T(8,128)} fusion(bf16[2048,1664]{1,0:T(8,128)(2,1)} %bitcast.298, bf16[1536,2048]{1,0:T(8,128)(2,1)} %all-gather.4.cloned.1.call-done.refs_1_, f32[2048]{0:T(1024)S(1)} %get-tuple-element.125, f32[1536]{0:T(1024)S(1)} %add_rsqrt_fusion.1), kind=kOutput, calls=%fused_computation.65 | convolution fusion | flops 10481565696 | bytes 23345152 | tf_op jit(solution)/shard_map/dot_general | solution.py:704
  255.6 28.4 %attend.1 = bf16[1536,512]{1,0:T(8,128)(2,1)S(1)} custom-call(s32[1536,1]{1,0:T(8,128)S(1)} %broadcast_in_dim.171.seq_rows, s32[1,1536]{1,0:T(1,128)S(1)} %broadcast_in_dim.146.seq_cols, bf16[1536,512]{1,0:T(8,128)(2,1)S(1)} %get-tuple-element.32.query, bf16[1536,512]{1,0:T(8,128)(2,1)S(1)} %get-tuple-element.33.key, bf16[1536,512]{1,0:T(8,128)(2,1)} %copy-done.15), custom_call_target="tpu_custom_call" | custom-call | flops 4831838208 | bytes 6291456 | tf_op jit(solution)/shard_map/attend/pallas_call | solution.py:421
  306.4 33.6 %collective-permute-done.4 = bf16[384,512]{1,0:T(8,128)(2,1)S(1)} collective-permute-done((bf16[384,512]{1,0:T(8,128)(2,1)S(1)}, bf16[384,512]{1,0:T(8,128)(2,1)S(1)}, u32[]{:S(2)}, u32[]{:S(2)}) %collective-permute-start.4) | collective-permute-done | bytes 393248 | tf_op jit(solution)/shard_map/ppermute | solution.py:773
  388.3 107.1 %all-gather.8.cloned.1.call-done.refs_1_.refs_0_ = bf16[1536,2048]{1,0:T(8,128)(2,1)} async-done(((bf16[384,2048]{1,0:T(8,128)(2,1)}), bf16[1536,2048]{1,0:T(8,128)(2,1)}) %all-gather.8.cloned.1.call-update) | async-done | bytes 6291472 | tf_op jit(solution)/shard_map/all_gather | solution.py:853
  500.6 41.6 %collective-permute-done.6.refs_2_ = bf16[512,1024]{1,0:T(8,128)(2,1)} collective-permute-done((bf16[512,1024]{1,0:T(8,128)(2,1)}, bf16[512,1024]{1,0:T(8,128)(2,1)}, u32[]{:S(2)}, u32[]{:S(2)}) %collective-permute-start.6) | collective-permute-done | bytes 1048608 | tf_op jit(solution)/shard_map/ppermute | solution.py:773
  571.9 19.8 %collective-permute-done.8 = bf16[512,1024]{1,0:T(8,128)(2,1)} collective-permute-done((bf16[512,1024]{1,0:T(8,128)(2,1)}, bf16[512,1024]{1,0:T(8,128)(2,1)}, u32[]{:S(2)}, u32[]{:S(2)}) %collective-permute-start.8) | collective-permute-done | bytes 1048608 | tf_op jit(solution)/shard_map/ppermute | solution.py:773
  591.7 21.0 %collective-permute-start.13 = (bf16[256,2048]{1,0:T(8,128)(2,1)}, bf16[256,2048]{1,0:T(8,128)(2,1)}, u32[]{:S(2)}, u32[]{:S(2)}) collective-permute-start(bf16[256,2048]{1,0:T(8,128)(2,1)} %tie.45), channel_id=1, source_target_pairs={{0,16},{8,24},{16,0},{24,8},{1,17},{9,25},{17,1},{25,9},{2,18},{10... | collective-permute-start | bytes 3145736 | tf_op jit(solution)/shard_map/ppermute | solution.py:773
  617.5 61.3 %collective-permute-done.10 = bf16[512,1024]{1,0:T(8,128)(2,1)} collective-permute-done((bf16[512,1024]{1,0:T(8,128)(2,1)}, bf16[512,1024]{1,0:T(8,128)(2,1)}, u32[]{:S(2)}, u32[]{:S(2)}) %collective-permute-start.10) | collective-permute-done | bytes 1048608 | tf_op jit(solution)/shard_map/ppermute | solution.py:773
  686.0 50.2 %all-to-all-done.4 = bf16[8,4,120,2048]{3,2,1,0:T(8,128)(2,1)} async-done(((bf16[8,4,120,2048]{3,2,1,0:T(8,128)(2,1)}), bf16[8,4,120,2048]{3,2,1,0:T(8,128)(2,1)}, u32[]{:S(2)}, u32[]{:S(2)}) %all-to-all-start.4) | async-done | bytes 15728672 | tf_op jit(solution)/shard_map/all_to_all | solution.py:859
  736.2 44.6 %expert_in.1 = (f32[3840,1024]{1,0:T(8,128)}, f32[3840,1024]{1,0:T(8,128)}, bf16[3840,1024]{1,0:T(8,128)(2,1)}, f32[3840,1]{1,0:T(8,128)}) custom-call(bf16[3840,2048]{1,0:T(8,128)(2,1)} %bitcast.38.rows, bf16[2048,1024]{1,0:T(8,128)(2,1)} %pad_maximum_fusion.2.gate, bf16[2048,1024]{1,0:T(8,128)(2,1)} %pad_maximum_fusion.4.up, ...), custom_call_target="tpu_custom_call" | custom-call | flops 32212254720 | bytes 63438848 | tf_op jit(solution)/shard_map/expert_in/pallas_call | solution.py:638
  780.8 22.5 %convolution_convert_fusion.5.refs_1_ = bf16[1024,2048]{1,0:T(8,128)(2,1)} fusion(bf16[3840,1024]{1,0:T(8,128)(2,1)} %get-tuple-element.35.refs_1_, bf16[3840,2048]{1,0:T(8,128)(2,1)} %bitcast.34.refs_1_.grad), kind=kOutput, calls=%fused_computation.40 | convolution fusion | flops 16108224512 | bytes 27787264 | tf_op jit(solution)/shard_map/dot_general | solution.py:714
  833.7 63.4 %expert_back.1 = (bf16[3840,1024]{1,0:T(8,128)(2,1)}, bf16[3840,1024]{1,0:T(8,128)(2,1)}, f32[3840,1]{1,0:T(8,128)}, bf16[3840,2048]{1,0:T(8,128)(2,1)}) custom-call(bf16[3840,2048]{1,0:T(8,128)(2,1)} %bitcast.34.refs_1_.grad, f32[3840,1024]{1,0:T(8,128)} %tie.49.gate_in, f32[3840,1024]{1,0:T(8,128)} %get-tuple-element.37.up_in, ...), custom_call_target="tpu_custom_call" | custom-call | flops 48318382080 | bytes 91226112 | tf_op jit(solution)/shard_map/expert_back/pallas_call | solution.py:670
  909.9 21.5 %convolution_convert_fusion.3 = bf16[2048,1024]{1,0:T(8,128)(2,1)S(1)} fusion(bf16[3840,2048]{1,0:T(8,128)(2,1)} %bitcast.38.rows, bf16[3840,1024]{1,0:T(8,128)(2,1)} %get-tuple-element.41), kind=kOutput, calls=%fused_computation.38 | convolution fusion | flops 16108224512 | bytes 27787264 | tf_op jit(solution)/shard_map/dot_general | solution.py:714
  937.8 21.4 %convolution_convert_fusion.4 = bf16[2048,1024]{1,0:T(8,128)(2,1)S(1)} fusion(bf16[3840,2048]{1,0:T(8,128)(2,1)} %bitcast.38.rows, bf16[3840,1024]{1,0:T(8,128)(2,1)} %get-tuple-element.40), kind=kOutput, calls=%fused_computation.39 | convolution fusion | flops 16108224512 | bytes 27787264 | tf_op jit(solution)/shard_map/dot_general | solution.py:714
  963.2 84.4 %collective-permute-done.20.refs_1_ = bf16[512,1024]{1,0:T(8,128)(2,1)} collective-permute-done((bf16[512,1024]{1,0:T(8,128)(2,1)}, bf16[512,1024]{1,0:T(8,128)(2,1)}, u32[]{:S(2)}, u32[]{:S(2)}) %collective-permute-start.20) | collective-permute-done | bytes 1048608 | tf_op jit(solution)/shard_map/ppermute | solution.py:773
  1050.5 32.4 %all-to-all-done.6.refs_1_.refs_0_ = bf16[8,480,2048]{2,1,0:T(8,128)(2,1)} async-done(((bf16[8,480,2048]{2,1,0:T(8,128)(2,1)}), bf16[8,480,2048]{2,1,0:T(8,128)(2,1)}, u32[]{:S(2)}, u32[]{:S(2)}) %all-to-all-start.6) | async-done | bytes 15728672 | tf_op jit(solution)/shard_map/all_to_all | solution.py:878
  1089.2 22.4 %convolution_convert_fusion.refs_4_ = bf16[3840,2048]{1,0:T(8,128)(2,1)} fusion(bf16[3840,1024]{1,0:T(8,128)(2,1)} %get-tuple-element.35.refs_1_, bf16[256,2048]{1,0:T(8,128)(2,1)} %get-tuple-element.167, bf16[256,2048]{1,0:T(8,128)(2,1)} %get-tuple-element.168, bf16[256,2048]{1,0:T(8,128)(2,1)} %get-tuple-element.169, bf16[256,2048]{1,0:T(8,128)(2,1)} %get-tuple-element.166), kind=kOutput, calls=%fused_computation.6 | convolution fusion | flops 16130768896 | bytes 27787264 | tf_op jit(solution)/shard_map/dot_general | solution.py:704
  1144.3 95.3 %reduce-scatter.4.cloned.1.call-done = bf16[384,2048]{1,0:T(8,128)(2,1)} async-done(((bf16[1536,2048]{1,0:T(8,128)(2,1)}), bf16[384,2048]{1,0:T(8,128)(2,1)}) %reduce-scatter.4.cloned.1.call-update) | async-done | bytes 1572880 | tf_op jit(solution)/shard_map/reduce_scatter | solution.py:893
  1328.9 45.7 %attend_back.1 = (f32[1536,512]{1,0:T(8,128)}, f32[1536,512]{1,0:T(8,128)}, f32[1536,512]{1,0:T(8,128)}) custom-call(s32[1536,1]{1,0:T(8,128)S(1)} %broadcast_in_dim.171.seq_rows, s32[1,1536]{1,0:T(1,128)S(1)} %copy-done.10, bf16[1536,512]{1,0:T(8,128)(2,1)S(1)} %copy-done.12, bf16[1536,512]{1,0:T(8,128)(2,1)S(1)} %copy-done.14, ...), custom_call_target="tpu_custom_call" | custom-call | flops 12079595520 | bytes 15728640 | tf_op jit(solution)/shard_map/attend_back/pallas_call | solution.py:440
  1449.9 24.9 %all_to_all.67 = f32[32,1,2304]{2,1,0:T(1,128)S(1)} all-to-all(f32[32,1,2304]{2,1,0:T(1,128)S(1)} %all_to_all.54), channel_id=1, replica_groups=mesh['ctx'=4,'fsdp'=8] {'ctx','fsdp'}, dimensions={0} | all-to-all | bytes 589824 | tf_op jit(solution)/shard_map/all_to_all | solution.py:948
  1533.9 36.8 %all-to-all-done.10 = bf16[8,4,64,1536]{3,2,1,0:T(8,128)(2,1)} async-done(((bf16[8,4,64,1536]{3,2,1,0:T(8,128)(2,1)}), bf16[8,4,64,1536]{3,2,1,0:T(8,128)(2,1)}, u32[]{:S(2)}, u32[]{:S(2)}) %all-to-all-start.10) | async-done | bytes 6291488 | tf_op jit(solution)/shard_map/all_to_all | solution.py:954
  (466 shorter events, 577.1 us)
Async XLA Ops:
  27.7 159.9 %all-gather.4.cloned.1.call-start = ((), (), s32[]{:S(2)}) async-start(), calls=%async_computation.15 | async-start | bytes 7864320 | tf_op jit(solution)/shard_map/all_gather | solution.py:760
  77.9 82.3 %all-to-all-start.1 = ((bf16[8,4,64,1664]{3,2,1,0:T(8,128)(2,1)}), bf16[8,4,64,1664]{3,2,1,0:T(8,128)(2,1)}, u32[]{:S(2)}, u32[]{:S(2)}) async-start(bf16[8,4,64,1664]{3,2,1,0:T(8,128)(2,1)} %broadcast_in_dim.153), calls=%async_computation.1 | async-start | bytes 13631488 | tf_op jit(solution)/shard_map/all_to_all | solution.py:766
  83.0 259.9 %all-gather.6.cloned.1.call-start = ((), (), s32[]{:S(2)}) async-start(), calls=%async_computation.16 | async-start | bytes 7864320 | tf_op jit(solution)/shard_map/all_gather | solution.py:799
  196.4 160.1 %all-to-all-start.2 = ((bf16[8,4,64,2048]{3,2,1,0:T(8,128)(2,1)}), bf16[8,4,64,2048]{3,2,1,0:T(8,128)(2,1)}, u32[]{:S(2)}, u32[]{:S(2)}) async-start(bf16[8,4,64,2048]{3,2,1,0:T(8,128)(2,1)} %broadcast_in_dim.157.refs_3_), calls=%async_computation.2 | async-start | bytes 16777216 | tf_op jit(solution)/shard_map/all_to_all | solution.py:802
  356.5 187.8 %all-to-all-start.3 = ((bf16[8,4,120,2048]{3,2,1,0:T(8,128)(2,1)}), bf16[8,4,120,2048]{3,2,1,0:T(8,128)(2,1)}, u32[]{:S(2)}, u32[]{:S(2)}) async-start(bf16[8,4,120,2048]{3,2,1,0:T(8,128)(2,1)} %dispatch.2.refs_1_), calls=%async_computation.3 | async-start | bytes 31457280 | tf_op jit(solution)/shard_map/all_to_all | solution.py:847
  362.1 133.3 %all-gather.8.cloned.1.call-start = ((), (), s32[]{:S(2)}) async-start(), calls=%async_computation.17 | async-start | bytes 7864320 | tf_op jit(solution)/shard_map/all_gather | solution.py:853
  557.8 178.4 %all-to-all-start.4 = ((bf16[8,4,120,2048]{3,2,1,0:T(8,128)(2,1)}), bf16[8,4,120,2048]{3,2,1,0:T(8,128)(2,1)}, u32[]{:S(2)}, u32[]{:S(2)}) async-start(bf16[8,4,120,2048]{3,2,1,0:T(8,128)(2,1)} %dispatch.3), calls=%async_computation.4 | async-start | bytes 31457280 | tf_op jit(solution)/shard_map/all_to_all | solution.py:859
  565.1 113.7 %collective-permute-start.10 = (bf16[512,1024]{1,0:T(8,128)(2,1)}, bf16[512,1024]{1,0:T(8,128)(2,1)}, u32[]{:S(2)}, u32[]{:S(2)}) collective-permute-start(bf16[512,1024]{1,0:T(8,128)(2,1)} %tie.41), channel_id=1, source_target_pairs={{0,16},{8,24},{16,0},{24,8},{1,17},{9,25},{17,1},{25,9},{2,18},{10... | collective-permute-start | bytes 3145736 | tf_op jit(solution)/shard_map/ppermute | solution.py:773
  567.9 110.9 %collective-permute-start.11 = (bf16[512,1024]{1,0:T(8,128)(2,1)}, bf16[512,1024]{1,0:T(8,128)(2,1)}, u32[]{:S(2)}, u32[]{:S(2)}) collective-permute-start(bf16[512,1024]{1,0:T(8,128)(2,1)} %tie.42), channel_id=1, source_target_pairs={{0,24},{8,16},{16,8},{24,0},{1,25},{9,17},{17,9},{25,1},{2,26},{10... | collective-permute-start | bytes 3145736 | tf_op jit(solution)/shard_map/ppermute | solution.py:773
  571.9 231.4 %collective-permute-start.12 = (bf16[256,2048]{1,0:T(8,128)(2,1)}, bf16[256,2048]{1,0:T(8,128)(2,1)}, u32[]{:S(2)}, u32[]{:S(2)}) collective-permute-start(bf16[256,2048]{1,0:T(8,128)(2,1)} %tie.43), channel_id=1, source_target_pairs={{0,8},{8,0},{16,24},{24,16},{1,9},{9,1},{17,25},{25,17},{2,10},{10... | collective-permute-start | bytes 3145736 | tf_op jit(solution)/shard_map/ppermute | solution.py:773
  591.7 211.6 %collective-permute-start.13 = (bf16[256,2048]{1,0:T(8,128)(2,1)}, bf16[256,2048]{1,0:T(8,128)(2,1)}, u32[]{:S(2)}, u32[]{:S(2)}) collective-permute-start(bf16[256,2048]{1,0:T(8,128)(2,1)} %tie.45), channel_id=1, source_target_pairs={{0,16},{8,24},{16,0},{24,8},{1,17},{9,25},{17,1},{25,9},{2,18},{10... | collective-permute-start | bytes 3145736 | tf_op jit(solution)/shard_map/ppermute | solution.py:773
  616.5 186.7 %collective-permute-start.14 = (bf16[256,2048]{1,0:T(8,128)(2,1)}, bf16[256,2048]{1,0:T(8,128)(2,1)}, u32[]{:S(2)}, u32[]{:S(2)}) collective-permute-start(bf16[256,2048]{1,0:T(8,128)(2,1)} %tie.47), channel_id=1, source_target_pairs={{0,24},{8,16},{16,8},{24,0},{1,25},{9,17},{17,9},{25,1},{2,26},{10... | collective-permute-start | bytes 3145736 | tf_op jit(solution)/shard_map/ppermute | solution.py:773
  812.2 85.0 %collective-permute-start.17 = (bf16[256,2048]{1,0:T(8,128)(2,1)}, bf16[256,2048]{1,0:T(8,128)(2,1)}, u32[]{:S(2)}, u32[]{:S(2)}) collective-permute-start(bf16[256,2048]{1,0:T(8,128)(2,1)} %get-tuple-element.147), channel_id=1, source_target_pairs={{0,24},{8,16},{16,8},{24,0},{1,25},{9,17},{17,9},{25,1},{2,26},{10... | collective-permute-start | bytes 3145736 | tf_op jit(solution)/shard_map/ppermute | solution.py:773
  813.8 89.9 %collective-permute-start.16 = (bf16[256,2048]{1,0:T(8,128)(2,1)S(1)}, bf16[256,2048]{1,0:T(8,128)(2,1)}, u32[]{:S(2)}, u32[]{:S(2)}) collective-permute-start(bf16[256,2048]{1,0:T(8,128)(2,1)S(1)} %get-tuple-element.148), channel_id=1, source_target_pairs={{0,16},{8,24},{16,0},{24,8},{1,17},{9,25},{17,1},{25,9},{2,18},{10... | collective-permute-start | bytes 3145736 | tf_op jit(solution)/shard_map/ppermute | solution.py:773
  903.7 179.3 %all-to-all-start.6 = ((bf16[8,480,2048]{2,1,0:T(8,128)(2,1)}), bf16[8,480,2048]{2,1,0:T(8,128)(2,1)}, u32[]{:S(2)}, u32[]{:S(2)}) async-start(bf16[8,480,2048]{2,1,0:T(8,128)(2,1)} %bitcast.291), calls=%async_computation.6 | async-start | bytes 31457280 | tf_op jit(solution)/shard_map/all_to_all | solution.py:878
  935.0 112.7 %collective-permute-start.20 = (bf16[512,1024]{1,0:T(8,128)(2,1)}, bf16[512,1024]{1,0:T(8,128)(2,1)}, u32[]{:S(2)}, u32[]{:S(2)}) collective-permute-start(bf16[512,1024]{1,0:T(8,128)(2,1)} %tie.53), channel_id=1, source_target_pairs={{0,16},{8,24},{16,0},{24,8},{1,17},{9,25},{17,1},{25,9},{2,18},{10... | collective-permute-start | bytes 3145736 | tf_op jit(solution)/shard_map/ppermute | solution.py:773
  935.0 112.7 %collective-permute-start.18 = (bf16[512,1024]{1,0:T(8,128)(2,1)}, bf16[512,1024]{1,0:T(8,128)(2,1)}, u32[]{:S(2)}, u32[]{:S(2)}) collective-permute-start(bf16[512,1024]{1,0:T(8,128)(2,1)} %tie.51), channel_id=1, source_target_pairs={{0,8},{8,0},{16,24},{24,16},{1,9},{9,1},{17,25},{25,17},{2,10},{10... | collective-permute-start | bytes 3145736 | tf_op jit(solution)/shard_map/ppermute | solution.py:773
  961.6 149.9 %collective-permute-start.23 = (bf16[512,1024]{1,0:T(8,128)(2,1)}, bf16[512,1024]{1,0:T(8,128)(2,1)}, u32[]{:S(2)}, u32[]{:S(2)}) collective-permute-start(bf16[512,1024]{1,0:T(8,128)(2,1)} %tie.56), channel_id=1, source_target_pairs={{0,24},{8,16},{16,8},{24,0},{1,25},{9,17},{17,9},{25,1},{2,26},{10... | collective-permute-start | bytes 3145736 | tf_op jit(solution)/shard_map/ppermute | solution.py:773
  1089.1 150.5 %reduce-scatter.4.cloned.1.call-start = ((), (), s32[]{:S(2)}) async-start(), calls=%async_computation.18 | async-start | bytes 7864320 | tf_op jit(solution)/shard_map/reduce_scatter | solution.py:893
  1127.2 178.4 %all-to-all-start.5 = ((bf16[8,480,2048]{2,1,0:T(8,128)(2,1)}), bf16[8,480,2048]{2,1,0:T(8,128)(2,1)}, u32[]{:S(2)}, u32[]{:S(2)}) async-start(bf16[8,480,2048]{2,1,0:T(8,128)(2,1)} %bitcast.290), calls=%async_computation.5 | async-start | bytes 31457280 | tf_op jit(solution)/shard_map/all_to_all | solution.py:890
  1132.8 296.7 %reduce-scatter.6.cloned.1.call-start = ((), (), s32[]{:S(2)}) async-start(), calls=%async_computation.19 | async-start | bytes 7864320 | tf_op jit(solution)/shard_map/reduce_scatter | solution.py:918
  1318.7 99.1 %all-to-all-start.8 = ((bf16[8,4,64,2048]{3,2,1,0:T(8,128)(2,1)}), bf16[8,4,64,2048]{3,2,1,0:T(8,128)(2,1)}, u32[]{:S(2)}, u32[]{:S(2)}) async-start(bf16[8,4,64,2048]{3,2,1,0:T(8,128)(2,1)} %tie.61), calls=%async_computation.10 | async-start | bytes 16777216 | tf_op jit(solution)/shard_map/all_to_all | solution.py:920
  1323.7 291.6 %reduce-scatter.8.cloned.1.call-start = ((), (), s32[]{:S(2)}) async-start(), calls=%async_computation.20 | async-start | bytes 7864320 | tf_op jit(solution)/shard_map/reduce_scatter | solution.py:940
  1493.8 76.9 %all-to-all-start.10 = ((bf16[8,4,64,1536]{3,2,1,0:T(8,128)(2,1)}), bf16[8,4,64,1536]{3,2,1,0:T(8,128)(2,1)}, u32[]{:S(2)}, u32[]{:S(2)}) async-start(bf16[8,4,64,1536]{3,2,1,0:T(8,128)(2,1)} %bitcast.303), calls=%async_computation.13 | async-start | bytes 12582912 | tf_op jit(solution)/shard_map/all_to_all | solution.py:954
  (104 other events, 2375.0 us)
Sparse Core Ops, SparseCore 0:
  73.1 114.4 all-gather.3
  192.2 144.0 all-gather.5
  381.4 113.8 all-gather.7
  1127.3 112.3 reduce-scatter.3
  1318.8 110.7 reduce-scatter.5
  1446.5 131.5 reduce-scatter.7

commit v4 on v3

--- a/solution.py
+++ b/solution.py
@@ -800,7 +800,6 @@
         tie(grad_output[0], hidden_all, packed, out_rows), "ctx", axis=0, tiled=True
     )
     full_out = lax.all_to_all(out_rows, "fsdp", 0, 0, tiled=True)
-    full_out = full_out.transpose(1, 0, 2, 3).reshape(width, width)
 
     seq_ids, places = seq_layout(token_order[0], lengths[0])
     experts_here = w_gate.shape[0]
@@ -841,9 +840,10 @@
     )
     query, key, values = turn(raw, scales, gains, cosine, sine)
     attended = attend(seq_ids, query, key, values)
+    full_out = tie(full_out, attended).transpose(1, 0, 2, 3).reshape(width, width)
+    grad_send = dispatch(position, capacity, tie(grad_all, attended, full_out))
     attended = attended.reshape(planes, row_count, share)
-    attended = jnp.concatenate(exchange(attended), axis=1)
-    grad_send = dispatch(position, capacity, tie(grad_all, attended))
+    attended = jnp.concatenate(exchange(attended, grad_all), axis=1)
     grad_in = lax.all_to_all(grad_send, "fsdp", 0, 0, tiled=True).reshape(-1, width)
     middle = hidden[0].astype(f32) + mm(attended, full_out)
     scale_two = lax.rsqrt(jnp.mean(middle * middle, axis=-1, keepdims=True) + epsilon)
@@ -853,7 +853,7 @@
     h_two_all = lax.all_gather(tie(h_two, grad_send), "ctx", axis=0, tiled=True)
     came = [swap(tie(w_gate[plane ^ step], h_two_all), step) for step in range(1, planes)]
     gate = jnp.concatenate(by_plane([w_gate[plane]] + came))
-    h_all = tie(h_two_all, grad_in, *came[:-1])
+    h_all = tie(h_two_all, grad_in, came[0])
     up = jnp.concatenate(exchange(w_up, h_two_all))
     probs = jax.nn.softmax(mm(h_two, full_router), axis=-1)
     rows_in = lax.all_to_all(dispatch(position, capacity, h_all), "fsdp", 0, 0, tiled=True)
@@ -909,9 +909,12 @@
         grad_hat - middle_hat * jnp.mean(grad_hat * middle_hat, axis=-1, keepdims=True)
     )
     grad_branch = grad_middle.astype(bf16)
-    grad_att = mm_t(grad_branch, full_out).astype(bf16)
-    grad_att = grad_att.reshape(row_count, planes, share).transpose(1, 0, 2)
-    grad_att = jnp.concatenate(exchange(grad_att))
+    def grad_heads(where):
+        rows = lax.dynamic_slice_in_dim(full_out, where * share, share)
+        return mm_t(grad_branch, rows).astype(bf16)
+
+    came = [swap(grad_heads(plane ^ step), step) for step in range(1, planes)]
+    grad_att = jnp.concatenate(by_plane([grad_heads(plane)] + came))
     grad_out_w = t_mm(attended, grad_branch).astype(bf16)
     grad_out_w = grad_out_w.reshape(planes, columns, strip, width).transpose(1, 0, 2, 3)
     mixed_part = combine(tie(expert_out, grad_att, grad_out_w))
@@ -934,11 +937,9 @@
         ],
         axis=1,
     ).astype(bf16)
-    grad_qkv = tie(grad_qkv, mixed, grad_out_w)
-    grad_out_w = jnp.sum(grad_out_w.astype(f32), axis=0).astype(bf16)
     grad_part = mm_t(grad_qkv, packed[:, : 3 * share])
     grad_h_one = lax.psum_scatter(
-        grad_part.astype(bf16), "ctx", scatter_dimension=0, tiled=True
+        tie(grad_part.astype(bf16), mixed, grad_out_w), "ctx", scatter_dimension=0, tiled=True
     ).astype(f32)
     grad_attn_gain = jnp.sum(grad_part * (hidden_wide * scale_one), axis=0)
     rows_of = jnp.arange(planes)[:, None] == plane
@@ -946,14 +947,15 @@
     gains = [g[:, None] for g in [grad_attn_gain, grad_ffn_gain] + gains]
     small = jnp.concatenate([grad_router] + gains, axis=1).reshape(planes * columns, -1)
     small = lax.all_to_all(small, both, 0, 0, tiled=True)
-    grad_qkv = tie(grad_qkv, small)
-    small = jnp.sum(small, axis=0).reshape(strip, -1)
-    grad_out_w = sum(x.astype(f32) for x in exchange(grad_out_w))
     sums = t_mm(h_one, grad_qkv).astype(bf16)
     sums = sums.reshape(planes, columns, strip, -1).transpose(1, 0, 2, 3)
-    sums = lax.all_to_all(sums, "fsdp", 0, 0, tiled=True)
+    sums = lax.all_to_all(tie(sums, small), "fsdp", 0, 0, tiled=True)
+    grad_out_w = jnp.sum(grad_out_w.astype(f32), axis=0).astype(bf16)
+    small = jnp.sum(small, axis=0).reshape(strip, -1)
+    came = [swap(grad_out_w[plane ^ step], step) for step in range(1, planes)]
+    grad_out_w = sum(x.astype(f32) for x in [grad_out_w[plane]] + came)
     sums = jnp.sum(sums.astype(f32), axis=0).astype(bf16)
-    sums = lax.all_to_all(sums, "ctx", 0, 0, tiled=True)
+    sums = lax.all_to_all(tie(sums, *came), "ctx", 0, 0, tiled=True)
     grad_qkv_w = sums.reshape(planes, strip, 3, share).transpose(2, 1, 0, 3)
     grad_qkv_w = grad_qkv_w.reshape(3, strip, width).astype(f32)
 

time: 1640 us -> 1630 us (level)
  starting transfers between devices: 142 us -> 198 us
  blocking collectives: 24.9 us -> 0 us
  waiting for transfers between devices: 800 us -> 778 us
    ppermute x36, starting transfers between devices: 83.4 us -> 136 us  [swap(): return lax.ppermute(part, 'ctx', [(i, i ^ step) for i in range(planes)])]
    all_to_all x1, waiting for transfers between devices: 50.2 us -> 0.01 us  [plane_shards(): lax.all_to_all(dispatch(position, capacity, h_all), 'fsdp', 0, 0, tiled=T...]
    all_to_all x1 -> x0, blocking collectives: 24.9 us -> none  [plane_shards(): small = lax.all_to_all(small, both, 0, 0, tiled=True)]
    all_to_all x1, waiting for transfers between devices: 1.01 us -> 22.9 us  [plane_shards(): lax.all_to_all(expert_out.reshape(columns, planes * capacity, width), 'fs...]
    ppermute x36, waiting for transfers between devices: 301 us -> 279 us  [swap(): return lax.ppermute(part, 'ctx', [(i, i ^ step) for i in range(planes)])]
    all_to_all x2 -> x3, waiting for transfers between devices: 53.5 us -> 71.1 us  [the longest x1 43.2 us: plane_shards(): sums = lax.all_to_all(tie(sums, small), 'fsdp', 0, 0, tiled=True)]
    unnamed x163 -> x173, local copies, waits for them, and re-layouts: 40 us -> 40.3 us
  transfers between devices with their start and end apart: 53 -> 54, of which waited for: 31 -> 28; matrix products, arithmetic and copies ran while one was open for 20% -> 20% of each run, Pallas kernels for 13% -> 12%
where the time goes in v4:
time: 1630 us; the launch traced here: 1620 us
  waiting for transfers between devices  778 us (48%)
  Pallas kernels  220 us (13%)
  starting transfers between devices  198 us (12%)
  matrix products  184 us (11%)
  local copies, waits for them, and re-layouts  132 us (8%)
  other arithmetic  93.4 us (6%)
    ppermute x36, waiting for transfers between devices, swap(): return lax.ppermute(part, 'ctx', [(i, i ^ step) for i in range(planes)])  279 us
    ppermute x36, starting transfers between devices, swap(): return lax.ppermute(part, 'ctx', [(i, i ^ step) for i in range(planes)])  136 us
    all_gather x1, waiting for transfers between devices, plane_shards(): h_two_all = lax.all_gather(tie(h_two, grad_send), 'ctx', axis=0, tiled=True)  115 us
    reduce_scatter x1, waiting for transfers between devices, plane_shards(): lax.psum_scatter(combine(grad_rows), 'ctx', scatter_dimension=0, tiled=True)  94.9 us
    dot_general x6, matrix products, t_mm(): lax.dot_general(left, right, (((0,), (0,)), ((), ())), preferred_element_...  86.8 us
    all_to_all x1, waiting for transfers between devices, plane_shards(): packed = lax.all_to_all(packed, 'fsdp', 0, 0, tiled=True)  76 us
    pallas_call x1, Pallas kernels, expert_back(): pl.pallas_call(expert_back_kernel, grid=(count // block,), in_specs=[wide...  63.4 us
    dot_general x4, matrix products, mm(): return jnp.dot(left, right, preferred_element_type=jnp.float32)  47.1 us
  transfers between devices with their start and end apart: 54, of which 28 were waited for; matrix products, arithmetic and copies ran while one was open for 20% of the time, Pallas kernels for 12%

profile of v4, /device:TPU:0, one launch (start us, length us, event | category | flops | bytes accessed | tf_op | source)
XLA Modules:
  0.0 1621.4 jit_solution(13503476094058932834)
XLA Ops:
  28.8 42.8 %all-to-all-done.refs_1_ = bf16[4,64,3712]{2,1,0:T(8,128)(2,1)S(1)} async-done(((bf16[4,64,3712]{2,1,0:T(8,128)(2,1)}), bf16[4,64,3712]{2,1,0:T(8,128)(2,1)S(1)}, u32[]{:S(2)}, u32[]{:S(2)}) %all-to-all-start) | async-done | bytes 1900576 | tf_op jit(solution)/shard_map/all_to_all | solution.py:759
  84.2 76.0 %all-to-all-done.1 = bf16[8,4,64,1664]{3,2,1,0:T(8,128)(2,1)} async-done(((bf16[8,4,64,1664]{3,2,1,0:T(8,128)(2,1)}), bf16[8,4,64,1664]{3,2,1,0:T(8,128)(2,1)}, u32[]{:S(2)}, u32[]{:S(2)}) %all-to-all-start.1) | async-done | bytes 6815776 | tf_op jit(solution)/shard_map/all_to_all | solution.py:766
  166.6 21.0 %all-gather.4.cloned.1.call-done.refs_1_ = bf16[1536,2048]{1,0:T(8,128)(2,1)} async-done(((bf16[384,2048]{1,0:T(8,128)(2,1)}), bf16[1536,2048]{1,0:T(8,128)(2,1)}) %all-gather.4.cloned.1.call-update) | async-done | bytes 6291472 | tf_op jit(solution)/shard_map/all_gather | solution.py:760
  215.6 16.0 fusion.34.raw
  247.6 28.0 %attend.1.refs_1_ = bf16[1536,512]{1,0:T(8,128)(2,1)S(1)} custom-call(s32[1536,1]{1,0:T(8,128)S(1)} %broadcast_in_dim.171.seq_rows, s32[1,1536]{1,0:T(1,128)S(1)} %broadcast_in_dim.146.seq_cols, bf16[1536,512]{1,0:T(8,128)(2,1)S(1)} %get-tuple-element.32.query, bf16[1536,512]{1,0:T(8,128)(2,1)S(1)} %get-tuple-element.33.key, bf16[1536,512]{1,0:T(8,128)(2,1)} %copy-done.17), custom_call_target="tpu_custom_call" | custom-call | flops 4831838208 | bytes 6291456 | tf_op jit(solution)/shard_map/attend/pallas_call | solution.py:421
  375.4 114.8 %all-gather.8.cloned.1.call-done.refs_1_.refs_0_ = bf16[1536,2048]{1,0:T(8,128)(2,1)} async-done(((bf16[384,2048]{1,0:T(8,128)(2,1)}), bf16[1536,2048]{1,0:T(8,128)(2,1)}) %all-gather.8.cloned.1.call-update) | async-done | bytes 6291472 | tf_op jit(solution)/shard_map/all_gather | solution.py:853
  494.2 21.5 %collective-permute-done.6.refs_2_ = bf16[512,1024]{1,0:T(8,128)(2,1)} collective-permute-done((bf16[512,1024]{1,0:T(8,128)(2,1)}, bf16[512,1024]{1,0:T(8,128)(2,1)}, u32[]{:S(2)}, u32[]{:S(2)}) %collective-permute-start.6) | collective-permute-done | bytes 1048608 | tf_op jit(solution)/shard_map/ppermute | solution.py:773
  544.5 62.5 %collective-permute-done.7 = bf16[512,1024]{1,0:T(8,128)(2,1)} collective-permute-done((bf16[512,1024]{1,0:T(8,128)(2,1)}, bf16[512,1024]{1,0:T(8,128)(2,1)}, u32[]{:S(2)}, u32[]{:S(2)}) %collective-permute-start.7) | collective-permute-done | bytes 1048608 | tf_op jit(solution)/shard_map/ppermute | solution.py:773
  607.0 67.0 %collective-permute-start.13 = (bf16[256,2048]{1,0:T(8,128)(2,1)}, bf16[256,2048]{1,0:T(8,128)(2,1)}, u32[]{:S(2)}, u32[]{:S(2)}) collective-permute-start(bf16[256,2048]{1,0:T(8,128)(2,1)} %tie.54), channel_id=1, source_target_pairs={{0,16},{8,24},{16,0},{24,8},{1,17},{9,25},{17,1},{25,9},{2,18},{10... | collective-permute-start | bytes 3145736 | tf_op jit(solution)/shard_map/ppermute | solution.py:773
  679.9 61.5 %collective-permute-done.10 = bf16[512,1024]{1,0:T(8,128)(2,1)} collective-permute-done((bf16[512,1024]{1,0:T(8,128)(2,1)}, bf16[512,1024]{1,0:T(8,128)(2,1)}, u32[]{:S(2)}, u32[]{:S(2)}) %collective-permute-start.10) | collective-permute-done | bytes 1048608 | tf_op jit(solution)/shard_map/ppermute | solution.py:773
  748.6 44.6 %expert_in.1 = (f32[3840,1024]{1,0:T(8,128)}, f32[3840,1024]{1,0:T(8,128)}, bf16[3840,1024]{1,0:T(8,128)(2,1)}, f32[3840,1]{1,0:T(8,128)}) custom-call(bf16[3840,2048]{1,0:T(8,128)(2,1)} %bitcast.37.rows, bf16[2048,1024]{1,0:T(8,128)(2,1)} %pad_maximum_fusion.2.gate, bf16[2048,1024]{1,0:T(8,128)(2,1)} %pad_maximum_fusion.4.up, ...), custom_call_target="tpu_custom_call" | custom-call | flops 32212254720 | bytes 63438848 | tf_op jit(solution)/shard_map/expert_in/pallas_call | solution.py:638
  793.1 22.5 %convolution_convert_fusion.5.refs_1_ = bf16[1024,2048]{1,0:T(8,128)(2,1)} fusion(bf16[3840,1024]{1,0:T(8,128)(2,1)} %get-tuple-element.35.refs_1_, bf16[3840,2048]{1,0:T(8,128)(2,1)} %bitcast.34.refs_1_.grad), kind=kOutput, calls=%fused_computation.40 | convolution fusion | flops 16108224512 | bytes 27787264 | tf_op jit(solution)/shard_map/dot_general | solution.py:714
  825.3 23.5 %collective-permute-start.16 = (bf16[256,2048]{1,0:T(8,128)(2,1)S(1)}, bf16[256,2048]{1,0:T(8,128)(2,1)}, u32[]{:S(2)}, u32[]{:S(2)}) collective-permute-start(bf16[256,2048]{1,0:T(8,128)(2,1)S(1)} %get-tuple-element.150), channel_id=1, source_target_pairs={{0,16},{8,24},{16,0},{24,8},{1,17},{9,25},{17,1},{25,9},{2,18},{10... | collective-permute-start | bytes 3145736 | tf_op jit(solution)/shard_map/ppermute | solution.py:773
  851.1 63.4 %expert_back.1 = (bf16[3840,1024]{1,0:T(8,128)(2,1)}, bf16[3840,1024]{1,0:T(8,128)(2,1)}, f32[3840,1]{1,0:T(8,128)}, bf16[3840,2048]{1,0:T(8,128)(2,1)}) custom-call(bf16[3840,2048]{1,0:T(8,128)(2,1)} %bitcast.34.refs_1_.grad, f32[3840,1024]{1,0:T(8,128)} %tie.58.gate_in, f32[3840,1024]{1,0:T(8,128)} %get-tuple-element.37.up_in, ...), custom_call_target="tpu_custom_call" | custom-call | flops 48318382080 | bytes 91226112 | tf_op jit(solution)/shard_map/expert_back/pallas_call | solution.py:670
  925.0 21.4 %convolution_convert_fusion.3 = bf16[2048,1024]{1,0:T(8,128)(2,1)S(1)} fusion(bf16[3840,2048]{1,0:T(8,128)(2,1)} %bitcast.37.rows, bf16[3840,1024]{1,0:T(8,128)(2,1)} %get-tuple-element.41), kind=kOutput, calls=%fused_computation.38 | convolution fusion | flops 16108224512 | bytes 27787264 | tf_op jit(solution)/shard_map/dot_general | solution.py:714
  952.9 21.4 %convolution_convert_fusion.4 = bf16[2048,1024]{1,0:T(8,128)(2,1)S(1)} fusion(bf16[3840,2048]{1,0:T(8,128)(2,1)} %bitcast.37.rows, bf16[3840,1024]{1,0:T(8,128)(2,1)} %get-tuple-element.40), kind=kOutput, calls=%fused_computation.39 | convolution fusion | flops 16108224512 | bytes 27787264 | tf_op jit(solution)/shard_map/dot_general | solution.py:714
  977.9 84.8 %collective-permute-done.20.refs_1_ = bf16[512,1024]{1,0:T(8,128)(2,1)} collective-permute-done((bf16[512,1024]{1,0:T(8,128)(2,1)}, bf16[512,1024]{1,0:T(8,128)(2,1)}, u32[]{:S(2)}, u32[]{:S(2)}) %collective-permute-start.20) | collective-permute-done | bytes 1048608 | tf_op jit(solution)/shard_map/ppermute | solution.py:773
  1065.5 32.1 %all-to-all-done.6.refs_1_.refs_0_ = bf16[8,480,2048]{2,1,0:T(8,128)(2,1)} async-done(((bf16[8,480,2048]{2,1,0:T(8,128)(2,1)}), bf16[8,480,2048]{2,1,0:T(8,128)(2,1)}, u32[]{:S(2)}, u32[]{:S(2)}) %all-to-all-start.6) | async-done | bytes 15728672 | tf_op jit(solution)/shard_map/all_to_all | solution.py:878
  1103.9 22.7 %convolution_convert_fusion.refs_4_ = bf16[3840,2048]{1,0:T(8,128)(2,1)} fusion(bf16[3840,1024]{1,0:T(8,128)(2,1)} %get-tuple-element.35.refs_1_, bf16[256,2048]{1,0:T(8,128)(2,1)} %get-tuple-element.169, bf16[256,2048]{1,0:T(8,128)(2,1)} %get-tuple-element.170, bf16[256,2048]{1,0:T(8,128)(2,1)} %get-tuple-element.171, bf16[256,2048]{1,0:T(8,128)(2,1)} %get-tuple-element.168), kind=kOutput, calls=%fused_computation.6 | convolution fusion | flops 16130768896 | bytes 27787264 | tf_op jit(solution)/shard_map/dot_general | solution.py:704
  1159.1 94.9 %reduce-scatter.4.cloned.1.call-done = bf16[384,2048]{1,0:T(8,128)(2,1)} async-done(((bf16[1536,2048]{1,0:T(8,128)(2,1)}), bf16[384,2048]{1,0:T(8,128)(2,1)}) %reduce-scatter.4.cloned.1.call-update) | async-done | bytes 1572880 | tf_op jit(solution)/shard_map/reduce_scatter | solution.py:893
  1297.8 22.9 %all-to-all-done.5.refs_0_ = bf16[8,480,2048]{2,1,0:T(8,128)(2,1)} async-done(((bf16[8,480,2048]{2,1,0:T(8,128)(2,1)}), bf16[8,480,2048]{2,1,0:T(8,128)(2,1)}, u32[]{:S(2)}, u32[]{:S(2)}) %all-to-all-start.5) | async-done | bytes 15728672 | tf_op jit(solution)/shard_map/all_to_all | solution.py:890
  1342.5 45.9 %attend_back.1 = (f32[1536,512]{1,0:T(8,128)}, f32[1536,512]{1,0:T(8,128)}, f32[1536,512]{1,0:T(8,128)}) custom-call(s32[1536,1]{1,0:T(8,128)S(1)} %broadcast_in_dim.171.seq_rows, s32[1,1536]{1,0:T(1,128)S(1)} %broadcast_in_dim.146.seq_cols, bf16[1536,512]{1,0:T(8,128)(2,1)S(1)} %copy-done.14, bf16[1536,512]{1,0:T(8,128)(2,1)S(1)} %copy-done.16, ...), custom_call_target="tpu_custom_call" | custom-call | flops 12079595520 | bytes 15728640 | tf_op jit(solution)/shard_map/attend_back/pallas_call | solution.py:440
  1507.4 43.2 %all-to-all-done.10 = bf16[8,4,64,1536]{3,2,1,0:T(8,128)(2,1)} async-done(((bf16[8,4,64,1536]{3,2,1,0:T(8,128)(2,1)}), bf16[8,4,64,1536]{3,2,1,0:T(8,128)(2,1)}, u32[]{:S(2)}, u32[]{:S(2)}) %all-to-all-start.10) | async-done | bytes 6291488 | tf_op jit(solution)/shard_map/all_to_all | solution.py:952
  1570.9 24.4 %all-to-all-done.11 = bf16[4,64,1536]{2,1,0:T(8,128)(2,1)S(1)} async-done(((bf16[4,64,1536]{2,1,0:T(8,128)(2,1)}), bf16[4,64,1536]{2,1,0:T(8,128)(2,1)S(1)}, u32[]{:S(2)}, u32[]{:S(2)}) %all-to-all-start.11) | async-done | bytes 786464 | tf_op jit(solution)/shard_map/all_to_all | solution.py:958
  (480 shorter events, 526.5 us)
Async XLA Ops:
  27.7 159.9 %all-gather.4.cloned.1.call-start = ((), (), s32[]{:S(2)}) async-start(), calls=%async_computation.15 | async-start | bytes 7864320 | tf_op jit(solution)/shard_map/all_gather | solution.py:760
  77.9 82.3 %all-to-all-start.1 = ((bf16[8,4,64,1664]{3,2,1,0:T(8,128)(2,1)}), bf16[8,4,64,1664]{3,2,1,0:T(8,128)(2,1)}, u32[]{:S(2)}, u32[]{:S(2)}) async-start(bf16[8,4,64,1664]{3,2,1,0:T(8,128)(2,1)} %broadcast_in_dim.153), calls=%async_computation.1 | async-start | bytes 13631488 | tf_op jit(solution)/shard_map/all_to_all | solution.py:766
  83.0 223.8 %all-gather.6.cloned.1.call-start = ((), (), s32[]{:S(2)}) async-start(), calls=%async_computation.16 | async-start | bytes 7864320 | tf_op jit(solution)/shard_map/all_gather | solution.py:799
  193.0 99.3 %all-to-all-start.2 = ((bf16[8,4,64,2048]{3,2,1,0:T(8,128)(2,1)}), bf16[8,4,64,2048]{3,2,1,0:T(8,128)(2,1)}, u32[]{:S(2)}, u32[]{:S(2)}) async-start(bf16[8,4,64,2048]{3,2,1,0:T(8,128)(2,1)} %broadcast_in_dim.157.refs_3_), calls=%async_computation.2 | async-start | bytes 16777216 | tf_op jit(solution)/shard_map/all_to_all | solution.py:802
  320.3 195.3 %all-to-all-start.3 = ((bf16[8,4,120,2048]{3,2,1,0:T(8,128)(2,1)}), bf16[8,4,120,2048]{3,2,1,0:T(8,128)(2,1)}, u32[]{:S(2)}, u32[]{:S(2)}) async-start(bf16[8,4,120,2048]{3,2,1,0:T(8,128)(2,1)} %dispatch.2.refs_1_), calls=%async_computation.3 | async-start | bytes 31457280 | tf_op jit(solution)/shard_map/all_to_all | solution.py:847
  326.0 164.2 %all-gather.8.cloned.1.call-start = ((), (), s32[]{:S(2)}) async-start(), calls=%async_computation.17 | async-start | bytes 7864320 | tf_op jit(solution)/shard_map/all_gather | solution.py:853
  529.2 219.3 %all-to-all-start.4 = ((bf16[8,4,120,2048]{3,2,1,0:T(8,128)(2,1)}), bf16[8,4,120,2048]{3,2,1,0:T(8,128)(2,1)}, u32[]{:S(2)}, u32[]{:S(2)}) async-start(bf16[8,4,120,2048]{3,2,1,0:T(8,128)(2,1)} %dispatch.3), calls=%async_computation.4 | async-start | bytes 31457280 | tf_op jit(solution)/shard_map/all_to_all | solution.py:859
  537.7 139.2 %collective-permute-start.9 = (bf16[512,1024]{1,0:T(8,128)(2,1)}, bf16[512,1024]{1,0:T(8,128)(2,1)}, u32[]{:S(2)}, u32[]{:S(2)}) collective-permute-start(bf16[512,1024]{1,0:T(8,128)(2,1)} %tie.49), channel_id=1, source_target_pairs={{0,8},{8,0},{16,24},{24,16},{1,9},{9,1},{17,25},{25,17},{2,10},{10... | collective-permute-start | bytes 3145736 | tf_op jit(solution)/shard_map/ppermute | solution.py:773
  538.6 202.8 %collective-permute-start.10 = (bf16[512,1024]{1,0:T(8,128)(2,1)}, bf16[512,1024]{1,0:T(8,128)(2,1)}, u32[]{:S(2)}, u32[]{:S(2)}) collective-permute-start(bf16[512,1024]{1,0:T(8,128)(2,1)} %tie.50), channel_id=1, source_target_pairs={{0,16},{8,24},{16,0},{24,8},{1,17},{9,25},{17,1},{25,9},{2,18},{10... | collective-permute-start | bytes 3145736 | tf_op jit(solution)/shard_map/ppermute | solution.py:773
  539.9 201.5 %collective-permute-start.11 = (bf16[512,1024]{1,0:T(8,128)(2,1)}, bf16[512,1024]{1,0:T(8,128)(2,1)}, u32[]{:S(2)}, u32[]{:S(2)}) collective-permute-start(bf16[512,1024]{1,0:T(8,128)(2,1)} %tie.51), channel_id=1, source_target_pairs={{0,24},{8,16},{16,8},{24,0},{1,25},{9,17},{17,9},{25,1},{2,26},{10... | collective-permute-start | bytes 3145736 | tf_op jit(solution)/shard_map/ppermute | solution.py:773
  607.0 208.6 %collective-permute-start.12 = (bf16[256,2048]{1,0:T(8,128)(2,1)}, bf16[256,2048]{1,0:T(8,128)(2,1)}, u32[]{:S(2)}, u32[]{:S(2)}) collective-permute-start(bf16[256,2048]{1,0:T(8,128)(2,1)} %tie.52), channel_id=1, source_target_pairs={{0,8},{8,0},{16,24},{24,16},{1,9},{9,1},{17,25},{25,17},{2,10},{10... | collective-permute-start | bytes 3145736 | tf_op jit(solution)/shard_map/ppermute | solution.py:773
  607.0 208.6 %collective-permute-start.13 = (bf16[256,2048]{1,0:T(8,128)(2,1)}, bf16[256,2048]{1,0:T(8,128)(2,1)}, u32[]{:S(2)}, u32[]{:S(2)}) collective-permute-start(bf16[256,2048]{1,0:T(8,128)(2,1)} %tie.54), channel_id=1, source_target_pairs={{0,16},{8,24},{16,0},{24,8},{1,17},{9,25},{17,1},{25,9},{2,18},{10... | collective-permute-start | bytes 3145736 | tf_op jit(solution)/shard_map/ppermute | solution.py:773
  677.0 138.6 %collective-permute-start.14 = (bf16[256,2048]{1,0:T(8,128)(2,1)}, bf16[256,2048]{1,0:T(8,128)(2,1)}, u32[]{:S(2)}, u32[]{:S(2)}) collective-permute-start(bf16[256,2048]{1,0:T(8,128)(2,1)} %tie.56), channel_id=1, source_target_pairs={{0,24},{8,16},{16,8},{24,0},{1,25},{9,17},{17,9},{25,1},{2,26},{10... | collective-permute-start | bytes 3145736 | tf_op jit(solution)/shard_map/ppermute | solution.py:773
  824.3 90.2 %collective-permute-start.17 = (bf16[256,2048]{1,0:T(8,128)(2,1)}, bf16[256,2048]{1,0:T(8,128)(2,1)S(1)}, u32[]{:S(2)}, u32[]{:S(2)}) collective-permute-start(bf16[256,2048]{1,0:T(8,128)(2,1)} %get-tuple-element.149), channel_id=1, source_target_pairs={{0,24},{8,16},{16,8},{24,0},{1,25},{9,17},{17,9},{25,1},{2,26},{10... | collective-permute-start | bytes 3145736 | tf_op jit(solution)/shard_map/ppermute | solution.py:773
  825.3 93.6 %collective-permute-start.16 = (bf16[256,2048]{1,0:T(8,128)(2,1)S(1)}, bf16[256,2048]{1,0:T(8,128)(2,1)}, u32[]{:S(2)}, u32[]{:S(2)}) collective-permute-start(bf16[256,2048]{1,0:T(8,128)(2,1)S(1)} %get-tuple-element.150), channel_id=1, source_target_pairs={{0,16},{8,24},{16,0},{24,8},{1,17},{9,25},{17,1},{25,9},{2,18},{10... | collective-permute-start | bytes 3145736 | tf_op jit(solution)/shard_map/ppermute | solution.py:773
  918.9 178.7 %all-to-all-start.6 = ((bf16[8,480,2048]{2,1,0:T(8,128)(2,1)}), bf16[8,480,2048]{2,1,0:T(8,128)(2,1)}, u32[]{:S(2)}, u32[]{:S(2)}) async-start(bf16[8,480,2048]{2,1,0:T(8,128)(2,1)} %bitcast.282), calls=%async_computation.6 | async-start | bytes 31457280 | tf_op jit(solution)/shard_map/all_to_all | solution.py:878
  948.8 113.9 %collective-permute-start.20 = (bf16[512,1024]{1,0:T(8,128)(2,1)}, bf16[512,1024]{1,0:T(8,128)(2,1)}, u32[]{:S(2)}, u32[]{:S(2)}) collective-permute-start(bf16[512,1024]{1,0:T(8,128)(2,1)} %tie.62), channel_id=1, source_target_pairs={{0,16},{8,24},{16,0},{24,8},{1,17},{9,25},{17,1},{25,9},{2,18},{10... | collective-permute-start | bytes 3145736 | tf_op jit(solution)/shard_map/ppermute | solution.py:773
  948.8 113.9 %collective-permute-start.18 = (bf16[512,1024]{1,0:T(8,128)(2,1)}, bf16[512,1024]{1,0:T(8,128)(2,1)}, u32[]{:S(2)}, u32[]{:S(2)}) collective-permute-start(bf16[512,1024]{1,0:T(8,128)(2,1)} %tie.60), channel_id=1, source_target_pairs={{0,8},{8,0},{16,24},{24,16},{1,9},{9,1},{17,25},{25,17},{2,10},{10... | collective-permute-start | bytes 3145736 | tf_op jit(solution)/shard_map/ppermute | solution.py:773
  977.6 149.0 %collective-permute-start.23 = (bf16[512,1024]{1,0:T(8,128)(2,1)}, bf16[512,1024]{1,0:T(8,128)(2,1)S(1)}, u32[]{:S(2)}, u32[]{:S(2)}) collective-permute-start(bf16[512,1024]{1,0:T(8,128)(2,1)} %tie.65), channel_id=1, source_target_pairs={{0,24},{8,16},{16,8},{24,0},{1,25},{9,17},{17,9},{25,1},{2,26},{10... | collective-permute-start | bytes 3145736 | tf_op jit(solution)/shard_map/ppermute | solution.py:773
  1103.8 150.1 %reduce-scatter.4.cloned.1.call-start = ((), (), s32[]{:S(2)}) async-start(), calls=%async_computation.18 | async-start | bytes 7864320 | tf_op jit(solution)/shard_map/reduce_scatter | solution.py:893
  1142.2 178.5 %all-to-all-start.5 = ((bf16[8,480,2048]{2,1,0:T(8,128)(2,1)}), bf16[8,480,2048]{2,1,0:T(8,128)(2,1)}, u32[]{:S(2)}, u32[]{:S(2)}) async-start(bf16[8,480,2048]{2,1,0:T(8,128)(2,1)} %bitcast.281), calls=%async_computation.5 | async-start | bytes 31457280 | tf_op jit(solution)/shard_map/all_to_all | solution.py:890
  1148.0 294.8 %reduce-scatter.6.cloned.1.call-start = ((), (), s32[]{:S(2)}) async-start(), calls=%async_computation.19 | async-start | bytes 7864320 | tf_op jit(solution)/shard_map/reduce_scatter | solution.py:921
  1333.1 105.0 %all-to-all-start.8 = ((bf16[8,4,64,2048]{3,2,1,0:T(8,128)(2,1)}), bf16[8,4,64,2048]{3,2,1,0:T(8,128)(2,1)}, u32[]{:S(2)}, u32[]{:S(2)}) async-start(bf16[8,4,64,2048]{3,2,1,0:T(8,128)(2,1)} %tie.70), calls=%async_computation.10 | async-start | bytes 16777216 | tf_op jit(solution)/shard_map/all_to_all | solution.py:923
  1338.0 269.8 %reduce-scatter.8.cloned.1.call-start = ((), (), s32[]{:S(2)}) async-start(), calls=%async_computation.20 | async-start | bytes 7864320 | tf_op jit(solution)/shard_map/reduce_scatter | solution.py:941
  (112 other events, 2254.6 us)
Sparse Core Ops, SparseCore 0:
  73.1 114.4 all-gather.3
  192.2 114.5 all-gather.5
  368.6 121.5 all-gather.7
  1142.3 111.6 reduce-scatter.3
  1333.2 109.6 reduce-scatter.5
  1445.0 143.6 reduce-scatter.7

commit v5 on v4

--- a/solution.py
+++ b/solution.py
@@ -757,7 +757,7 @@
     own_out = jnp.broadcast_to(w_out[None], (planes,) + w_out.shape)
     packed = jnp.concatenate([qkv, small, own_out], axis=2)
     packed = lax.all_to_all(packed, "ctx", 0, 0, tiled=True)
-    hidden_all = lax.all_gather(tie(hidden[0], packed), "ctx", axis=0, tiled=True)
+    hidden_all = lax.all_gather(hidden[0], "ctx", axis=0, tiled=True)
     packed, out_rows = packed[:, :, :-width], packed[:, :, -width:]
     routes_at = 3 * share + experts + 4
     routes_all = packed[:, :, routes_at : packed.shape[2] - spare].astype(jnp.int32)
@@ -797,7 +797,7 @@
 
     out_rows = jnp.broadcast_to(out_rows[None], (columns,) + out_rows.shape)
     grad_all = lax.all_gather(
-        tie(grad_output[0], hidden_all, packed, out_rows), "ctx", axis=0, tiled=True
+        tie(grad_output[0], hidden_all), "ctx", axis=0, tiled=True
     )
     full_out = lax.all_to_all(out_rows, "fsdp", 0, 0, tiled=True)
 
@@ -851,20 +851,24 @@
     h_two = (middle_hat * gain_ffn).astype(bf16)
 
     h_two_all = lax.all_gather(tie(h_two, grad_send), "ctx", axis=0, tiled=True)
-    came = [swap(tie(w_gate[plane ^ step], h_two_all), step) for step in range(1, planes)]
-    gate = jnp.concatenate(by_plane([w_gate[plane]] + came))
-    h_all = tie(h_two_all, grad_in, came[0])
-    up = jnp.concatenate(exchange(w_up, h_two_all))
+    h_all = tie(h_two_all, grad_in)
+    gate = jnp.concatenate(exchange(w_gate, h_two_all))
+    came_up = [swap(tie(w_up[plane ^ step], h_two_all), step) for step in range(1, planes)]
+    up = jnp.concatenate(by_plane([w_up[plane]] + came_up))
     probs = jax.nn.softmax(mm(h_two, full_router), axis=-1)
     rows_in = lax.all_to_all(dispatch(position, capacity, h_all), "fsdp", 0, 0, tiled=True)
-    rows_in = rows_in.reshape(-1, width)
+    came = [
+        swap(tie(w_down[plane ^ step], before), step) for step, before in enumerate(came_up, 1)
+    ]
+    rows_in = tie(rows_in, *came[:-1]).reshape(-1, width)
     own = experts_here * lax.axis_index("fsdp") + plane
     own = (jnp.arange(experts)[None, :] == own).astype(f32)
     slot_block = planes * capacity
     gate_pre, up_pre, act_picked, picked = expert_in(
         rows_in, gate, up, full_router, own, slot_block
     )
-    down = jnp.concatenate(exchange(w_down, h_two_all, act_picked))
+    came = [tie(part, act_picked) for part in came]
+    down = jnp.concatenate(by_plane([w_down[plane]] + came))
     grad_down_w = t_mm(act_picked, grad_in).astype(bf16)
     grad_gate, grad_up, grad_picked, grad_rows = expert_back(
         grad_in, tie(gate_pre, grad_down_w), up_pre, picked, gate, up, down, slot_block
@@ -880,13 +884,13 @@
     )
     grad_gate_w = t_mm(rows_in, grad_gate).astype(bf16)
     grad_up_w = t_mm(rows_in, grad_up).astype(bf16)
-    came, up_grad = exchange_after(blocks(grad_up_w), came)
+    came_up, up_grad = exchange_after(blocks(grad_up_w), came)
     came, gate_grad = exchange_after(blocks(grad_gate_w), came)
     expert_out = mm(act_picked, down).astype(bf16)
     grad_picked = lax.all_to_all(
         tie(grad_picked, grad_rows).reshape(columns, planes, capacity), "fsdp", 0, 0, tiled=True
     )
-    grad_rows = tie(grad_rows, *came, expert_out, grad_picked)
+    grad_rows = tie(grad_rows, *came, *came_up, expert_out, grad_picked)
     expert_out = lax.all_to_all(
         expert_out.reshape(columns, planes * capacity, width), "fsdp", 0, 0, tiled=True
     )
@@ -952,10 +956,9 @@
     sums = lax.all_to_all(tie(sums, small), "fsdp", 0, 0, tiled=True)
     grad_out_w = jnp.sum(grad_out_w.astype(f32), axis=0).astype(bf16)
     small = jnp.sum(small, axis=0).reshape(strip, -1)
-    came = [swap(grad_out_w[plane ^ step], step) for step in range(1, planes)]
-    grad_out_w = sum(x.astype(f32) for x in [grad_out_w[plane]] + came)
-    sums = jnp.sum(sums.astype(f32), axis=0).astype(bf16)
-    sums = lax.all_to_all(tie(sums, *came), "ctx", 0, 0, tiled=True)
+    sums = tie(jnp.sum(sums.astype(f32), axis=0).astype(bf16), grad_out_w)
+    grad_out_w = sum(x.astype(f32) for x in exchange(grad_out_w, sums))
+    sums = lax.all_to_all(sums, "ctx", 0, 0, tiled=True)
     grad_qkv_w = sums.reshape(planes, strip, 3, share).transpose(2, 1, 0, 3)
     grad_qkv_w = grad_qkv_w.reshape(3, strip, width).astype(f32)
 

time: 1630 us -> 1700 us (1.043)
  blocking collectives: 0 us -> 101 us
  starting transfers between devices: 198 us -> 173 us
    all_to_all x0 -> x1, blocking collectives: none -> 101 us  [plane_shards(): packed = lax.all_to_all(packed, 'ctx', 0, 0, tiled=True)]
    all_to_all x1, waiting for transfers between devices: 32.1 us -> 119 us  [plane_shards(): lax.all_to_all(grad_rows.reshape(columns, planes * capacity, width), 'fsd...]
    all_to_all x2 -> x1, waiting for transfers between devices: 67.2 us -> 0.01 us  [plane_shards(): sums = lax.all_to_all(sums, 'ctx', 0, 0, tiled=True)]
    all_to_all x1, waiting for transfers between devices: 76 us -> 37.8 us  [plane_shards(): packed = lax.all_to_all(packed, 'fsdp', 0, 0, tiled=True)]
    ppermute x36, starting transfers between devices: 136 us -> 117 us  [swap(): return lax.ppermute(part, 'ctx', [(i, i ^ step) for i in range(planes)])]
    unnamed x173 -> x172, local copies, waits for them, and re-layouts: 40.3 us -> 34.5 us
  transfers between devices with their start and end apart: 54 -> 53, of which waited for: 28 -> 30; matrix products, arithmetic and copies ran while one was open for 20% -> 19% of each run, Pallas kernels for 12% -> 12%
where the time goes in v5:
time: 1700 us; the launch traced here: 1680 us
  waiting for transfers between devices  778 us (46%)
  Pallas kernels  220 us (13%)
  matrix products  179 us (11%)
  starting transfers between devices  173 us (10%)
  local copies, waits for them, and re-layouts  124 us (7%)
  blocking collectives  101 us (6%)
  other arithmetic  91.3 us (5%)
    ppermute x36, waiting for transfers between devices, swap(): return lax.ppermute(part, 'ctx', [(i, i ^ step) for i in range(planes)])  266 us
    all_to_all x1, waiting for transfers between devices, plane_shards(): lax.all_to_all(grad_rows.reshape(columns, planes * capacity, width), 'fsd...  119 us
    ppermute x36, starting transfers between devices, swap(): return lax.ppermute(part, 'ctx', [(i, i ^ step) for i in range(planes)])  117 us
    all_gather x1, waiting for transfers between devices, plane_shards(): h_two_all = lax.all_gather(tie(h_two, grad_send), 'ctx', axis=0, tiled=True)  115 us
    all_to_all x1, blocking collectives, plane_shards(): packed = lax.all_to_all(packed, 'ctx', 0, 0, tiled=True)  101 us
    reduce_scatter x1, waiting for transfers between devices, plane_shards(): lax.psum_scatter(combine(grad_rows), 'ctx', scatter_dimension=0, tiled=True)  94.6 us
    dot_general x6, matrix products, t_mm(): lax.dot_general(left, right, (((0,), (0,)), ((), ())), preferred_element_...  86.7 us
    pallas_call x1, Pallas kernels, expert_back(): pl.pallas_call(expert_back_kernel, grid=(count // block,), in_specs=[wide...  63.4 us
  transfers between devices with their start and end apart: 53, of which 30 were waited for; matrix products, arithmetic and copies ran while one was open for 19% of the time, Pallas kernels for 12%

profile of v5, /device:TPU:0, one launch (start us, length us, event | category | flops | bytes accessed | tf_op | source)
XLA Modules:
  0.0 1683.6 jit_solution(1094594817634766665)
XLA Ops:
  19.9 101.1 %all_to_all.67 = bf16[4,64,3712]{2,1,0:T(8,128)(2,1)S(1)} all-to-all(bf16[4,64,3712]{2,1,0:T(8,128)(2,1)S(1)} %pad_maximum_fusion.12), channel_id=1, replica_groups=mesh['ctx'=4,'fsdp'=8] {'ctx'}, dimensions={0} | all-to-all | bytes 3801088 | tf_op jit(solution)/shard_map/all_to_all | solution.py:759
  130.9 37.1 %all-gather.9.cloned.1.call-done = bf16[1,1536,2048]{2,1,0:T(8,128)(2,1)} async-done(((bf16[1,384,2048]{2,1,0:T(8,128)(2,1)}), bf16[1,1536,2048]{2,1,0:T(8,128)(2,1)}) %all-gather.9.cloned.1.call-update) | async-done | bytes 6291472 | tf_op jit(solution)/shard_map/all_gather | solution.py:760
  169.1 37.8 %all-to-all-done.1 = bf16[8,4,64,1664]{3,2,1,0:T(8,128)(2,1)} async-done(((bf16[8,4,64,1664]{3,2,1,0:T(8,128)(2,1)}), bf16[8,4,64,1664]{3,2,1,0:T(8,128)(2,1)}, u32[]{:S(2)}, u32[]{:S(2)}) %all-to-all-start.1) | async-done | bytes 6815776 | tf_op jit(solution)/shard_map/all_to_all | solution.py:766
  267.5 28.4 %attend.1.refs_1_ = bf16[1536,512]{1,0:T(8,128)(2,1)S(1)} custom-call(s32[1536,1]{1,0:T(8,128)S(1)} %broadcast_in_dim.171.seq_rows, s32[1,1536]{1,0:T(1,128)S(1)} %broadcast_in_dim.146.seq_cols, bf16[1536,512]{1,0:T(8,128)(2,1)S(1)} %get-tuple-element.32.query, bf16[1536,512]{1,0:T(8,128)(2,1)S(1)} %get-tuple-element.33.key, bf16[1536,512]{1,0:T(8,128)(2,1)} %copy-done.16), custom_call_target="tpu_custom_call" | custom-call | flops 4831838208 | bytes 6291456 | tf_op jit(solution)/shard_map/attend/pallas_call | solution.py:421
  387.3 114.8 %all-gather.7.cloned.1.call-done.refs_0_.refs_1_ = bf16[1536,2048]{1,0:T(8,128)(2,1)} async-done(((bf16[384,2048]{1,0:T(8,128)(2,1)}), bf16[1536,2048]{1,0:T(8,128)(2,1)}) %all-gather.7.cloned.1.call-update) | async-done | bytes 6291472 | tf_op jit(solution)/shard_map/all_gather | solution.py:853
  536.4 41.0 %collective-permute-done.6.refs_1_ = bf16[512,1024]{1,0:T(8,128)(2,1)S(1)} collective-permute-done((bf16[512,1024]{1,0:T(8,128)(2,1)}, bf16[512,1024]{1,0:T(8,128)(2,1)S(1)}, u32[]{:S(2)}, u32[]{:S(2)}) %collective-permute-start.6) | collective-permute-done | bytes 1048608 | tf_op jit(solution)/shard_map/ppermute | solution.py:773
  586.5 16.0 collective-permute-done.8.refs_1_
  602.6 67.9 %collective-permute-start.9 = (bf16[256,2048]{1,0:T(8,128)(2,1)}, bf16[256,2048]{1,0:T(8,128)(2,1)}, u32[]{:S(2)}, u32[]{:S(2)}) collective-permute-start(bf16[256,2048]{1,0:T(8,128)(2,1)} %tie.51), channel_id=1, source_target_pairs={{0,16},{8,24},{16,0},{24,8},{1,17},{9,25},{17,1},{25,9},{2,18},{10... | collective-permute-start | bytes 3145736 | tf_op jit(solution)/shard_map/ppermute | solution.py:773
  672.9 64.5 %collective-permute-done.11 = bf16[512,1024]{1,0:T(8,128)(2,1)} collective-permute-done((bf16[512,1024]{1,0:T(8,128)(2,1)}, bf16[512,1024]{1,0:T(8,128)(2,1)}, u32[]{:S(2)}, u32[]{:S(2)}) %collective-permute-start.11) | collective-permute-done | bytes 1048608 | tf_op jit(solution)/shard_map/ppermute | solution.py:773
  748.2 34.1 %collective-permute-done.9.refs_2_.refs_0_ = bf16[256,2048]{1,0:T(8,128)(2,1)} collective-permute-done((bf16[256,2048]{1,0:T(8,128)(2,1)}, bf16[256,2048]{1,0:T(8,128)(2,1)}, u32[]{:S(2)}, u32[]{:S(2)}) %collective-permute-start.9) | collective-permute-done | bytes 1048608 | tf_op jit(solution)/shard_map/ppermute | solution.py:773
  782.3 44.6 %expert_in.1 = (f32[3840,1024]{1,0:T(8,128)}, f32[3840,1024]{1,0:T(8,128)}, bf16[3840,1024]{1,0:T(8,128)(2,1)}, f32[3840,1]{1,0:T(8,128)}) custom-call(bf16[3840,2048]{1,0:T(8,128)(2,1)} %bitcast.41.rows, bf16[2048,1024]{1,0:T(8,128)(2,1)} %pad_maximum_fusion.2.gate, bf16[2048,1024]{1,0:T(8,128)(2,1)} %pad_maximum_fusion.4.up, ...), custom_call_target="tpu_custom_call" | custom-call | flops 32212254720 | bytes 63438848 | tf_op jit(solution)/shard_map/expert_in/pallas_call | solution.py:638
  826.9 22.5 %convolution_convert_fusion.5.refs_1_ = bf16[1024,2048]{1,0:T(8,128)(2,1)} fusion(bf16[3840,1024]{1,0:T(8,128)(2,1)} %get-tuple-element.35.refs_1_, bf16[3840,2048]{1,0:T(8,128)(2,1)} %bitcast.35.refs_1_.grad), kind=kOutput, calls=%fused_computation.40 | convolution fusion | flops 16108224512 | bytes 27787264 | tf_op jit(solution)/shard_map/dot_general | solution.py:714
  866.0 63.4 %expert_back.1 = (bf16[3840,1024]{1,0:T(8,128)(2,1)}, bf16[3840,1024]{1,0:T(8,128)(2,1)}, f32[3840,1]{1,0:T(8,128)}, bf16[3840,2048]{1,0:T(8,128)(2,1)}) custom-call(bf16[3840,2048]{1,0:T(8,128)(2,1)} %bitcast.35.refs_1_.grad, f32[3840,1024]{1,0:T(8,128)} %tie.61.gate_in, f32[3840,1024]{1,0:T(8,128)} %get-tuple-element.37.up_in, ...), custom_call_target="tpu_custom_call" | custom-call | flops 48318382080 | bytes 91226112 | tf_op jit(solution)/shard_map/expert_back/pallas_call | solution.py:670
  929.4 19.9 %collective-permute-done.16.refs_2_.refs_1_ = bf16[256,2048]{1,0:T(8,128)(2,1)} collective-permute-done((bf16[256,2048]{1,0:T(8,128)(2,1)S(1)}, bf16[256,2048]{1,0:T(8,128)(2,1)}, u32[]{:S(2)}, u32[]{:S(2)}) %collective-permute-start.16) | collective-permute-done | bytes 1048608 | tf_op jit(solution)/shard_map/ppermute | solution.py:773
  955.3 21.4 %convolution_convert_fusion.4 = bf16[2048,1024]{1,0:T(8,128)(2,1)S(1)} fusion(bf16[3840,2048]{1,0:T(8,128)(2,1)} %bitcast.41.rows, bf16[3840,1024]{1,0:T(8,128)(2,1)} %get-tuple-element.40), kind=kOutput, calls=%fused_computation.39 | convolution fusion | flops 16108224512 | bytes 27787264 | tf_op jit(solution)/shard_map/dot_general | solution.py:714
  981.3 21.4 %convolution_convert_fusion.3 = bf16[2048,1024]{1,0:T(8,128)(2,1)S(1)} fusion(bf16[3840,2048]{1,0:T(8,128)(2,1)} %bitcast.41.rows, bf16[3840,1024]{1,0:T(8,128)(2,1)} %get-tuple-element.41), kind=kOutput, calls=%fused_computation.38 | convolution fusion | flops 16108224512 | bytes 27787264 | tf_op jit(solution)/shard_map/dot_general | solution.py:714
  1009.3 118.7 %all-to-all-done.6.refs_1_.refs_0_ = bf16[8,480,2048]{2,1,0:T(8,128)(2,1)} async-done(((bf16[8,480,2048]{2,1,0:T(8,128)(2,1)}), bf16[8,480,2048]{2,1,0:T(8,128)(2,1)}, u32[]{:S(2)}, u32[]{:S(2)}) %all-to-all-start.6) | async-done | bytes 15728672 | tf_op jit(solution)/shard_map/all_to_all | solution.py:882
  1134.4 22.7 %convolution_convert_fusion.refs_7_ = bf16[3840,2048]{1,0:T(8,128)(2,1)} fusion(bf16[3840,1024]{1,0:T(8,128)(2,1)} %get-tuple-element.35.refs_1_, bf16[256,2048]{1,0:T(8,128)(2,1)} %get-tuple-element.169, bf16[256,2048]{1,0:T(8,128)(2,1)} %get-tuple-element.170, bf16[256,2048]{1,0:T(8,128)(2,1)} %get-tuple-element.171, bf16[256,2048]{1,0:T(8,128)(2,1)} %get-tuple-element.168), kind=kOutput, calls=%fused_computation.6 | convolution fusion | flops 16130768896 | bytes 27787264 | tf_op jit(solution)/shard_map/dot_general | solution.py:704
  1161.1 22.4 %collective-permute-done.21.refs_4_ = bf16[512,1024]{1,0:T(8,128)(2,1)} collective-permute-done((bf16[512,1024]{1,0:T(8,128)(2,1)S(1)}, bf16[512,1024]{1,0:T(8,128)(2,1)}, u32[]{:S(2)}, u32[]{:S(2)}) %collective-permute-start.21) | collective-permute-done | bytes 1048608 | tf_op jit(solution)/shard_map/ppermute | solution.py:773
  1212.2 94.6 %reduce-scatter.4.cloned.1.call-done = bf16[384,2048]{1,0:T(8,128)(2,1)} async-done(((bf16[1536,2048]{1,0:T(8,128)(2,1)}), bf16[384,2048]{1,0:T(8,128)(2,1)}) %reduce-scatter.4.cloned.1.call-update) | async-done | bytes 1572880 | tf_op jit(solution)/shard_map/reduce_scatter | solution.py:897
  1350.9 23.6 %all-to-all-done.5.refs_0_ = bf16[8,480,2048]{2,1,0:T(8,128)(2,1)} async-done(((bf16[8,480,2048]{2,1,0:T(8,128)(2,1)}), bf16[8,480,2048]{2,1,0:T(8,128)(2,1)}, u32[]{:S(2)}, u32[]{:S(2)}) %all-to-all-start.5) | async-done | bytes 15728672 | tf_op jit(solution)/shard_map/all_to_all | solution.py:894
  1395.9 46.0 %attend_back.1 = (f32[1536,512]{1,0:T(8,128)}, f32[1536,512]{1,0:T(8,128)}, f32[1536,512]{1,0:T(8,128)}) custom-call(s32[1536,1]{1,0:T(8,128)S(1)} %broadcast_in_dim.171.seq_rows, s32[1,1536]{1,0:T(1,128)S(1)} %broadcast_in_dim.146.seq_cols, bf16[1536,512]{1,0:T(8,128)(2,1)S(1)} %copy-done.13, bf16[1536,512]{1,0:T(8,128)(2,1)S(1)} %copy-done.15, ...), custom_call_target="tpu_custom_call" | custom-call | flops 12079595520 | bytes 15728640 | tf_op jit(solution)/shard_map/attend_back/pallas_call | solution.py:440
  1549.5 54.2 %all-to-all-done.10 = bf16[8,4,64,1536]{3,2,1,0:T(8,128)(2,1)} async-done(((bf16[8,4,64,1536]{3,2,1,0:T(8,128)(2,1)}), bf16[8,4,64,1536]{3,2,1,0:T(8,128)(2,1)}, u32[]{:S(2)}, u32[]{:S(2)}) %all-to-all-start.10) | async-done | bytes 6291488 | tf_op jit(solution)/shard_map/all_to_all | solution.py:956
  1638.5 16.7 collective-permute-done.34
  (482 shorter events, 532.9 us)
Async XLA Ops:
  7.2 160.8 %all-gather.9.cloned.1.call-start = ((), (), s32[]{:S(2)}) async-start(), calls=%async_computation.20 | async-start | bytes 7864320 | tf_op jit(solution)/shard_map/all_gather | solution.py:760
  129.7 189.2 %all-gather.5.cloned.1.call-start = ((), (), s32[]{:S(2)}) async-start(), calls=%async_computation.15 | async-start | bytes 7864320 | tf_op jit(solution)/shard_map/all_gather | solution.py:799
  211.4 99.0 %all-to-all-start.2 = ((bf16[8,4,64,2048]{3,2,1,0:T(8,128)(2,1)}), bf16[8,4,64,2048]{3,2,1,0:T(8,128)(2,1)}, u32[]{:S(2)}, u32[]{:S(2)}) async-start(bf16[8,4,64,2048]{3,2,1,0:T(8,128)(2,1)} %broadcast_in_dim.157), calls=%async_computation.2 | async-start | bytes 16777216 | tf_op jit(solution)/shard_map/all_to_all | solution.py:802
  332.4 178.3 %all-to-all-start.3 = ((bf16[8,4,120,2048]{3,2,1,0:T(8,128)(2,1)}), bf16[8,4,120,2048]{3,2,1,0:T(8,128)(2,1)}, u32[]{:S(2)}, u32[]{:S(2)}) async-start(bf16[8,4,120,2048]{3,2,1,0:T(8,128)(2,1)} %dispatch.2.refs_1_), calls=%async_computation.3 | async-start | bytes 31457280 | tf_op jit(solution)/shard_map/all_to_all | solution.py:847
  338.1 164.1 %all-gather.7.cloned.1.call-start = ((), (), s32[]{:S(2)}) async-start(), calls=%async_computation.16 | async-start | bytes 7864320 | tf_op jit(solution)/shard_map/all_gather | solution.py:853
  524.4 257.9 %all-to-all-start.4 = ((bf16[8,4,120,2048]{3,2,1,0:T(8,128)(2,1)}), bf16[8,4,120,2048]{3,2,1,0:T(8,128)(2,1)}, u32[]{:S(2)}, u32[]{:S(2)}) async-start(bf16[8,4,120,2048]{3,2,1,0:T(8,128)(2,1)} %dispatch.3), calls=%async_computation.4 | async-start | bytes 31457280 | tf_op jit(solution)/shard_map/all_to_all | solution.py:859
  534.7 135.8 %collective-permute-start.10 = (bf16[512,1024]{1,0:T(8,128)(2,1)}, bf16[512,1024]{1,0:T(8,128)(2,1)}, u32[]{:S(2)}, u32[]{:S(2)}) collective-permute-start(bf16[512,1024]{1,0:T(8,128)(2,1)} %tie.53), channel_id=1, source_target_pairs={{0,8},{8,0},{16,24},{24,16},{1,9},{9,1},{17,25},{25,17},{2,10},{10... | collective-permute-start | bytes 3145736 | tf_op jit(solution)/shard_map/ppermute | solution.py:773
  534.7 202.7 %collective-permute-start.11 = (bf16[512,1024]{1,0:T(8,128)(2,1)}, bf16[512,1024]{1,0:T(8,128)(2,1)}, u32[]{:S(2)}, u32[]{:S(2)}) collective-permute-start(bf16[512,1024]{1,0:T(8,128)(2,1)} %tie.54), channel_id=1, source_target_pairs={{0,16},{8,24},{16,0},{24,8},{1,17},{9,25},{17,1},{25,9},{2,18},{10... | collective-permute-start | bytes 3145736 | tf_op jit(solution)/shard_map/ppermute | solution.py:773
  577.5 159.9 %collective-permute-start.12 = (bf16[512,1024]{1,0:T(8,128)(2,1)}, bf16[512,1024]{1,0:T(8,128)(2,1)}, u32[]{:S(2)}, u32[]{:S(2)}) collective-permute-start(bf16[512,1024]{1,0:T(8,128)(2,1)} %tie.55), channel_id=1, source_target_pairs={{0,24},{8,16},{16,8},{24,0},{1,25},{9,17},{17,9},{25,1},{2,26},{10... | collective-permute-start | bytes 3145736 | tf_op jit(solution)/shard_map/ppermute | solution.py:773
  602.6 145.6 %collective-permute-start.7 = (bf16[256,2048]{1,0:T(8,128)(2,1)}, bf16[256,2048]{1,0:T(8,128)(2,1)S(1)}, u32[]{:S(2)}, u32[]{:S(2)}) collective-permute-start(bf16[256,2048]{1,0:T(8,128)(2,1)} %tie.49), channel_id=1, source_target_pairs={{0,8},{8,0},{16,24},{24,16},{1,9},{9,1},{17,25},{25,17},{2,10},{10... | collective-permute-start | bytes 3145736 | tf_op jit(solution)/shard_map/ppermute | solution.py:773
  602.6 179.8 %collective-permute-start.9 = (bf16[256,2048]{1,0:T(8,128)(2,1)}, bf16[256,2048]{1,0:T(8,128)(2,1)}, u32[]{:S(2)}, u32[]{:S(2)}) collective-permute-start(bf16[256,2048]{1,0:T(8,128)(2,1)} %tie.51), channel_id=1, source_target_pairs={{0,16},{8,24},{16,0},{24,8},{1,17},{9,25},{17,1},{25,9},{2,18},{10... | collective-permute-start | bytes 3145736 | tf_op jit(solution)/shard_map/ppermute | solution.py:773
  670.5 178.9 %collective-permute-start.14 = (bf16[256,2048]{1,0:T(8,128)(2,1)}, bf16[256,2048]{1,0:T(8,128)(2,1)}, u32[]{:S(2)}, u32[]{:S(2)}) collective-permute-start(bf16[256,2048]{1,0:T(8,128)(2,1)} %tie.59), channel_id=1, source_target_pairs={{0,24},{8,16},{16,8},{24,0},{1,25},{9,17},{17,9},{25,1},{2,26},{10... | collective-permute-start | bytes 3145736 | tf_op jit(solution)/shard_map/ppermute | solution.py:773
  860.6 88.6 %collective-permute-start.16 = (bf16[256,2048]{1,0:T(8,128)(2,1)S(1)}, bf16[256,2048]{1,0:T(8,128)(2,1)}, u32[]{:S(2)}, u32[]{:S(2)}) collective-permute-start(bf16[256,2048]{1,0:T(8,128)(2,1)S(1)} %get-tuple-element.150), channel_id=1, source_target_pairs={{0,16},{8,24},{16,0},{24,8},{1,17},{9,25},{17,1},{25,9},{2,18},{10... | collective-permute-start | bytes 3145736 | tf_op jit(solution)/shard_map/ppermute | solution.py:773
  949.3 178.7 %all-to-all-start.6 = ((bf16[8,480,2048]{2,1,0:T(8,128)(2,1)}), bf16[8,480,2048]{2,1,0:T(8,128)(2,1)}, u32[]{:S(2)}, u32[]{:S(2)}) async-start(bf16[8,480,2048]{2,1,0:T(8,128)(2,1)} %bitcast.296), calls=%async_computation.6 | async-start | bytes 31457280 | tf_op jit(solution)/shard_map/all_to_all | solution.py:882
  978.9 155.4 %collective-permute-start.20 = (bf16[512,1024]{1,0:T(8,128)(2,1)}, bf16[512,1024]{1,0:T(8,128)(2,1)}, u32[]{:S(2)}, u32[]{:S(2)}) collective-permute-start(bf16[512,1024]{1,0:T(8,128)(2,1)} %tie.65), channel_id=1, source_target_pairs={{0,24},{8,16},{16,8},{24,0},{1,25},{9,17},{17,9},{25,1},{2,26},{10... | collective-permute-start | bytes 3145736 | tf_op jit(solution)/shard_map/ppermute | solution.py:773
  1004.9 152.2 %collective-permute-start.23 = (bf16[512,1024]{1,0:T(8,128)(2,1)}, bf16[512,1024]{1,0:T(8,128)(2,1)}, u32[]{:S(2)}, u32[]{:S(2)}) collective-permute-start(bf16[512,1024]{1,0:T(8,128)(2,1)} %tie.68), channel_id=1, source_target_pairs={{0,24},{8,16},{16,8},{24,0},{1,25},{9,17},{17,9},{25,1},{2,26},{10... | collective-permute-start | bytes 3145736 | tf_op jit(solution)/shard_map/ppermute | solution.py:773
  1006.3 150.8 %collective-permute-start.19 = (bf16[512,1024]{1,0:T(8,128)(2,1)}, bf16[512,1024]{1,0:T(8,128)(2,1)}, u32[]{:S(2)}, u32[]{:S(2)}) collective-permute-start(bf16[512,1024]{1,0:T(8,128)(2,1)} %tie.64), channel_id=1, source_target_pairs={{0,16},{8,24},{16,0},{24,8},{1,17},{9,25},{17,1},{25,9},{2,18},{10... | collective-permute-start | bytes 3145736 | tf_op jit(solution)/shard_map/ppermute | solution.py:773
  1006.3 154.8 %collective-permute-start.22 = (bf16[512,1024]{1,0:T(8,128)(2,1)}, bf16[512,1024]{1,0:T(8,128)(2,1)}, u32[]{:S(2)}, u32[]{:S(2)}) collective-permute-start(bf16[512,1024]{1,0:T(8,128)(2,1)} %tie.67), channel_id=1, source_target_pairs={{0,16},{8,24},{16,0},{24,8},{1,17},{9,25},{17,1},{25,9},{2,18},{10... | collective-permute-start | bytes 3145736 | tf_op jit(solution)/shard_map/ppermute | solution.py:773
  1009.2 151.9 %collective-permute-start.18 = (bf16[512,1024]{1,0:T(8,128)(2,1)}, bf16[512,1024]{1,0:T(8,128)(2,1)}, u32[]{:S(2)}, u32[]{:S(2)}) collective-permute-start(bf16[512,1024]{1,0:T(8,128)(2,1)} %tie.63), channel_id=1, source_target_pairs={{0,8},{8,0},{16,24},{24,16},{1,9},{9,1},{17,25},{25,17},{2,10},{10... | collective-permute-start | bytes 3145736 | tf_op jit(solution)/shard_map/ppermute | solution.py:773
  1134.3 172.6 %reduce-scatter.4.cloned.1.call-start = ((), (), s32[]{:S(2)}) async-start(), calls=%async_computation.17 | async-start | bytes 7864320 | tf_op jit(solution)/shard_map/reduce_scatter | solution.py:897
  1196.0 178.5 %all-to-all-start.5 = ((bf16[8,480,2048]{2,1,0:T(8,128)(2,1)}), bf16[8,480,2048]{2,1,0:T(8,128)(2,1)}, u32[]{:S(2)}, u32[]{:S(2)}) async-start(bf16[8,480,2048]{2,1,0:T(8,128)(2,1)} %bitcast.295), calls=%async_computation.5 | async-start | bytes 31457280 | tf_op jit(solution)/shard_map/all_to_all | solution.py:894
  1201.8 293.7 %reduce-scatter.6.cloned.1.call-start = ((), (), s32[]{:S(2)}) async-start(), calls=%async_computation.18 | async-start | bytes 7864320 | tf_op jit(solution)/shard_map/reduce_scatter | solution.py:925
  1386.6 104.2 %all-to-all-start.8 = ((bf16[8,4,64,2048]{3,2,1,0:T(8,128)(2,1)}), bf16[8,4,64,2048]{3,2,1,0:T(8,128)(2,1)}, u32[]{:S(2)}, u32[]{:S(2)}) async-start(bf16[8,4,64,2048]{3,2,1,0:T(8,128)(2,1)} %tie.73), calls=%async_computation.10 | async-start | bytes 16777216 | tf_op jit(solution)/shard_map/all_to_all | solution.py:927
  1391.7 278.5 %reduce-scatter.8.cloned.1.call-start = ((), (), s32[]{:S(2)}) async-start(), calls=%async_computation.19 | async-start | bytes 7864320 | tf_op jit(solution)/shard_map/reduce_scatter | solution.py:945
  (110 other events, 2148.2 us)
Sparse Core Ops, SparseCore 0:
  9.6 158.3 all-gather.8
  170.2 114.4 all-gather.4
  380.6 121.5 all-gather.6
  1196.1 110.7 reduce-scatter.3
  1386.8 108.7 reduce-scatter.5
  1497.7 115.9 reduce-scatter.7

commit v6 on v4

--- a/solution.py
+++ b/solution.py
@@ -851,10 +851,15 @@
     h_two = (middle_hat * gain_ffn).astype(bf16)
 
     h_two_all = lax.all_gather(tie(h_two, grad_send), "ctx", axis=0, tiled=True)
-    came = [swap(tie(w_gate[plane ^ step], h_two_all), step) for step in range(1, planes)]
-    gate = jnp.concatenate(by_plane([w_gate[plane]] + came))
-    h_all = tie(h_two_all, grad_in, came[0])
-    up = jnp.concatenate(exchange(w_up, h_two_all))
+    h_all = tie(h_two_all, grad_in)
+    steps = range(1, planes)
+    came_gate = [swap(tie(w_gate[plane ^ step], h_two_all), step) for step in steps]
+    gate = jnp.concatenate(by_plane([w_gate[plane]] + came_gate))
+    came_up = [
+        swap(tie(w_up[plane ^ step], before), step) for step, before in zip(steps, came_gate)
+    ]
+    up = jnp.concatenate(by_plane([w_up[plane]] + came_up))
+    came_down = [swap(tie(w_down[plane ^ step], *came_up), step) for step in steps]
     probs = jax.nn.softmax(mm(h_two, full_router), axis=-1)
     rows_in = lax.all_to_all(dispatch(position, capacity, h_all), "fsdp", 0, 0, tiled=True)
     rows_in = rows_in.reshape(-1, width)
@@ -864,7 +869,8 @@
     gate_pre, up_pre, act_picked, picked = expert_in(
         rows_in, gate, up, full_router, own, slot_block
     )
-    down = jnp.concatenate(exchange(w_down, h_two_all, act_picked))
+    came_down = [tie(part, act_picked) for part in came_down]
+    down = jnp.concatenate(by_plane([w_down[plane]] + came_down))
     grad_down_w = t_mm(act_picked, grad_in).astype(bf16)
     grad_gate, grad_up, grad_picked, grad_rows = expert_back(
         grad_in, tie(gate_pre, grad_down_w), up_pre, picked, gate, up, down, slot_block
@@ -938,24 +944,23 @@
         axis=1,
     ).astype(bf16)
     grad_part = mm_t(grad_qkv, packed[:, : 3 * share])
+    sums = t_mm(h_one, grad_qkv).astype(bf16)
+    sums = sums.reshape(planes, columns, strip, -1).transpose(1, 0, 2, 3)
     grad_h_one = lax.psum_scatter(
-        tie(grad_part.astype(bf16), mixed, grad_out_w), "ctx", scatter_dimension=0, tiled=True
+        tie(grad_part.astype(bf16), mixed, grad_out_w, sums), "ctx", scatter_dimension=0, tiled=True
     ).astype(f32)
     grad_attn_gain = jnp.sum(grad_part * (hidden_wide * scale_one), axis=0)
     rows_of = jnp.arange(planes)[:, None] == plane
     gains = [jnp.where(rows_of, g[None], 0.0).reshape(width) for g in grad_gains]
     gains = [g[:, None] for g in [grad_attn_gain, grad_ffn_gain] + gains]
     small = jnp.concatenate([grad_router] + gains, axis=1).reshape(planes * columns, -1)
-    small = lax.all_to_all(small, both, 0, 0, tiled=True)
-    sums = t_mm(h_one, grad_qkv).astype(bf16)
-    sums = sums.reshape(planes, columns, strip, -1).transpose(1, 0, 2, 3)
-    sums = lax.all_to_all(tie(sums, small), "fsdp", 0, 0, tiled=True)
+    sums = lax.all_to_all(sums, "fsdp", 0, 0, tiled=True)
+    small = lax.all_to_all(tie(small, sums), both, 0, 0, tiled=True)
+    small = jnp.sum(small, axis=0).reshape(strip, -1)
     grad_out_w = jnp.sum(grad_out_w.astype(f32), axis=0).astype(bf16)
-    small = jnp.sum(small, axis=0).reshape(strip, -1)
-    came = [swap(grad_out_w[plane ^ step], step) for step in range(1, planes)]
-    grad_out_w = sum(x.astype(f32) for x in [grad_out_w[plane]] + came)
-    sums = jnp.sum(sums.astype(f32), axis=0).astype(bf16)
-    sums = lax.all_to_all(tie(sums, *came), "ctx", 0, 0, tiled=True)
+    sums = tie(jnp.sum(sums.astype(f32), axis=0).astype(bf16), grad_out_w, small)
+    grad_out_w = sum(x.astype(f32) for x in exchange(grad_out_w, sums))
+    sums = lax.all_to_all(sums, "ctx", 0, 0, tiled=True)
     grad_qkv_w = sums.reshape(planes, strip, 3, share).transpose(2, 1, 0, 3)
     grad_qkv_w = grad_qkv_w.reshape(3, strip, width).astype(f32)
 

time: 1630 us -> 1630 us (level)
  starting transfers between devices: 198 us -> 168 us
  waiting for transfers between devices: 778 us -> 802 us
    ppermute x36, starting transfers between devices: 136 us -> 109 us  [swap(): return lax.ppermute(part, 'ctx', [(i, i ^ step) for i in range(planes)])]
    ppermute x36, waiting for transfers between devices: 279 us -> 302 us  [swap(): return lax.ppermute(part, 'ctx', [(i, i ^ step) for i in range(planes)])]
    unnamed x173 -> x178, local copies, waits for them, and re-layouts: 40.3 us -> 38.2 us
  transfers between devices with their start and end apart: 54 -> 54, of which waited for: 28 -> 31; matrix products, arithmetic and copies ran while one was open for 20% -> 20% of each run, Pallas kernels for 12% -> 12%
where the time goes in v6:
time: 1630 us; the launch traced here: 1610 us
  waiting for transfers between devices  802 us (49%)
  Pallas kernels  220 us (13%)
  matrix products  183 us (11%)
  starting transfers between devices  168 us (10%)
  local copies, waits for them, and re-layouts  132 us (8%)
  other arithmetic  94.3 us (6%)
    ppermute x36, waiting for transfers between devices, swap(): return lax.ppermute(part, 'ctx', [(i, i ^ step) for i in range(planes)])  302 us
    all_gather x1, waiting for transfers between devices, plane_shards(): h_two_all = lax.all_gather(tie(h_two, grad_send), 'ctx', axis=0, tiled=True)  117 us
    ppermute x36, starting transfers between devices, swap(): return lax.ppermute(part, 'ctx', [(i, i ^ step) for i in range(planes)])  109 us
    reduce_scatter x1, waiting for transfers between devices, plane_shards(): lax.psum_scatter(combine(grad_rows), 'ctx', scatter_dimension=0, tiled=True)  94.4 us
    dot_general x6, matrix products, t_mm(): lax.dot_general(left, right, (((0,), (0,)), ((), ())), preferred_element_...  85.5 us
    all_to_all x1, waiting for transfers between devices, plane_shards(): packed = lax.all_to_all(packed, 'fsdp', 0, 0, tiled=True)  76 us
    pallas_call x1, Pallas kernels, expert_back(): pl.pallas_call(expert_back_kernel, grid=(count // block,), in_specs=[wide...  63.4 us
    all_to_all x1, waiting for transfers between devices, plane_shards(): sums = lax.all_to_all(sums, 'fsdp', 0, 0, tiled=True)  56.2 us
  transfers between devices with their start and end apart: 54, of which 31 were waited for; matrix products, arithmetic and copies ran while one was open for 20% of the time, Pallas kernels for 12%

profile of v6, /device:TPU:0, one launch (start us, length us, event | category | flops | bytes accessed | tf_op | source)
XLA Modules:
  0.0 1614.9 jit_solution(8148568597733871393)
XLA Ops:
  28.8 42.8 %all-to-all-done.refs_1_ = bf16[4,64,3712]{2,1,0:T(8,128)(2,1)S(1)} async-done(((bf16[4,64,3712]{2,1,0:T(8,128)(2,1)}), bf16[4,64,3712]{2,1,0:T(8,128)(2,1)S(1)}, u32[]{:S(2)}, u32[]{:S(2)}) %all-to-all-start) | async-done | bytes 1900576 | tf_op jit(solution)/shard_map/all_to_all | solution.py:759
  84.1 76.0 %all-to-all-done.1 = bf16[8,4,64,1664]{3,2,1,0:T(8,128)(2,1)} async-done(((bf16[8,4,64,1664]{3,2,1,0:T(8,128)(2,1)}), bf16[8,4,64,1664]{3,2,1,0:T(8,128)(2,1)}, u32[]{:S(2)}, u32[]{:S(2)}) %all-to-all-start.1) | async-done | bytes 6815776 | tf_op jit(solution)/shard_map/all_to_all | solution.py:766
  166.6 21.0 %all-gather.4.cloned.1.call-done.refs_1_ = bf16[1536,2048]{1,0:T(8,128)(2,1)} async-done(((bf16[384,2048]{1,0:T(8,128)(2,1)}), bf16[1536,2048]{1,0:T(8,128)(2,1)}) %all-gather.4.cloned.1.call-update) | async-done | bytes 6291472 | tf_op jit(solution)/shard_map/all_gather | solution.py:760
  215.7 16.0 fusion.34.raw
  247.6 28.0 %attend.1.refs_1_ = bf16[1536,512]{1,0:T(8,128)(2,1)S(1)} custom-call(s32[1536,1]{1,0:T(8,128)S(1)} %broadcast_in_dim.171.seq_rows, s32[1,1536]{1,0:T(1,128)S(1)} %broadcast_in_dim.146.seq_cols, bf16[1536,512]{1,0:T(8,128)(2,1)S(1)} %get-tuple-element.32.query, bf16[1536,512]{1,0:T(8,128)(2,1)S(1)} %get-tuple-element.33.key, bf16[1536,512]{1,0:T(8,128)(2,1)} %copy-done.17), custom_call_target="tpu_custom_call" | custom-call | flops 4831838208 | bytes 6291456 | tf_op jit(solution)/shard_map/attend/pallas_call | solution.py:421
  373.0 117.3 %all-gather.8.cloned.1.call-done.refs_0_.refs_1_ = bf16[1536,2048]{1,0:T(8,128)(2,1)} async-done(((bf16[384,2048]{1,0:T(8,128)(2,1)}), bf16[1536,2048]{1,0:T(8,128)(2,1)}) %all-gather.8.cloned.1.call-update) | async-done | bytes 6291472 | tf_op jit(solution)/shard_map/all_gather | solution.py:853
  529.1 36.1 %collective-permute-done.6.refs_1_ = bf16[512,1024]{1,0:T(8,128)(2,1)S(1)} collective-permute-done((bf16[512,1024]{1,0:T(8,128)(2,1)}, bf16[512,1024]{1,0:T(8,128)(2,1)S(1)}, u32[]{:S(2)}, u32[]{:S(2)}) %collective-permute-start.6) | collective-permute-done | bytes 1048608 | tf_op jit(solution)/shard_map/ppermute | solution.py:773
  566.2 24.3 %collective-permute-done.7.refs_1_ = bf16[512,1024]{1,0:T(8,128)(2,1)} collective-permute-done((bf16[512,1024]{1,0:T(8,128)(2,1)}, bf16[512,1024]{1,0:T(8,128)(2,1)}, u32[]{:S(2)}, u32[]{:S(2)}) %collective-permute-start.7) | collective-permute-done | bytes 1048608 | tf_op jit(solution)/shard_map/ppermute | solution.py:773
  612.4 68.0 %collective-permute-done.10.refs_2_ = bf16[512,1024]{1,0:T(8,128)(2,1)} collective-permute-done((bf16[512,1024]{1,0:T(8,128)(2,1)}, bf16[512,1024]{1,0:T(8,128)(2,1)}, u32[]{:S(2)}, u32[]{:S(2)}) %collective-permute-start.10) | collective-permute-done | bytes 1048608 | tf_op jit(solution)/shard_map/ppermute | solution.py:773
  680.4 22.6 %collective-permute-start.12 = (bf16[256,2048]{1,0:T(8,128)(2,1)}, bf16[256,2048]{1,0:T(8,128)(2,1)}, u32[]{:S(2)}, u32[]{:S(2)}) collective-permute-start(bf16[256,2048]{1,0:T(8,128)(2,1)} %tie.55), channel_id=1, source_target_pairs={{0,8},{8,0},{16,24},{24,16},{1,9},{9,1},{17,25},{25,17},{2,10},{10... | collective-permute-start | bytes 3145736 | tf_op jit(solution)/shard_map/ppermute | solution.py:773
  710.3 44.6 %expert_in.1 = (f32[3840,1024]{1,0:T(8,128)}, f32[3840,1024]{1,0:T(8,128)}, bf16[3840,1024]{1,0:T(8,128)(2,1)}, f32[3840,1]{1,0:T(8,128)}) custom-call(bf16[3840,2048]{1,0:T(8,128)(2,1)} %bitcast.36.rows, bf16[2048,1024]{1,0:T(8,128)(2,1)} %pad_maximum_fusion.2.gate, bf16[2048,1024]{1,0:T(8,128)(2,1)} %pad_maximum_fusion.4.up, ...), custom_call_target="tpu_custom_call" | custom-call | flops 32212254720 | bytes 63438848 | tf_op jit(solution)/shard_map/expert_in/pallas_call | solution.py:638
  754.9 22.5 %convolution_convert_fusion.5.refs_1_ = bf16[1024,2048]{1,0:T(8,128)(2,1)} fusion(bf16[3840,1024]{1,0:T(8,128)(2,1)} %get-tuple-element.35.refs_1_, bf16[3840,2048]{1,0:T(8,128)(2,1)} %bitcast.34.refs_1_.grad), kind=kOutput, calls=%fused_computation.40 | convolution fusion | flops 16108224512 | bytes 27787264 | tf_op jit(solution)/shard_map/dot_general | solution.py:714
  788.7 41.8 %collective-permute-start.16 = (bf16[256,2048]{1,0:T(8,128)(2,1)S(1)}, bf16[256,2048]{1,0:T(8,128)(2,1)}, u32[]{:S(2)}, u32[]{:S(2)}) collective-permute-start(bf16[256,2048]{1,0:T(8,128)(2,1)S(1)} %get-tuple-element.164), channel_id=1, source_target_pairs={{0,16},{8,24},{16,0},{24,8},{1,17},{9,25},{17,1},{25,9},{2,18},{10... | collective-permute-start | bytes 3145736 | tf_op jit(solution)/shard_map/ppermute | solution.py:773
  832.8 63.4 %expert_back.1 = (bf16[3840,1024]{1,0:T(8,128)(2,1)}, bf16[3840,1024]{1,0:T(8,128)(2,1)}, f32[3840,1]{1,0:T(8,128)}, bf16[3840,2048]{1,0:T(8,128)(2,1)}) custom-call(bf16[3840,2048]{1,0:T(8,128)(2,1)} %bitcast.34.refs_1_.grad, f32[3840,1024]{1,0:T(8,128)} %tie.61.gate_in, f32[3840,1024]{1,0:T(8,128)} %get-tuple-element.37.up_in, ...), custom_call_target="tpu_custom_call" | custom-call | flops 48318382080 | bytes 91226112 | tf_op jit(solution)/shard_map/expert_back/pallas_call | solution.py:670
  903.1 21.4 %convolution_convert_fusion.3 = bf16[2048,1024]{1,0:T(8,128)(2,1)S(1)} fusion(bf16[3840,2048]{1,0:T(8,128)(2,1)} %bitcast.36.rows, bf16[3840,1024]{1,0:T(8,128)(2,1)} %get-tuple-element.41), kind=kOutput, calls=%fused_computation.38 | convolution fusion | flops 16108224512 | bytes 27787264 | tf_op jit(solution)/shard_map/dot_general | solution.py:714
  931.0 21.4 %convolution_convert_fusion.4 = bf16[2048,1024]{1,0:T(8,128)(2,1)S(1)} fusion(bf16[3840,2048]{1,0:T(8,128)(2,1)} %bitcast.36.rows, bf16[3840,1024]{1,0:T(8,128)(2,1)} %get-tuple-element.40), kind=kOutput, calls=%fused_computation.39 | convolution fusion | flops 16108224512 | bytes 27787264 | tf_op jit(solution)/shard_map/dot_general | solution.py:714
  957.1 87.0 %collective-permute-done.20.refs_1_ = bf16[512,1024]{1,0:T(8,128)(2,1)} collective-permute-done((bf16[512,1024]{1,0:T(8,128)(2,1)}, bf16[512,1024]{1,0:T(8,128)(2,1)}, u32[]{:S(2)}, u32[]{:S(2)}) %collective-permute-start.20) | collective-permute-done | bytes 1048608 | tf_op jit(solution)/shard_map/ppermute | solution.py:773
  1045.9 29.9 %all-to-all-done.6.refs_1_.refs_0_ = bf16[8,480,2048]{2,1,0:T(8,128)(2,1)} async-done(((bf16[8,480,2048]{2,1,0:T(8,128)(2,1)}), bf16[8,480,2048]{2,1,0:T(8,128)(2,1)}, u32[]{:S(2)}, u32[]{:S(2)}) %all-to-all-start.6) | async-done | bytes 15728672 | tf_op jit(solution)/shard_map/all_to_all | solution.py:884
  1082.0 22.5 %convolution_convert_fusion.refs_4_ = bf16[3840,2048]{1,0:T(8,128)(2,1)} fusion(bf16[3840,1024]{1,0:T(8,128)(2,1)} %get-tuple-element.35.refs_1_, bf16[256,2048]{1,0:T(8,128)(2,1)} %get-tuple-element.183, bf16[256,2048]{1,0:T(8,128)(2,1)} %get-tuple-element.184, bf16[256,2048]{1,0:T(8,128)(2,1)} %get-tuple-element.185, bf16[256,2048]{1,0:T(8,128)(2,1)} %get-tuple-element.182), kind=kOutput, calls=%fused_computation.6 | convolution fusion | flops 16130768896 | bytes 27787264 | tf_op jit(solution)/shard_map/dot_general | solution.py:704
  1139.8 94.4 %reduce-scatter.4.cloned.1.call-done = bf16[384,2048]{1,0:T(8,128)(2,1)} async-done(((bf16[1536,2048]{1,0:T(8,128)(2,1)}), bf16[384,2048]{1,0:T(8,128)(2,1)}) %reduce-scatter.4.cloned.1.call-update) | async-done | bytes 1572880 | tf_op jit(solution)/shard_map/reduce_scatter | solution.py:899
  1278.7 23.4 %all-to-all-done.5.refs_0_ = bf16[8,480,2048]{2,1,0:T(8,128)(2,1)} async-done(((bf16[8,480,2048]{2,1,0:T(8,128)(2,1)}), bf16[8,480,2048]{2,1,0:T(8,128)(2,1)}, u32[]{:S(2)}, u32[]{:S(2)}) %all-to-all-start.5) | async-done | bytes 15728672 | tf_op jit(solution)/shard_map/all_to_all | solution.py:896
  1324.1 45.9 %attend_back.1 = (f32[1536,512]{1,0:T(8,128)}, f32[1536,512]{1,0:T(8,128)}, f32[1536,512]{1,0:T(8,128)}) custom-call(s32[1536,1]{1,0:T(8,128)S(1)} %broadcast_in_dim.171.seq_rows, s32[1,1536]{1,0:T(1,128)S(1)} %broadcast_in_dim.146.seq_cols, bf16[1536,512]{1,0:T(8,128)(2,1)S(1)} %copy-done.14, bf16[1536,512]{1,0:T(8,128)(2,1)S(1)} %copy-done.16, ...), custom_call_target="tpu_custom_call" | custom-call | flops 12079595520 | bytes 15728640 | tf_op jit(solution)/shard_map/attend_back/pallas_call | solution.py:440
  1418.4 15.8 fusion.7
  1454.5 56.2 %all-to-all-done.9.refs_1_ = bf16[8,4,64,1536]{3,2,1,0:T(8,128)(2,1)} async-done(((bf16[8,4,64,1536]{3,2,1,0:T(8,128)(2,1)}), bf16[8,4,64,1536]{3,2,1,0:T(8,128)(2,1)}, u32[]{:S(2)}, u32[]{:S(2)}) %all-to-all-start.9) | async-done | bytes 6291488 | tf_op jit(solution)/shard_map/all_to_all | solution.py:957
  (492 shorter events, 556.6 us)
Async XLA Ops:
  27.7 159.9 %all-gather.4.cloned.1.call-start = ((), (), s32[]{:S(2)}) async-start(), calls=%async_computation.15 | async-start | bytes 7864320 | tf_op jit(solution)/shard_map/all_gather | solution.py:760
  77.9 82.3 %all-to-all-start.1 = ((bf16[8,4,64,1664]{3,2,1,0:T(8,128)(2,1)}), bf16[8,4,64,1664]{3,2,1,0:T(8,128)(2,1)}, u32[]{:S(2)}, u32[]{:S(2)}) async-start(bf16[8,4,64,1664]{3,2,1,0:T(8,128)(2,1)} %broadcast_in_dim.153), calls=%async_computation.1 | async-start | bytes 13631488 | tf_op jit(solution)/shard_map/all_to_all | solution.py:766
  82.9 223.8 %all-gather.6.cloned.1.call-start = ((), (), s32[]{:S(2)}) async-start(), calls=%async_computation.16 | async-start | bytes 7864320 | tf_op jit(solution)/shard_map/all_gather | solution.py:799
  193.0 99.2 %all-to-all-start.2 = ((bf16[8,4,64,2048]{3,2,1,0:T(8,128)(2,1)}), bf16[8,4,64,2048]{3,2,1,0:T(8,128)(2,1)}, u32[]{:S(2)}, u32[]{:S(2)}) async-start(bf16[8,4,64,2048]{3,2,1,0:T(8,128)(2,1)} %broadcast_in_dim.157.refs_3_), calls=%async_computation.2 | async-start | bytes 16777216 | tf_op jit(solution)/shard_map/all_to_all | solution.py:802
  320.4 178.4 %all-to-all-start.3 = ((bf16[8,4,120,2048]{3,2,1,0:T(8,128)(2,1)}), bf16[8,4,120,2048]{3,2,1,0:T(8,128)(2,1)}, u32[]{:S(2)}, u32[]{:S(2)}) async-start(bf16[8,4,120,2048]{3,2,1,0:T(8,128)(2,1)} %dispatch.2.refs_1_), calls=%async_computation.3 | async-start | bytes 31457280 | tf_op jit(solution)/shard_map/all_to_all | solution.py:847
  326.1 164.3 %all-gather.8.cloned.1.call-start = ((), (), s32[]{:S(2)}) async-start(), calls=%async_computation.17 | async-start | bytes 7864320 | tf_op jit(solution)/shard_map/all_gather | solution.py:853
  512.3 197.9 %all-to-all-start.4 = ((bf16[8,4,120,2048]{3,2,1,0:T(8,128)(2,1)}), bf16[8,4,120,2048]{3,2,1,0:T(8,128)(2,1)}, u32[]{:S(2)}, u32[]{:S(2)}) async-start(bf16[8,4,120,2048]{3,2,1,0:T(8,128)(2,1)} %dispatch.3), calls=%async_computation.4 | async-start | bytes 31457280 | tf_op jit(solution)/shard_map/all_to_all | solution.py:864
  590.5 89.9 %collective-permute-start.10 = (bf16[512,1024]{1,0:T(8,128)(2,1)}, bf16[512,1024]{1,0:T(8,128)(2,1)}, u32[]{:S(2)}, u32[]{:S(2)}) collective-permute-start(bf16[512,1024]{1,0:T(8,128)(2,1)} %tie.53), channel_id=1, source_target_pairs={{0,16},{8,24},{16,0},{24,8},{1,17},{9,25},{17,1},{25,9},{2,18},{10... | collective-permute-start | bytes 3145736 | tf_op jit(solution)/shard_map/ppermute | solution.py:773
  590.5 89.9 %collective-permute-start.11 = (bf16[512,1024]{1,0:T(8,128)(2,1)}, bf16[512,1024]{1,0:T(8,128)(2,1)}, u32[]{:S(2)}, u32[]{:S(2)}) collective-permute-start(bf16[512,1024]{1,0:T(8,128)(2,1)} %tie.54), channel_id=1, source_target_pairs={{0,24},{8,16},{16,8},{24,0},{1,25},{9,17},{17,9},{25,1},{2,26},{10... | collective-permute-start | bytes 3145736 | tf_op jit(solution)/shard_map/ppermute | solution.py:773
  680.4 97.0 %collective-permute-start.12 = (bf16[256,2048]{1,0:T(8,128)(2,1)}, bf16[256,2048]{1,0:T(8,128)(2,1)}, u32[]{:S(2)}, u32[]{:S(2)}) collective-permute-start(bf16[256,2048]{1,0:T(8,128)(2,1)} %tie.55), channel_id=1, source_target_pairs={{0,8},{8,0},{16,24},{24,16},{1,9},{9,1},{17,25},{25,17},{2,10},{10... | collective-permute-start | bytes 3145736 | tf_op jit(solution)/shard_map/ppermute | solution.py:773
  703.0 74.4 %collective-permute-start.13 = (bf16[256,2048]{1,0:T(8,128)(2,1)}, bf16[256,2048]{1,0:T(8,128)(2,1)}, u32[]{:S(2)}, u32[]{:S(2)}) collective-permute-start(bf16[256,2048]{1,0:T(8,128)(2,1)} %tie.57), channel_id=1, source_target_pairs={{0,16},{8,24},{16,0},{24,8},{1,17},{9,25},{17,1},{25,9},{2,18},{10... | collective-permute-start | bytes 3145736 | tf_op jit(solution)/shard_map/ppermute | solution.py:773
  703.0 74.3 %collective-permute-start.14 = (bf16[256,2048]{1,0:T(8,128)(2,1)}, bf16[256,2048]{1,0:T(8,128)(2,1)}, u32[]{:S(2)}, u32[]{:S(2)}) collective-permute-start(bf16[256,2048]{1,0:T(8,128)(2,1)} %tie.59), channel_id=1, source_target_pairs={{0,24},{8,16},{16,8},{24,0},{1,25},{9,17},{17,9},{25,1},{2,26},{10... | collective-permute-start | bytes 3145736 | tf_op jit(solution)/shard_map/ppermute | solution.py:773
  787.2 109.0 %collective-permute-start.17 = (bf16[256,2048]{1,0:T(8,128)(2,1)}, bf16[256,2048]{1,0:T(8,128)(2,1)S(1)}, u32[]{:S(2)}, u32[]{:S(2)}) collective-permute-start(bf16[256,2048]{1,0:T(8,128)(2,1)} %get-tuple-element.163), channel_id=1, source_target_pairs={{0,24},{8,16},{16,8},{24,0},{1,25},{9,17},{17,9},{25,1},{2,26},{10... | collective-permute-start | bytes 3145736 | tf_op jit(solution)/shard_map/ppermute | solution.py:773
  788.7 108.6 %collective-permute-start.16 = (bf16[256,2048]{1,0:T(8,128)(2,1)S(1)}, bf16[256,2048]{1,0:T(8,128)(2,1)}, u32[]{:S(2)}, u32[]{:S(2)}) collective-permute-start(bf16[256,2048]{1,0:T(8,128)(2,1)S(1)} %get-tuple-element.164), channel_id=1, source_target_pairs={{0,16},{8,24},{16,0},{24,8},{1,17},{9,25},{17,1},{25,9},{2,18},{10... | collective-permute-start | bytes 3145736 | tf_op jit(solution)/shard_map/ppermute | solution.py:773
  897.3 178.5 %all-to-all-start.6 = ((bf16[8,480,2048]{2,1,0:T(8,128)(2,1)}), bf16[8,480,2048]{2,1,0:T(8,128)(2,1)}, u32[]{:S(2)}, u32[]{:S(2)}) async-start(bf16[8,480,2048]{2,1,0:T(8,128)(2,1)} %bitcast.282), calls=%async_computation.6 | async-start | bytes 31457280 | tf_op jit(solution)/shard_map/all_to_all | solution.py:884
  928.0 116.1 %collective-permute-start.20 = (bf16[512,1024]{1,0:T(8,128)(2,1)}, bf16[512,1024]{1,0:T(8,128)(2,1)}, u32[]{:S(2)}, u32[]{:S(2)}) collective-permute-start(bf16[512,1024]{1,0:T(8,128)(2,1)} %tie.65), channel_id=1, source_target_pairs={{0,16},{8,24},{16,0},{24,8},{1,17},{9,25},{17,1},{25,9},{2,18},{10... | collective-permute-start | bytes 3145736 | tf_op jit(solution)/shard_map/ppermute | solution.py:773
  930.1 114.0 %collective-permute-start.18 = (bf16[512,1024]{1,0:T(8,128)(2,1)}, bf16[512,1024]{1,0:T(8,128)(2,1)}, u32[]{:S(2)}, u32[]{:S(2)}) collective-permute-start(bf16[512,1024]{1,0:T(8,128)(2,1)} %tie.63), channel_id=1, source_target_pairs={{0,8},{8,0},{16,24},{24,16},{1,9},{9,1},{17,25},{25,17},{2,10},{10... | collective-permute-start | bytes 3145736 | tf_op jit(solution)/shard_map/ppermute | solution.py:773
  955.7 148.7 %collective-permute-start.23 = (bf16[512,1024]{1,0:T(8,128)(2,1)}, bf16[512,1024]{1,0:T(8,128)(2,1)S(1)}, u32[]{:S(2)}, u32[]{:S(2)}) collective-permute-start(bf16[512,1024]{1,0:T(8,128)(2,1)} %tie.68), channel_id=1, source_target_pairs={{0,24},{8,16},{16,8},{24,0},{1,25},{9,17},{17,9},{25,1},{2,26},{10... | collective-permute-start | bytes 3145736 | tf_op jit(solution)/shard_map/ppermute | solution.py:773
  1082.0 152.3 %reduce-scatter.4.cloned.1.call-start = ((), (), s32[]{:S(2)}) async-start(), calls=%async_computation.18 | async-start | bytes 7864320 | tf_op jit(solution)/shard_map/reduce_scatter | solution.py:899
  1123.6 178.5 %all-to-all-start.5 = ((bf16[8,480,2048]{2,1,0:T(8,128)(2,1)}), bf16[8,480,2048]{2,1,0:T(8,128)(2,1)}, u32[]{:S(2)}, u32[]{:S(2)}) async-start(bf16[8,480,2048]{2,1,0:T(8,128)(2,1)} %bitcast.281), calls=%async_computation.5 | async-start | bytes 31457280 | tf_op jit(solution)/shard_map/all_to_all | solution.py:896
  1129.4 304.7 %reduce-scatter.6.cloned.1.call-start = ((), (), s32[]{:S(2)}) async-start(), calls=%async_computation.19 | async-start | bytes 7864320 | tf_op jit(solution)/shard_map/reduce_scatter | solution.py:927
  1314.5 119.7 %all-to-all-start.8 = ((bf16[8,4,64,2048]{3,2,1,0:T(8,128)(2,1)}), bf16[8,4,64,2048]{3,2,1,0:T(8,128)(2,1)}, u32[]{:S(2)}, u32[]{:S(2)}) async-start(bf16[8,4,64,2048]{3,2,1,0:T(8,128)(2,1)} %tie.73), calls=%async_computation.10 | async-start | bytes 16777216 | tf_op jit(solution)/shard_map/all_to_all | solution.py:929
  1319.7 281.7 %reduce-scatter.8.cloned.1.call-start = ((), (), s32[]{:S(2)}) async-start(), calls=%async_computation.20 | async-start | bytes 7864320 | tf_op jit(solution)/shard_map/reduce_scatter | solution.py:949
  1434.2 76.5 %all-to-all-start.9 = ((bf16[8,4,64,1536]{3,2,1,0:T(8,128)(2,1)}), bf16[8,4,64,1536]{3,2,1,0:T(8,128)(2,1)}, u32[]{:S(2)}, u32[]{:S(2)}) async-start(bf16[8,4,64,1536]{3,2,1,0:T(8,128)(2,1)} %bitcast.284), calls=%async_computation.12 | async-start | bytes 12582912 | tf_op jit(solution)/shard_map/all_to_all | solution.py:957
  (115 other events, 2362.8 us)
Sparse Core Ops, SparseCore 0:
  73.1 114.4 all-gather.3
  192.2 114.5 all-gather.5
  368.8 121.5 all-gather.7
  1123.7 110.5 reduce-scatter.3
  1314.6 108.4 reduce-scatter.5
  1434.3 113.6 reduce-scatter.7

commit v7 on v6

--- a/solution.py
+++ b/solution.py
@@ -851,9 +851,9 @@
     h_two = (middle_hat * gain_ffn).astype(bf16)
 
     h_two_all = lax.all_gather(tie(h_two, grad_send), "ctx", axis=0, tiled=True)
-    h_all = tie(h_two_all, grad_in)
     steps = range(1, planes)
     came_gate = [swap(tie(w_gate[plane ^ step], h_two_all), step) for step in steps]
+    h_all = tie(h_two_all, grad_in, came_gate[planes // 2 - 1])
     gate = jnp.concatenate(by_plane([w_gate[plane]] + came_gate))
     came_up = [
         swap(tie(w_up[plane ^ step], before), step) for step, before in zip(steps, came_gate)
@@ -944,23 +944,25 @@
         axis=1,
     ).astype(bf16)
     grad_part = mm_t(grad_qkv, packed[:, : 3 * share])
+    grad_out_w = jnp.sum(grad_out_w.astype(f32), axis=0).astype(bf16)
+    came_out = [swap(grad_out_w[plane ^ step], step) for step in steps]
+    grad_out_w = sum(x.astype(f32) for x in [grad_out_w[plane]] + came_out)
     sums = t_mm(h_one, grad_qkv).astype(bf16)
     sums = sums.reshape(planes, columns, strip, -1).transpose(1, 0, 2, 3)
     grad_h_one = lax.psum_scatter(
-        tie(grad_part.astype(bf16), mixed, grad_out_w, sums), "ctx", scatter_dimension=0, tiled=True
+        tie(grad_part.astype(bf16), mixed, sums, *came_out), "ctx", scatter_dimension=0, tiled=True
     ).astype(f32)
     grad_attn_gain = jnp.sum(grad_part * (hidden_wide * scale_one), axis=0)
     rows_of = jnp.arange(planes)[:, None] == plane
     gains = [jnp.where(rows_of, g[None], 0.0).reshape(width) for g in grad_gains]
     gains = [g[:, None] for g in [grad_attn_gain, grad_ffn_gain] + gains]
-    small = jnp.concatenate([grad_router] + gains, axis=1).reshape(planes * columns, -1)
+    small = jnp.concatenate([grad_router] + gains, axis=1).reshape(planes, columns, -1)
+    small = sum([small[plane]] + [swap(small[plane ^ step], step) for step in steps])
     sums = lax.all_to_all(sums, "fsdp", 0, 0, tiled=True)
-    small = lax.all_to_all(tie(small, sums), both, 0, 0, tiled=True)
+    small = lax.all_to_all(tie(small, sums), "fsdp", 0, 0, tiled=True)
     small = jnp.sum(small, axis=0).reshape(strip, -1)
-    grad_out_w = jnp.sum(grad_out_w.astype(f32), axis=0).astype(bf16)
-    sums = tie(jnp.sum(sums.astype(f32), axis=0).astype(bf16), grad_out_w, small)
-    grad_out_w = sum(x.astype(f32) for x in exchange(grad_out_w, sums))
-    sums = lax.all_to_all(sums, "ctx", 0, 0, tiled=True)
+    sums = jnp.sum(sums.astype(f32), axis=0).astype(bf16)
+    sums = lax.all_to_all(tie(sums, small), "ctx", 0, 0, tiled=True)
     grad_qkv_w = sums.reshape(planes, strip, 3, share).transpose(2, 1, 0, 3)
     grad_qkv_w = grad_qkv_w.reshape(3, strip, width).astype(f32)
 

time: 1630 us -> 1610 us (0.988)
  starting transfers between devices: 168 us -> 134 us
  waiting for transfers between devices: 802 us -> 820 us
    ppermute x36 -> x39, starting transfers between devices: 109 us -> 73.6 us  [swap(): return lax.ppermute(part, 'ctx', [(i, i ^ step) for i in range(planes)])]
    all_to_all x1, waiting for transfers between devices: 0.01 us -> 25.4 us  [plane_shards(): lax.all_to_all(dispatch(position, capacity, h_all), 'fsdp', 0, 0, tiled=T...]
    ppermute x36 -> x39, waiting for transfers between devices: 302 us -> 305 us  [swap(): return lax.ppermute(part, 'ctx', [(i, i ^ step) for i in range(planes)])]
    unnamed x178 -> x184, local copies, waits for them, and re-layouts: 38.2 us -> 41.1 us
  transfers between devices with their start and end apart: 54 -> 57, of which waited for: 31 -> 30; matrix products, arithmetic and copies ran while one was open for 20% -> 20% of each run, Pallas kernels for 12% -> 12%
where the time goes in v7:
time: 1610 us
  waiting for transfers between devices  820 us (51%)
  Pallas kernels  220 us (14%)
  matrix products  184 us (11%)
  local copies, waits for them, and re-layouts  137 us (9%)
  starting transfers between devices  134 us (8%)
  other arithmetic  94.8 us (6%)
    ppermute x39, waiting for transfers between devices, swap(): return lax.ppermute(part, 'ctx', [(i, i ^ step) for i in range(planes)])  305 us
    all_gather x1, waiting for transfers between devices, plane_shards(): h_two_all = lax.all_gather(tie(h_two, grad_send), 'ctx', axis=0, tiled=True)  117 us
    reduce_scatter x1, waiting for transfers between devices, plane_shards(): lax.psum_scatter(combine(grad_rows), 'ctx', scatter_dimension=0, tiled=True)  94.9 us
    dot_general x6, matrix products, t_mm(): lax.dot_general(left, right, (((0,), (0,)), ((), ())), preferred_element_...  86.9 us
    all_to_all x1, waiting for transfers between devices, plane_shards(): packed = lax.all_to_all(packed, 'fsdp', 0, 0, tiled=True)  76 us
    ppermute x39, starting transfers between devices, swap(): return lax.ppermute(part, 'ctx', [(i, i ^ step) for i in range(planes)])  73.6 us
    pallas_call x1, Pallas kernels, expert_back(): pl.pallas_call(expert_back_kernel, grid=(count // block,), in_specs=[wide...  63.4 us
    dot_general x4, matrix products, mm(): return jnp.dot(left, right, preferred_element_type=jnp.float32)  47 us
  transfers between devices with their start and end apart: 57, of which 30 were waited for; matrix products, arithmetic and copies ran while one was open for 20% of the time, Pallas kernels for 12%

profile of v7, /device:TPU:0, one launch (start us, length us, event | category | flops | bytes accessed | tf_op | source)
XLA Modules:
  0.0 1606.3 jit_solution(16098197152588294547)
XLA Ops:
  28.8 42.8 %all-to-all-done.refs_1_ = bf16[4,64,3712]{2,1,0:T(8,128)(2,1)S(1)} async-done(((bf16[4,64,3712]{2,1,0:T(8,128)(2,1)}), bf16[4,64,3712]{2,1,0:T(8,128)(2,1)S(1)}, u32[]{:S(2)}, u32[]{:S(2)}) %all-to-all-start) | async-done | bytes 1900576 | tf_op jit(solution)/shard_map/all_to_all | solution.py:759
  84.2 76.0 %all-to-all-done.1 = bf16[8,4,64,1664]{3,2,1,0:T(8,128)(2,1)} async-done(((bf16[8,4,64,1664]{3,2,1,0:T(8,128)(2,1)}), bf16[8,4,64,1664]{3,2,1,0:T(8,128)(2,1)}, u32[]{:S(2)}, u32[]{:S(2)}) %all-to-all-start.1) | async-done | bytes 6815776 | tf_op jit(solution)/shard_map/all_to_all | solution.py:766
  166.6 21.0 %all-gather.4.cloned.1.call-done.refs_1_ = bf16[1536,2048]{1,0:T(8,128)(2,1)} async-done(((bf16[384,2048]{1,0:T(8,128)(2,1)}), bf16[1536,2048]{1,0:T(8,128)(2,1)}) %all-gather.4.cloned.1.call-update) | async-done | bytes 6291472 | tf_op jit(solution)/shard_map/all_gather | solution.py:760
  247.4 28.0 %attend.1.refs_1_ = bf16[1536,512]{1,0:T(8,128)(2,1)S(1)} custom-call(s32[1536,1]{1,0:T(8,128)S(1)} %broadcast_in_dim.171.seq_rows, s32[1,1536]{1,0:T(1,128)S(1)} %broadcast_in_dim.146.seq_cols, bf16[1536,512]{1,0:T(8,128)(2,1)S(1)} %get-tuple-element.32.query, bf16[1536,512]{1,0:T(8,128)(2,1)S(1)} %get-tuple-element.33.key, bf16[1536,512]{1,0:T(8,128)(2,1)} %copy-done.17), custom_call_target="tpu_custom_call" | custom-call | flops 4831838208 | bytes 6291456 | tf_op jit(solution)/shard_map/attend/pallas_call | solution.py:421
  372.9 117.4 %all-gather.8.cloned.1.call-done.refs_1_.refs_0_ = bf16[1536,2048]{1,0:T(8,128)(2,1)} async-done(((bf16[384,2048]{1,0:T(8,128)(2,1)}), bf16[1536,2048]{1,0:T(8,128)(2,1)}) %all-gather.8.cloned.1.call-update) | async-done | bytes 6291472 | tf_op jit(solution)/shard_map/all_gather | solution.py:853
  490.9 45.9 %collective-permute-done.6.refs_2_.refs_1_ = bf16[512,1024]{1,0:T(8,128)(2,1)S(1)} collective-permute-done((bf16[512,1024]{1,0:T(8,128)(2,1)}, bf16[512,1024]{1,0:T(8,128)(2,1)S(1)}, u32[]{:S(2)}, u32[]{:S(2)}) %collective-permute-start.6) | collective-permute-done | bytes 1048608 | tf_op jit(solution)/shard_map/ppermute | solution.py:773
  583.9 23.0 %collective-permute-done.8.refs_1_ = bf16[512,1024]{1,0:T(8,128)(2,1)} collective-permute-done((bf16[512,1024]{1,0:T(8,128)(2,1)}, bf16[512,1024]{1,0:T(8,128)(2,1)}, u32[]{:S(2)}, u32[]{:S(2)}) %collective-permute-start.8) | collective-permute-done | bytes 1048608 | tf_op jit(solution)/shard_map/ppermute | solution.py:773
  616.0 59.1 %collective-permute-done.10.refs_2_ = bf16[512,1024]{1,0:T(8,128)(2,1)S(1)} collective-permute-done((bf16[512,1024]{1,0:T(8,128)(2,1)}, bf16[512,1024]{1,0:T(8,128)(2,1)S(1)}, u32[]{:S(2)}, u32[]{:S(2)}) %collective-permute-start.10) | collective-permute-done | bytes 1048608 | tf_op jit(solution)/shard_map/ppermute | solution.py:773
  676.1 21.4 %collective-permute-start.12 = (bf16[256,2048]{1,0:T(8,128)(2,1)}, bf16[256,2048]{1,0:T(8,128)(2,1)}, u32[]{:S(2)}, u32[]{:S(2)}) collective-permute-start(bf16[256,2048]{1,0:T(8,128)(2,1)} %tie.52), channel_id=1, source_target_pairs={{0,8},{8,0},{16,24},{24,16},{1,9},{9,1},{17,25},{25,17},{2,10},{10... | collective-permute-start | bytes 3145736 | tf_op jit(solution)/shard_map/ppermute | solution.py:773
  704.8 25.4 %all-to-all-done.4 = bf16[8,4,120,2048]{3,2,1,0:T(8,128)(2,1)} async-done(((bf16[8,4,120,2048]{3,2,1,0:T(8,128)(2,1)}), bf16[8,4,120,2048]{3,2,1,0:T(8,128)(2,1)}, u32[]{:S(2)}, u32[]{:S(2)}) %all-to-all-start.4) | async-done | bytes 15728672 | tf_op jit(solution)/shard_map/all_to_all | solution.py:864
  730.2 44.6 %expert_in.1 = (f32[3840,1024]{1,0:T(8,128)}, f32[3840,1024]{1,0:T(8,128)}, bf16[3840,1024]{1,0:T(8,128)(2,1)}, f32[3840,1]{1,0:T(8,128)}) custom-call(bf16[3840,2048]{1,0:T(8,128)(2,1)} %bitcast.37.rows, bf16[2048,1024]{1,0:T(8,128)(2,1)} %pad_maximum_fusion.2.gate, bf16[2048,1024]{1,0:T(8,128)(2,1)} %pad_maximum_fusion.4.up, ...), custom_call_target="tpu_custom_call" | custom-call | flops 32212254720 | bytes 63438848 | tf_op jit(solution)/shard_map/expert_in/pallas_call | solution.py:638
  774.8 22.5 %convolution_convert_fusion.5.refs_1_ = bf16[1024,2048]{1,0:T(8,128)(2,1)} fusion(bf16[3840,1024]{1,0:T(8,128)(2,1)} %get-tuple-element.35.refs_1_, bf16[3840,2048]{1,0:T(8,128)(2,1)} %bitcast.34.refs_1_.grad), kind=kOutput, calls=%fused_computation.40 | convolution fusion | flops 16108224512 | bytes 27787264 | tf_op jit(solution)/shard_map/dot_general | solution.py:714
  813.9 63.4 %expert_back.1 = (bf16[3840,1024]{1,0:T(8,128)(2,1)}, bf16[3840,1024]{1,0:T(8,128)(2,1)}, f32[3840,1]{1,0:T(8,128)}, bf16[3840,2048]{1,0:T(8,128)(2,1)}) custom-call(bf16[3840,2048]{1,0:T(8,128)(2,1)} %bitcast.34.refs_1_.grad, f32[3840,1024]{1,0:T(8,128)} %tie.58.gate_in, f32[3840,1024]{1,0:T(8,128)} %get-tuple-element.37.up_in, ...), custom_call_target="tpu_custom_call" | custom-call | flops 48318382080 | bytes 91226112 | tf_op jit(solution)/shard_map/expert_back/pallas_call | solution.py:670
  877.3 18.7 %collective-permute-done.16.refs_2_.refs_1_ = bf16[256,2048]{1,0:T(8,128)(2,1)} collective-permute-done((bf16[256,2048]{1,0:T(8,128)(2,1)S(1)}, bf16[256,2048]{1,0:T(8,128)(2,1)}, u32[]{:S(2)}, u32[]{:S(2)}) %collective-permute-start.16) | collective-permute-done | bytes 1048608 | tf_op jit(solution)/shard_map/ppermute | solution.py:773
  901.8 21.4 %convolution_convert_fusion.3 = bf16[2048,1024]{1,0:T(8,128)(2,1)S(1)} fusion(bf16[3840,2048]{1,0:T(8,128)(2,1)} %bitcast.37.rows, bf16[3840,1024]{1,0:T(8,128)(2,1)} %get-tuple-element.41), kind=kOutput, calls=%fused_computation.38 | convolution fusion | flops 16108224512 | bytes 27787264 | tf_op jit(solution)/shard_map/dot_general | solution.py:714
  929.7 21.4 %convolution_convert_fusion.4 = bf16[2048,1024]{1,0:T(8,128)(2,1)S(1)} fusion(bf16[3840,2048]{1,0:T(8,128)(2,1)} %bitcast.37.rows, bf16[3840,1024]{1,0:T(8,128)(2,1)} %get-tuple-element.40), kind=kOutput, calls=%fused_computation.39 | convolution fusion | flops 16108224512 | bytes 27787264 | tf_op jit(solution)/shard_map/dot_general | solution.py:714
  955.8 83.5 %collective-permute-done.20.refs_1_ = bf16[512,1024]{1,0:T(8,128)(2,1)} collective-permute-done((bf16[512,1024]{1,0:T(8,128)(2,1)}, bf16[512,1024]{1,0:T(8,128)(2,1)}, u32[]{:S(2)}, u32[]{:S(2)}) %collective-permute-start.20) | collective-permute-done | bytes 1048608 | tf_op jit(solution)/shard_map/ppermute | solution.py:773
  1042.4 32.1 %all-to-all-done.6.refs_1_.refs_0_ = bf16[8,480,2048]{2,1,0:T(8,128)(2,1)} async-done(((bf16[8,480,2048]{2,1,0:T(8,128)(2,1)}), bf16[8,480,2048]{2,1,0:T(8,128)(2,1)}, u32[]{:S(2)}, u32[]{:S(2)}) %all-to-all-start.6) | async-done | bytes 15728672 | tf_op jit(solution)/shard_map/all_to_all | solution.py:884
  1080.7 22.5 %convolution_convert_fusion.refs_4_ = bf16[3840,2048]{1,0:T(8,128)(2,1)} fusion(bf16[3840,1024]{1,0:T(8,128)(2,1)} %get-tuple-element.35.refs_1_, bf16[256,2048]{1,0:T(8,128)(2,1)} %get-tuple-element.183, bf16[256,2048]{1,0:T(8,128)(2,1)} %get-tuple-element.184, bf16[256,2048]{1,0:T(8,128)(2,1)} %get-tuple-element.185, bf16[256,2048]{1,0:T(8,128)(2,1)} %get-tuple-element.182), kind=kOutput, calls=%fused_computation.6 | convolution fusion | flops 16130768896 | bytes 27787264 | tf_op jit(solution)/shard_map/dot_general | solution.py:704
  1135.8 94.9 %reduce-scatter.4.cloned.1.call-done = bf16[384,2048]{1,0:T(8,128)(2,1)} async-done(((bf16[1536,2048]{1,0:T(8,128)(2,1)}), bf16[384,2048]{1,0:T(8,128)(2,1)}) %reduce-scatter.4.cloned.1.call-update) | async-done | bytes 1572880 | tf_op jit(solution)/shard_map/reduce_scatter | solution.py:899
  1274.6 22.8 %all-to-all-done.5.refs_0_ = bf16[8,480,2048]{2,1,0:T(8,128)(2,1)} async-done(((bf16[8,480,2048]{2,1,0:T(8,128)(2,1)}), bf16[8,480,2048]{2,1,0:T(8,128)(2,1)}, u32[]{:S(2)}, u32[]{:S(2)}) %all-to-all-start.5) | async-done | bytes 15728672 | tf_op jit(solution)/shard_map/all_to_all | solution.py:896
  1318.7 46.1 %attend_back.1 = (f32[1536,512]{1,0:T(8,128)}, f32[1536,512]{1,0:T(8,128)}, f32[1536,512]{1,0:T(8,128)}) custom-call(s32[1536,1]{1,0:T(8,128)S(1)} %broadcast_in_dim.171.seq_rows, s32[1,1536]{1,0:T(1,128)S(1)} %broadcast_in_dim.146.seq_cols, bf16[1536,512]{1,0:T(8,128)(2,1)S(1)} %copy-done.14, bf16[1536,512]{1,0:T(8,128)(2,1)S(1)} %copy-done.16, ...), custom_call_target="tpu_custom_call" | custom-call | flops 12079595520 | bytes 15728640 | tf_op jit(solution)/shard_map/attend_back/pallas_call | solution.py:440
  1482.9 40.4 %all-to-all-done.9.refs_1_ = bf16[8,4,64,1536]{3,2,1,0:T(8,128)(2,1)} async-done(((bf16[8,4,64,1536]{3,2,1,0:T(8,128)(2,1)}), bf16[8,4,64,1536]{3,2,1,0:T(8,128)(2,1)}, u32[]{:S(2)}, u32[]{:S(2)}) %all-to-all-start.9) | async-done | bytes 6291488 | tf_op jit(solution)/shard_map/all_to_all | solution.py:961
  1554.3 24.0 %all-to-all-done.11 = bf16[4,64,1536]{2,1,0:T(8,128)(2,1)S(1)} async-done(((bf16[4,64,1536]{2,1,0:T(8,128)(2,1)}), bf16[4,64,1536]{2,1,0:T(8,128)(2,1)S(1)}, u32[]{:S(2)}, u32[]{:S(2)}) %all-to-all-start.11) | async-done | bytes 786464 | tf_op jit(solution)/shard_map/all_to_all | solution.py:965
  (502 shorter events, 571.8 us)
Async XLA Ops:
  27.7 159.9 %all-gather.4.cloned.1.call-start = ((), (), s32[]{:S(2)}) async-start(), calls=%async_computation.15 | async-start | bytes 7864320 | tf_op jit(solution)/shard_map/all_gather | solution.py:760
  77.9 82.3 %all-to-all-start.1 = ((bf16[8,4,64,1664]{3,2,1,0:T(8,128)(2,1)}), bf16[8,4,64,1664]{3,2,1,0:T(8,128)(2,1)}, u32[]{:S(2)}, u32[]{:S(2)}) async-start(bf16[8,4,64,1664]{3,2,1,0:T(8,128)(2,1)} %broadcast_in_dim.153), calls=%async_computation.1 | async-start | bytes 13631488 | tf_op jit(solution)/shard_map/all_to_all | solution.py:766
  82.9 223.8 %all-gather.6.cloned.1.call-start = ((), (), s32[]{:S(2)}) async-start(), calls=%async_computation.16 | async-start | bytes 7864320 | tf_op jit(solution)/shard_map/all_gather | solution.py:799
  193.0 99.2 %all-to-all-start.2 = ((bf16[8,4,64,2048]{3,2,1,0:T(8,128)(2,1)}), bf16[8,4,64,2048]{3,2,1,0:T(8,128)(2,1)}, u32[]{:S(2)}, u32[]{:S(2)}) async-start(bf16[8,4,64,2048]{3,2,1,0:T(8,128)(2,1)} %broadcast_in_dim.157.refs_3_), calls=%async_computation.2 | async-start | bytes 16777216 | tf_op jit(solution)/shard_map/all_to_all | solution.py:802
  320.4 216.5 %all-to-all-start.3 = ((bf16[8,4,120,2048]{3,2,1,0:T(8,128)(2,1)}), bf16[8,4,120,2048]{3,2,1,0:T(8,128)(2,1)}, u32[]{:S(2)}, u32[]{:S(2)}) async-start(bf16[8,4,120,2048]{3,2,1,0:T(8,128)(2,1)} %dispatch.2.refs_1_), calls=%async_computation.3 | async-start | bytes 31457280 | tf_op jit(solution)/shard_map/all_to_all | solution.py:847
  326.0 164.2 %all-gather.8.cloned.1.call-start = ((), (), s32[]{:S(2)}) async-start(), calls=%async_computation.17 | async-start | bytes 7864320 | tf_op jit(solution)/shard_map/all_gather | solution.py:853
  551.4 178.8 %all-to-all-start.4 = ((bf16[8,4,120,2048]{3,2,1,0:T(8,128)(2,1)}), bf16[8,4,120,2048]{3,2,1,0:T(8,128)(2,1)}, u32[]{:S(2)}, u32[]{:S(2)}) async-start(bf16[8,4,120,2048]{3,2,1,0:T(8,128)(2,1)} %dispatch.3), calls=%async_computation.4 | async-start | bytes 31457280 | tf_op jit(solution)/shard_map/all_to_all | solution.py:864
  566.7 108.5 %collective-permute-start.10 = (bf16[512,1024]{1,0:T(8,128)(2,1)}, bf16[512,1024]{1,0:T(8,128)(2,1)S(1)}, u32[]{:S(2)}, u32[]{:S(2)}) collective-permute-start(bf16[512,1024]{1,0:T(8,128)(2,1)} %tie.50), channel_id=1, source_target_pairs={{0,16},{8,24},{16,0},{24,8},{1,17},{9,25},{17,1},{25,9},{2,18},{10... | collective-permute-start | bytes 3145736 | tf_op jit(solution)/shard_map/ppermute | solution.py:773
  583.3 91.8 %collective-permute-start.9 = (bf16[512,1024]{1,0:T(8,128)(2,1)}, bf16[512,1024]{1,0:T(8,128)(2,1)}, u32[]{:S(2)}, u32[]{:S(2)}) collective-permute-start(bf16[512,1024]{1,0:T(8,128)(2,1)} %tie.49), channel_id=1, source_target_pairs={{0,8},{8,0},{16,24},{24,16},{1,9},{9,1},{17,25},{25,17},{2,10},{10... | collective-permute-start | bytes 3145736 | tf_op jit(solution)/shard_map/ppermute | solution.py:773
  676.1 121.2 %collective-permute-start.12 = (bf16[256,2048]{1,0:T(8,128)(2,1)}, bf16[256,2048]{1,0:T(8,128)(2,1)}, u32[]{:S(2)}, u32[]{:S(2)}) collective-permute-start(bf16[256,2048]{1,0:T(8,128)(2,1)} %tie.52), channel_id=1, source_target_pairs={{0,8},{8,0},{16,24},{24,16},{1,9},{9,1},{17,25},{25,17},{2,10},{10... | collective-permute-start | bytes 3145736 | tf_op jit(solution)/shard_map/ppermute | solution.py:773
  697.5 99.8 %collective-permute-start.13 = (bf16[256,2048]{1,0:T(8,128)(2,1)}, bf16[256,2048]{1,0:T(8,128)(2,1)}, u32[]{:S(2)}, u32[]{:S(2)}) collective-permute-start(bf16[256,2048]{1,0:T(8,128)(2,1)} %tie.54), channel_id=1, source_target_pairs={{0,16},{8,24},{16,0},{24,8},{1,17},{9,25},{17,1},{25,9},{2,18},{10... | collective-permute-start | bytes 3145736 | tf_op jit(solution)/shard_map/ppermute | solution.py:773
  698.5 98.8 %collective-permute-start.14 = (bf16[256,2048]{1,0:T(8,128)(2,1)}, bf16[256,2048]{1,0:T(8,128)(2,1)}, u32[]{:S(2)}, u32[]{:S(2)}) collective-permute-start(bf16[256,2048]{1,0:T(8,128)(2,1)} %tie.56), channel_id=1, source_target_pairs={{0,24},{8,16},{16,8},{24,0},{1,25},{9,17},{17,9},{25,1},{2,26},{10... | collective-permute-start | bytes 3145736 | tf_op jit(solution)/shard_map/ppermute | solution.py:773
  809.6 86.4 %collective-permute-start.16 = (bf16[256,2048]{1,0:T(8,128)(2,1)S(1)}, bf16[256,2048]{1,0:T(8,128)(2,1)}, u32[]{:S(2)}, u32[]{:S(2)}) collective-permute-start(bf16[256,2048]{1,0:T(8,128)(2,1)S(1)} %get-tuple-element.164), channel_id=1, source_target_pairs={{0,16},{8,24},{16,0},{24,8},{1,17},{9,25},{17,1},{25,9},{2,18},{10... | collective-permute-start | bytes 3145736 | tf_op jit(solution)/shard_map/ppermute | solution.py:773
  809.6 86.4 %collective-permute-start.15 = (bf16[256,2048]{1,0:T(8,128)(2,1)S(1)}, bf16[256,2048]{1,0:T(8,128)(2,1)}, u32[]{:S(2)}, u32[]{:S(2)}) collective-permute-start(bf16[256,2048]{1,0:T(8,128)(2,1)S(1)} %get-tuple-element.165), channel_id=1, source_target_pairs={{0,8},{8,0},{16,24},{24,16},{1,9},{9,1},{17,25},{25,17},{2,10},{10... | collective-permute-start | bytes 3145736 | tf_op jit(solution)/shard_map/ppermute | solution.py:773
  896.0 178.5 %all-to-all-start.6 = ((bf16[8,480,2048]{2,1,0:T(8,128)(2,1)}), bf16[8,480,2048]{2,1,0:T(8,128)(2,1)}, u32[]{:S(2)}, u32[]{:S(2)}) async-start(bf16[8,480,2048]{2,1,0:T(8,128)(2,1)} %bitcast.292), calls=%async_computation.6 | async-start | bytes 31457280 | tf_op jit(solution)/shard_map/all_to_all | solution.py:884
  926.7 112.7 %collective-permute-start.20 = (bf16[512,1024]{1,0:T(8,128)(2,1)}, bf16[512,1024]{1,0:T(8,128)(2,1)}, u32[]{:S(2)}, u32[]{:S(2)}) collective-permute-start(bf16[512,1024]{1,0:T(8,128)(2,1)} %tie.62), channel_id=1, source_target_pairs={{0,16},{8,24},{16,0},{24,8},{1,17},{9,25},{17,1},{25,9},{2,18},{10... | collective-permute-start | bytes 3145736 | tf_op jit(solution)/shard_map/ppermute | solution.py:773
  926.7 112.7 %collective-permute-start.18 = (bf16[512,1024]{1,0:T(8,128)(2,1)}, bf16[512,1024]{1,0:T(8,128)(2,1)}, u32[]{:S(2)}, u32[]{:S(2)}) collective-permute-start(bf16[512,1024]{1,0:T(8,128)(2,1)} %tie.60), channel_id=1, source_target_pairs={{0,8},{8,0},{16,24},{24,16},{1,9},{9,1},{17,25},{25,17},{2,10},{10... | collective-permute-start | bytes 3145736 | tf_op jit(solution)/shard_map/ppermute | solution.py:773
  954.4 148.8 %collective-permute-start.23 = (bf16[512,1024]{1,0:T(8,128)(2,1)}, bf16[512,1024]{1,0:T(8,128)(2,1)S(1)}, u32[]{:S(2)}, u32[]{:S(2)}) collective-permute-start(bf16[512,1024]{1,0:T(8,128)(2,1)} %tie.65), channel_id=1, source_target_pairs={{0,24},{8,16},{16,8},{24,0},{1,25},{9,17},{17,9},{25,1},{2,26},{10... | collective-permute-start | bytes 3145736 | tf_op jit(solution)/shard_map/ppermute | solution.py:773
  1080.6 150.0 %reduce-scatter.4.cloned.1.call-start = ((), (), s32[]{:S(2)}) async-start(), calls=%async_computation.18 | async-start | bytes 7864320 | tf_op jit(solution)/shard_map/reduce_scatter | solution.py:899
  1118.8 178.5 %all-to-all-start.5 = ((bf16[8,480,2048]{2,1,0:T(8,128)(2,1)}), bf16[8,480,2048]{2,1,0:T(8,128)(2,1)}, u32[]{:S(2)}, u32[]{:S(2)}) async-start(bf16[8,480,2048]{2,1,0:T(8,128)(2,1)} %bitcast.291), calls=%async_computation.5 | async-start | bytes 31457280 | tf_op jit(solution)/shard_map/all_to_all | solution.py:896
  1124.6 321.4 %reduce-scatter.6.cloned.1.call-start = ((), (), s32[]{:S(2)}) async-start(), calls=%async_computation.19 | async-start | bytes 7864320 | tf_op jit(solution)/shard_map/reduce_scatter | solution.py:927
  1309.3 104.0 %all-to-all-start.8 = ((bf16[8,4,64,2048]{3,2,1,0:T(8,128)(2,1)}), bf16[8,4,64,2048]{3,2,1,0:T(8,128)(2,1)}, u32[]{:S(2)}, u32[]{:S(2)}) async-start(bf16[8,4,64,2048]{3,2,1,0:T(8,128)(2,1)} %tie.70), calls=%async_computation.10 | async-start | bytes 16777216 | tf_op jit(solution)/shard_map/all_to_all | solution.py:929
  1314.3 278.5 %reduce-scatter.8.cloned.1.call-start = ((), (), s32[]{:S(2)}) async-start(), calls=%async_computation.20 | async-start | bytes 7864320 | tf_op jit(solution)/shard_map/reduce_scatter | solution.py:952
  1446.9 76.5 %all-to-all-start.9 = ((bf16[8,4,64,1536]{3,2,1,0:T(8,128)(2,1)}), bf16[8,4,64,1536]{3,2,1,0:T(8,128)(2,1)}, u32[]{:S(2)}, u32[]{:S(2)}) async-start(bf16[8,4,64,1536]{3,2,1,0:T(8,128)(2,1)} %bitcast.297), calls=%async_computation.12 | async-start | bytes 12582912 | tf_op jit(solution)/shard_map/all_to_all | solution.py:961
  (121 other events, 1996.2 us)
Sparse Core Ops, SparseCore 0:
  73.1 114.4 all-gather.3
  192.2 114.5 all-gather.5
  368.7 121.5 all-gather.7
  1118.9 111.7 reduce-scatter.3
  1309.4 109.7 reduce-scatter.5
  1447.0 124.6 reduce-scatter.7

commit v8 on v7

--- a/solution.py
+++ b/solution.py
@@ -786,7 +786,7 @@
 
     def exchange_after(parts, earlier):
         came = [
-            swap(part if before is None else tie(part, before), step)
+            swap(tie(part, *before) if before else part, step)
             for step, before in enumerate(earlier, 1)
             for part in [parts[plane ^ step]]
         ]
@@ -879,15 +879,15 @@
     def blocks(matrix):
         return matrix.reshape(planes, matrix.shape[0] // planes, matrix.shape[1])
 
-    came, down_grad = exchange_after(blocks(grad_down_w), [None] * (planes - 1))
-    grad_rows = tie(grad_rows, *came)
+    came, down_grad = exchange_after(blocks(grad_down_w), [()] * (planes - 1))
+    grad_up_w = t_mm(rows_in, grad_up).astype(bf16)
+    grad_rows = tie(grad_rows, *came, grad_up_w)
     grad_rows = lax.all_to_all(
         grad_rows.reshape(columns, planes * capacity, width), "fsdp", 0, 0, tiled=True
     )
     grad_gate_w = t_mm(rows_in, grad_gate).astype(bf16)
-    grad_up_w = t_mm(rows_in, grad_up).astype(bf16)
-    came, up_grad = exchange_after(blocks(grad_up_w), came)
-    came, gate_grad = exchange_after(blocks(grad_gate_w), came)
+    came, up_grad = exchange_after(blocks(grad_up_w), [(part,) for part in came])
+    came, gate_grad = exchange_after(blocks(grad_gate_w), [(part,) for part in came])
     expert_out = mm(act_picked, down).astype(bf16)
     grad_picked = lax.all_to_all(
         tie(grad_picked, grad_rows).reshape(columns, planes, capacity), "fsdp", 0, 0, tiled=True
@@ -944,13 +944,10 @@
         axis=1,
     ).astype(bf16)
     grad_part = mm_t(grad_qkv, packed[:, : 3 * share])
-    grad_out_w = jnp.sum(grad_out_w.astype(f32), axis=0).astype(bf16)
-    came_out = [swap(grad_out_w[plane ^ step], step) for step in steps]
-    grad_out_w = sum(x.astype(f32) for x in [grad_out_w[plane]] + came_out)
     sums = t_mm(h_one, grad_qkv).astype(bf16)
     sums = sums.reshape(planes, columns, strip, -1).transpose(1, 0, 2, 3)
     grad_h_one = lax.psum_scatter(
-        tie(grad_part.astype(bf16), mixed, sums, *came_out), "ctx", scatter_dimension=0, tiled=True
+        tie(grad_part.astype(bf16), mixed, grad_out_w), "ctx", scatter_dimension=0, tiled=True
     ).astype(f32)
     grad_attn_gain = jnp.sum(grad_part * (hidden_wide * scale_one), axis=0)
     rows_of = jnp.arange(planes)[:, None] == plane
@@ -959,7 +956,10 @@
     small = jnp.concatenate([grad_router] + gains, axis=1).reshape(planes, columns, -1)
     small = sum([small[plane]] + [swap(small[plane ^ step], step) for step in steps])
     sums = lax.all_to_all(sums, "fsdp", 0, 0, tiled=True)
-    small = lax.all_to_all(tie(small, sums), "fsdp", 0, 0, tiled=True)
+    grad_out_w = jnp.sum(grad_out_w.astype(f32), axis=0).astype(bf16)
+    came_out = [swap(grad_out_w[plane ^ step], step) for step in steps]
+    grad_out_w = sum(x.astype(f32) for x in [grad_out_w[plane]] + came_out)
+    small = lax.all_to_all(tie(small, sums, *came_out), "fsdp", 0, 0, tiled=True)
     small = jnp.sum(small, axis=0).reshape(strip, -1)
     sums = jnp.sum(sums.astype(f32), axis=0).astype(bf16)
     sums = lax.all_to_all(tie(sums, small), "ctx", 0, 0, tiled=True)

time: 1610 us -> 1610 us (level)
    ppermute x39, waiting for transfers between devices: 305 us -> 287 us  [swap(): return lax.ppermute(part, 'ctx', [(i, i ^ step) for i in range(planes)])]
    all_to_all x1, waiting for transfers between devices: 32.1 us -> 49.9 us  [plane_shards(): lax.all_to_all(grad_rows.reshape(columns, planes * capacity, width), 'fsd...]
    unnamed x184 -> x174, local copies, waits for them, and re-layouts: 41.1 us -> 43.6 us
  transfers between devices with their start and end apart: 57 -> 57, of which waited for: 30 -> 29; matrix products, arithmetic and copies ran while one was open for 20% -> 20% of each run, Pallas kernels for 12% -> 12%
where the time goes in v8:
time: 1610 us
  waiting for transfers between devices  812 us (50%)
  Pallas kernels  220 us (14%)
  matrix products  184 us (11%)
  local copies, waits for them, and re-layouts  142 us (9%)
  starting transfers between devices  137 us (9%)
  other arithmetic  95 us (6%)
    ppermute x39, waiting for transfers between devices, swap(): return lax.ppermute(part, 'ctx', [(i, i ^ step) for i in range(planes)])  287 us
    all_gather x1, waiting for transfers between devices, plane_shards(): h_two_all = lax.all_gather(tie(h_two, grad_send), 'ctx', axis=0, tiled=True)  117 us
    reduce_scatter x1, waiting for transfers between devices, plane_shards(): lax.psum_scatter(combine(grad_rows), 'ctx', scatter_dimension=0, tiled=True)  95.1 us
    dot_general x6, matrix products, t_mm(): lax.dot_general(left, right, (((0,), (0,)), ((), ())), preferred_element_...  87.6 us
    all_to_all x1, waiting for transfers between devices, plane_shards(): packed = lax.all_to_all(packed, 'fsdp', 0, 0, tiled=True)  76 us
    ppermute x39, starting transfers between devices, swap(): return lax.ppermute(part, 'ctx', [(i, i ^ step) for i in range(planes)])  75.4 us
    pallas_call x1, Pallas kernels, expert_back(): pl.pallas_call(expert_back_kernel, grid=(count // block,), in_specs=[wide...  63.4 us
    all_to_all x1, waiting for transfers between devices, plane_shards(): lax.all_to_all(grad_rows.reshape(columns, planes * capacity, width), 'fsd...  49.9 us
  transfers between devices with their start and end apart: 57, of which 29 were waited for; matrix products, arithmetic and copies ran while one was open for 20% of the time, Pallas kernels for 12%

profile of v8, /device:TPU:0, one launch (start us, length us, event | category | flops | bytes accessed | tf_op | source)
XLA Modules:
  0.0 1606.3 jit_solution(10641986708308489559)
XLA Ops:
  28.8 42.8 %all-to-all-done.refs_1_ = bf16[4,64,3712]{2,1,0:T(8,128)(2,1)S(1)} async-done(((bf16[4,64,3712]{2,1,0:T(8,128)(2,1)}), bf16[4,64,3712]{2,1,0:T(8,128)(2,1)S(1)}, u32[]{:S(2)}, u32[]{:S(2)}) %all-to-all-start) | async-done | bytes 1900576 | tf_op jit(solution)/shard_map/all_to_all | solution.py:759
  84.1 76.0 %all-to-all-done.1 = bf16[8,4,64,1664]{3,2,1,0:T(8,128)(2,1)} async-done(((bf16[8,4,64,1664]{3,2,1,0:T(8,128)(2,1)}), bf16[8,4,64,1664]{3,2,1,0:T(8,128)(2,1)}, u32[]{:S(2)}, u32[]{:S(2)}) %all-to-all-start.1) | async-done | bytes 6815776 | tf_op jit(solution)/shard_map/all_to_all | solution.py:766
  166.6 21.0 %all-gather.4.cloned.1.call-done.refs_1_ = bf16[1536,2048]{1,0:T(8,128)(2,1)} async-done(((bf16[384,2048]{1,0:T(8,128)(2,1)}), bf16[1536,2048]{1,0:T(8,128)(2,1)}) %all-gather.4.cloned.1.call-update) | async-done | bytes 6291472 | tf_op jit(solution)/shard_map/all_gather | solution.py:760
  215.7 16.0 fusion.34.raw
  247.6 28.0 %attend.1.refs_1_ = bf16[1536,512]{1,0:T(8,128)(2,1)S(1)} custom-call(s32[1536,1]{1,0:T(8,128)S(1)} %broadcast_in_dim.171.seq_rows, s32[1,1536]{1,0:T(1,128)S(1)} %broadcast_in_dim.146.seq_cols, bf16[1536,512]{1,0:T(8,128)(2,1)S(1)} %get-tuple-element.32.query, bf16[1536,512]{1,0:T(8,128)(2,1)S(1)} %get-tuple-element.33.key, bf16[1536,512]{1,0:T(8,128)(2,1)} %copy-done.17), custom_call_target="tpu_custom_call" | custom-call | flops 4831838208 | bytes 6291456 | tf_op jit(solution)/shard_map/attend/pallas_call | solution.py:421
  372.9 117.4 %all-gather.8.cloned.1.call-done.refs_1_.refs_0_ = bf16[1536,2048]{1,0:T(8,128)(2,1)} async-done(((bf16[384,2048]{1,0:T(8,128)(2,1)}), bf16[1536,2048]{1,0:T(8,128)(2,1)}) %all-gather.8.cloned.1.call-update) | async-done | bytes 6291472 | tf_op jit(solution)/shard_map/all_gather | solution.py:853
  491.0 45.9 %collective-permute-done.6.refs_2_.refs_1_ = bf16[512,1024]{1,0:T(8,128)(2,1)S(1)} collective-permute-done((bf16[512,1024]{1,0:T(8,128)(2,1)}, bf16[512,1024]{1,0:T(8,128)(2,1)S(1)}, u32[]{:S(2)}, u32[]{:S(2)}) %collective-permute-start.6) | collective-permute-done | bytes 1048608 | tf_op jit(solution)/shard_map/ppermute | solution.py:773
  583.7 23.0 %collective-permute-done.8.refs_1_ = bf16[512,1024]{1,0:T(8,128)(2,1)} collective-permute-done((bf16[512,1024]{1,0:T(8,128)(2,1)}, bf16[512,1024]{1,0:T(8,128)(2,1)}, u32[]{:S(2)}, u32[]{:S(2)}) %collective-permute-start.8) | collective-permute-done | bytes 1048608 | tf_op jit(solution)/shard_map/ppermute | solution.py:773
  615.8 59.1 %collective-permute-done.10.refs_2_ = bf16[512,1024]{1,0:T(8,128)(2,1)S(1)} collective-permute-done((bf16[512,1024]{1,0:T(8,128)(2,1)}, bf16[512,1024]{1,0:T(8,128)(2,1)S(1)}, u32[]{:S(2)}, u32[]{:S(2)}) %collective-permute-start.10) | collective-permute-done | bytes 1048608 | tf_op jit(solution)/shard_map/ppermute | solution.py:773
  675.9 21.4 %collective-permute-start.12 = (bf16[256,2048]{1,0:T(8,128)(2,1)}, bf16[256,2048]{1,0:T(8,128)(2,1)}, u32[]{:S(2)}, u32[]{:S(2)}) collective-permute-start(bf16[256,2048]{1,0:T(8,128)(2,1)} %tie.52), channel_id=1, source_target_pairs={{0,8},{8,0},{16,24},{24,16},{1,9},{9,1},{17,25},{25,17},{2,10},{10... | collective-permute-start | bytes 3145736 | tf_op jit(solution)/shard_map/ppermute | solution.py:773
  704.6 25.4 %all-to-all-done.4 = bf16[8,4,120,2048]{3,2,1,0:T(8,128)(2,1)} async-done(((bf16[8,4,120,2048]{3,2,1,0:T(8,128)(2,1)}), bf16[8,4,120,2048]{3,2,1,0:T(8,128)(2,1)}, u32[]{:S(2)}, u32[]{:S(2)}) %all-to-all-start.4) | async-done | bytes 15728672 | tf_op jit(solution)/shard_map/all_to_all | solution.py:864
  730.0 44.6 %expert_in.1 = (f32[3840,1024]{1,0:T(8,128)}, f32[3840,1024]{1,0:T(8,128)}, bf16[3840,1024]{1,0:T(8,128)(2,1)}, f32[3840,1]{1,0:T(8,128)}) custom-call(bf16[3840,2048]{1,0:T(8,128)(2,1)} %bitcast.37.rows, bf16[2048,1024]{1,0:T(8,128)(2,1)} %pad_maximum_fusion.2.gate, bf16[2048,1024]{1,0:T(8,128)(2,1)} %pad_maximum_fusion.4.up, ...), custom_call_target="tpu_custom_call" | custom-call | flops 32212254720 | bytes 63438848 | tf_op jit(solution)/shard_map/expert_in/pallas_call | solution.py:638
  774.5 22.5 %convolution_convert_fusion.5.refs_1_ = bf16[1024,2048]{1,0:T(8,128)(2,1)} fusion(bf16[3840,1024]{1,0:T(8,128)(2,1)} %get-tuple-element.35.refs_1_, bf16[3840,2048]{1,0:T(8,128)(2,1)} %bitcast.34.refs_1_.grad), kind=kOutput, calls=%fused_computation.40 | convolution fusion | flops 16108224512 | bytes 27787264 | tf_op jit(solution)/shard_map/dot_general | solution.py:714
  813.7 63.4 %expert_back.1 = (bf16[3840,1024]{1,0:T(8,128)(2,1)}, bf16[3840,1024]{1,0:T(8,128)(2,1)}, f32[3840,1]{1,0:T(8,128)}, bf16[3840,2048]{1,0:T(8,128)(2,1)}) custom-call(bf16[3840,2048]{1,0:T(8,128)(2,1)} %bitcast.34.refs_1_.grad, f32[3840,1024]{1,0:T(8,128)} %tie.58.gate_in, f32[3840,1024]{1,0:T(8,128)} %get-tuple-element.37.up_in, ...), custom_call_target="tpu_custom_call" | custom-call | flops 48318382080 | bytes 91226112 | tf_op jit(solution)/shard_map/expert_back/pallas_call | solution.py:670
  877.1 22.4 %convolution_convert_fusion.4.refs_4_ = bf16[2048,1024]{1,0:T(8,128)(2,1)} fusion(bf16[3840,2048]{1,0:T(8,128)(2,1)} %bitcast.37.rows, bf16[3840,1024]{1,0:T(8,128)(2,1)} %get-tuple-element.40), kind=kOutput, calls=%fused_computation.39 | convolution fusion | flops 16108224512 | bytes 27787264 | tf_op jit(solution)/shard_map/dot_general | solution.py:714
  915.3 21.4 %convolution_convert_fusion.3 = bf16[2048,1024]{1,0:T(8,128)(2,1)S(1)} fusion(bf16[3840,2048]{1,0:T(8,128)(2,1)} %bitcast.37.rows, bf16[3840,1024]{1,0:T(8,128)(2,1)} %get-tuple-element.41), kind=kOutput, calls=%fused_computation.38 | convolution fusion | flops 16108224512 | bytes 27787264 | tf_op jit(solution)/shard_map/dot_general | solution.py:714
  942.4 84.2 %collective-permute-done.20.refs_1_ = bf16[512,1024]{1,0:T(8,128)(2,1)} collective-permute-done((bf16[512,1024]{1,0:T(8,128)(2,1)}, bf16[512,1024]{1,0:T(8,128)(2,1)}, u32[]{:S(2)}, u32[]{:S(2)}) %collective-permute-start.20) | collective-permute-done | bytes 1048608 | tf_op jit(solution)/shard_map/ppermute | solution.py:773
  1029.5 49.9 %all-to-all-done.6.refs_1_.refs_0_ = bf16[8,480,2048]{2,1,0:T(8,128)(2,1)} async-done(((bf16[8,480,2048]{2,1,0:T(8,128)(2,1)}), bf16[8,480,2048]{2,1,0:T(8,128)(2,1)}, u32[]{:S(2)}, u32[]{:S(2)}) %all-to-all-start.6) | async-done | bytes 15728672 | tf_op jit(solution)/shard_map/all_to_all | solution.py:885
  1085.6 22.1 %convolution_convert_fusion.refs_4_ = bf16[3840,2048]{1,0:T(8,128)(2,1)} fusion(bf16[3840,1024]{1,0:T(8,128)(2,1)} %get-tuple-element.35.refs_1_, bf16[256,2048]{1,0:T(8,128)(2,1)} %get-tuple-element.183, bf16[256,2048]{1,0:T(8,128)(2,1)} %get-tuple-element.184, bf16[256,2048]{1,0:T(8,128)(2,1)} %get-tuple-element.185, bf16[256,2048]{1,0:T(8,128)(2,1)} %get-tuple-element.182), kind=kOutput, calls=%fused_computation.6 | convolution fusion | flops 16130768896 | bytes 27787264 | tf_op jit(solution)/shard_map/dot_general | solution.py:704
  1138.3 95.1 %reduce-scatter.4.cloned.1.call-done = bf16[384,2048]{1,0:T(8,128)(2,1)} async-done(((bf16[1536,2048]{1,0:T(8,128)(2,1)}), bf16[384,2048]{1,0:T(8,128)(2,1)}) %reduce-scatter.4.cloned.1.call-update) | async-done | bytes 1572880 | tf_op jit(solution)/shard_map/reduce_scatter | solution.py:899
  1277.2 22.6 %all-to-all-done.5.refs_0_ = bf16[8,480,2048]{2,1,0:T(8,128)(2,1)} async-done(((bf16[8,480,2048]{2,1,0:T(8,128)(2,1)}), bf16[8,480,2048]{2,1,0:T(8,128)(2,1)}, u32[]{:S(2)}, u32[]{:S(2)}) %all-to-all-start.5) | async-done | bytes 15728672 | tf_op jit(solution)/shard_map/all_to_all | solution.py:896
  1321.4 45.9 %attend_back.1 = (f32[1536,512]{1,0:T(8,128)}, f32[1536,512]{1,0:T(8,128)}, f32[1536,512]{1,0:T(8,128)}) custom-call(s32[1536,1]{1,0:T(8,128)S(1)} %broadcast_in_dim.171.seq_rows, s32[1,1536]{1,0:T(1,128)S(1)} %broadcast_in_dim.146.seq_cols, bf16[1536,512]{1,0:T(8,128)(2,1)S(1)} %copy-done.14, bf16[1536,512]{1,0:T(8,128)(2,1)S(1)} %copy-done.16, ...), custom_call_target="tpu_custom_call" | custom-call | flops 12079595520 | bytes 15728640 | tf_op jit(solution)/shard_map/attend_back/pallas_call | solution.py:440
  1483.1 33.2 %all-to-all-done.9.refs_1_ = bf16[8,4,64,1536]{3,2,1,0:T(8,128)(2,1)} async-done(((bf16[8,4,64,1536]{3,2,1,0:T(8,128)(2,1)}), bf16[8,4,64,1536]{3,2,1,0:T(8,128)(2,1)}, u32[]{:S(2)}, u32[]{:S(2)}) %all-to-all-start.9) | async-done | bytes 6291488 | tf_op jit(solution)/shard_map/all_to_all | solution.py:958
  1561.1 19.0 %all-to-all-done.11 = bf16[4,64,1536]{2,1,0:T(8,128)(2,1)S(1)} async-done(((bf16[4,64,1536]{2,1,0:T(8,128)(2,1)}), bf16[4,64,1536]{2,1,0:T(8,128)(2,1)S(1)}, u32[]{:S(2)}, u32[]{:S(2)}) %all-to-all-start.11) | async-done | bytes 786464 | tf_op jit(solution)/shard_map/all_to_all | solution.py:965
  (491 shorter events, 568.1 us)
Async XLA Ops:
  27.7 159.9 %all-gather.4.cloned.1.call-start = ((), (), s32[]{:S(2)}) async-start(), calls=%async_computation.15 | async-start | bytes 7864320 | tf_op jit(solution)/shard_map/all_gather | solution.py:760
  77.9 82.3 %all-to-all-start.1 = ((bf16[8,4,64,1664]{3,2,1,0:T(8,128)(2,1)}), bf16[8,4,64,1664]{3,2,1,0:T(8,128)(2,1)}, u32[]{:S(2)}, u32[]{:S(2)}) async-start(bf16[8,4,64,1664]{3,2,1,0:T(8,128)(2,1)} %broadcast_in_dim.153), calls=%async_computation.1 | async-start | bytes 13631488 | tf_op jit(solution)/shard_map/all_to_all | solution.py:766
  82.9 223.8 %all-gather.6.cloned.1.call-start = ((), (), s32[]{:S(2)}) async-start(), calls=%async_computation.16 | async-start | bytes 7864320 | tf_op jit(solution)/shard_map/all_gather | solution.py:799
  193.0 99.2 %all-to-all-start.2 = ((bf16[8,4,64,2048]{3,2,1,0:T(8,128)(2,1)}), bf16[8,4,64,2048]{3,2,1,0:T(8,128)(2,1)}, u32[]{:S(2)}, u32[]{:S(2)}) async-start(bf16[8,4,64,2048]{3,2,1,0:T(8,128)(2,1)} %broadcast_in_dim.157.refs_3_), calls=%async_computation.2 | async-start | bytes 16777216 | tf_op jit(solution)/shard_map/all_to_all | solution.py:802
  320.4 216.5 %all-to-all-start.3 = ((bf16[8,4,120,2048]{3,2,1,0:T(8,128)(2,1)}), bf16[8,4,120,2048]{3,2,1,0:T(8,128)(2,1)}, u32[]{:S(2)}, u32[]{:S(2)}) async-start(bf16[8,4,120,2048]{3,2,1,0:T(8,128)(2,1)} %dispatch.2.refs_1_), calls=%async_computation.3 | async-start | bytes 31457280 | tf_op jit(solution)/shard_map/all_to_all | solution.py:847
  326.1 164.3 %all-gather.8.cloned.1.call-start = ((), (), s32[]{:S(2)}) async-start(), calls=%async_computation.17 | async-start | bytes 7864320 | tf_op jit(solution)/shard_map/all_gather | solution.py:853
  551.5 178.5 %all-to-all-start.4 = ((bf16[8,4,120,2048]{3,2,1,0:T(8,128)(2,1)}), bf16[8,4,120,2048]{3,2,1,0:T(8,128)(2,1)}, u32[]{:S(2)}, u32[]{:S(2)}) async-start(bf16[8,4,120,2048]{3,2,1,0:T(8,128)(2,1)} %dispatch.3), calls=%async_computation.4 | async-start | bytes 31457280 | tf_op jit(solution)/shard_map/all_to_all | solution.py:864
  566.5 108.4 %collective-permute-start.10 = (bf16[512,1024]{1,0:T(8,128)(2,1)}, bf16[512,1024]{1,0:T(8,128)(2,1)S(1)}, u32[]{:S(2)}, u32[]{:S(2)}) collective-permute-start(bf16[512,1024]{1,0:T(8,128)(2,1)} %tie.50), channel_id=1, source_target_pairs={{0,16},{8,24},{16,0},{24,8},{1,17},{9,25},{17,1},{25,9},{2,18},{10... | collective-permute-start | bytes 3145736 | tf_op jit(solution)/shard_map/ppermute | solution.py:773
  583.1 91.8 %collective-permute-start.9 = (bf16[512,1024]{1,0:T(8,128)(2,1)}, bf16[512,1024]{1,0:T(8,128)(2,1)}, u32[]{:S(2)}, u32[]{:S(2)}) collective-permute-start(bf16[512,1024]{1,0:T(8,128)(2,1)} %tie.49), channel_id=1, source_target_pairs={{0,8},{8,0},{16,24},{24,16},{1,9},{9,1},{17,25},{25,17},{2,10},{10... | collective-permute-start | bytes 3145736 | tf_op jit(solution)/shard_map/ppermute | solution.py:773
  675.9 121.1 %collective-permute-start.12 = (bf16[256,2048]{1,0:T(8,128)(2,1)}, bf16[256,2048]{1,0:T(8,128)(2,1)}, u32[]{:S(2)}, u32[]{:S(2)}) collective-permute-start(bf16[256,2048]{1,0:T(8,128)(2,1)} %tie.52), channel_id=1, source_target_pairs={{0,8},{8,0},{16,24},{24,16},{1,9},{9,1},{17,25},{25,17},{2,10},{10... | collective-permute-start | bytes 3145736 | tf_op jit(solution)/shard_map/ppermute | solution.py:773
  697.3 99.7 %collective-permute-start.13 = (bf16[256,2048]{1,0:T(8,128)(2,1)}, bf16[256,2048]{1,0:T(8,128)(2,1)}, u32[]{:S(2)}, u32[]{:S(2)}) collective-permute-start(bf16[256,2048]{1,0:T(8,128)(2,1)} %tie.54), channel_id=1, source_target_pairs={{0,16},{8,24},{16,0},{24,8},{1,17},{9,25},{17,1},{25,9},{2,18},{10... | collective-permute-start | bytes 3145736 | tf_op jit(solution)/shard_map/ppermute | solution.py:773
  698.3 98.7 %collective-permute-start.14 = (bf16[256,2048]{1,0:T(8,128)(2,1)}, bf16[256,2048]{1,0:T(8,128)(2,1)}, u32[]{:S(2)}, u32[]{:S(2)}) collective-permute-start(bf16[256,2048]{1,0:T(8,128)(2,1)} %tie.56), channel_id=1, source_target_pairs={{0,24},{8,16},{16,8},{24,0},{1,25},{9,17},{17,9},{25,1},{2,26},{10... | collective-permute-start | bytes 3145736 | tf_op jit(solution)/shard_map/ppermute | solution.py:773
  806.9 92.6 %collective-permute-start.17 = (bf16[256,2048]{1,0:T(8,128)(2,1)}, bf16[256,2048]{1,0:T(8,128)(2,1)S(1)}, u32[]{:S(2)}, u32[]{:S(2)}) collective-permute-start(bf16[256,2048]{1,0:T(8,128)(2,1)} %get-tuple-element.163), channel_id=1, source_target_pairs={{0,24},{8,16},{16,8},{24,0},{1,25},{9,17},{17,9},{25,1},{2,26},{10... | collective-permute-start | bytes 3145736 | tf_op jit(solution)/shard_map/ppermute | solution.py:773
  809.3 90.2 %collective-permute-start.16 = (bf16[256,2048]{1,0:T(8,128)(2,1)S(1)}, bf16[256,2048]{1,0:T(8,128)(2,1)}, u32[]{:S(2)}, u32[]{:S(2)}) collective-permute-start(bf16[256,2048]{1,0:T(8,128)(2,1)S(1)} %get-tuple-element.164), channel_id=1, source_target_pairs={{0,16},{8,24},{16,0},{24,8},{1,17},{9,25},{17,1},{25,9},{2,18},{10... | collective-permute-start | bytes 3145736 | tf_op jit(solution)/shard_map/ppermute | solution.py:773
  809.3 90.2 %collective-permute-start.15 = (bf16[256,2048]{1,0:T(8,128)(2,1)S(1)}, bf16[256,2048]{1,0:T(8,128)(2,1)}, u32[]{:S(2)}, u32[]{:S(2)}) collective-permute-start(bf16[256,2048]{1,0:T(8,128)(2,1)S(1)} %get-tuple-element.165), channel_id=1, source_target_pairs={{0,8},{8,0},{16,24},{24,16},{1,9},{9,1},{17,25},{25,17},{2,10},{10... | collective-permute-start | bytes 3145736 | tf_op jit(solution)/shard_map/ppermute | solution.py:773
  900.5 178.9 %all-to-all-start.6 = ((bf16[8,480,2048]{2,1,0:T(8,128)(2,1)}), bf16[8,480,2048]{2,1,0:T(8,128)(2,1)}, u32[]{:S(2)}, u32[]{:S(2)}) async-start(bf16[8,480,2048]{2,1,0:T(8,128)(2,1)} %bitcast.291), calls=%async_computation.6 | async-start | bytes 31457280 | tf_op jit(solution)/shard_map/all_to_all | solution.py:885
  913.3 113.2 %collective-permute-start.20 = (bf16[512,1024]{1,0:T(8,128)(2,1)}, bf16[512,1024]{1,0:T(8,128)(2,1)}, u32[]{:S(2)}, u32[]{:S(2)}) collective-permute-start(bf16[512,1024]{1,0:T(8,128)(2,1)} %tie.62), channel_id=1, source_target_pairs={{0,16},{8,24},{16,0},{24,8},{1,17},{9,25},{17,1},{25,9},{2,18},{10... | collective-permute-start | bytes 3145736 | tf_op jit(solution)/shard_map/ppermute | solution.py:773
  913.3 113.2 %collective-permute-start.18 = (bf16[512,1024]{1,0:T(8,128)(2,1)}, bf16[512,1024]{1,0:T(8,128)(2,1)}, u32[]{:S(2)}, u32[]{:S(2)}) collective-permute-start(bf16[512,1024]{1,0:T(8,128)(2,1)} %tie.60), channel_id=1, source_target_pairs={{0,8},{8,0},{16,24},{24,16},{1,9},{9,1},{17,25},{25,17},{2,10},{10... | collective-permute-start | bytes 3145736 | tf_op jit(solution)/shard_map/ppermute | solution.py:773
  940.0 167.7 %collective-permute-start.23 = (bf16[512,1024]{1,0:T(8,128)(2,1)}, bf16[512,1024]{1,0:T(8,128)(2,1)S(1)}, u32[]{:S(2)}, u32[]{:S(2)}) collective-permute-start(bf16[512,1024]{1,0:T(8,128)(2,1)} %tie.65), channel_id=1, source_target_pairs={{0,24},{8,16},{16,8},{24,0},{1,25},{9,17},{17,9},{25,1},{2,26},{10... | collective-permute-start | bytes 3145736 | tf_op jit(solution)/shard_map/ppermute | solution.py:773
  1085.6 147.8 %reduce-scatter.4.cloned.1.call-start = ((), (), s32[]{:S(2)}) async-start(), calls=%async_computation.18 | async-start | bytes 7864320 | tf_op jit(solution)/shard_map/reduce_scatter | solution.py:899
  1121.3 178.5 %all-to-all-start.5 = ((bf16[8,480,2048]{2,1,0:T(8,128)(2,1)}), bf16[8,480,2048]{2,1,0:T(8,128)(2,1)}, u32[]{:S(2)}, u32[]{:S(2)}) async-start(bf16[8,480,2048]{2,1,0:T(8,128)(2,1)} %bitcast.292), calls=%async_computation.5 | async-start | bytes 31457280 | tf_op jit(solution)/shard_map/all_to_all | solution.py:896
  1127.1 294.7 %reduce-scatter.6.cloned.1.call-start = ((), (), s32[]{:S(2)}) async-start(), calls=%async_computation.19 | async-start | bytes 7864320 | tf_op jit(solution)/shard_map/reduce_scatter | solution.py:927
  1311.9 105.1 %all-to-all-start.8 = ((bf16[8,4,64,2048]{3,2,1,0:T(8,128)(2,1)}), bf16[8,4,64,2048]{3,2,1,0:T(8,128)(2,1)}, u32[]{:S(2)}, u32[]{:S(2)}) async-start(bf16[8,4,64,2048]{3,2,1,0:T(8,128)(2,1)} %tie.70), calls=%async_computation.10 | async-start | bytes 16777216 | tf_op jit(solution)/shard_map/all_to_all | solution.py:929
  1316.9 275.9 %reduce-scatter.8.cloned.1.call-start = ((), (), s32[]{:S(2)}) async-start(), calls=%async_computation.20 | async-start | bytes 7864320 | tf_op jit(solution)/shard_map/reduce_scatter | solution.py:949
  (116 other events, 2043.2 us)
Sparse Core Ops, SparseCore 0:
  73.1 114.4 all-gather.3
  192.2 114.5 all-gather.5
  368.8 121.5 all-gather.7
  1121.4 111.9 reduce-scatter.3
  1312.0 109.7 reduce-scatter.5
  1424.0 133.4 reduce-scatter.7

commit v9 on v8

--- a/solution.py
+++ b/solution.py
@@ -887,8 +887,9 @@
     )
     grad_gate_w = t_mm(rows_in, grad_gate).astype(bf16)
     came, up_grad = exchange_after(blocks(grad_up_w), [(part,) for part in came])
-    came, gate_grad = exchange_after(blocks(grad_gate_w), [(part,) for part in came])
-    expert_out = mm(act_picked, down).astype(bf16)
+    expert_out = mm(tie(act_picked, came[-1]), down).astype(bf16)
+    earlier = [(came[0], expert_out)] + [(part,) for part in came[1:]]
+    came, gate_grad = exchange_after(blocks(grad_gate_w), earlier)
     grad_picked = lax.all_to_all(
         tie(grad_picked, grad_rows).reshape(columns, planes, capacity), "fsdp", 0, 0, tiled=True
     )

time: 1610 us -> 1600 us (level)
  waiting for transfers between devices: 812 us -> 766 us
  starting transfers between devices: 137 us -> 171 us
    ppermute x39, waiting for transfers between devices: 287 us -> 231 us  [swap(): return lax.ppermute(part, 'ctx', [(i, i ^ step) for i in range(planes)])]
    all_to_all x1, waiting for transfers between devices: 49.9 us -> 73.2 us  [plane_shards(): lax.all_to_all(grad_rows.reshape(columns, planes * capacity, width), 'fsd...]
    ppermute x39, starting transfers between devices: 75.4 us -> 97.5 us  [swap(): return lax.ppermute(part, 'ctx', [(i, i ^ step) for i in range(planes)])]
    unnamed x174 -> x176, local copies, waits for them, and re-layouts: 43.6 us -> 42.4 us
  transfers between devices with their start and end apart: 57 -> 57, of which waited for: 29 -> 31; matrix products, arithmetic and copies ran while one was open for 20% -> 21% of each run, Pallas kernels for 12% -> 12%
where the time goes in v9:
time: 1600 us; the launch traced here: 1590 us
  waiting for transfers between devices  766 us (48%)
  Pallas kernels  220 us (14%)
  matrix products  184 us (12%)
  starting transfers between devices  171 us (11%)
  local copies, waits for them, and re-layouts  140 us (9%)
  other arithmetic  95.1 us (6%)
    ppermute x39, waiting for transfers between devices, swap(): return lax.ppermute(part, 'ctx', [(i, i ^ step) for i in range(planes)])  231 us
    all_gather x1, waiting for transfers between devices, plane_shards(): h_two_all = lax.all_gather(tie(h_two, grad_send), 'ctx', axis=0, tiled=True)  112 us
    ppermute x39, starting transfers between devices, swap(): return lax.ppermute(part, 'ctx', [(i, i ^ step) for i in range(planes)])  97.5 us
    reduce_scatter x1, waiting for transfers between devices, plane_shards(): lax.psum_scatter(combine(grad_rows), 'ctx', scatter_dimension=0, tiled=True)  94.3 us
    dot_general x6, matrix products, t_mm(): lax.dot_general(left, right, (((0,), (0,)), ((), ())), preferred_element_...  87.7 us
    all_to_all x1, waiting for transfers between devices, plane_shards(): packed = lax.all_to_all(packed, 'fsdp', 0, 0, tiled=True)  76 us
    all_to_all x1, waiting for transfers between devices, plane_shards(): lax.all_to_all(grad_rows.reshape(columns, planes * capacity, width), 'fsd...  73.2 us
    pallas_call x1, Pallas kernels, expert_back(): pl.pallas_call(expert_back_kernel, grid=(count // block,), in_specs=[wide...  63.4 us
  transfers between devices with their start and end apart: 57, of which 31 were waited for; matrix products, arithmetic and copies ran while one was open for 21% of the time, Pallas kernels for 12%

profile of v9, /device:TPU:0, one launch (start us, length us, event | category | flops | bytes accessed | tf_op | source)
XLA Modules:
  0.0 1592.2 jit_solution(2773237703004174193)
XLA Ops:
  28.8 42.8 %all-to-all-done.refs_1_ = bf16[4,64,3712]{2,1,0:T(8,128)(2,1)S(1)} async-done(((bf16[4,64,3712]{2,1,0:T(8,128)(2,1)}), bf16[4,64,3712]{2,1,0:T(8,128)(2,1)S(1)}, u32[]{:S(2)}, u32[]{:S(2)}) %all-to-all-start) | async-done | bytes 1900576 | tf_op jit(solution)/shard_map/all_to_all | solution.py:759
  84.1 76.0 %all-to-all-done.1 = bf16[8,4,64,1664]{3,2,1,0:T(8,128)(2,1)} async-done(((bf16[8,4,64,1664]{3,2,1,0:T(8,128)(2,1)}), bf16[8,4,64,1664]{3,2,1,0:T(8,128)(2,1)}, u32[]{:S(2)}, u32[]{:S(2)}) %all-to-all-start.1) | async-done | bytes 6815776 | tf_op jit(solution)/shard_map/all_to_all | solution.py:766
  166.6 21.0 %all-gather.4.cloned.1.call-done.refs_1_ = bf16[1536,2048]{1,0:T(8,128)(2,1)} async-done(((bf16[384,2048]{1,0:T(8,128)(2,1)}), bf16[1536,2048]{1,0:T(8,128)(2,1)}) %all-gather.4.cloned.1.call-update) | async-done | bytes 6291472 | tf_op jit(solution)/shard_map/all_gather | solution.py:760
  251.4 27.7 %attend.1.refs_1_ = bf16[1536,512]{1,0:T(8,128)(2,1)S(1)} custom-call(s32[1536,1]{1,0:T(8,128)S(1)} %broadcast_in_dim.171.seq_rows, s32[1,1536]{1,0:T(1,128)S(1)} %broadcast_in_dim.146.seq_cols, bf16[1536,512]{1,0:T(8,128)(2,1)S(1)} %get-tuple-element.32.query, bf16[1536,512]{1,0:T(8,128)(2,1)S(1)} %get-tuple-element.33.key, bf16[1536,512]{1,0:T(8,128)(2,1)} %copy-done.17), custom_call_target="tpu_custom_call" | custom-call | flops 4831838208 | bytes 6291456 | tf_op jit(solution)/shard_map/attend/pallas_call | solution.py:421
  340.3 21.3 %collective-permute-done.4 = bf16[384,512]{1,0:T(8,128)(2,1)S(1)} collective-permute-done((bf16[384,512]{1,0:T(8,128)(2,1)}, bf16[384,512]{1,0:T(8,128)(2,1)S(1)}, u32[]{:S(2)}, u32[]{:S(2)}) %collective-permute-start.4) | collective-permute-done | bytes 393248 | tf_op jit(solution)/shard_map/ppermute | solution.py:773
  378.1 111.7 %all-gather.8.cloned.1.call-done.refs_1_.refs_0_ = bf16[1536,2048]{1,0:T(8,128)(2,1)} async-done(((bf16[384,2048]{1,0:T(8,128)(2,1)}), bf16[1536,2048]{1,0:T(8,128)(2,1)}) %all-gather.8.cloned.1.call-update) | async-done | bytes 6291472 | tf_op jit(solution)/shard_map/all_gather | solution.py:853
  490.5 45.9 %collective-permute-done.6.refs_2_.refs_1_ = bf16[512,1024]{1,0:T(8,128)(2,1)S(1)} collective-permute-done((bf16[512,1024]{1,0:T(8,128)(2,1)}, bf16[512,1024]{1,0:T(8,128)(2,1)S(1)}, u32[]{:S(2)}, u32[]{:S(2)}) %collective-permute-start.6) | collective-permute-done | bytes 1048608 | tf_op jit(solution)/shard_map/ppermute | solution.py:773
  565.9 18.9 %collective-permute-done.8.refs_1_ = bf16[512,1024]{1,0:T(8,128)(2,1)S(1)} collective-permute-done((bf16[512,1024]{1,0:T(8,128)(2,1)}, bf16[512,1024]{1,0:T(8,128)(2,1)S(1)}, u32[]{:S(2)}, u32[]{:S(2)}) %collective-permute-start.8) | collective-permute-done | bytes 1048608 | tf_op jit(solution)/shard_map/ppermute | solution.py:773
  588.2 18.9 %collective-permute-start.10 = (bf16[512,1024]{1,0:T(8,128)(2,1)}, bf16[512,1024]{1,0:T(8,128)(2,1)}, u32[]{:S(2)}, u32[]{:S(2)}) collective-permute-start(bf16[512,1024]{1,0:T(8,128)(2,1)} %tie.51), channel_id=1, source_target_pairs={{0,16},{8,24},{16,0},{24,8},{1,17},{9,25},{17,1},{25,9},{2,18},{10... | collective-permute-start | bytes 3145736 | tf_op jit(solution)/shard_map/ppermute | solution.py:773
  629.9 66.9 %collective-permute-done.10.refs_2_ = bf16[512,1024]{1,0:T(8,128)(2,1)} collective-permute-done((bf16[512,1024]{1,0:T(8,128)(2,1)}, bf16[512,1024]{1,0:T(8,128)(2,1)}, u32[]{:S(2)}, u32[]{:S(2)}) %collective-permute-start.10) | collective-permute-done | bytes 1048608 | tf_op jit(solution)/shard_map/ppermute | solution.py:773
  706.1 23.3 %all-to-all-done.4 = bf16[8,4,120,2048]{3,2,1,0:T(8,128)(2,1)} async-done(((bf16[8,4,120,2048]{3,2,1,0:T(8,128)(2,1)}), bf16[8,4,120,2048]{3,2,1,0:T(8,128)(2,1)}, u32[]{:S(2)}, u32[]{:S(2)}) %all-to-all-start.4) | async-done | bytes 15728672 | tf_op jit(solution)/shard_map/all_to_all | solution.py:864
  729.4 44.6 %expert_in.1 = (f32[3840,1024]{1,0:T(8,128)}, f32[3840,1024]{1,0:T(8,128)}, bf16[3840,1024]{1,0:T(8,128)(2,1)}, f32[3840,1]{1,0:T(8,128)}) custom-call(bf16[3840,2048]{1,0:T(8,128)(2,1)} %bitcast.37.rows, bf16[2048,1024]{1,0:T(8,128)(2,1)} %pad_maximum_fusion.2.gate, bf16[2048,1024]{1,0:T(8,128)(2,1)} %pad_maximum_fusion.4.up, ...), custom_call_target="tpu_custom_call" | custom-call | flops 32212254720 | bytes 63438848 | tf_op jit(solution)/shard_map/expert_in/pallas_call | solution.py:638
  774.0 22.5 %convolution_convert_fusion.5.refs_1_ = bf16[1024,2048]{1,0:T(8,128)(2,1)} fusion(bf16[3840,1024]{1,0:T(8,128)(2,1)} %get-tuple-element.35.refs_1_.refs_0_, bf16[3840,2048]{1,0:T(8,128)(2,1)} %bitcast.34.refs_1_.grad), kind=kOutput, calls=%fused_computation.40 | convolution fusion | flops 16108224512 | bytes 27787264 | tf_op jit(solution)/shard_map/dot_general | solution.py:714
  813.1 63.4 %expert_back.1 = (bf16[3840,1024]{1,0:T(8,128)(2,1)}, bf16[3840,1024]{1,0:T(8,128)(2,1)}, f32[3840,1]{1,0:T(8,128)}, bf16[3840,2048]{1,0:T(8,128)(2,1)}) custom-call(bf16[3840,2048]{1,0:T(8,128)(2,1)} %bitcast.34.refs_1_.grad, f32[3840,1024]{1,0:T(8,128)} %tie.53.gate_in, f32[3840,1024]{1,0:T(8,128)} %get-tuple-element.37.up_in, ...), custom_call_target="tpu_custom_call" | custom-call | flops 48318382080 | bytes 91226112 | tf_op jit(solution)/shard_map/expert_back/pallas_call | solution.py:670
  876.5 22.4 %convolution_convert_fusion.4.refs_4_ = bf16[2048,1024]{1,0:T(8,128)(2,1)} fusion(bf16[3840,2048]{1,0:T(8,128)(2,1)} %bitcast.37.rows, bf16[3840,1024]{1,0:T(8,128)(2,1)} %get-tuple-element.39), kind=kOutput, calls=%fused_computation.39 | convolution fusion | flops 16108224512 | bytes 27787264 | tf_op jit(solution)/shard_map/dot_general | solution.py:714
  912.6 21.4 %convolution_convert_fusion.3 = bf16[2048,1024]{1,0:T(8,128)(2,1)S(1)} fusion(bf16[3840,2048]{1,0:T(8,128)(2,1)} %bitcast.37.rows, bf16[3840,1024]{1,0:T(8,128)(2,1)} %get-tuple-element.41), kind=kOutput, calls=%fused_computation.38 | convolution fusion | flops 16108224512 | bytes 27787264 | tf_op jit(solution)/shard_map/dot_general | solution.py:714
  939.1 22.1 %convolution_convert_fusion.refs_2_.refs_4_ = bf16[3840,2048]{1,0:T(8,128)(2,1)} fusion(bf16[3840,1024]{1,0:T(8,128)(2,1)} %tie.61, bf16[256,2048]{1,0:T(8,128)(2,1)} %get-tuple-element.183, bf16[256,2048]{1,0:T(8,128)(2,1)} %get-tuple-element.184, bf16[256,2048]{1,0:T(8,128)(2,1)} %get-tuple-element.185, bf16[256,2048]{1,0:T(8,128)(2,1)} %get-tuple-element.182), kind=kOutput, calls=%fused_computation.6 | convolution fusion | flops 16130768896 | bytes 27787264 | tf_op jit(solution)/shard_map/dot_general | solution.py:704
  982.0 21.1 %collective-permute-done.21.refs_1_ = bf16[512,1024]{1,0:T(8,128)(2,1)} collective-permute-done((bf16[512,1024]{1,0:T(8,128)(2,1)}, bf16[512,1024]{1,0:T(8,128)(2,1)}, u32[]{:S(2)}, u32[]{:S(2)}) %collective-permute-start.21) | collective-permute-done | bytes 1048608 | tf_op jit(solution)/shard_map/ppermute | solution.py:773
  1005.4 73.2 %all-to-all-done.6.refs_1_.refs_0_ = bf16[8,480,2048]{2,1,0:T(8,128)(2,1)} async-done(((bf16[8,480,2048]{2,1,0:T(8,128)(2,1)}), bf16[8,480,2048]{2,1,0:T(8,128)(2,1)}, u32[]{:S(2)}, u32[]{:S(2)}) %all-to-all-start.6) | async-done | bytes 15728672 | tf_op jit(solution)/shard_map/all_to_all | solution.py:885
  1124.7 94.3 %reduce-scatter.4.cloned.1.call-done = bf16[384,2048]{1,0:T(8,128)(2,1)} async-done(((bf16[1536,2048]{1,0:T(8,128)(2,1)}), bf16[384,2048]{1,0:T(8,128)(2,1)}) %reduce-scatter.4.cloned.1.call-update) | async-done | bytes 1572880 | tf_op jit(solution)/shard_map/reduce_scatter | solution.py:900
  1301.9 46.0 %attend_back.1 = (f32[1536,512]{1,0:T(8,128)}, f32[1536,512]{1,0:T(8,128)}, f32[1536,512]{1,0:T(8,128)}) custom-call(s32[1536,1]{1,0:T(8,128)S(1)} %broadcast_in_dim.171.seq_rows, s32[1,1536]{1,0:T(1,128)S(1)} %broadcast_in_dim.146.seq_cols, bf16[1536,512]{1,0:T(8,128)(2,1)S(1)} %copy-done.14, bf16[1536,512]{1,0:T(8,128)(2,1)S(1)} %copy-done.16, ...), custom_call_target="tpu_custom_call" | custom-call | flops 12079595520 | bytes 15728640 | tf_op jit(solution)/shard_map/attend_back/pallas_call | solution.py:440
  1466.8 35.8 %all-to-all-done.9.refs_1_ = bf16[8,4,64,1536]{3,2,1,0:T(8,128)(2,1)} async-done(((bf16[8,4,64,1536]{3,2,1,0:T(8,128)(2,1)}), bf16[8,4,64,1536]{3,2,1,0:T(8,128)(2,1)}, u32[]{:S(2)}, u32[]{:S(2)}) %all-to-all-start.9) | async-done | bytes 6291488 | tf_op jit(solution)/shard_map/all_to_all | solution.py:959
  1519.2 17.1 %all-to-all-start.11 = ((bf16[4,64,1536]{2,1,0:T(8,128)(2,1)}), bf16[4,64,1536]{2,1,0:T(8,128)(2,1)S(1)}, u32[]{:S(2)}, u32[]{:S(2)}) async-start(bf16[4,64,1536]{2,1,0:T(8,128)(2,1)} %tie.75), calls=%async_computation.14 | async-start | bytes 1572864 | tf_op jit(solution)/shard_map/all_to_all | solution.py:966
  1546.1 19.9 %all-to-all-done.11 = bf16[4,64,1536]{2,1,0:T(8,128)(2,1)S(1)} async-done(((bf16[4,64,1536]{2,1,0:T(8,128)(2,1)}), bf16[4,64,1536]{2,1,0:T(8,128)(2,1)S(1)}, u32[]{:S(2)}, u32[]{:S(2)}) %all-to-all-start.11) | async-done | bytes 786464 | tf_op jit(solution)/shard_map/all_to_all | solution.py:966
  (494 shorter events, 597.9 us)
Async XLA Ops:
  27.7 159.9 %all-gather.4.cloned.1.call-start = ((), (), s32[]{:S(2)}) async-start(), calls=%async_computation.15 | async-start | bytes 7864320 | tf_op jit(solution)/shard_map/all_gather | solution.py:760
  77.9 82.3 %all-to-all-start.1 = ((bf16[8,4,64,1664]{3,2,1,0:T(8,128)(2,1)}), bf16[8,4,64,1664]{3,2,1,0:T(8,128)(2,1)}, u32[]{:S(2)}, u32[]{:S(2)}) async-start(bf16[8,4,64,1664]{3,2,1,0:T(8,128)(2,1)} %broadcast_in_dim.153), calls=%async_computation.1 | async-start | bytes 13631488 | tf_op jit(solution)/shard_map/all_to_all | solution.py:766
  82.9 223.8 %all-gather.6.cloned.1.call-start = ((), (), s32[]{:S(2)}) async-start(), calls=%async_computation.16 | async-start | bytes 7864320 | tf_op jit(solution)/shard_map/all_gather | solution.py:799
  193.0 99.2 %all-to-all-start.2 = ((bf16[8,4,64,2048]{3,2,1,0:T(8,128)(2,1)}), bf16[8,4,64,2048]{3,2,1,0:T(8,128)(2,1)}, u32[]{:S(2)}, u32[]{:S(2)}) async-start(bf16[8,4,64,2048]{3,2,1,0:T(8,128)(2,1)} %broadcast_in_dim.157.refs_3_), calls=%async_computation.2 | async-start | bytes 16777216 | tf_op jit(solution)/shard_map/all_to_all | solution.py:802
  320.4 216.0 %all-to-all-start.3 = ((bf16[8,4,120,2048]{3,2,1,0:T(8,128)(2,1)}), bf16[8,4,120,2048]{3,2,1,0:T(8,128)(2,1)}, u32[]{:S(2)}, u32[]{:S(2)}) async-start(bf16[8,4,120,2048]{3,2,1,0:T(8,128)(2,1)} %dispatch.2.refs_1_), calls=%async_computation.3 | async-start | bytes 31457280 | tf_op jit(solution)/shard_map/all_to_all | solution.py:847
  326.1 163.7 %all-gather.8.cloned.1.call-start = ((), (), s32[]{:S(2)}) async-start(), calls=%async_computation.17 | async-start | bytes 7864320 | tf_op jit(solution)/shard_map/all_gather | solution.py:853
  550.9 178.5 %all-to-all-start.4 = ((bf16[8,4,120,2048]{3,2,1,0:T(8,128)(2,1)}), bf16[8,4,120,2048]{3,2,1,0:T(8,128)(2,1)}, u32[]{:S(2)}, u32[]{:S(2)}) async-start(bf16[8,4,120,2048]{3,2,1,0:T(8,128)(2,1)} %dispatch.3), calls=%async_computation.4 | async-start | bytes 31457280 | tf_op jit(solution)/shard_map/all_to_all | solution.py:864
  588.2 108.6 %collective-permute-start.10 = (bf16[512,1024]{1,0:T(8,128)(2,1)}, bf16[512,1024]{1,0:T(8,128)(2,1)}, u32[]{:S(2)}, u32[]{:S(2)}) collective-permute-start(bf16[512,1024]{1,0:T(8,128)(2,1)} %tie.51), channel_id=1, source_target_pairs={{0,16},{8,24},{16,0},{24,8},{1,17},{9,25},{17,1},{25,9},{2,18},{10... | collective-permute-start | bytes 3145736 | tf_op jit(solution)/shard_map/ppermute | solution.py:773
  607.4 89.4 %collective-permute-start.9 = (bf16[512,1024]{1,0:T(8,128)(2,1)}, bf16[512,1024]{1,0:T(8,128)(2,1)}, u32[]{:S(2)}, u32[]{:S(2)}) collective-permute-start(bf16[512,1024]{1,0:T(8,128)(2,1)} %tie.50), channel_id=1, source_target_pairs={{0,8},{8,0},{16,24},{24,16},{1,9},{9,1},{17,25},{25,17},{2,10},{10... | collective-permute-start | bytes 3145736 | tf_op jit(solution)/shard_map/ppermute | solution.py:773
  696.8 99.6 %collective-permute-start.14 = (bf16[256,2048]{1,0:T(8,128)(2,1)}, bf16[256,2048]{1,0:T(8,128)(2,1)}, u32[]{:S(2)}, u32[]{:S(2)}) collective-permute-start(bf16[256,2048]{1,0:T(8,128)(2,1)} %tie.58), channel_id=1, source_target_pairs={{0,24},{8,16},{16,8},{24,0},{1,25},{9,17},{17,9},{25,1},{2,26},{10... | collective-permute-start | bytes 3145736 | tf_op jit(solution)/shard_map/ppermute | solution.py:773
  698.9 97.6 %collective-permute-start.13 = (bf16[256,2048]{1,0:T(8,128)(2,1)}, bf16[256,2048]{1,0:T(8,128)(2,1)}, u32[]{:S(2)}, u32[]{:S(2)}) collective-permute-start(bf16[256,2048]{1,0:T(8,128)(2,1)} %tie.56), channel_id=1, source_target_pairs={{0,16},{8,24},{16,0},{24,8},{1,17},{9,25},{17,1},{25,9},{2,18},{10... | collective-permute-start | bytes 3145736 | tf_op jit(solution)/shard_map/ppermute | solution.py:773
  698.9 97.6 %collective-permute-start.12 = (bf16[256,2048]{1,0:T(8,128)(2,1)}, bf16[256,2048]{1,0:T(8,128)(2,1)}, u32[]{:S(2)}, u32[]{:S(2)}) collective-permute-start(bf16[256,2048]{1,0:T(8,128)(2,1)} %tie.54), channel_id=1, source_target_pairs={{0,8},{8,0},{16,24},{24,16},{1,9},{9,1},{17,25},{25,17},{2,10},{10... | collective-permute-start | bytes 3145736 | tf_op jit(solution)/shard_map/ppermute | solution.py:773
  806.4 92.5 %collective-permute-start.15 = (bf16[256,2048]{1,0:T(8,128)(2,1)}, bf16[256,2048]{1,0:T(8,128)(2,1)S(1)}, u32[]{:S(2)}, u32[]{:S(2)}) collective-permute-start(bf16[256,2048]{1,0:T(8,128)(2,1)} %get-tuple-element.165), channel_id=1, source_target_pairs={{0,24},{8,16},{16,8},{24,0},{1,25},{9,17},{17,9},{25,1},{2,26},{10... | collective-permute-start | bytes 3145736 | tf_op jit(solution)/shard_map/ppermute | solution.py:773
  808.8 90.1 %collective-permute-start.17 = (bf16[256,2048]{1,0:T(8,128)(2,1)S(1)}, bf16[256,2048]{1,0:T(8,128)(2,1)}, u32[]{:S(2)}, u32[]{:S(2)}) collective-permute-start(bf16[256,2048]{1,0:T(8,128)(2,1)S(1)} %get-tuple-element.164), channel_id=1, source_target_pairs={{0,8},{8,0},{16,24},{24,16},{1,9},{9,1},{17,25},{25,17},{2,10},{10... | collective-permute-start | bytes 3145736 | tf_op jit(solution)/shard_map/ppermute | solution.py:773
  808.8 90.1 %collective-permute-start.18 = (bf16[256,2048]{1,0:T(8,128)(2,1)S(1)}, bf16[256,2048]{1,0:T(8,128)(2,1)}, u32[]{:S(2)}, u32[]{:S(2)}) collective-permute-start(bf16[256,2048]{1,0:T(8,128)(2,1)S(1)} %get-tuple-element.163), channel_id=1, source_target_pairs={{0,16},{8,24},{16,0},{24,8},{1,17},{9,25},{17,1},{25,9},{2,18},{10... | collective-permute-start | bytes 3145736 | tf_op jit(solution)/shard_map/ppermute | solution.py:773
  899.9 178.8 %all-to-all-start.6 = ((bf16[8,480,2048]{2,1,0:T(8,128)(2,1)}), bf16[8,480,2048]{2,1,0:T(8,128)(2,1)}, u32[]{:S(2)}, u32[]{:S(2)}) async-start(bf16[8,480,2048]{2,1,0:T(8,128)(2,1)} %bitcast.292), calls=%async_computation.6 | async-start | bytes 31457280 | tf_op jit(solution)/shard_map/all_to_all | solution.py:885
  965.1 119.8 %collective-permute-start.20 = (bf16[512,1024]{1,0:T(8,128)(2,1)}, bf16[512,1024]{1,0:T(8,128)(2,1)S(1)}, u32[]{:S(2)}, u32[]{:S(2)}) collective-permute-start(bf16[512,1024]{1,0:T(8,128)(2,1)} %tie.64), channel_id=1, source_target_pairs={{0,8},{8,0},{16,24},{24,16},{1,9},{9,1},{17,25},{25,17},{2,10},{10... | collective-permute-start | bytes 3145736 | tf_op jit(solution)/shard_map/ppermute | solution.py:773
  1003.1 81.9 %collective-permute-start.22 = (bf16[512,1024]{1,0:T(8,128)(2,1)}, bf16[512,1024]{1,0:T(8,128)(2,1)}, u32[]{:S(2)}, u32[]{:S(2)}) collective-permute-start(bf16[512,1024]{1,0:T(8,128)(2,1)} %tie.66), channel_id=1, source_target_pairs={{0,16},{8,24},{16,0},{24,8},{1,17},{9,25},{17,1},{25,9},{2,18},{10... | collective-permute-start | bytes 3145736 | tf_op jit(solution)/shard_map/ppermute | solution.py:773
  1003.1 81.9 %collective-permute-start.23 = (bf16[512,1024]{1,0:T(8,128)(2,1)}, bf16[512,1024]{1,0:T(8,128)(2,1)}, u32[]{:S(2)}, u32[]{:S(2)}) collective-permute-start(bf16[512,1024]{1,0:T(8,128)(2,1)} %tie.67), channel_id=1, source_target_pairs={{0,24},{8,16},{16,8},{24,0},{1,25},{9,17},{17,9},{25,1},{2,26},{10... | collective-permute-start | bytes 3145736 | tf_op jit(solution)/shard_map/ppermute | solution.py:773
  1084.9 134.1 %reduce-scatter.4.cloned.1.call-start = ((), (), s32[]{:S(2)}) async-start(), calls=%async_computation.18 | async-start | bytes 7864320 | tf_op jit(solution)/shard_map/reduce_scatter | solution.py:900
  1102.1 178.5 %all-to-all-start.5 = ((bf16[8,480,2048]{2,1,0:T(8,128)(2,1)}), bf16[8,480,2048]{2,1,0:T(8,128)(2,1)}, u32[]{:S(2)}, u32[]{:S(2)}) async-start(bf16[8,480,2048]{2,1,0:T(8,128)(2,1)} %bitcast.289), calls=%async_computation.5 | async-start | bytes 31457280 | tf_op jit(solution)/shard_map/all_to_all | solution.py:897
  1107.9 300.1 %reduce-scatter.6.cloned.1.call-start = ((), (), s32[]{:S(2)}) async-start(), calls=%async_computation.19 | async-start | bytes 7864320 | tf_op jit(solution)/shard_map/reduce_scatter | solution.py:928
  1292.8 110.6 %all-to-all-start.8 = ((bf16[8,4,64,2048]{3,2,1,0:T(8,128)(2,1)}), bf16[8,4,64,2048]{3,2,1,0:T(8,128)(2,1)}, u32[]{:S(2)}, u32[]{:S(2)}) async-start(bf16[8,4,64,2048]{3,2,1,0:T(8,128)(2,1)} %tie.72), calls=%async_computation.10 | async-start | bytes 16777216 | tf_op jit(solution)/shard_map/all_to_all | solution.py:930
  1297.7 281.0 %reduce-scatter.8.cloned.1.call-start = ((), (), s32[]{:S(2)}) async-start(), calls=%async_computation.20 | async-start | bytes 7864320 | tf_op jit(solution)/shard_map/reduce_scatter | solution.py:950
  (117 other events, 2053.4 us)
Sparse Core Ops, SparseCore 0:
  73.1 114.4 all-gather.3
  192.2 114.5 all-gather.5
  374.0 115.7 all-gather.7
  1102.2 116.7 reduce-scatter.3
  1292.9 115.0 reduce-scatter.5
  1410.1 136.2 reduce-scatter.7

commit v10 on v9

--- a/solution.py
+++ b/solution.py
@@ -958,12 +958,11 @@
     small = sum([small[plane]] + [swap(small[plane ^ step], step) for step in steps])
     sums = lax.all_to_all(sums, "fsdp", 0, 0, tiled=True)
     grad_out_w = jnp.sum(grad_out_w.astype(f32), axis=0).astype(bf16)
-    came_out = [swap(grad_out_w[plane ^ step], step) for step in steps]
-    grad_out_w = sum(x.astype(f32) for x in [grad_out_w[plane]] + came_out)
-    small = lax.all_to_all(tie(small, sums, *came_out), "fsdp", 0, 0, tiled=True)
+    small = lax.all_to_all(tie(small, sums, grad_out_w), "fsdp", 0, 0, tiled=True)
     small = jnp.sum(small, axis=0).reshape(strip, -1)
-    sums = jnp.sum(sums.astype(f32), axis=0).astype(bf16)
-    sums = lax.all_to_all(tie(sums, small), "ctx", 0, 0, tiled=True)
+    sums = tie(jnp.sum(sums.astype(f32), axis=0).astype(bf16), small)
+    grad_out_w = sum(x.astype(f32) for x in exchange(grad_out_w, sums))
+    sums = lax.all_to_all(sums, "ctx", 0, 0, tiled=True)
     grad_qkv_w = sums.reshape(planes, strip, 3, share).transpose(2, 1, 0, 3)
     grad_qkv_w = grad_qkv_w.reshape(3, strip, width).astype(f32)
 

time: 1600 us -> 1600 us (level)
  waiting for transfers between devices: 766 us -> 782 us
    ppermute x39, waiting for transfers between devices: 231 us -> 272 us  [swap(): return lax.ppermute(part, 'ctx', [(i, i ^ step) for i in range(planes)])]
    all_to_all x2, waiting for transfers between devices: 19.9 us -> 0.01 us  [the longest x1 0.01 us: plane_shards(): lax.all_to_all(tie(small, sums, grad_out_w), 'fsdp', 0, 0, tiled=True)]
    unnamed x176 -> x172, local copies, waits for them, and re-layouts: 42.4 us -> 41.1 us
  transfers between devices with their start and end apart: 57 -> 57, of which waited for: 31 -> 33; matrix products, arithmetic and copies ran while one was open for 21% -> 21% of each run, Pallas kernels for 12% -> 12%
where the time goes in v10:
time: 1600 us
  waiting for transfers between devices  782 us (49%)
  Pallas kernels  220 us (14%)
  matrix products  184 us (12%)
  starting transfers between devices  159 us (10%)
  local copies, waits for them, and re-layouts  138 us (9%)
  other arithmetic  96 us (6%)
    ppermute x39, waiting for transfers between devices, swap(): return lax.ppermute(part, 'ctx', [(i, i ^ step) for i in range(planes)])  272 us
    all_gather x1, waiting for transfers between devices, plane_shards(): h_two_all = lax.all_gather(tie(h_two, grad_send), 'ctx', axis=0, tiled=True)  112 us
    ppermute x39, starting transfers between devices, swap(): return lax.ppermute(part, 'ctx', [(i, i ^ step) for i in range(planes)])  97.7 us
    reduce_scatter x1, waiting for transfers between devices, plane_shards(): lax.psum_scatter(combine(grad_rows), 'ctx', scatter_dimension=0, tiled=True)  94.3 us
    dot_general x6, matrix products, t_mm(): lax.dot_general(left, right, (((0,), (0,)), ((), ())), preferred_element_...  87.6 us
    all_to_all x1, waiting for transfers between devices, plane_shards(): packed = lax.all_to_all(packed, 'fsdp', 0, 0, tiled=True)  76 us
    all_to_all x1, waiting for transfers between devices, plane_shards(): lax.all_to_all(grad_rows.reshape(columns, planes * capacity, width), 'fsd...  73.2 us
    pallas_call x1, Pallas kernels, expert_back(): pl.pallas_call(expert_back_kernel, grid=(count // block,), in_specs=[wide...  63.4 us
  transfers between devices with their start and end apart: 57, of which 33 were waited for; matrix products, arithmetic and copies ran while one was open for 21% of the time, Pallas kernels for 12%

profile of v10, /device:TPU:0, one launch (start us, length us, event | category | flops | bytes accessed | tf_op | source)
XLA Modules:
  0.0 1595.1 jit_solution(17862349809496285597)
XLA Ops:
  28.8 42.8 %all-to-all-done.refs_1_ = bf16[4,64,3712]{2,1,0:T(8,128)(2,1)S(1)} async-done(((bf16[4,64,3712]{2,1,0:T(8,128)(2,1)}), bf16[4,64,3712]{2,1,0:T(8,128)(2,1)S(1)}, u32[]{:S(2)}, u32[]{:S(2)}) %all-to-all-start) | async-done | bytes 1900576 | tf_op jit(solution)/shard_map/all_to_all | solution.py:759
  84.1 76.0 %all-to-all-done.1 = bf16[8,4,64,1664]{3,2,1,0:T(8,128)(2,1)} async-done(((bf16[8,4,64,1664]{3,2,1,0:T(8,128)(2,1)}), bf16[8,4,64,1664]{3,2,1,0:T(8,128)(2,1)}, u32[]{:S(2)}, u32[]{:S(2)}) %all-to-all-start.1) | async-done | bytes 6815776 | tf_op jit(solution)/shard_map/all_to_all | solution.py:766
  166.6 21.0 %all-gather.4.cloned.1.call-done.refs_1_ = bf16[1536,2048]{1,0:T(8,128)(2,1)} async-done(((bf16[384,2048]{1,0:T(8,128)(2,1)}), bf16[1536,2048]{1,0:T(8,128)(2,1)}) %all-gather.4.cloned.1.call-update) | async-done | bytes 6291472 | tf_op jit(solution)/shard_map/all_gather | solution.py:760
  251.5 27.7 %attend.1.refs_1_ = bf16[1536,512]{1,0:T(8,128)(2,1)S(1)} custom-call(s32[1536,1]{1,0:T(8,128)S(1)} %broadcast_in_dim.171.seq_rows, s32[1,1536]{1,0:T(1,128)S(1)} %broadcast_in_dim.146.seq_cols, bf16[1536,512]{1,0:T(8,128)(2,1)S(1)} %get-tuple-element.32.query, bf16[1536,512]{1,0:T(8,128)(2,1)S(1)} %get-tuple-element.33.key, bf16[1536,512]{1,0:T(8,128)(2,1)} %copy-done.17), custom_call_target="tpu_custom_call" | custom-call | flops 4831838208 | bytes 6291456 | tf_op jit(solution)/shard_map/attend/pallas_call | solution.py:421
  340.3 21.3 %collective-permute-done.4 = bf16[384,512]{1,0:T(8,128)(2,1)S(1)} collective-permute-done((bf16[384,512]{1,0:T(8,128)(2,1)}, bf16[384,512]{1,0:T(8,128)(2,1)S(1)}, u32[]{:S(2)}, u32[]{:S(2)}) %collective-permute-start.4) | collective-permute-done | bytes 393248 | tf_op jit(solution)/shard_map/ppermute | solution.py:773
  378.3 111.7 %all-gather.8.cloned.1.call-done.refs_1_.refs_0_ = bf16[1536,2048]{1,0:T(8,128)(2,1)} async-done(((bf16[384,2048]{1,0:T(8,128)(2,1)}), bf16[1536,2048]{1,0:T(8,128)(2,1)}) %all-gather.8.cloned.1.call-update) | async-done | bytes 6291472 | tf_op jit(solution)/shard_map/all_gather | solution.py:853
  490.6 45.9 %collective-permute-done.6.refs_2_.refs_1_ = bf16[512,1024]{1,0:T(8,128)(2,1)S(1)} collective-permute-done((bf16[512,1024]{1,0:T(8,128)(2,1)}, bf16[512,1024]{1,0:T(8,128)(2,1)S(1)}, u32[]{:S(2)}, u32[]{:S(2)}) %collective-permute-start.6) | collective-permute-done | bytes 1048608 | tf_op jit(solution)/shard_map/ppermute | solution.py:773
  566.0 19.0 %collective-permute-done.8.refs_1_ = bf16[512,1024]{1,0:T(8,128)(2,1)S(1)} collective-permute-done((bf16[512,1024]{1,0:T(8,128)(2,1)}, bf16[512,1024]{1,0:T(8,128)(2,1)S(1)}, u32[]{:S(2)}, u32[]{:S(2)}) %collective-permute-start.8) | collective-permute-done | bytes 1048608 | tf_op jit(solution)/shard_map/ppermute | solution.py:773
  588.4 18.9 %collective-permute-start.10 = (bf16[512,1024]{1,0:T(8,128)(2,1)}, bf16[512,1024]{1,0:T(8,128)(2,1)}, u32[]{:S(2)}, u32[]{:S(2)}) collective-permute-start(bf16[512,1024]{1,0:T(8,128)(2,1)} %tie.54), channel_id=1, source_target_pairs={{0,16},{8,24},{16,0},{24,8},{1,17},{9,25},{17,1},{25,9},{2,18},{10... | collective-permute-start | bytes 3145736 | tf_op jit(solution)/shard_map/ppermute | solution.py:773
  630.1 66.9 %collective-permute-done.10.refs_2_ = bf16[512,1024]{1,0:T(8,128)(2,1)} collective-permute-done((bf16[512,1024]{1,0:T(8,128)(2,1)}, bf16[512,1024]{1,0:T(8,128)(2,1)}, u32[]{:S(2)}, u32[]{:S(2)}) %collective-permute-start.10) | collective-permute-done | bytes 1048608 | tf_op jit(solution)/shard_map/ppermute | solution.py:773
  706.3 23.3 %all-to-all-done.4 = bf16[8,4,120,2048]{3,2,1,0:T(8,128)(2,1)} async-done(((bf16[8,4,120,2048]{3,2,1,0:T(8,128)(2,1)}), bf16[8,4,120,2048]{3,2,1,0:T(8,128)(2,1)}, u32[]{:S(2)}, u32[]{:S(2)}) %all-to-all-start.4) | async-done | bytes 15728672 | tf_op jit(solution)/shard_map/all_to_all | solution.py:864
  729.6 44.6 %expert_in.1 = (f32[3840,1024]{1,0:T(8,128)}, f32[3840,1024]{1,0:T(8,128)}, bf16[3840,1024]{1,0:T(8,128)(2,1)}, f32[3840,1]{1,0:T(8,128)}) custom-call(bf16[3840,2048]{1,0:T(8,128)(2,1)} %bitcast.37.rows, bf16[2048,1024]{1,0:T(8,128)(2,1)} %pad_maximum_fusion.2.gate, bf16[2048,1024]{1,0:T(8,128)(2,1)} %pad_maximum_fusion.4.up, ...), custom_call_target="tpu_custom_call" | custom-call | flops 32212254720 | bytes 63438848 | tf_op jit(solution)/shard_map/expert_in/pallas_call | solution.py:638
  774.2 22.5 %convolution_convert_fusion.5.refs_1_ = bf16[1024,2048]{1,0:T(8,128)(2,1)} fusion(bf16[3840,1024]{1,0:T(8,128)(2,1)} %get-tuple-element.35.refs_1_.refs_0_, bf16[3840,2048]{1,0:T(8,128)(2,1)} %bitcast.34.refs_1_.grad), kind=kOutput, calls=%fused_computation.40 | convolution fusion | flops 16108224512 | bytes 27787264 | tf_op jit(solution)/shard_map/dot_general | solution.py:714
  813.3 63.4 %expert_back.1 = (bf16[3840,1024]{1,0:T(8,128)(2,1)}, bf16[3840,1024]{1,0:T(8,128)(2,1)}, f32[3840,1]{1,0:T(8,128)}, bf16[3840,2048]{1,0:T(8,128)(2,1)}) custom-call(bf16[3840,2048]{1,0:T(8,128)(2,1)} %bitcast.34.refs_1_.grad, f32[3840,1024]{1,0:T(8,128)} %tie.56.gate_in, f32[3840,1024]{1,0:T(8,128)} %get-tuple-element.37.up_in, ...), custom_call_target="tpu_custom_call" | custom-call | flops 48318382080 | bytes 91226112 | tf_op jit(solution)/shard_map/expert_back/pallas_call | solution.py:670
  876.7 22.4 %convolution_convert_fusion.4.refs_4_ = bf16[2048,1024]{1,0:T(8,128)(2,1)} fusion(bf16[3840,2048]{1,0:T(8,128)(2,1)} %bitcast.37.rows, bf16[3840,1024]{1,0:T(8,128)(2,1)} %get-tuple-element.39), kind=kOutput, calls=%fused_computation.39 | convolution fusion | flops 16108224512 | bytes 27787264 | tf_op jit(solution)/shard_map/dot_general | solution.py:714
  912.8 21.4 %convolution_convert_fusion.3 = bf16[2048,1024]{1,0:T(8,128)(2,1)S(1)} fusion(bf16[3840,2048]{1,0:T(8,128)(2,1)} %bitcast.37.rows, bf16[3840,1024]{1,0:T(8,128)(2,1)} %get-tuple-element.41), kind=kOutput, calls=%fused_computation.38 | convolution fusion | flops 16108224512 | bytes 27787264 | tf_op jit(solution)/shard_map/dot_general | solution.py:714
  939.3 22.1 %convolution_convert_fusion.refs_2_.refs_4_ = bf16[3840,2048]{1,0:T(8,128)(2,1)} fusion(bf16[3840,1024]{1,0:T(8,128)(2,1)} %tie.64, bf16[256,2048]{1,0:T(8,128)(2,1)} %get-tuple-element.183, bf16[256,2048]{1,0:T(8,128)(2,1)} %get-tuple-element.184, bf16[256,2048]{1,0:T(8,128)(2,1)} %get-tuple-element.185, bf16[256,2048]{1,0:T(8,128)(2,1)} %get-tuple-element.182), kind=kOutput, calls=%fused_computation.6 | convolution fusion | flops 16130768896 | bytes 27787264 | tf_op jit(solution)/shard_map/dot_general | solution.py:704
  965.3 17.0 %collective-permute-start.20 = (bf16[512,1024]{1,0:T(8,128)(2,1)}, bf16[512,1024]{1,0:T(8,128)(2,1)S(1)}, u32[]{:S(2)}, u32[]{:S(2)}) collective-permute-start(bf16[512,1024]{1,0:T(8,128)(2,1)} %tie.67), channel_id=1, source_target_pairs={{0,8},{8,0},{16,24},{24,16},{1,9},{9,1},{17,25},{25,17},{2,10},{10... | collective-permute-start | bytes 3145736 | tf_op jit(solution)/shard_map/ppermute | solution.py:773
  982.2 21.1 %collective-permute-done.21.refs_1_ = bf16[512,1024]{1,0:T(8,128)(2,1)} collective-permute-done((bf16[512,1024]{1,0:T(8,128)(2,1)}, bf16[512,1024]{1,0:T(8,128)(2,1)}, u32[]{:S(2)}, u32[]{:S(2)}) %collective-permute-start.21) | collective-permute-done | bytes 1048608 | tf_op jit(solution)/shard_map/ppermute | solution.py:773
  1005.7 73.2 %all-to-all-done.6.refs_1_.refs_0_ = bf16[8,480,2048]{2,1,0:T(8,128)(2,1)} async-done(((bf16[8,480,2048]{2,1,0:T(8,128)(2,1)}), bf16[8,480,2048]{2,1,0:T(8,128)(2,1)}, u32[]{:S(2)}, u32[]{:S(2)}) %all-to-all-start.6) | async-done | bytes 15728672 | tf_op jit(solution)/shard_map/all_to_all | solution.py:885
  1124.9 94.3 %reduce-scatter.4.cloned.1.call-done = bf16[384,2048]{1,0:T(8,128)(2,1)} async-done(((bf16[1536,2048]{1,0:T(8,128)(2,1)}), bf16[384,2048]{1,0:T(8,128)(2,1)}) %reduce-scatter.4.cloned.1.call-update) | async-done | bytes 1572880 | tf_op jit(solution)/shard_map/reduce_scatter | solution.py:900
  1302.2 46.0 %attend_back.1 = (f32[1536,512]{1,0:T(8,128)}, f32[1536,512]{1,0:T(8,128)}, f32[1536,512]{1,0:T(8,128)}) custom-call(s32[1536,1]{1,0:T(8,128)S(1)} %broadcast_in_dim.171.seq_rows, s32[1,1536]{1,0:T(1,128)S(1)} %broadcast_in_dim.146.seq_cols, bf16[1536,512]{1,0:T(8,128)(2,1)S(1)} %copy-done.14, bf16[1536,512]{1,0:T(8,128)(2,1)S(1)} %copy-done.16, ...), custom_call_target="tpu_custom_call" | custom-call | flops 12079595520 | bytes 15728640 | tf_op jit(solution)/shard_map/attend_back/pallas_call | solution.py:440
  1471.4 31.6 %all-to-all-done.9.refs_1_ = bf16[8,4,64,1536]{3,2,1,0:T(8,128)(2,1)} async-done(((bf16[8,4,64,1536]{3,2,1,0:T(8,128)(2,1)}), bf16[8,4,64,1536]{3,2,1,0:T(8,128)(2,1)}, u32[]{:S(2)}, u32[]{:S(2)}) %all-to-all-start.9) | async-done | bytes 6291488 | tf_op jit(solution)/shard_map/all_to_all | solution.py:959
  1546.2 20.4 %collective-permute-done.37 = bf16[64,2048]{1,0:T(8,128)(2,1)} collective-permute-done((bf16[64,2048]{1,0:T(8,128)(2,1)}, bf16[64,2048]{1,0:T(8,128)(2,1)}, u32[]{:S(2)}, u32[]{:S(2)}) %collective-permute-start.37) | collective-permute-done | bytes 262176 | tf_op jit(solution)/shard_map/ppermute | solution.py:773
  (494 shorter events, 604.7 us)
Async XLA Ops:
  27.7 159.9 %all-gather.4.cloned.1.call-start = ((), (), s32[]{:S(2)}) async-start(), calls=%async_computation.15 | async-start | bytes 7864320 | tf_op jit(solution)/shard_map/all_gather | solution.py:760
  77.9 82.3 %all-to-all-start.1 = ((bf16[8,4,64,1664]{3,2,1,0:T(8,128)(2,1)}), bf16[8,4,64,1664]{3,2,1,0:T(8,128)(2,1)}, u32[]{:S(2)}, u32[]{:S(2)}) async-start(bf16[8,4,64,1664]{3,2,1,0:T(8,128)(2,1)} %broadcast_in_dim.153), calls=%async_computation.1 | async-start | bytes 13631488 | tf_op jit(solution)/shard_map/all_to_all | solution.py:766
  82.9 223.9 %all-gather.6.cloned.1.call-start = ((), (), s32[]{:S(2)}) async-start(), calls=%async_computation.16 | async-start | bytes 7864320 | tf_op jit(solution)/shard_map/all_gather | solution.py:799
  193.0 99.2 %all-to-all-start.2 = ((bf16[8,4,64,2048]{3,2,1,0:T(8,128)(2,1)}), bf16[8,4,64,2048]{3,2,1,0:T(8,128)(2,1)}, u32[]{:S(2)}, u32[]{:S(2)}) async-start(bf16[8,4,64,2048]{3,2,1,0:T(8,128)(2,1)} %broadcast_in_dim.157.refs_3_), calls=%async_computation.2 | async-start | bytes 16777216 | tf_op jit(solution)/shard_map/all_to_all | solution.py:802
  320.4 216.2 %all-to-all-start.3 = ((bf16[8,4,120,2048]{3,2,1,0:T(8,128)(2,1)}), bf16[8,4,120,2048]{3,2,1,0:T(8,128)(2,1)}, u32[]{:S(2)}, u32[]{:S(2)}) async-start(bf16[8,4,120,2048]{3,2,1,0:T(8,128)(2,1)} %dispatch.2.refs_1_), calls=%async_computation.3 | async-start | bytes 31457280 | tf_op jit(solution)/shard_map/all_to_all | solution.py:847
  326.1 163.9 %all-gather.8.cloned.1.call-start = ((), (), s32[]{:S(2)}) async-start(), calls=%async_computation.17 | async-start | bytes 7864320 | tf_op jit(solution)/shard_map/all_gather | solution.py:853
  551.1 178.5 %all-to-all-start.4 = ((bf16[8,4,120,2048]{3,2,1,0:T(8,128)(2,1)}), bf16[8,4,120,2048]{3,2,1,0:T(8,128)(2,1)}, u32[]{:S(2)}, u32[]{:S(2)}) async-start(bf16[8,4,120,2048]{3,2,1,0:T(8,128)(2,1)} %dispatch.3), calls=%async_computation.4 | async-start | bytes 31457280 | tf_op jit(solution)/shard_map/all_to_all | solution.py:864
  588.4 108.7 %collective-permute-start.10 = (bf16[512,1024]{1,0:T(8,128)(2,1)}, bf16[512,1024]{1,0:T(8,128)(2,1)}, u32[]{:S(2)}, u32[]{:S(2)}) collective-permute-start(bf16[512,1024]{1,0:T(8,128)(2,1)} %tie.54), channel_id=1, source_target_pairs={{0,16},{8,24},{16,0},{24,8},{1,17},{9,25},{17,1},{25,9},{2,18},{10... | collective-permute-start | bytes 3145736 | tf_op jit(solution)/shard_map/ppermute | solution.py:773
  607.6 89.4 %collective-permute-start.9 = (bf16[512,1024]{1,0:T(8,128)(2,1)}, bf16[512,1024]{1,0:T(8,128)(2,1)}, u32[]{:S(2)}, u32[]{:S(2)}) collective-permute-start(bf16[512,1024]{1,0:T(8,128)(2,1)} %tie.53), channel_id=1, source_target_pairs={{0,8},{8,0},{16,24},{24,16},{1,9},{9,1},{17,25},{25,17},{2,10},{10... | collective-permute-start | bytes 3145736 | tf_op jit(solution)/shard_map/ppermute | solution.py:773
  697.0 99.6 %collective-permute-start.14 = (bf16[256,2048]{1,0:T(8,128)(2,1)}, bf16[256,2048]{1,0:T(8,128)(2,1)}, u32[]{:S(2)}, u32[]{:S(2)}) collective-permute-start(bf16[256,2048]{1,0:T(8,128)(2,1)} %tie.61), channel_id=1, source_target_pairs={{0,24},{8,16},{16,8},{24,0},{1,25},{9,17},{17,9},{25,1},{2,26},{10... | collective-permute-start | bytes 3145736 | tf_op jit(solution)/shard_map/ppermute | solution.py:773
  699.1 97.6 %collective-permute-start.13 = (bf16[256,2048]{1,0:T(8,128)(2,1)}, bf16[256,2048]{1,0:T(8,128)(2,1)}, u32[]{:S(2)}, u32[]{:S(2)}) collective-permute-start(bf16[256,2048]{1,0:T(8,128)(2,1)} %tie.59), channel_id=1, source_target_pairs={{0,16},{8,24},{16,0},{24,8},{1,17},{9,25},{17,1},{25,9},{2,18},{10... | collective-permute-start | bytes 3145736 | tf_op jit(solution)/shard_map/ppermute | solution.py:773
  699.1 97.6 %collective-permute-start.12 = (bf16[256,2048]{1,0:T(8,128)(2,1)}, bf16[256,2048]{1,0:T(8,128)(2,1)}, u32[]{:S(2)}, u32[]{:S(2)}) collective-permute-start(bf16[256,2048]{1,0:T(8,128)(2,1)} %tie.57), channel_id=1, source_target_pairs={{0,8},{8,0},{16,24},{24,16},{1,9},{9,1},{17,25},{25,17},{2,10},{10... | collective-permute-start | bytes 3145736 | tf_op jit(solution)/shard_map/ppermute | solution.py:773
  806.6 92.5 %collective-permute-start.15 = (bf16[256,2048]{1,0:T(8,128)(2,1)}, bf16[256,2048]{1,0:T(8,128)(2,1)S(1)}, u32[]{:S(2)}, u32[]{:S(2)}) collective-permute-start(bf16[256,2048]{1,0:T(8,128)(2,1)} %get-tuple-element.165), channel_id=1, source_target_pairs={{0,24},{8,16},{16,8},{24,0},{1,25},{9,17},{17,9},{25,1},{2,26},{10... | collective-permute-start | bytes 3145736 | tf_op jit(solution)/shard_map/ppermute | solution.py:773
  809.0 90.1 %collective-permute-start.17 = (bf16[256,2048]{1,0:T(8,128)(2,1)S(1)}, bf16[256,2048]{1,0:T(8,128)(2,1)}, u32[]{:S(2)}, u32[]{:S(2)}) collective-permute-start(bf16[256,2048]{1,0:T(8,128)(2,1)S(1)} %get-tuple-element.164), channel_id=1, source_target_pairs={{0,8},{8,0},{16,24},{24,16},{1,9},{9,1},{17,25},{25,17},{2,10},{10... | collective-permute-start | bytes 3145736 | tf_op jit(solution)/shard_map/ppermute | solution.py:773
  809.0 90.1 %collective-permute-start.18 = (bf16[256,2048]{1,0:T(8,128)(2,1)S(1)}, bf16[256,2048]{1,0:T(8,128)(2,1)}, u32[]{:S(2)}, u32[]{:S(2)}) collective-permute-start(bf16[256,2048]{1,0:T(8,128)(2,1)S(1)} %get-tuple-element.163), channel_id=1, source_target_pairs={{0,16},{8,24},{16,0},{24,8},{1,17},{9,25},{17,1},{25,9},{2,18},{10... | collective-permute-start | bytes 3145736 | tf_op jit(solution)/shard_map/ppermute | solution.py:773
  900.1 178.8 %all-to-all-start.6 = ((bf16[8,480,2048]{2,1,0:T(8,128)(2,1)}), bf16[8,480,2048]{2,1,0:T(8,128)(2,1)}, u32[]{:S(2)}, u32[]{:S(2)}) async-start(bf16[8,480,2048]{2,1,0:T(8,128)(2,1)} %bitcast.294), calls=%async_computation.6 | async-start | bytes 31457280 | tf_op jit(solution)/shard_map/all_to_all | solution.py:885
  965.3 119.8 %collective-permute-start.20 = (bf16[512,1024]{1,0:T(8,128)(2,1)}, bf16[512,1024]{1,0:T(8,128)(2,1)S(1)}, u32[]{:S(2)}, u32[]{:S(2)}) collective-permute-start(bf16[512,1024]{1,0:T(8,128)(2,1)} %tie.67), channel_id=1, source_target_pairs={{0,8},{8,0},{16,24},{24,16},{1,9},{9,1},{17,25},{25,17},{2,10},{10... | collective-permute-start | bytes 3145736 | tf_op jit(solution)/shard_map/ppermute | solution.py:773
  1003.3 81.8 %collective-permute-start.22 = (bf16[512,1024]{1,0:T(8,128)(2,1)}, bf16[512,1024]{1,0:T(8,128)(2,1)}, u32[]{:S(2)}, u32[]{:S(2)}) collective-permute-start(bf16[512,1024]{1,0:T(8,128)(2,1)} %tie.69), channel_id=1, source_target_pairs={{0,16},{8,24},{16,0},{24,8},{1,17},{9,25},{17,1},{25,9},{2,18},{10... | collective-permute-start | bytes 3145736 | tf_op jit(solution)/shard_map/ppermute | solution.py:773
  1003.3 81.8 %collective-permute-start.23 = (bf16[512,1024]{1,0:T(8,128)(2,1)}, bf16[512,1024]{1,0:T(8,128)(2,1)}, u32[]{:S(2)}, u32[]{:S(2)}) collective-permute-start(bf16[512,1024]{1,0:T(8,128)(2,1)} %tie.70), channel_id=1, source_target_pairs={{0,24},{8,16},{16,8},{24,0},{1,25},{9,17},{17,9},{25,1},{2,26},{10... | collective-permute-start | bytes 3145736 | tf_op jit(solution)/shard_map/ppermute | solution.py:773
  1085.0 134.1 %reduce-scatter.4.cloned.1.call-start = ((), (), s32[]{:S(2)}) async-start(), calls=%async_computation.18 | async-start | bytes 7864320 | tf_op jit(solution)/shard_map/reduce_scatter | solution.py:900
  1102.3 178.5 %all-to-all-start.5 = ((bf16[8,480,2048]{2,1,0:T(8,128)(2,1)}), bf16[8,480,2048]{2,1,0:T(8,128)(2,1)}, u32[]{:S(2)}, u32[]{:S(2)}) async-start(bf16[8,480,2048]{2,1,0:T(8,128)(2,1)} %bitcast.291), calls=%async_computation.5 | async-start | bytes 31457280 | tf_op jit(solution)/shard_map/all_to_all | solution.py:897
  1108.1 300.1 %reduce-scatter.6.cloned.1.call-start = ((), (), s32[]{:S(2)}) async-start(), calls=%async_computation.19 | async-start | bytes 7864320 | tf_op jit(solution)/shard_map/reduce_scatter | solution.py:928
  1293.0 110.6 %all-to-all-start.8 = ((bf16[8,4,64,2048]{3,2,1,0:T(8,128)(2,1)}), bf16[8,4,64,2048]{3,2,1,0:T(8,128)(2,1)}, u32[]{:S(2)}, u32[]{:S(2)}) async-start(bf16[8,4,64,2048]{3,2,1,0:T(8,128)(2,1)} %tie.75), calls=%async_computation.10 | async-start | bytes 16777216 | tf_op jit(solution)/shard_map/all_to_all | solution.py:930
  1297.9 283.6 %reduce-scatter.8.cloned.1.call-start = ((), (), s32[]{:S(2)}) async-start(), calls=%async_computation.20 | async-start | bytes 7864320 | tf_op jit(solution)/shard_map/reduce_scatter | solution.py:950
  (115 other events, 2015.5 us)
Sparse Core Ops, SparseCore 0:
  73.0 114.4 all-gather.3
  192.2 114.5 all-gather.5
  374.2 115.7 all-gather.7
  1102.4 116.7 reduce-scatter.3
  1293.1 115.1 reduce-scatter.5
  1410.4 115.9 reduce-scatter.7

commit v11 on v9

--- a/solution.py
+++ b/solution.py
@@ -814,9 +814,9 @@
     select = holds.astype(bf16)
 
     def combine(rows):
-        rows = rows.reshape(columns, planes, capacity, width)
+        rows = rows.reshape(columns, planes, capacity, -1)
         sums = jnp.einsum("fbsr,fbsd->brd", select, rows, preferred_element_type=f32)
-        return sums.reshape(group_rows, width).astype(bf16)
+        return sums.reshape(group_rows, -1).astype(bf16)
 
 
     frequency = rope_base ** (
@@ -887,16 +887,18 @@
     )
     grad_gate_w = t_mm(rows_in, grad_gate).astype(bf16)
     came, up_grad = exchange_after(blocks(grad_up_w), [(part,) for part in came])
-    expert_out = mm(tie(act_picked, came[-1]), down).astype(bf16)
-    earlier = [(came[0], expert_out)] + [(part,) for part in came[1:]]
+    late_act = tie(act_picked, came[-1])
+    halves = [mm(late_act, half).astype(bf16) for half in jnp.split(down, 2, axis=1)]
+    earlier = [(came[0], *halves)] + [(part,) for part in came[1:]]
     came, gate_grad = exchange_after(blocks(grad_gate_w), earlier)
     grad_picked = lax.all_to_all(
         tie(grad_picked, grad_rows).reshape(columns, planes, capacity), "fsdp", 0, 0, tiled=True
     )
-    grad_rows = tie(grad_rows, *came, expert_out, grad_picked)
-    expert_out = lax.all_to_all(
-        expert_out.reshape(columns, planes * capacity, width), "fsdp", 0, 0, tiled=True
-    )
+    grad_rows = tie(grad_rows, *came, *halves, grad_picked)
+    halves = [
+        lax.all_to_all(half.reshape(columns, planes * capacity, -1), "fsdp", 0, 0, tiled=True)
+        for half in halves
+    ]
     grad_h_two = lax.psum_scatter(
         combine(grad_rows), "ctx", scatter_dimension=0, tiled=True
     ).astype(f32)
@@ -924,14 +926,17 @@
     grad_att = jnp.concatenate(by_plane([grad_heads(plane)] + came))
     grad_out_w = t_mm(attended, grad_branch).astype(bf16)
     grad_out_w = grad_out_w.reshape(planes, columns, strip, width).transpose(1, 0, 2, 3)
-    mixed_part = combine(tie(expert_out, grad_att, grad_out_w))
-    mixed = lax.psum_scatter(mixed_part, "ctx", scatter_dimension=0, tiled=True)
-    output = (middle + mixed.astype(f32)).astype(bf16)
+    first_part = combine(halves[0])
+    first_mixed = lax.psum_scatter(first_part, "ctx", scatter_dimension=0, tiled=True)
+    grad_att = tie(grad_att, first_part, grad_out_w)
+    grad_query, grad_key, grad_value = attend_back(seq_ids, query, key, values, grad_att)
+    last_part = combine(tie(halves[1], grad_query))
+    last_mixed = lax.psum_scatter(last_part, "ctx", scatter_dimension=0, tiled=True)
+    mixed = jnp.concatenate([first_mixed, last_mixed], axis=1).astype(f32)
+    output = (middle + mixed).astype(bf16)
     grad_out_w = lax.all_to_all(
-        tie(grad_out_w, mixed_part), "fsdp", 0, 0, tiled=True
-    )
-    grad_att = tie(grad_att, mixed_part)
-    grad_query, grad_key, grad_value = attend_back(seq_ids, query, key, values, grad_att)
+        tie(grad_out_w, last_part), "fsdp", 0, 0, tiled=True
+    )
     grad_query, grad_key, dots, grad_gains = turn_back(
         raw, scales, gains, cosine, sine, grad_query, grad_key
     )
@@ -948,7 +953,7 @@
     sums = t_mm(h_one, grad_qkv).astype(bf16)
     sums = sums.reshape(planes, columns, strip, -1).transpose(1, 0, 2, 3)
     grad_h_one = lax.psum_scatter(
-        tie(grad_part.astype(bf16), mixed, grad_out_w), "ctx", scatter_dimension=0, tiled=True
+        tie(grad_part.astype(bf16), first_mixed, last_mixed), "ctx", scatter_dimension=0, tiled=True
     ).astype(f32)
     grad_attn_gain = jnp.sum(grad_part * (hidden_wide * scale_one), axis=0)
     rows_of = jnp.arange(planes)[:, None] == plane
@@ -956,7 +961,7 @@
     gains = [g[:, None] for g in [grad_attn_gain, grad_ffn_gain] + gains]
     small = jnp.concatenate([grad_router] + gains, axis=1).reshape(planes, columns, -1)
     small = sum([small[plane]] + [swap(small[plane ^ step], step) for step in steps])
-    sums = lax.all_to_all(sums, "fsdp", 0, 0, tiled=True)
+    sums = lax.all_to_all(tie(sums, grad_out_w), "fsdp", 0, 0, tiled=True)
     grad_out_w = jnp.sum(grad_out_w.astype(f32), axis=0).astype(bf16)
     came_out = [swap(grad_out_w[plane ^ step], step) for step in steps]
     grad_out_w = sum(x.astype(f32) for x in [grad_out_w[plane]] + came_out)

time: 1600 us -> 1640 us (1.025)
  waiting for transfers between devices: 766 us -> 810 us
    reduce_scatter x1, waiting for transfers between devices: 94.3 us -> 0.02 us  [plane_shards(): lax.psum_scatter(combine(grad_rows), 'ctx', scatter_dimension=0, tiled=True)]
    all_to_all x3 -> x4, waiting for transfers between devices: 48.8 us -> 134 us  [the longest x2 86.8 us: plane_shards(): lax.all_to_all(half.reshape(columns, planes * capacity, -1), 'fsdp', 0, 0...]
    ppermute x39, waiting for transfers between devices: 231 us -> 290 us  [swap(): return lax.ppermute(part, 'ctx', [(i, i ^ step) for i in range(planes)])]
    dot_general x4 -> x5, matrix products: 46.2 us -> 48.5 us  [mm(): return jnp.dot(left, right, preferred_element_type=jnp.float32)]
    unnamed x176 -> x186, local copies, waits for them, and re-layouts: 42.4 us -> 41.3 us
  transfers between devices with their start and end apart: 57 -> 59, of which waited for: 31 -> 31; matrix products, arithmetic and copies ran while one was open for 21% -> 21% of each run, Pallas kernels for 12% -> 12%
where the time goes in v11:
time: 1640 us; the launch traced here: 1630 us
  waiting for transfers between devices  810 us (49%)
  Pallas kernels  220 us (13%)
  matrix products  191 us (12%)
  starting transfers between devices  163 us (10%)
  local copies, waits for them, and re-layouts  137 us (8%)
  other arithmetic  95.5 us (6%)
    ppermute x39, waiting for transfers between devices, swap(): return lax.ppermute(part, 'ctx', [(i, i ^ step) for i in range(planes)])  290 us
    all_gather x1, waiting for transfers between devices, plane_shards(): h_two_all = lax.all_gather(tie(h_two, grad_send), 'ctx', axis=0, tiled=True)  112 us
    ppermute x39, starting transfers between devices, swap(): return lax.ppermute(part, 'ctx', [(i, i ^ step) for i in range(planes)])  95.4 us
    dot_general x6, matrix products, t_mm(): lax.dot_general(left, right, (((0,), (0,)), ((), ())), preferred_element_...  87.8 us
    all_to_all x2, waiting for transfers between devices, plane_shards(): lax.all_to_all(half.reshape(columns, planes * capacity, -1), 'fsdp', 0, 0...  86.8 us
    all_to_all x1, waiting for transfers between devices, plane_shards(): packed = lax.all_to_all(packed, 'fsdp', 0, 0, tiled=True)  76 us
    all_to_all x1, waiting for transfers between devices, plane_shards(): lax.all_to_all(grad_rows.reshape(columns, planes * capacity, width), 'fsd...  73.2 us
    pallas_call x1, Pallas kernels, expert_back(): pl.pallas_call(expert_back_kernel, grid=(count // block,), in_specs=[wide...  63.4 us
  transfers between devices with their start and end apart: 59, of which 31 were waited for; matrix products, arithmetic and copies ran while one was open for 21% of the time, Pallas kernels for 12%

profile of v11, /device:TPU:0, one launch (start us, length us, event | category | flops | bytes accessed | tf_op | source)
XLA Modules:
  0.0 1633.0 jit_solution(5890419688553519166)
XLA Ops:
  28.8 42.8 %all-to-all-done.refs_1_ = bf16[4,64,3712]{2,1,0:T(8,128)(2,1)S(1)} async-done(((bf16[4,64,3712]{2,1,0:T(8,128)(2,1)}), bf16[4,64,3712]{2,1,0:T(8,128)(2,1)S(1)}, u32[]{:S(2)}, u32[]{:S(2)}) %all-to-all-start) | async-done | bytes 1900576 | tf_op jit(solution)/shard_map/all_to_all | solution.py:759
  84.1 76.0 %all-to-all-done.1 = bf16[8,4,64,1664]{3,2,1,0:T(8,128)(2,1)} async-done(((bf16[8,4,64,1664]{3,2,1,0:T(8,128)(2,1)}), bf16[8,4,64,1664]{3,2,1,0:T(8,128)(2,1)}, u32[]{:S(2)}, u32[]{:S(2)}) %all-to-all-start.1) | async-done | bytes 6815776 | tf_op jit(solution)/shard_map/all_to_all | solution.py:766
  166.6 21.0 %all-gather.4.cloned.1.call-done.refs_1_ = bf16[1536,2048]{1,0:T(8,128)(2,1)} async-done(((bf16[384,2048]{1,0:T(8,128)(2,1)}), bf16[1536,2048]{1,0:T(8,128)(2,1)}) %all-gather.4.cloned.1.call-update) | async-done | bytes 6291472 | tf_op jit(solution)/shard_map/all_gather | solution.py:760
  251.6 27.7 %attend.1.refs_1_ = bf16[1536,512]{1,0:T(8,128)(2,1)S(1)} custom-call(s32[1536,1]{1,0:T(8,128)S(1)} %broadcast_in_dim.171.seq_rows, s32[1,1536]{1,0:T(1,128)S(1)} %broadcast_in_dim.146.seq_cols, bf16[1536,512]{1,0:T(8,128)(2,1)S(1)} %get-tuple-element.32.query, bf16[1536,512]{1,0:T(8,128)(2,1)S(1)} %get-tuple-element.33.key, bf16[1536,512]{1,0:T(8,128)(2,1)} %copy-done.17), custom_call_target="tpu_custom_call" | custom-call | flops 4831838208 | bytes 6291456 | tf_op jit(solution)/shard_map/attend/pallas_call | solution.py:421
  340.2 21.3 %collective-permute-done.4 = bf16[384,512]{1,0:T(8,128)(2,1)S(1)} collective-permute-done((bf16[384,512]{1,0:T(8,128)(2,1)}, bf16[384,512]{1,0:T(8,128)(2,1)S(1)}, u32[]{:S(2)}, u32[]{:S(2)}) %collective-permute-start.4) | collective-permute-done | bytes 393248 | tf_op jit(solution)/shard_map/ppermute | solution.py:773
  378.0 111.7 %all-gather.8.cloned.1.call-done.refs_1_.refs_0_ = bf16[1536,2048]{1,0:T(8,128)(2,1)} async-done(((bf16[384,2048]{1,0:T(8,128)(2,1)}), bf16[1536,2048]{1,0:T(8,128)(2,1)}) %all-gather.8.cloned.1.call-update) | async-done | bytes 6291472 | tf_op jit(solution)/shard_map/all_gather | solution.py:853
  490.4 45.9 %collective-permute-done.6.refs_2_.refs_1_ = bf16[512,1024]{1,0:T(8,128)(2,1)S(1)} collective-permute-done((bf16[512,1024]{1,0:T(8,128)(2,1)}, bf16[512,1024]{1,0:T(8,128)(2,1)S(1)}, u32[]{:S(2)}, u32[]{:S(2)}) %collective-permute-start.6) | collective-permute-done | bytes 1048608 | tf_op jit(solution)/shard_map/ppermute | solution.py:773
  565.8 19.0 %collective-permute-done.8.refs_1_ = bf16[512,1024]{1,0:T(8,128)(2,1)S(1)} collective-permute-done((bf16[512,1024]{1,0:T(8,128)(2,1)}, bf16[512,1024]{1,0:T(8,128)(2,1)S(1)}, u32[]{:S(2)}, u32[]{:S(2)}) %collective-permute-start.8) | collective-permute-done | bytes 1048608 | tf_op jit(solution)/shard_map/ppermute | solution.py:773
  588.2 18.9 %collective-permute-start.10 = (bf16[512,1024]{1,0:T(8,128)(2,1)}, bf16[512,1024]{1,0:T(8,128)(2,1)}, u32[]{:S(2)}, u32[]{:S(2)}) collective-permute-start(bf16[512,1024]{1,0:T(8,128)(2,1)} %tie.52), channel_id=1, source_target_pairs={{0,16},{8,24},{16,0},{24,8},{1,17},{9,25},{17,1},{25,9},{2,18},{10... | collective-permute-start | bytes 3145736 | tf_op jit(solution)/shard_map/ppermute | solution.py:773
  629.9 66.9 %collective-permute-done.10.refs_2_ = bf16[512,1024]{1,0:T(8,128)(2,1)} collective-permute-done((bf16[512,1024]{1,0:T(8,128)(2,1)}, bf16[512,1024]{1,0:T(8,128)(2,1)}, u32[]{:S(2)}, u32[]{:S(2)}) %collective-permute-start.10) | collective-permute-done | bytes 1048608 | tf_op jit(solution)/shard_map/ppermute | solution.py:773
  706.1 23.3 %all-to-all-done.4 = bf16[8,4,120,2048]{3,2,1,0:T(8,128)(2,1)} async-done(((bf16[8,4,120,2048]{3,2,1,0:T(8,128)(2,1)}), bf16[8,4,120,2048]{3,2,1,0:T(8,128)(2,1)}, u32[]{:S(2)}, u32[]{:S(2)}) %all-to-all-start.4) | async-done | bytes 15728672 | tf_op jit(solution)/shard_map/all_to_all | solution.py:864
  729.4 44.6 %expert_in.1 = (f32[3840,1024]{1,0:T(8,128)}, f32[3840,1024]{1,0:T(8,128)}, bf16[3840,1024]{1,0:T(8,128)(2,1)}, f32[3840,1]{1,0:T(8,128)}) custom-call(bf16[3840,2048]{1,0:T(8,128)(2,1)} %bitcast.37.rows, bf16[2048,1024]{1,0:T(8,128)(2,1)} %pad_maximum_fusion.2.gate, bf16[2048,1024]{1,0:T(8,128)(2,1)} %pad_maximum_fusion.4.up, ...), custom_call_target="tpu_custom_call" | custom-call | flops 32212254720 | bytes 63438848 | tf_op jit(solution)/shard_map/expert_in/pallas_call | solution.py:638
  774.0 22.5 %convolution_convert_fusion.6.refs_1_ = bf16[1024,2048]{1,0:T(8,128)(2,1)} fusion(bf16[3840,1024]{1,0:T(8,128)(2,1)} %get-tuple-element.35.refs_1_.refs_0_, bf16[3840,2048]{1,0:T(8,128)(2,1)} %bitcast.34.refs_1_.grad), kind=kOutput, calls=%fused_computation.44 | convolution fusion | flops 16108224512 | bytes 27787264 | tf_op jit(solution)/shard_map/dot_general | solution.py:714
  812.9 63.4 %expert_back.1 = (bf16[3840,1024]{1,0:T(8,128)(2,1)}, bf16[3840,1024]{1,0:T(8,128)(2,1)}, f32[3840,1]{1,0:T(8,128)}, bf16[3840,2048]{1,0:T(8,128)(2,1)}) custom-call(bf16[3840,2048]{1,0:T(8,128)(2,1)} %bitcast.34.refs_1_.grad, f32[3840,1024]{1,0:T(8,128)} %tie.54.gate_in, f32[3840,1024]{1,0:T(8,128)} %get-tuple-element.37.up_in, ...), custom_call_target="tpu_custom_call" | custom-call | flops 48318382080 | bytes 91226112 | tf_op jit(solution)/shard_map/expert_back/pallas_call | solution.py:670
  876.3 22.5 %convolution_convert_fusion.5.refs_4_ = bf16[2048,1024]{1,0:T(8,128)(2,1)} fusion(bf16[3840,2048]{1,0:T(8,128)(2,1)} %bitcast.37.rows, bf16[3840,1024]{1,0:T(8,128)(2,1)} %get-tuple-element.39), kind=kOutput, calls=%fused_computation.43 | convolution fusion | flops 16108224512 | bytes 27787264 | tf_op jit(solution)/shard_map/dot_general | solution.py:714
  912.5 21.4 %convolution_convert_fusion.4 = bf16[2048,1024]{1,0:T(8,128)(2,1)S(1)} fusion(bf16[3840,2048]{1,0:T(8,128)(2,1)} %bitcast.37.rows, bf16[3840,1024]{1,0:T(8,128)(2,1)} %get-tuple-element.41), kind=kOutput, calls=%fused_computation.42 | convolution fusion | flops 16108224512 | bytes 27787264 | tf_op jit(solution)/shard_map/dot_general | solution.py:714
  965.1 19.1 %collective-permute-start.20 = (bf16[512,1024]{1,0:T(8,128)(2,1)}, bf16[512,1024]{1,0:T(8,128)(2,1)S(1)}, u32[]{:S(2)}, u32[]{:S(2)}) collective-permute-start(bf16[512,1024]{1,0:T(8,128)(2,1)} %tie.65), channel_id=1, source_target_pairs={{0,8},{8,0},{16,24},{24,16},{1,9},{9,1},{17,25},{25,17},{2,10},{10... | collective-permute-start | bytes 3145736 | tf_op jit(solution)/shard_map/ppermute | solution.py:773
  984.3 18.7 %collective-permute-done.21.refs_1_ = bf16[512,1024]{1,0:T(8,128)(2,1)} collective-permute-done((bf16[512,1024]{1,0:T(8,128)(2,1)}, bf16[512,1024]{1,0:T(8,128)(2,1)}, u32[]{:S(2)}, u32[]{:S(2)}) %collective-permute-start.21) | collective-permute-done | bytes 1048608 | tf_op jit(solution)/shard_map/ppermute | solution.py:773
  1005.4 73.2 %all-to-all-done.7.refs_1_.refs_0_ = bf16[8,480,2048]{2,1,0:T(8,128)(2,1)} async-done(((bf16[8,480,2048]{2,1,0:T(8,128)(2,1)}), bf16[8,480,2048]{2,1,0:T(8,128)(2,1)}, u32[]{:S(2)}, u32[]{:S(2)}) %all-to-all-start.7) | async-done | bytes 15728672 | tf_op jit(solution)/shard_map/all_to_all | solution.py:885
  1108.8 86.8 %all-to-all-done.5 = bf16[8,480,1024]{2,1,0:T(8,128)(2,1)} async-done(((bf16[8,480,1024]{2,1,0:T(8,128)(2,1)}), bf16[8,480,1024]{2,1,0:T(8,128)(2,1)}, u32[]{:S(2)}, u32[]{:S(2)}) %all-to-all-start.5) | async-done | bytes 7864352 | tf_op jit(solution)/shard_map/all_to_all | solution.py:899
  1255.5 52.9 %collective-permute-done.28 = bf16[384,512]{1,0:T(8,128)(2,1)S(1)} collective-permute-done((bf16[384,512]{1,0:T(8,128)(2,1)S(1)}, bf16[384,512]{1,0:T(8,128)(2,1)S(1)}, u32[]{:S(2)}, u32[]{:S(2)}) %collective-permute-start.28) | collective-permute-done | bytes 393248 | tf_op jit(solution)/shard_map/ppermute | solution.py:773
  1314.2 45.7 %attend_back.1 = (f32[1536,512]{1,0:T(8,128)}, f32[1536,512]{1,0:T(8,128)}, f32[1536,512]{1,0:T(8,128)}) custom-call(s32[1536,1]{1,0:T(8,128)S(1)} %broadcast_in_dim.171.seq_rows, s32[1,1536]{1,0:T(1,128)S(1)} %broadcast_in_dim.146.seq_cols, bf16[1536,512]{1,0:T(8,128)(2,1)S(1)} %copy-done.14, bf16[1536,512]{1,0:T(8,128)(2,1)S(1)} %copy-done.16, ...), custom_call_target="tpu_custom_call" | custom-call | flops 12079595520 | bytes 15728640 | tf_op jit(solution)/shard_map/attend_back/pallas_call | solution.py:440
  1447.2 43.1 %all-to-all-done.9.refs_1_ = bf16[8,4,64,2048]{3,2,1,0:T(8,128)(2,1)} async-done(((bf16[8,4,64,2048]{3,2,1,0:T(8,128)(2,1)}), bf16[8,4,64,2048]{3,2,1,0:T(8,128)(2,1)}, u32[]{:S(2)}, u32[]{:S(2)}) %all-to-all-start.9) | async-done | bytes 8388640 | tf_op jit(solution)/shard_map/all_to_all | solution.py:937
  1533.1 16.6 %collective-permute-done.36.refs_2_ = bf16[64,2048]{1,0:T(8,128)(2,1)S(1)} collective-permute-done((bf16[64,2048]{1,0:T(8,128)(2,1)S(1)}, bf16[64,2048]{1,0:T(8,128)(2,1)S(1)}, u32[]{:S(2)}, u32[]{:S(2)}) %collective-permute-start.36) | collective-permute-done | bytes 262176 | tf_op jit(solution)/shard_map/ppermute | solution.py:773
  (512 shorter events, 611.8 us)
Async XLA Ops:
  27.7 159.9 %all-gather.4.cloned.1.call-start = ((), (), s32[]{:S(2)}) async-start(), calls=%async_computation.17 | async-start | bytes 7864320 | tf_op jit(solution)/shard_map/all_gather | solution.py:760
  77.9 82.3 %all-to-all-start.1 = ((bf16[8,4,64,1664]{3,2,1,0:T(8,128)(2,1)}), bf16[8,4,64,1664]{3,2,1,0:T(8,128)(2,1)}, u32[]{:S(2)}, u32[]{:S(2)}) async-start(bf16[8,4,64,1664]{3,2,1,0:T(8,128)(2,1)} %broadcast_in_dim.153), calls=%async_computation.1 | async-start | bytes 13631488 | tf_op jit(solution)/shard_map/all_to_all | solution.py:766
  82.9 223.8 %all-gather.6.cloned.1.call-start = ((), (), s32[]{:S(2)}) async-start(), calls=%async_computation.18 | async-start | bytes 7864320 | tf_op jit(solution)/shard_map/all_gather | solution.py:799
  193.0 99.3 %all-to-all-start.2 = ((bf16[8,4,64,2048]{3,2,1,0:T(8,128)(2,1)}), bf16[8,4,64,2048]{3,2,1,0:T(8,128)(2,1)}, u32[]{:S(2)}, u32[]{:S(2)}) async-start(bf16[8,4,64,2048]{3,2,1,0:T(8,128)(2,1)} %broadcast_in_dim.157.refs_3_), calls=%async_computation.2 | async-start | bytes 16777216 | tf_op jit(solution)/shard_map/all_to_all | solution.py:802
  320.4 216.0 %all-to-all-start.3 = ((bf16[8,4,120,2048]{3,2,1,0:T(8,128)(2,1)}), bf16[8,4,120,2048]{3,2,1,0:T(8,128)(2,1)}, u32[]{:S(2)}, u32[]{:S(2)}) async-start(bf16[8,4,120,2048]{3,2,1,0:T(8,128)(2,1)} %dispatch.2.refs_1_), calls=%async_computation.3 | async-start | bytes 31457280 | tf_op jit(solution)/shard_map/all_to_all | solution.py:847
  326.0 163.8 %all-gather.8.cloned.1.call-start = ((), (), s32[]{:S(2)}) async-start(), calls=%async_computation.19 | async-start | bytes 7864320 | tf_op jit(solution)/shard_map/all_gather | solution.py:853
  550.9 178.5 %all-to-all-start.4 = ((bf16[8,4,120,2048]{3,2,1,0:T(8,128)(2,1)}), bf16[8,4,120,2048]{3,2,1,0:T(8,128)(2,1)}, u32[]{:S(2)}, u32[]{:S(2)}) async-start(bf16[8,4,120,2048]{3,2,1,0:T(8,128)(2,1)} %dispatch.3), calls=%async_computation.4 | async-start | bytes 31457280 | tf_op jit(solution)/shard_map/all_to_all | solution.py:864
  588.2 108.6 %collective-permute-start.10 = (bf16[512,1024]{1,0:T(8,128)(2,1)}, bf16[512,1024]{1,0:T(8,128)(2,1)}, u32[]{:S(2)}, u32[]{:S(2)}) collective-permute-start(bf16[512,1024]{1,0:T(8,128)(2,1)} %tie.52), channel_id=1, source_target_pairs={{0,16},{8,24},{16,0},{24,8},{1,17},{9,25},{17,1},{25,9},{2,18},{10... | collective-permute-start | bytes 3145736 | tf_op jit(solution)/shard_map/ppermute | solution.py:773
  607.4 89.4 %collective-permute-start.9 = (bf16[512,1024]{1,0:T(8,128)(2,1)}, bf16[512,1024]{1,0:T(8,128)(2,1)}, u32[]{:S(2)}, u32[]{:S(2)}) collective-permute-start(bf16[512,1024]{1,0:T(8,128)(2,1)} %tie.51), channel_id=1, source_target_pairs={{0,8},{8,0},{16,24},{24,16},{1,9},{9,1},{17,25},{25,17},{2,10},{10... | collective-permute-start | bytes 3145736 | tf_op jit(solution)/shard_map/ppermute | solution.py:773
  696.8 99.6 %collective-permute-start.14 = (bf16[256,2048]{1,0:T(8,128)(2,1)}, bf16[256,2048]{1,0:T(8,128)(2,1)}, u32[]{:S(2)}, u32[]{:S(2)}) collective-permute-start(bf16[256,2048]{1,0:T(8,128)(2,1)} %tie.59), channel_id=1, source_target_pairs={{0,24},{8,16},{16,8},{24,0},{1,25},{9,17},{17,9},{25,1},{2,26},{10... | collective-permute-start | bytes 3145736 | tf_op jit(solution)/shard_map/ppermute | solution.py:773
  698.9 97.6 %collective-permute-start.13 = (bf16[256,2048]{1,0:T(8,128)(2,1)}, bf16[256,2048]{1,0:T(8,128)(2,1)}, u32[]{:S(2)}, u32[]{:S(2)}) collective-permute-start(bf16[256,2048]{1,0:T(8,128)(2,1)} %tie.57), channel_id=1, source_target_pairs={{0,16},{8,24},{16,0},{24,8},{1,17},{9,25},{17,1},{25,9},{2,18},{10... | collective-permute-start | bytes 3145736 | tf_op jit(solution)/shard_map/ppermute | solution.py:773
  698.9 97.6 %collective-permute-start.12 = (bf16[256,2048]{1,0:T(8,128)(2,1)}, bf16[256,2048]{1,0:T(8,128)(2,1)}, u32[]{:S(2)}, u32[]{:S(2)}) collective-permute-start(bf16[256,2048]{1,0:T(8,128)(2,1)} %tie.55), channel_id=1, source_target_pairs={{0,8},{8,0},{16,24},{24,16},{1,9},{9,1},{17,25},{25,17},{2,10},{10... | collective-permute-start | bytes 3145736 | tf_op jit(solution)/shard_map/ppermute | solution.py:773
  806.2 92.6 %collective-permute-start.15 = (bf16[256,2048]{1,0:T(8,128)(2,1)}, bf16[256,2048]{1,0:T(8,128)(2,1)S(1)}, u32[]{:S(2)}, u32[]{:S(2)}) collective-permute-start(bf16[256,2048]{1,0:T(8,128)(2,1)} %get-tuple-element.165), channel_id=1, source_target_pairs={{0,24},{8,16},{16,8},{24,0},{1,25},{9,17},{17,9},{25,1},{2,26},{10... | collective-permute-start | bytes 3145736 | tf_op jit(solution)/shard_map/ppermute | solution.py:773
  808.6 90.2 %collective-permute-start.17 = (bf16[256,2048]{1,0:T(8,128)(2,1)S(1)}, bf16[256,2048]{1,0:T(8,128)(2,1)}, u32[]{:S(2)}, u32[]{:S(2)}) collective-permute-start(bf16[256,2048]{1,0:T(8,128)(2,1)S(1)} %get-tuple-element.164), channel_id=1, source_target_pairs={{0,8},{8,0},{16,24},{24,16},{1,9},{9,1},{17,25},{25,17},{2,10},{10... | collective-permute-start | bytes 3145736 | tf_op jit(solution)/shard_map/ppermute | solution.py:773
  808.6 90.2 %collective-permute-start.18 = (bf16[256,2048]{1,0:T(8,128)(2,1)S(1)}, bf16[256,2048]{1,0:T(8,128)(2,1)}, u32[]{:S(2)}, u32[]{:S(2)}) collective-permute-start(bf16[256,2048]{1,0:T(8,128)(2,1)S(1)} %get-tuple-element.163), channel_id=1, source_target_pairs={{0,16},{8,24},{16,0},{24,8},{1,17},{9,25},{17,1},{25,9},{2,18},{10... | collective-permute-start | bytes 3145736 | tf_op jit(solution)/shard_map/ppermute | solution.py:773
  899.8 178.7 %all-to-all-start.7 = ((bf16[8,480,2048]{2,1,0:T(8,128)(2,1)}), bf16[8,480,2048]{2,1,0:T(8,128)(2,1)}, u32[]{:S(2)}, u32[]{:S(2)}) async-start(bf16[8,480,2048]{2,1,0:T(8,128)(2,1)} %bitcast.300), calls=%async_computation.8 | async-start | bytes 31457280 | tf_op jit(solution)/shard_map/all_to_all | solution.py:885
  965.1 119.7 %collective-permute-start.20 = (bf16[512,1024]{1,0:T(8,128)(2,1)}, bf16[512,1024]{1,0:T(8,128)(2,1)S(1)}, u32[]{:S(2)}, u32[]{:S(2)}) collective-permute-start(bf16[512,1024]{1,0:T(8,128)(2,1)} %tie.65), channel_id=1, source_target_pairs={{0,8},{8,0},{16,24},{24,16},{1,9},{9,1},{17,25},{25,17},{2,10},{10... | collective-permute-start | bytes 3145736 | tf_op jit(solution)/shard_map/ppermute | solution.py:773
  1084.7 135.6 %reduce-scatter.7.cloned.1.call-start = ((), (), s32[]{:S(2)}) async-start(), calls=%async_computation.21 | async-start | bytes 7864320 | tf_op jit(solution)/shard_map/reduce_scatter | solution.py:902
  1102.1 93.5 %all-to-all-start.5 = ((bf16[8,480,1024]{2,1,0:T(8,128)(2,1)}), bf16[8,480,1024]{2,1,0:T(8,128)(2,1)}, u32[]{:S(2)}, u32[]{:S(2)}) async-start(bf16[8,480,1024]{2,1,0:T(8,128)(2,1)} %bitcast.299), calls=%async_computation.5 | async-start | bytes 15728640 | tf_op jit(solution)/shard_map/all_to_all | solution.py:899
  1195.6 164.3 %all-to-all-start.6 = ((bf16[8,480,1024]{2,1,0:T(8,128)(2,1)}), bf16[8,480,1024]{2,1,0:T(8,128)(2,1)}, u32[]{:S(2)}, u32[]{:S(2)}) async-start(bf16[8,480,1024]{2,1,0:T(8,128)(2,1)} %bitcast.298), calls=%async_computation.7 | async-start | bytes 15728640 | tf_op jit(solution)/shard_map/all_to_all | solution.py:899
  1200.7 219.8 %reduce-scatter.5.cloned.1.call-start = ((), (), s32[]{:S(2)}) async-start(), calls=%async_computation.20 | async-start | bytes 3932160 | tf_op jit(solution)/shard_map/reduce_scatter | solution.py:930
  1219.9 209.8 %reduce-scatter.9.cloned.1.call-start = ((), (), s32[]{:S(2)}) async-start(), calls=%async_computation.22 | async-start | bytes 3932160 | tf_op jit(solution)/shard_map/reduce_scatter | solution.py:934
  1391.3 99.0 %all-to-all-start.9 = ((bf16[8,4,64,2048]{3,2,1,0:T(8,128)(2,1)}), bf16[8,4,64,2048]{3,2,1,0:T(8,128)(2,1)}, u32[]{:S(2)}, u32[]{:S(2)}) async-start(bf16[8,4,64,2048]{3,2,1,0:T(8,128)(2,1)} %tie.74), calls=%async_computation.13 | async-start | bytes 16777216 | tf_op jit(solution)/shard_map/all_to_all | solution.py:937
  1396.3 223.2 %reduce-scatter.11.cloned.1.call-start = ((), (), s32[]{:S(2)}) async-start(), calls=%async_computation.23 | async-start | bytes 7864320 | tf_op jit(solution)/shard_map/reduce_scatter | solution.py:955
  (124 other events, 1952.9 us)
Sparse Core Ops, SparseCore 0:
  73.1 114.4 all-gather.3
  192.2 114.5 all-gather.5
  373.9 115.7 all-gather.7
  1102.2 117.1 reduce-scatter.6
  1221.5 89.0 reduce-scatter.4
  1368.6 61.0 reduce-scatter.8
  1432.0 132.1 reduce-scatter.10
